TPU v7x, 32 devices: a whole 2x2x4 slice. The times are simulated.
32 devices in a mesh: chaos: 4 (over x, core), tile: 8 (over z, y).
Axes of the slice: x: 2, y: 2, z: 4, core: 2. Of those that a mesh axis runs over, the one named last changes fastest.
Arguments:
- slot_field: float32 [288, 64, 1024], P('chaos', 'tile'), may hold values from -6 to 6
- stiffness: float32 [11, 64, 1024], P(None, 'tile'), may hold values from -6 to 6
- triple_modes: int32 [1606], replicated, may hold values from 0 to 10, as said below
- triple_rows: int32 [1606], replicated, may hold values from 0 to 285
- triple_cols: int32 [1606], replicated, may hold values from 0 to 285
- triple_weights: bfloat16 [1606], replicated
- slot_of: int32 [288], replicated, may hold values from 0 to 287, each once
Outputs:
- first_apply: float32 [288, 64, 1024], P('chaos', 'tile')
- second_apply: float32 [288, 64, 1024], P('chaos', 'tile')
Inputs may be any that keep to these rules, and one draw needn't show every extreme that they name: slot_of is a permutation of the slots; entry c for c < 286 is the slot of chaos index c, the remaining slots hold no chaos index. `triple_modes`: the entries list the nonzero Galerkin triple products of the order-3 Hermite chaos in 10 variables, each (mode, row, col) once, in some order: mode 0 pairs each chaos index with itself, mode k pairs chaos indices whose multi-indices differ by one in variable k.
All inputs are finite; a program needn't handle non-finite values.
Results may differ from a plain program's by a relative error of at most 0.0034.
Values may be sent and summed in bfloat16 or wider, within the bound.
No kernel may reach another device: no remote copies, remote signals or barrier semaphores. Data moves between devices by JAX's collectives and lax.ppermute only.
A program may use at most 64 MiB of HBM per device.

v0:
```python
import jax
import jax.numpy as jnp
from jax import lax
from jax.sharding import PartitionSpec as P


def extended_2(block, sides, width):
    for axis, dim in sides:
        count = lax.axis_size(axis)
        forward = [(i, i + 1) for i in range(count - 1)]
        backward = [(target, source) for source, target in forward]
        low = lax.ppermute(
            lax.slice_in_dim(block, block.shape[dim] - width, None, axis=dim), axis, forward
        )
        high = lax.ppermute(lax.slice_in_dim(block, 0, width, axis=dim), axis, backward)
        block = jnp.concatenate([low, block, high], axis=dim)
    return block


def five_point(extended):
    padded = jnp.pad(extended, ((0, 0), (0, 0), (1, 1)))
    center = padded[:, 1:-1, 1:-1]
    return (
        padded[:, 2:, 1:-1]
        + padded[:, :-2, 1:-1]
        + padded[:, 1:-1, 2:]
        + padded[:, 1:-1, :-2]
        - 4.0 * center
    )


def couple(bent, stiffness, tables):
    slot_local = bent.shape[0]
    band_rows = bent.shape[1]
    flattened = bent.reshape(slot_local, -1)
    stiff_flat = stiffness.reshape(stiffness.shape[0], -1)
    term_count = stiffness.shape[0]
    own_start = lax.axis_index("chaos") * slot_local
    col_tables = lax.dynamic_slice_in_dim(tables, own_start, slot_local, 2)

    def add_mode(mode, running):
        product = jnp.dot(col_tables[mode], flattened, preferred_element_type=jnp.float32)
        return running + stiff_flat[mode][None, :] * product

    start_total = jnp.zeros((slot_local * lax.axis_size("chaos"), flattened.shape[1]), jnp.float32)
    moment = lax.psum_scatter(
        lax.fori_loop(0, term_count, add_mode, start_total),
        "chaos",
        scatter_dimension=0,
        tiled=True,
    )
    return moment.reshape(slot_local, band_rows, -1)


def body(slot_field, stiffness, triple_modes, triple_rows, triple_cols, triple_weights, slot_of):
    slot_total = slot_field.shape[0] * lax.axis_size("chaos")
    term_count = stiffness.shape[0]
    tables = jnp.zeros((term_count, slot_total, slot_total), jnp.float32)
    tables = tables.at[triple_modes, slot_of[triple_rows], slot_of[triple_cols]].add(
        triple_weights.astype(jnp.float32)
    )
    tables = tables.astype(jnp.bfloat16)

    def operator_apply(current):
        extended = extended_2(current, (("tile", 1),), 1)
        bent = five_point(extended).astype(jnp.bfloat16)
        moment = couple(bent, stiffness, tables)
        moment_wide = extended_2(moment, (("tile", 1),), 1)
        return five_point(moment_wide)

    first_apply = operator_apply(slot_field)
    second_apply = operator_apply(first_apply)
    return (first_apply, second_apply)


def solution(mesh):
    return jax.shard_map(
        body,
        mesh=mesh,
        in_specs=(P("chaos", "tile", None), P(None, "tile", None), P(), P(), P(), P(), P()),
        out_specs=(P("chaos", "tile", None), P("chaos", "tile", None)),
        check_vma=False,
    )
```

profile of v0, /device:TPU:0, one launch (start us, length us, event | category | flops | bytes accessed | tf_op | source)
XLA Modules:
  0.0 522.7 jit_solution(13746869586444172898)
XLA Ops:
  18.6 10.3 %gather_fusion = s32[1606]{0:T(1024)S(1)} fusion(s32[288]{0:T(512)S(1)} %copy-done, s32[2048]{0:T(1024)S(1)} %pad_clamp_fusion.1), kind=kCustom, calls=%fused_computation | custom fusion | bytes 19272 | tf_op jit(solution)/shard_map/gather | solution.py:59
  28.9 10.3 %gather_fusion.1 = s32[1606]{0:T(1024)S(1)} fusion(s32[288]{0:T(512)S(1)} %copy-done, s32[2048]{0:T(1024)S(1)} %pad_clamp_fusion), kind=kCustom, calls=%fused_computation.1 | custom fusion | bytes 19272 | tf_op jit(solution)/shard_map/gather | solution.py:59
  39.5 12.1 %scatter_custom_fusion = f32[912384]{0:T(1024)} fusion(s32[1606]{0:T(1024)S(1)} %broadcast_select_fusion, f32[1606]{0:T(1024)S(1)} %convert_element_type.17, f32[]{:T(128)} %constant.59.clone.1), kind=kCustom, calls=%fused_computation.52 | custom fusion | flops 1606 | bytes 3649540
  69.8 103.7 %while.28 = (s32[]{:T(128)}, f32[288,8192]{1,0:T(8,128)}, f32[11,8192]{1,0:T(8,128)}, bf16[11,288,72]{2,1,0:T(8,128)(2,1)S(1)}, bf16[72,8192]{1,0:T(8,128)(2,1)S(1)}, /*index=5*/s32[]{:T(128)}, s32[]{:T(128)}) while((s32[]{:T(128)}, f32[288,8192]{1,0:T(8,128)}, f32[11,8192]{1,0:T(8,128)}, bf16[11,288,72]{2,1,0:T(8,128)(2,1)S(1)}, ...), condition=%wide.region_2.3_spmd.clone, body=%wide.region_1.2_spmd.clone.sunk | while | flops 346816512 | bytes 20226140 | solution.py:47
  86.6 8.8 %fusion.35 = f32[288,8192]{1,0:T(8,128)} fusion(bf16[72,8192]{1,0:T(8,128)(2,1)S(1)} %get-tuple-element.340, f32[288,8192]{1,0:T(8,128)} %get-tuple-element.330, f32[8192]{0:T(1024)S(1)} %bitcast.41, pred[]{:T(512)S(6)} %compare.60, bf16[11,288,72]{2,1,0:T(8,128)(2,1)S(1)} %get-tuple-element.339, s32[]{:T(128)} %get-tuple-element.329), kind=kOutput, calls=%fused_computation.4.clone.1 | convolution fusion | flops 346816512 | bytes 20160516 | tf_op jit(solution)/shard_map/while/body/eval_jaxpr/dot_general | solution.py:42
  96.4 8.8 %fusion.35 = f32[288,8192]{1,0:T(8,128)} fusion(bf16[72,8192]{1,0:T(8,128)(2,1)S(1)} %get-tuple-element.340, f32[288,8192]{1,0:T(8,128)} %get-tuple-element.330, f32[8192]{0:T(1024)S(1)} %bitcast.41, pred[]{:T(512)S(6)} %compare.60, bf16[11,288,72]{2,1,0:T(8,128)(2,1)S(1)} %get-tuple-element.339, s32[]{:T(128)} %get-tuple-element.329), kind=kOutput, calls=%fused_computation.4.clone.1 | convolution fusion | flops 346816512 | bytes 20160516 | tf_op jit(solution)/shard_map/while/body/eval_jaxpr/dot_general | solution.py:42
  106.2 8.8 %fusion.35 = f32[288,8192]{1,0:T(8,128)} fusion(bf16[72,8192]{1,0:T(8,128)(2,1)S(1)} %get-tuple-element.340, f32[288,8192]{1,0:T(8,128)} %get-tuple-element.330, f32[8192]{0:T(1024)S(1)} %bitcast.41, pred[]{:T(512)S(6)} %compare.60, bf16[11,288,72]{2,1,0:T(8,128)(2,1)S(1)} %get-tuple-element.339, s32[]{:T(128)} %get-tuple-element.329), kind=kOutput, calls=%fused_computation.4.clone.1 | convolution fusion | flops 346816512 | bytes 20160516 | tf_op jit(solution)/shard_map/while/body/eval_jaxpr/dot_general | solution.py:42
  115.9 8.8 %fusion.35 = f32[288,8192]{1,0:T(8,128)} fusion(bf16[72,8192]{1,0:T(8,128)(2,1)S(1)} %get-tuple-element.340, f32[288,8192]{1,0:T(8,128)} %get-tuple-element.330, f32[8192]{0:T(1024)S(1)} %bitcast.41, pred[]{:T(512)S(6)} %compare.60, bf16[11,288,72]{2,1,0:T(8,128)(2,1)S(1)} %get-tuple-element.339, s32[]{:T(128)} %get-tuple-element.329), kind=kOutput, calls=%fused_computation.4.clone.1 | convolution fusion | flops 346816512 | bytes 20160516 | tf_op jit(solution)/shard_map/while/body/eval_jaxpr/dot_general | solution.py:42
  125.7 8.8 %fusion.35 = f32[288,8192]{1,0:T(8,128)} fusion(bf16[72,8192]{1,0:T(8,128)(2,1)S(1)} %get-tuple-element.340, f32[288,8192]{1,0:T(8,128)} %get-tuple-element.330, f32[8192]{0:T(1024)S(1)} %bitcast.41, pred[]{:T(512)S(6)} %compare.60, bf16[11,288,72]{2,1,0:T(8,128)(2,1)S(1)} %get-tuple-element.339, s32[]{:T(128)} %get-tuple-element.329), kind=kOutput, calls=%fused_computation.4.clone.1 | convolution fusion | flops 346816512 | bytes 20160516 | tf_op jit(solution)/shard_map/while/body/eval_jaxpr/dot_general | solution.py:42
  135.4 8.8 %fusion.35 = f32[288,8192]{1,0:T(8,128)} fusion(bf16[72,8192]{1,0:T(8,128)(2,1)S(1)} %get-tuple-element.340, f32[288,8192]{1,0:T(8,128)} %get-tuple-element.330, f32[8192]{0:T(1024)S(1)} %bitcast.41, pred[]{:T(512)S(6)} %compare.60, bf16[11,288,72]{2,1,0:T(8,128)(2,1)S(1)} %get-tuple-element.339, s32[]{:T(128)} %get-tuple-element.329), kind=kOutput, calls=%fused_computation.4.clone.1 | convolution fusion | flops 346816512 | bytes 20160516 | tf_op jit(solution)/shard_map/while/body/eval_jaxpr/dot_general | solution.py:42
  145.2 8.8 %fusion.35 = f32[288,8192]{1,0:T(8,128)} fusion(bf16[72,8192]{1,0:T(8,128)(2,1)S(1)} %get-tuple-element.340, f32[288,8192]{1,0:T(8,128)} %get-tuple-element.330, f32[8192]{0:T(1024)S(1)} %bitcast.41, pred[]{:T(512)S(6)} %compare.60, bf16[11,288,72]{2,1,0:T(8,128)(2,1)S(1)} %get-tuple-element.339, s32[]{:T(128)} %get-tuple-element.329), kind=kOutput, calls=%fused_computation.4.clone.1 | convolution fusion | flops 346816512 | bytes 20160516 | tf_op jit(solution)/shard_map/while/body/eval_jaxpr/dot_general | solution.py:42
  154.9 8.8 %fusion.35 = f32[288,8192]{1,0:T(8,128)} fusion(bf16[72,8192]{1,0:T(8,128)(2,1)S(1)} %get-tuple-element.340, f32[288,8192]{1,0:T(8,128)} %get-tuple-element.330, f32[8192]{0:T(1024)S(1)} %bitcast.41, pred[]{:T(512)S(6)} %compare.60, bf16[11,288,72]{2,1,0:T(8,128)(2,1)S(1)} %get-tuple-element.339, s32[]{:T(128)} %get-tuple-element.329), kind=kOutput, calls=%fused_computation.4.clone.1 | convolution fusion | flops 346816512 | bytes 20160516 | tf_op jit(solution)/shard_map/while/body/eval_jaxpr/dot_general | solution.py:42
  164.7 8.8 %fusion.35 = f32[288,8192]{1,0:T(8,128)} fusion(bf16[72,8192]{1,0:T(8,128)(2,1)S(1)} %get-tuple-element.340, f32[288,8192]{1,0:T(8,128)} %get-tuple-element.330, f32[8192]{0:T(1024)S(1)} %bitcast.41, pred[]{:T(512)S(6)} %compare.60, bf16[11,288,72]{2,1,0:T(8,128)(2,1)S(1)} %get-tuple-element.339, s32[]{:T(128)} %get-tuple-element.329), kind=kOutput, calls=%fused_computation.4.clone.1 | convolution fusion | flops 346816512 | bytes 20160516 | tf_op jit(solution)/shard_map/while/body/eval_jaxpr/dot_general | solution.py:42
  173.5 79.5 %reduce-scatter.3.cloned.1.call-done = f32[72,8192]{1,0:T(8,128)} async-done(((f32[288,8192]{1,0:T(8,128)}), f32[72,8192]{1,0:T(8,128)}) %reduce-scatter.3.cloned.1.call-update) | async-done | bytes 2359312 | tf_op jit(solution)/shard_map/reduce_scatter | solution.py:46
  305.7 103.7 %while.29 = (s32[]{:T(128)}, f32[288,8192]{1,0:T(8,128)}, f32[11,8192]{1,0:T(8,128)}, bf16[11,288,72]{2,1,0:T(8,128)(2,1)S(1)}, bf16[72,8192]{1,0:T(8,128)(2,1)S(1)}, /*index=5*/s32[]{:T(128)}, s32[]{:T(128)}) while((s32[]{:T(128)}, f32[288,8192]{1,0:T(8,128)}, f32[11,8192]{1,0:T(8,128)}, bf16[11,288,72]{2,1,0:T(8,128)(2,1)S(1)}, ...), condition=%wide.region_5.6_spmd.clone, body=%wide.region_4.5_spmd.clone.sunk | while | flops 346816512 | bytes 20226140 | solution.py:47
  322.6 8.8 %fusion.38 = f32[288,8192]{1,0:T(8,128)} fusion(bf16[72,8192]{1,0:T(8,128)(2,1)S(1)} %get-tuple-element.361, f32[288,8192]{1,0:T(8,128)} %get-tuple-element.351, f32[8192]{0:T(1024)S(1)} %bitcast.42, pred[]{:T(512)S(6)} %compare.61, bf16[11,288,72]{2,1,0:T(8,128)(2,1)S(1)} %get-tuple-element.360, s32[]{:T(128)} %get-tuple-element.350), kind=kOutput, calls=%fused_computation.10.clone.1 | convolution fusion | flops 346816512 | bytes 20160516 | tf_op jit(solution)/shard_map/while/body/eval_jaxpr/dot_general | solution.py:42
  342.1 8.8 %fusion.38 = f32[288,8192]{1,0:T(8,128)} fusion(bf16[72,8192]{1,0:T(8,128)(2,1)S(1)} %get-tuple-element.361, f32[288,8192]{1,0:T(8,128)} %get-tuple-element.351, f32[8192]{0:T(1024)S(1)} %bitcast.42, pred[]{:T(512)S(6)} %compare.61, bf16[11,288,72]{2,1,0:T(8,128)(2,1)S(1)} %get-tuple-element.360, s32[]{:T(128)} %get-tuple-element.350), kind=kOutput, calls=%fused_computation.10.clone.1 | convolution fusion | flops 346816512 | bytes 20160516 | tf_op jit(solution)/shard_map/while/body/eval_jaxpr/dot_general | solution.py:42
  351.8 8.8 %fusion.38 = f32[288,8192]{1,0:T(8,128)} fusion(bf16[72,8192]{1,0:T(8,128)(2,1)S(1)} %get-tuple-element.361, f32[288,8192]{1,0:T(8,128)} %get-tuple-element.351, f32[8192]{0:T(1024)S(1)} %bitcast.42, pred[]{:T(512)S(6)} %compare.61, bf16[11,288,72]{2,1,0:T(8,128)(2,1)S(1)} %get-tuple-element.360, s32[]{:T(128)} %get-tuple-element.350), kind=kOutput, calls=%fused_computation.10.clone.1 | convolution fusion | flops 346816512 | bytes 20160516 | tf_op jit(solution)/shard_map/while/body/eval_jaxpr/dot_general | solution.py:42
  361.6 8.8 %fusion.38 = f32[288,8192]{1,0:T(8,128)} fusion(bf16[72,8192]{1,0:T(8,128)(2,1)S(1)} %get-tuple-element.361, f32[288,8192]{1,0:T(8,128)} %get-tuple-element.351, f32[8192]{0:T(1024)S(1)} %bitcast.42, pred[]{:T(512)S(6)} %compare.61, bf16[11,288,72]{2,1,0:T(8,128)(2,1)S(1)} %get-tuple-element.360, s32[]{:T(128)} %get-tuple-element.350), kind=kOutput, calls=%fused_computation.10.clone.1 | convolution fusion | flops 346816512 | bytes 20160516 | tf_op jit(solution)/shard_map/while/body/eval_jaxpr/dot_general | solution.py:42
  371.3 8.8 %fusion.38 = f32[288,8192]{1,0:T(8,128)} fusion(bf16[72,8192]{1,0:T(8,128)(2,1)S(1)} %get-tuple-element.361, f32[288,8192]{1,0:T(8,128)} %get-tuple-element.351, f32[8192]{0:T(1024)S(1)} %bitcast.42, pred[]{:T(512)S(6)} %compare.61, bf16[11,288,72]{2,1,0:T(8,128)(2,1)S(1)} %get-tuple-element.360, s32[]{:T(128)} %get-tuple-element.350), kind=kOutput, calls=%fused_computation.10.clone.1 | convolution fusion | flops 346816512 | bytes 20160516 | tf_op jit(solution)/shard_map/while/body/eval_jaxpr/dot_general | solution.py:42
  381.1 8.8 %fusion.38 = f32[288,8192]{1,0:T(8,128)} fusion(bf16[72,8192]{1,0:T(8,128)(2,1)S(1)} %get-tuple-element.361, f32[288,8192]{1,0:T(8,128)} %get-tuple-element.351, f32[8192]{0:T(1024)S(1)} %bitcast.42, pred[]{:T(512)S(6)} %compare.61, bf16[11,288,72]{2,1,0:T(8,128)(2,1)S(1)} %get-tuple-element.360, s32[]{:T(128)} %get-tuple-element.350), kind=kOutput, calls=%fused_computation.10.clone.1 | convolution fusion | flops 346816512 | bytes 20160516 | tf_op jit(solution)/shard_map/while/body/eval_jaxpr/dot_general | solution.py:42
  390.9 8.8 %fusion.38 = f32[288,8192]{1,0:T(8,128)} fusion(bf16[72,8192]{1,0:T(8,128)(2,1)S(1)} %get-tuple-element.361, f32[288,8192]{1,0:T(8,128)} %get-tuple-element.351, f32[8192]{0:T(1024)S(1)} %bitcast.42, pred[]{:T(512)S(6)} %compare.61, bf16[11,288,72]{2,1,0:T(8,128)(2,1)S(1)} %get-tuple-element.360, s32[]{:T(128)} %get-tuple-element.350), kind=kOutput, calls=%fused_computation.10.clone.1 | convolution fusion | flops 346816512 | bytes 20160516 | tf_op jit(solution)/shard_map/while/body/eval_jaxpr/dot_general | solution.py:42
  400.6 8.8 %fusion.38 = f32[288,8192]{1,0:T(8,128)} fusion(bf16[72,8192]{1,0:T(8,128)(2,1)S(1)} %get-tuple-element.361, f32[288,8192]{1,0:T(8,128)} %get-tuple-element.351, f32[8192]{0:T(1024)S(1)} %bitcast.42, pred[]{:T(512)S(6)} %compare.61, bf16[11,288,72]{2,1,0:T(8,128)(2,1)S(1)} %get-tuple-element.360, s32[]{:T(128)} %get-tuple-element.350), kind=kOutput, calls=%fused_computation.10.clone.1 | convolution fusion | flops 346816512 | bytes 20160516 | tf_op jit(solution)/shard_map/while/body/eval_jaxpr/dot_general | solution.py:42
  409.4 78.7 %reduce-scatter.5.cloned.1.call-done = f32[72,8192]{1,0:T(8,128)} async-done(((f32[288,8192]{1,0:T(8,128)}), f32[72,8192]{1,0:T(8,128)}) %reduce-scatter.5.cloned.1.call-update) | async-done | bytes 2359312 | tf_op jit(solution)/shard_map/reduce_scatter | solution.py:46
  (119 shorter events, 168.1 us)
Async XLA Ops:
  7.2 11.5 %copy-start = (s32[288]{0:T(512)S(1)}, s32[288]{0:T(512)}, u32[]{:S(2)}) copy-start(s32[288]{0:T(512)} %param.17) | copy-start | bytes 3460
  7.2 11.4 %copy-start.5 = (s32[1606]{0:T(1024)S(1)}, s32[1606]{0:T(1024)}, u32[]{:S(2)}) copy-start(s32[1606]{0:T(1024)} %param.14) | copy-start | bytes 19276
  7.2 11.4 %copy-start.6 = (s32[1606]{0:T(1024)S(1)}, s32[1606]{0:T(1024)}, u32[]{:S(2)}) copy-start(s32[1606]{0:T(1024)} %param.15) | copy-start | bytes 19276
  7.2 245.8 %reduce-scatter.3.cloned.1.call-start = ((), (), s32[]{:S(2)}) async-start(), calls=%async_computation.2 | async-start | bytes 11796480 | tf_op jit(solution)/shard_map/reduce_scatter | solution.py:46
  10.3 50.5 %collective-permute-start = (f32[72,1,1024]{2,0,1:T(8,128)S(1)}, f32[72,1,1024]{2,0,1:T(8,128)}, u32[]{:S(2)}, u32[]{:S(2)}) collective-permute-start(f32[72,1,1024]{2,0,1:T(8,128)S(1)} %copy.41), channel_id=1, source_target_pairs={{1,0},{2,1},{3,2},{4,3},{5,4},{6,5},{7,6},{9,8},{10,9},{11,10},{12... | collective-permute-start | bytes 884744 | tf_op jit(solution)/shard_map/ppermute | solution.py:15
  12.4 49.7 %collective-permute-start.1 = (f32[72,1,1024]{2,0,1:T(8,128)}, f32[72,1,1024]{2,0,1:T(8,128)}, u32[]{:S(2)}, u32[]{:S(2)}) collective-permute-start(f32[72,1,1024]{2,0,1:T(8,128)} %copy.42), channel_id=1, source_target_pairs={{0,1},{1,2},{2,3},{3,4},{4,5},{5,6},{6,7},{8,9},{9,10},{10,11},{11... | collective-permute-start | bytes 884744 | tf_op jit(solution)/shard_map/ppermute | solution.py:12
  28.9 10.3 %copy-start.7 = (s32[1606]{0:T(1024)S(1)}, s32[1606]{0:T(1024)}, u32[]{:S(2)}) copy-start(s32[1606]{0:T(1024)} %param.13) | copy-start | bytes 19276
  28.9 10.4 %copy-start.9 = (s32[3]{0:T(128)S(1)}, s32[3]{0:T(128)}, u32[]{:S(2)}) copy-start(s32[3]{0:T(128)} %constant.73) | copy-start | bytes 40
  28.9 10.5 %copy-start.10 = (s32[3]{0:T(128)S(1)}, s32[3]{0:T(128)}, u32[]{:S(2)}) copy-start(s32[3]{0:T(128)} %constant.76) | copy-start | bytes 40
  28.9 10.6 %copy-start.8 = (bf16[1606]{0:T(1024)(128)(2,1)S(1)}, bf16[1606]{0:T(1024)(128)(2,1)}, u32[]{:S(2)}) copy-start(bf16[1606]{0:T(1024)(128)(2,1)} %param.16) | copy-start | bytes 9640
  53.8 4.1 copy-start.4
  57.9 5.4 %copy-start.3 = (f32[72,8,1024]{2,1,0:T(8,128)S(1)}, f32[72,8,1024]{2,1,0:T(8,128)}, u32[]{:S(2)}) copy-start(f32[72,8,1024]{2,1,0:T(8,128)} %param.11) | copy-start | bytes 7077892
  173.5 314.6 %reduce-scatter.5.cloned.1.call-start = ((), (), s32[]{:S(2)}) async-start(), calls=%async_computation.3 | async-start | bytes 11796480 | tf_op jit(solution)/shard_map/reduce_scatter | solution.py:46
  256.5 10.6 %collective-permute-start.2 = (f32[72,1,1024]{2,0,1:T(8,128)S(1)}, f32[72,1,1024]{2,0,1:T(8,128)S(1)}, u32[]{:S(2)}, u32[]{:S(2)}) collective-permute-start(f32[72,1,1024]{2,0,1:T(8,128)S(1)} %copy.23), channel_id=1, source_target_pairs={{1,0},{2,1},{3,2},{4,3},{5,4},{6,5},{7,6},{9,8},{10,9},{11,10},{12... | collective-permute-start | bytes 884744 | tf_op jit(solution)/shard_map/ppermute | solution.py:15
  257.9 15.5 %collective-permute-start.3 = (f32[72,1,1024]{2,0,1:T(8,128)S(1)}, f32[72,1,1024]{2,0,1:T(8,128)S(1)}, u32[]{:S(2)}, u32[]{:S(2)}) collective-permute-start(f32[72,1,1024]{2,0,1:T(8,128)S(1)} %copy.25), channel_id=1, source_target_pairs={{0,1},{1,2},{2,3},{3,4},{4,5},{5,6},{6,7},{8,9},{9,10},{10,11},{11... | collective-permute-start | bytes 884744 | tf_op jit(solution)/shard_map/ppermute | solution.py:12
  279.4 23.7 %copy-start.2 = (f32[72,8,1024]{2,1,0:T(8,128)}, f32[72,8,1024]{2,1,0:T(8,128)S(1)}, u32[]{:S(2)}) copy-start(f32[72,8,1024]{2,1,0:T(8,128)S(1)} %fusion.14) | copy-start | bytes 7077892
  279.8 11.7 %collective-permute-start.4 = (f32[72,1,1024]{2,0,1:T(8,128)S(1)}, f32[72,1,1024]{2,0,1:T(8,128)}, u32[]{:S(2)}, u32[]{:S(2)}) collective-permute-start(f32[72,1,1024]{2,0,1:T(8,128)S(1)} %copy.29), channel_id=1, source_target_pairs={{1,0},{2,1},{3,2},{4,3},{5,4},{6,5},{7,6},{9,8},{10,9},{11,10},{12... | collective-permute-start | bytes 884744 | tf_op jit(solution)/shard_map/ppermute | solution.py:15
  281.9 16.1 %collective-permute-start.5 = (f32[72,1,1024]{2,0,1:T(8,128)}, f32[72,1,1024]{2,0,1:T(8,128)}, u32[]{:S(2)}, u32[]{:S(2)}) collective-permute-start(f32[72,1,1024]{2,0,1:T(8,128)} %copy.31), channel_id=1, source_target_pairs={{0,1},{1,2},{2,3},{3,4},{4,5},{5,6},{6,7},{8,9},{9,10},{10,11},{11... | collective-permute-start | bytes 884744 | tf_op jit(solution)/shard_map/ppermute | solution.py:12
  491.6 10.6 %collective-permute-start.6 = (f32[72,1,1024]{2,0,1:T(8,128)S(1)}, f32[72,1,1024]{2,0,1:T(8,128)S(1)}, u32[]{:S(2)}, u32[]{:S(2)}) collective-permute-start(f32[72,1,1024]{2,0,1:T(8,128)S(1)} %copy.35), channel_id=1, source_target_pairs={{1,0},{2,1},{3,2},{4,3},{5,4},{6,5},{7,6},{9,8},{10,9},{11,10},{12... | collective-permute-start | bytes 884744 | tf_op jit(solution)/shard_map/ppermute | solution.py:15
  492.9 15.5 %collective-permute-start.7 = (f32[72,1,1024]{2,0,1:T(8,128)S(1)}, f32[72,1,1024]{2,0,1:T(8,128)S(1)}, u32[]{:S(2)}, u32[]{:S(2)}) collective-permute-start(f32[72,1,1024]{2,0,1:T(8,128)S(1)} %copy.37), channel_id=1, source_target_pairs={{0,1},{1,2},{2,3},{3,4},{4,5},{5,6},{6,7},{8,9},{9,10},{10,11},{11... | collective-permute-start | bytes 884744 | tf_op jit(solution)/shard_map/ppermute | solution.py:12
  512.6 3.3 copy-start.1
Sparse Core Ops, SparseCore 0:
  173.6 79.3 reduce-scatter.2
  409.5 78.5 reduce-scatter.4
where the time goes:
time: 525 us; the launch traced here: 523 us
  waiting for transfers between devices  188 us (36%)
  matrix products  186 us (35%)
  local copies, waits for them, and re-layouts  68.7 us (13%)
  other arithmetic  38.8 us (7%)
  starting transfers between devices  26.8 us (5%)
  between operations  14.5 us (3%)
    dot_general x22, matrix products, add_mode(): jnp.dot(col_tables[mode], flattened, preferred_element_type=jnp.float32)  186 us
    reduce_scatter x2, waiting for transfers between devices, couple(): lax.psum_scatter(lax.fori_loop(0, term_count, add_mode, start_total), 'ch...  158 us
    ppermute x4, starting transfers between devices, extended_2(): lax.ppermute(lax.slice_in_dim(block, block.shape[dim] - width, None, axis...  21.5 us
    dynamic_slice x22, local copies, waits for them, and re-layouts, add_mode(): return running + stiff_flat[mode][None, :] * product  21.4 us
    ppermute x4, waiting for transfers between devices, extended_2(): lax.ppermute(lax.slice_in_dim(block, block.shape[dim] - width, None, axis...  17 us
    concatenate x4, other arithmetic, extended_2(): block = jnp.concatenate([low, block, high], axis=dim)  15.3 us
    ppermute x4, waiting for transfers between devices, extended_2(): lax.ppermute(lax.slice_in_dim(block, 0, width, axis=dim), axis, backward)  12.8 us
    unnamed x6, other arithmetic  12.3 us
  transfers between devices with their start and end apart: 10, of which 8 were waited for; matrix products, arithmetic and copies ran while one was open for 9% of the time, Pallas kernels for 0%

commit v1 on v0

v1 whole, which is shorter than its diff:
```python
import functools
import jax
import jax.numpy as jnp
from jax import lax
from jax.experimental import pallas as pl
from jax.experimental.pallas import tpu as pltpu
from jax.sharding import PartitionSpec as P

F32, BF16 = jnp.float32, jnp.bfloat16
VMEM = pl.BlockSpec(memory_space=pltpu.VMEM)
PARAMS = pltpu.CompilerParams(vmem_limit_bytes=48 * 1024 * 1024)
NT = (((1,), (1,)), ((), ()))
STEP = 16


def call(kernel, outs, scratch=(), flops=0, moved=0):
    return pl.pallas_call(
        kernel,
        out_shape=outs,
        scratch_shapes=scratch,
        compiler_params=PARAMS,
        cost_estimate=pl.CostEstimate(flops=flops, bytes_accessed=moved, transcendentals=0),
    )


def shape(dims, kind):
    return jax.ShapeDtypeStruct(dims, kind)


def core_side():
    return lax.rem(lax.axis_index("chaos"), 2)


def table_kernel(terms, pair, hubs, slot_total, entries, main_ref, send_ref, picks, cols):
    wide = entries.shape[1]
    modes = entries[0:1, :]
    rows = entries[1:2, :]
    colv = entries[2:3, :]
    weights = entries[3:4, :]
    slots = entries[4:5, :slot_total]
    chip = lax.axis_index("chaos") // 2
    base = (chip * pair).astype(F32)

    index_col = lax.broadcasted_iota(jnp.int32, (slot_total, wide), 0).astype(F32)
    row_hot = jnp.where(index_col == rows, 1.0, 0.0).astype(BF16)
    col_hot = jnp.where(index_col == colv, 1.0, 0.0).astype(BF16)
    ones = jnp.ones((8, wide), BF16)
    degree = lax.dot_general(ones, row_hot, NT, preferred_element_type=F32)
    zeroth = jnp.where(degree == float(terms), 1.0, 0.0)
    col_zeroth = lax.dot_general(
        zeroth.astype(BF16), col_hot, (((1,), (0,)), ((), ())), preferred_element_type=F32
    )
    beside = lax.dot_general(col_zeroth.astype(BF16), row_hot, NT, preferred_element_type=F32)
    even = jnp.where(degree > 5.0, jnp.where(beside > 0.5, zeroth, 1.0), 0.0)
    before = jnp.where(
        lax.broadcasted_iota(jnp.int32, (slot_total, slot_total), 0)
        < lax.broadcasted_iota(jnp.int32, (slot_total, slot_total), 1),
        1.0,
        0.0,
    ).astype(BF16)
    rank = lax.dot_general(
        even.astype(BF16), before, (((1,), (0,)), ((), ())), preferred_element_type=F32
    )
    rank = jnp.where(even > 0.5, rank, -1.0)[0:1, :]
    lane_index = lax.broadcasted_iota(jnp.int32, (hubs, slot_total), 1).astype(F32)
    hub_hit = lax.broadcasted_iota(jnp.int32, (hubs, slot_total), 0).astype(F32) == rank
    hub_index = jnp.sum(jnp.where(hub_hit, lane_index, 0.0), axis=1, keepdims=True)
    hub_slot = jnp.sum(jnp.where(hub_hit, slots, 0.0), axis=1, keepdims=True)
    hub_here = jnp.logical_and(hub_slot >= base, hub_slot < base + float(pair))
    hub_far = jnp.where(hub_here, -5.0, hub_index)
    hub_near = jnp.where(hub_here, hub_index, -5.0)

    place = lax.broadcasted_iota(jnp.int32, (pair, slot_total), 0).astype(F32) + base
    lanes = lax.broadcasted_iota(jnp.int32, (pair, slot_total), 1).astype(F32)
    own_index = jnp.sum(jnp.where(place == slots, lanes, 0.0), axis=1, keepdims=True)

    cols[0:pair, :] = jnp.where(own_index == colv, 1.0, 0.0).astype(BF16)
    tail = cols.shape[0] - pair
    far_pad = jnp.concatenate([hub_far, jnp.full((tail - hubs, 1), -5.0, F32)], axis=0)
    cols[pair:, :] = jnp.where(far_pad == colv, 1.0, 0.0).astype(BF16)

    for mode in range(terms):
        keyed = jnp.where(modes == float(mode), rows, -1.0)
        picks[mode * pair : (mode + 1) * pair, :] = jnp.where(
            own_index == keyed, weights, 0.0
        ).astype(BF16)
    start = terms * pair
    far16 = jnp.concatenate([hub_far, jnp.full((64 - hubs, 1), -5.0, F32)], axis=0)
    for mode in range(1, terms):
        keyed = jnp.where(modes == float(mode), rows, -1.0)
        at = start + (mode - 1) * 64
        picks[at : at + 64, :] = jnp.where(far16 == keyed, weights, 0.0).astype(BF16)

    for mode in range(terms):
        main_ref[mode] = lax.dot_general(
            picks[mode * pair : (mode + 1) * pair, :], cols[...], NT, preferred_element_type=F32
        ).astype(BF16)
    for mode in range(1, terms):
        at = start + (mode - 1) * 64
        send_ref[mode] = lax.dot_general(
            picks[at : at + 64, :], cols[0:pair, :], NT, preferred_element_type=F32
        ).astype(BF16)
    hub_lane = lax.broadcasted_iota(jnp.int32, (pair, cols.shape[0]), 1).astype(F32) - float(pair)
    own_rank = jnp.sum(
        jnp.where(lanes == own_index, rank, 0.0), axis=1, keepdims=True
    )
    main_ref[terms] = jnp.where(
        jnp.logical_and(own_rank >= 0.0, hub_lane == own_rank), 1.0, 0.0
    ).astype(BF16)
    near_rank = lax.broadcasted_iota(jnp.int32, (64, slot_total), 0).astype(F32)
    slot_row = slots
    near_slot = jnp.sum(jnp.where(near_rank == rank, slot_row, 0.0), axis=1, keepdims=True)
    near_has = jnp.sum(jnp.where(near_rank == rank, 1.0, 0.0), axis=1, keepdims=True)
    near_slot = jnp.where(near_has > 0.5, near_slot - base, -5.0)
    send_ref[0] = jnp.where(
        lax.broadcasted_iota(jnp.int32, (64, pair), 1).astype(F32) == near_slot, 1.0, 0.0
    ).astype(BF16)


def split_kernel(slots, rows, half, field, keep, send):
    side = core_side()
    lanes = 128
    tiles = keep.shape[2] // lanes
    for i in range(half + 1):
        near = jnp.where(side == 0, i, rows - 1 - i)
        far = rows - 1 - near
        for j in range(tiles):
            cut = slice(j * lanes, (j + 1) * lanes)
            keep[i, :, cut] = field[pl.ds(j * rows + near, slots, stride=tiles * rows), :]
            send[i, :, cut] = field[pl.ds(j * rows + far, slots, stride=tiles * rows), :]


def merge_kernel(slots, rows, half, keep, got, out):
    side = core_side()
    lanes = 128
    tiles = keep.shape[2] // lanes
    for i in range(half):
        near = jnp.where(side == 0, i, rows - 1 - i)
        far = rows - 1 - near
        for j in range(tiles):
            cut = slice(j * lanes, (j + 1) * lanes)
            out[pl.ds(j * rows + near, slots, stride=tiles * rows), :] = keep[i, :, cut]
            out[pl.ds(j * rows + far, slots, stride=tiles * rows), :] = got[i, :, cut]


def five_point(above, center, below):
    width = center.shape[1]
    lane = lax.broadcasted_iota(jnp.int32, center.shape, 1)
    left = jnp.where(lane == 0, 0.0, pltpu.roll(center, 1, 1))
    right = jnp.where(lane == width - 1, 0.0, pltpu.roll(center, width - 1, 1))
    return above + below + left + right - 4.0 * center


def fill_buffer(bent, stiff, send_table, buffer, row):
    hubs = buffer.shape[1]
    width = bent.shape[2]
    terms = send_table.shape[0]
    side = core_side()
    half = bent.shape[0]
    place = jnp.where(side == 0, row, 2 * half - 1 - row)
    for start in range(0, width, 256):
        cut = slice(start, start + 256)
        value = bent[row, :, cut]
        total = jnp.dot(send_table[0], value, preferred_element_type=F32)
        for mode in range(1, terms):
            part = jnp.dot(send_table[mode], value, preferred_element_type=F32)
            total = total + stiff[mode, pl.ds(place, 1), cut] * part
        buffer[row, :, cut] = total[:hubs].astype(BF16)


def first_bend_kernel(keep, got, halo, stiff, send_table, bent, buffer):
    side = core_side()
    half, pair, width = bent.shape
    own = keep.shape[1]

    def load(row, at, group):
        if row < 0:
            return halo[pl.ds(group * own + at, 8), :]
        mine = group == side
        return jnp.where(mine, keep[row, pl.ds(at, 8), :], got[row, pl.ds(at, 8), :])

    for group in range(2):

        def chunk(k, carry):
            at = pl.multiple_of(k * 8, 8)
            lines = [load(row, at, group) for row in range(-1, half + 1)]
            for row in range(half):
                value = five_point(lines[row], lines[row + 1], lines[row + 2])
                bent[row, pl.ds(group * own + at, 8), :] = value.astype(BF16)
            return carry

        lax.fori_loop(0, own // 8, chunk, 0)
    for row in range(half):
        fill_buffer(bent, stiff, send_table, buffer, row)


def couple_kernel(depth, bent, got, stiff, table, moment, outer, inner, stacked):
    half, pair, width = bent.shape
    hubs = got.shape[1]
    terms = stiff.shape[0]
    side = core_side()
    room = stacked.shape[0]
    stacked[pair + hubs :, :] = jnp.zeros((room - pair - hubs, width), BF16)
    for row in range(half):
        place = jnp.where(side == 0, row, 2 * half - 1 - row)
        stacked[0:pair, :] = bent[row]
        stacked[pair : pair + hubs, :] = got[row]
        for start in range(0, width, 256):
            cut = slice(start, start + 256)
            value = stacked[:, cut]
            total = jnp.dot(table[terms], value, preferred_element_type=F32)
            for mode in range(terms):
                part = jnp.dot(table[mode], value, preferred_element_type=F32)
                total = total + stiff[mode, pl.ds(place, 1), cut] * part
            moment[row, :, cut] = total
            if row < depth:
                outer[row, :, cut] = total.astype(BF16)
            if row >= half - depth:
                inner[half - 1 - row, :, cut] = total.astype(BF16)


def second_bend_kernel(moment, outer, inner, stiff, send_table, keep, send, bent, buffer, held):
    half, pair, width = moment.shape
    own = pair // 2
    side = core_side()
    tile = lax.axis_index("tile")
    last = lax.axis_size("tile") - 1
    at_edge = jnp.where(side == 0, tile == 0, tile == last)

    def chunk(k, carry):
        at = pl.multiple_of(k * STEP, STEP)
        cut = pl.ds(at, STEP)

        def load(row):
            if row < 0:
                return outer[-1 - row, cut, :].astype(F32)
            if row >= half:
                return inner[row - half, cut, :].astype(F32)
            return moment[row, cut, :]

        for row in range(-1, half + 1):
            value = five_point(load(row - 1), load(row), load(row + 1))
            if row < 0:
                value = jnp.where(at_edge, 0.0, value)
            held[row + 1, cut, :] = value
        for row in range(half):
            value = five_point(held[row, cut, :], held[row + 1, cut, :], held[row + 2, cut, :])
            bent[row, cut, :] = value.astype(BF16)
        return carry

    lax.fori_loop(0, pair // STEP, chunk, 0)
    near = pl.multiple_of(side * own, 8)
    far = pl.multiple_of((1 - side) * own, 8)
    for row in range(half):
        keep[row] = held[row + 1, pl.ds(near, own), :]
        send[row] = held[row + 1, pl.ds(far, own), :]
    for row in range(half):
        fill_buffer(bent, stiff, send_table, buffer, row)


def last_kernel(moment, outer, inner, keep, send):
    half, pair, width = moment.shape
    own = pair // 2
    side = core_side()

    for target, group in ((keep, side), (send, 1 - side)):

        def chunk(k, carry):
            at = pl.multiple_of(k * 8, 8)
            cut = pl.ds(pl.multiple_of(group * own + at, 8), 8)

            def load(row):
                if row < 0:
                    return outer[0, cut, :].astype(F32)
                if row >= half:
                    return inner[0, cut, :].astype(F32)
                return moment[row, cut, :]

            for row in range(half):
                target[row, pl.ds(at, 8), :] = five_point(load(row - 1), load(row), load(row + 1))
            return carry

        lax.fori_loop(0, own // 8, chunk, 0)


def body(slot_field, stiffness, triple_modes, triple_rows, triple_cols, triple_weights, slot_of):
    own, rows, width = slot_field.shape
    terms = stiffness.shape[0]
    pair = 2 * own
    half = rows // 2
    chaos = lax.axis_size("chaos")
    tiles = lax.axis_size("tile")
    slot_total = own * chaos
    modes = terms - 1
    hubs = 1 + modes * (modes + 1) // 2
    room = -(-(pair + hubs) // 16) * 16
    side = core_side()

    core_swap = [(i, i ^ 1) for i in range(chaos)]
    chip_swap = [(i, i ^ 2) for i in range(chaos)]
    tile_swap = []
    for high in range(0, chaos, 2):
        for tile in range(tiles - 1):
            one, two = (high + 1) * tiles + tile, high * tiles + tile + 1
            tile_swap += [(one, two), (two, one)]

    def by_core(value):
        return lax.ppermute(value, "chaos", core_swap)

    def by_chip(value):
        return lax.ppermute(value, "chaos", chip_swap)

    def by_tile(value):
        return lax.ppermute(value, ("chaos", "tile"), tile_swap)

    count = triple_modes.shape[0]
    wide = -(-count // 128) * 128

    def line(value, fill):
        value = value.astype(F32)
        return jnp.pad(value, (0, wide - value.shape[0]), constant_values=fill)

    entries = jnp.stack(
        [
            line(triple_modes, -1.0),
            line(triple_rows, -1.0),
            line(triple_cols, -1.0),
            line(triple_weights, 0.0),
            line(slot_of, -1.0),
        ]
        + [jnp.zeros((wide,), F32)] * 3
    )
    main_table, send_table = call(
        functools.partial(table_kernel, terms, pair, hubs, slot_total),
        (shape((terms + 1, pair, room), BF16), shape((terms, 64, pair), BF16)),
        [
            pltpu.VMEM((terms * pair + modes * 64, wide), BF16),
            pltpu.VMEM((room, wide), BF16),
        ],
        4 * 10**9,
        10**6,
    )(entries)

    lanes = width // 128
    flat = slot_field.reshape(own, rows, lanes, 128).transpose(0, 2, 1, 3).reshape(-1, 128)
    line_block = shape((half + 1, own, width), F32)
    keep, send = call(
        functools.partial(split_kernel, own, rows, half), (line_block, line_block), (), 0, 4 * 10**6
    )(flat)
    got = by_core(send)
    edge = jnp.where(
        side == 0,
        jnp.concatenate([keep[0], got[0]], axis=0),
        jnp.concatenate([got[0], keep[0]], axis=0),
    )
    halo = by_tile(edge)
    bent_shape = shape((half, pair, width), BF16)
    buffer_shape = shape((half, hubs, width), BF16)
    moment_shape = shape((half, pair, width), F32)
    out_block = shape((half, own, width), F32)
    bent, buffer = call(first_bend_kernel, (bent_shape, buffer_shape), (), 2 * 10**9, 4 * 10**6)(
        keep, got, halo, stiffness, send_table
    )

    def couple(bent, buffer, depth):
        other = by_chip(buffer)
        edge_shape = shape((depth, pair, width), BF16)
        moment, outer, inner = call(
            functools.partial(couple_kernel, depth),
            (moment_shape, edge_shape, edge_shape),
            [pltpu.VMEM((room, width), BF16)],
            4 * 10**9,
            4 * 10**6,
        )(bent, other, stiffness, main_table)
        return moment, by_tile(outer), by_core(inner)

    def assemble(keep, send):
        flat = call(
            functools.partial(merge_kernel, own, rows, half),
            shape((own * rows * lanes, 128), F32),
            (),
            0,
            4 * 10**6,
        )(keep, by_core(send))
        return flat.reshape(own, lanes, rows, 128).transpose(0, 2, 1, 3).reshape(own, rows, width)

    moment, outer, inner = couple(bent, buffer, 2)
    keep_one, send_one, bent, buffer = call(
        second_bend_kernel,
        (out_block, out_block, bent_shape, buffer_shape),
        [pltpu.VMEM((half + 2, pair, width), F32)],
        2 * 10**9,
        8 * 10**6,
    )(moment, outer, inner, stiffness, send_table)
    first_apply = assemble(keep_one, send_one)
    moment, outer, inner = couple(bent, buffer, 1)
    keep_two, send_two = call(last_kernel, (out_block, out_block), (), 10**7, 4 * 10**6)(
        moment, outer, inner
    )
    second_apply = assemble(keep_two, send_two)
    return first_apply, second_apply


def solution(mesh):
    return jax.shard_map(
        body,
        mesh=mesh,
        in_specs=(P("chaos", "tile", None), P(None, "tile", None), P(), P(), P(), P(), P()),
        out_specs=(P("chaos", "tile", None), P("chaos", "tile", None)),
        check_vma=False,
    )
```

time: 525 us -> 99.2 us (0.19)
  matrix products: 186 us -> 0 us
  waiting for transfers between devices: 188 us -> 19.3 us
  local copies, waits for them, and re-layouts: 68.7 us -> 1.88 us
  Pallas kernels: 0 us -> 41.3 us
  other arithmetic: 38.8 us -> 0.89 us
  between operations: 14.5 us -> 0.88 us
  starting transfers between devices: 26.8 us -> 34.6 us
    dot_general x22 -> x0, matrix products: 186 us -> none  [add_mode(): jnp.dot(col_tables[mode], flattened, preferred_element_type=jnp.float32)]
    reduce_scatter x2 -> x0, waiting for transfers between devices: 158 us -> none  [couple(): lax.psum_scatter(lax.fori_loop(0, term_count, add_mode, start_total), 'ch...]
    pallas_call x0 -> x9, Pallas kernels: none -> 41.3 us  [the longest x2 9.1 us: couple(): call(functools.partial(couple_kernel, depth), (moment_shape, edge_shape,...]
    dynamic_slice x23 -> x0, local copies, waits for them, and re-layouts: 23.2 us -> none  [the longest x22 21.4 us: add_mode(): return running + stiff_flat[mode][None, :] * product]
    gather x2 -> x0, local copies, waits for them, and re-layouts: 20.5 us -> none  [the longest x1 10.3 us: body(): slot_of[triple_rows]]
    concatenate x4 -> x0, other arithmetic: 15.3 us -> none  [extended_2(): block = jnp.concatenate([low, block, high], axis=dim)]
    unnamed x6 -> x0, other arithmetic: 12.3 us -> none
    ppermute x8 -> x10, waiting for transfers between devices: 29.9 us -> 19.3 us  [the longest x2 13.4 us: by_chip(): return lax.ppermute(value, 'chaos', chip_swap)]
  transfers between devices with their start and end apart: 10 -> 10, of which waited for: 8 -> 5; matrix products, arithmetic and copies ran while one was open for 9% -> 0% of each run, Pallas kernels for 0% -> 13%
where the time goes in v1:
time: 99.2 us; the launch traced here: 98.9 us
  Pallas kernels  41.3 us (42%)
  starting transfers between devices  34.6 us (35%)
  waiting for transfers between devices  19.3 us (19%)
  local copies, waits for them, and re-layouts  1.88 us (2%)
    ppermute x5, starting transfers between devices, by_core(): return lax.ppermute(value, 'chaos', core_swap)  27.1 us
    ppermute x2, waiting for transfers between devices, by_chip(): return lax.ppermute(value, 'chaos', chip_swap)  13.4 us
    pallas_call x2, Pallas kernels, couple(): call(functools.partial(couple_kernel, depth), (moment_shape, edge_shape,...  9.1 us
    pallas_call x2, Pallas kernels, assemble(): call(functools.partial(merge_kernel, own, rows, half), shape((own * rows...  7.52 us
    pallas_call x1, Pallas kernels, body(): call(second_bend_kernel, (out_block, out_block, bent_shape, buffer_shape)...  7.08 us
    pallas_call x1, Pallas kernels, body(): call(functools.partial(table_kernel, terms, pair, hubs, slot_total), (sha...  6.24 us
    ppermute x5, waiting for transfers between devices, by_core(): return lax.ppermute(value, 'chaos', core_swap)  5.84 us
    pallas_call x1, Pallas kernels, body(): call(first_bend_kernel, (bent_shape, buffer_shape), (), 2 * 10 ** 9, 4 *...  5.43 us
  transfers between devices with their start and end apart: 10, of which 5 were waited for; matrix products, arithmetic and copies ran while one was open for 0% of the time, Pallas kernels for 13%

profile of v1, /device:TPU:0, one launch (start us, length us, event | category | flops | bytes accessed | tf_op | source)
XLA Modules:
  0.0 98.9 jit_solution(2885900543880562818)
XLA Ops:
  0.6 1.7 %copy-done = f32[72,8,1024]{2,1,0:T(8,128)S(1)} copy-done((f32[72,8,1024]{2,1,0:T(8,128)S(1)}, f32[72,8,1024]{2,1,0:T(8,128)}, u32[]{:S(2)}) %copy-start) | copy-done | bytes 2359320
  2.3 3.5 %shard_map.86 = (f32[5,72,1024]{2,1,0:T(8,128)S(1)}, f32[5,72,1024]{2,1,0:T(8,128)}) custom-call(f32[4608,128]{1,0:T(8,128)S(1)} %bitcast.19), custom_call_target="tpu_custom_call" | custom-call | bytes 4000000 | tf_op jit(solution)/shard_map/pallas_call | solution.py:347
  6.3 3.1 %collective-permute-done.got = f32[5,72,1024]{2,1,0:T(8,128)S(1)} collective-permute-done((f32[5,72,1024]{2,1,0:T(8,128)}, f32[5,72,1024]{2,1,0:T(8,128)S(1)}, u32[]{:S(2)}, u32[]{:S(2)}) %collective-permute-start) | collective-permute-done | bytes 1474592 | tf_op jit(solution)/shard_map/ppermute | solution.py:308
  9.5 0.9 maximum_select_fusion
  10.3 1.5 %collective-permute-start.1 = (f32[144,1024]{1,0:T(8,128)}, f32[144,1024]{1,0:T(8,128)}, u32[]{:S(2)}, u32[]{:S(2)}) collective-permute-start(f32[144,1024]{1,0:T(8,128)} %maximum_select_fusion), channel_id=1, source_target_pairs={{8,1},{1,8},{9,2},{2,9},{10,3},{3,10},{11,4},{4,11},{12,5},{5,12},... | collective-permute-start | bytes 1769480 | tf_op jit(solution)/shard_map/ppermute | solution.py:314
  12.1 6.2 %shard_map.87 = (bf16[12,144,208]{2,1,0:T(8,128)(2,1)S(1)}, bf16[11,64,144]{2,1,0:T(8,128)(2,1)S(1)}) custom-call(f32[8,1664]{1,0:T(8,128)S(1)} %stack.31.entries), custom_call_target="tpu_custom_call" | custom-call | flops 4000000000 | bytes 1000000 | tf_op jit(solution)/shard_map/pallas_call | solution.py:333
  18.4 5.4 %shard_map.88 = (bf16[4,144,1024]{2,1,0:T(8,128)(2,1)S(1)}, bf16[4,56,1024]{2,1,0:T(8,128)(2,1)S(1)}) custom-call(f32[5,72,1024]{2,1,0:T(8,128)S(1)} %get-tuple-element.20.keep, f32[5,72,1024]{2,1,0:T(8,128)S(1)} %collective-permute-done.got, f32[144,1024]{1,0:T(8,128)} %collective-permute-done.1.halo, f32[11,8,1024]{2,1,0:T(8,128)S(1)} %copy-done.1, ...), custom_call_target="tpu_custom_call" | custom-call | flops 2000000000 | bytes 4000000 | tf_op jit(solution)/shard_map/pallas_call | solution.py:361
  23.9 2.9 %collective-permute-start.2 = (bf16[4,56,1024]{2,1,0:T(8,128)(2,1)S(1)}, bf16[4,56,1024]{2,1,0:T(8,128)(2,1)S(1)}, u32[]{:S(2)}, u32[]{:S(2)}) collective-permute-start(bf16[4,56,1024]{2,1,0:T(8,128)(2,1)S(1)} %get-tuple-element.24), channel_id=1, source_target_pairs={{0,16},{8,24},{16,0},{24,8},{1,17},{9,25},{17,1},{25,9},{2,18},{10... | collective-permute-start | bytes 1376264 | tf_op jit(solution)/shard_map/ppermute | solution.py:311
  26.8 6.5 %collective-permute-done.2.got = bf16[4,56,1024]{2,1,0:T(8,128)(2,1)S(1)} collective-permute-done((bf16[4,56,1024]{2,1,0:T(8,128)(2,1)S(1)}, bf16[4,56,1024]{2,1,0:T(8,128)(2,1)S(1)}, u32[]{:S(2)}, u32[]{:S(2)}) %collective-permute-start.2) | collective-permute-done | bytes 458784 | tf_op jit(solution)/shard_map/ppermute | solution.py:311
  33.2 5.3 %shard_map.89 = (f32[4,144,1024]{2,1,0:T(8,128)}, bf16[2,144,1024]{2,1,0:T(8,128)(2,1)S(1)}, bf16[2,144,1024]{2,1,0:T(8,128)(2,1)S(1)}) custom-call(bf16[4,144,1024]{2,1,0:T(8,128)(2,1)S(1)} %get-tuple-element.23.bent, bf16[4,56,1024]{2,1,0:T(8,128)(2,1)S(1)} %collective-permute-done.2.got, f32[11,8,1024]{2,1,0:T(8,128)S(1)} %copy-done.1, ...), custom_call_target="tpu_custom_call" | custom-call | flops 4000000000 | bytes 4000000 | tf_op jit(solution)/shard_map/pallas_call | solution.py:368
  38.5 0.9 collective-permute-start.3
  39.4 13.2 %collective-permute-start.4 = (bf16[2,144,1024]{2,1,0:T(8,128)(2,1)S(1)}, bf16[2,144,1024]{2,1,0:T(8,128)(2,1)S(1)}, u32[]{:S(2)}, u32[]{:S(2)}) collective-permute-start(bf16[2,144,1024]{2,1,0:T(8,128)(2,1)S(1)} %get-tuple-element.28), channel_id=1, source_target_pairs={{0,8},{8,0},{16,24},{24,16},{1,9},{9,1},{17,25},{25,17},{2,10},{10... | collective-permute-start | bytes 1769480 | tf_op jit(solution)/shard_map/ppermute | solution.py:308
  52.6 1.6 %collective-permute-done.4.inner = bf16[2,144,1024]{2,1,0:T(8,128)(2,1)S(1)} collective-permute-done((bf16[2,144,1024]{2,1,0:T(8,128)(2,1)S(1)}, bf16[2,144,1024]{2,1,0:T(8,128)(2,1)S(1)}, u32[]{:S(2)}, u32[]{:S(2)}) %collective-permute-start.4) | collective-permute-done | bytes 589856 | tf_op jit(solution)/shard_map/ppermute | solution.py:308
  54.2 7.1 %shard_map.90 = (f32[4,72,1024]{2,1,0:T(8,128)S(1)}, f32[4,72,1024]{2,1,0:T(8,128)S(1)}, bf16[4,144,1024]{2,1,0:T(8,128)(2,1)S(1)}, bf16[4,56,1024]{2,1,0:T(8,128)(2,1)S(1)}) custom-call(f32[4,144,1024]{2,1,0:T(8,128)} %get-tuple-element.26.moment, bf16[2,144,1024]{2,1,0:T(8,128)(2,1)S(1)} %collective-permute-done.3.outer, ...), custom_call_target="tpu_custom_call" | custom-call | flops 2000000000 | bytes 8000000 | tf_op jit(solution)/shard_map/pallas_call | solution.py:388
  61.3 1.6 %collective-permute-start.6 = (bf16[4,56,1024]{2,1,0:T(8,128)(2,1)S(1)}, bf16[4,56,1024]{2,1,0:T(8,128)(2,1)S(1)}, u32[]{:S(2)}, u32[]{:S(2)}) collective-permute-start(bf16[4,56,1024]{2,1,0:T(8,128)(2,1)S(1)} %get-tuple-element.32), channel_id=1, source_target_pairs={{0,16},{8,24},{16,0},{24,8},{1,17},{9,25},{17,1},{25,9},{2,18},{10... | collective-permute-start | bytes 1376264 | tf_op jit(solution)/shard_map/ppermute | solution.py:311
  62.9 7.0 %collective-permute-done.6.got = bf16[4,56,1024]{2,1,0:T(8,128)(2,1)S(1)} collective-permute-done((bf16[4,56,1024]{2,1,0:T(8,128)(2,1)S(1)}, bf16[4,56,1024]{2,1,0:T(8,128)(2,1)S(1)}, u32[]{:S(2)}, u32[]{:S(2)}) %collective-permute-start.6) | collective-permute-done | bytes 458784 | tf_op jit(solution)/shard_map/ppermute | solution.py:311
  69.8 3.8 %shard_map.92 = (f32[4,144,1024]{2,1,0:T(8,128)S(1)}, bf16[1,144,1024]{2,1,0:T(8,128)(2,1)S(1)}, bf16[1,144,1024]{2,1,0:T(8,128)(2,1)S(1)}) custom-call(bf16[4,144,1024]{2,1,0:T(8,128)(2,1)S(1)} %get-tuple-element.31.bent, bf16[4,56,1024]{2,1,0:T(8,128)(2,1)S(1)} %collective-permute-done.6.got, f32[11,8,1024]{2,1,0:T(8,128)S(1)} %copy-done.1, ...), custom_call_target="tpu_custom_call" | custom-call | flops 4000000000 | bytes 4000000 | tf_op jit(solution)/shard_map/pallas_call | solution.py:368
  73.7 0.7 collective-permute-start.7
  74.4 10.1 %collective-permute-start.8 = (bf16[1,144,1024]{2,1,0:T(8,128)(2,1)S(1)}, bf16[1,144,1024]{2,1,0:T(8,128)(2,1)S(1)}, u32[]{:S(2)}, u32[]{:S(2)}) collective-permute-start(bf16[1,144,1024]{2,1,0:T(8,128)(2,1)S(1)} %get-tuple-element.35), channel_id=1, source_target_pairs={{0,8},{8,0},{16,24},{24,16},{1,9},{9,1},{17,25},{25,17},{2,10},{10... | collective-permute-start | bytes 884744 | tf_op jit(solution)/shard_map/ppermute | solution.py:308
  84.6 1.1 %collective-permute-done.8.inner = bf16[1,144,1024]{2,1,0:T(8,128)(2,1)S(1)} collective-permute-done((bf16[1,144,1024]{2,1,0:T(8,128)(2,1)S(1)}, bf16[1,144,1024]{2,1,0:T(8,128)(2,1)S(1)}, u32[]{:S(2)}, u32[]{:S(2)}) %collective-permute-start.8) | collective-permute-done | bytes 294944 | tf_op jit(solution)/shard_map/ppermute | solution.py:308
  85.7 2.5 %shard_map.93 = (f32[4,72,1024]{2,1,0:T(8,128)S(1)}, f32[4,72,1024]{2,1,0:T(8,128)S(1)}) custom-call(f32[4,144,1024]{2,1,0:T(8,128)S(1)} %get-tuple-element.33.moment, bf16[1,144,1024]{2,1,0:T(8,128)(2,1)S(1)} %collective-permute-done.7.outer, bf16[1,144,1024]{2,1,0:T(8,128)(2,1)S(1)} %collective-permute-done.8.inner), custom_call_target="tpu_custom_call" | custom-call | flops 10000000 | bytes 4000000 | tf_op jit(solution)/shard_map/pallas_call | solution.py:397
  88.2 3.2 %collective-permute-start.9 = (f32[4,72,1024]{2,1,0:T(8,128)S(1)}, f32[4,72,1024]{2,1,0:T(8,128)S(1)}, u32[]{:S(2)}, u32[]{:S(2)}) collective-permute-start(f32[4,72,1024]{2,1,0:T(8,128)S(1)} %get-tuple-element.37), channel_id=1, source_target_pairs={{0,8},{8,0},{16,24},{24,16},{1,9},{9,1},{17,25},{25,17},{2,10},{10... | collective-permute-start | bytes 3538952 | tf_op jit(solution)/shard_map/ppermute | solution.py:308
  91.4 3.8 %shard_map.91 = f32[4608,128]{1,0:T(8,128)} custom-call(f32[4,72,1024]{2,1,0:T(8,128)S(1)} %get-tuple-element.29.keep, f32[4,72,1024]{2,1,0:T(8,128)S(1)} %collective-permute-done.5.got), custom_call_target="tpu_custom_call" | custom-call | bytes 4000000 | tf_op jit(solution)/shard_map/pallas_call | solution.py:378
  95.2 3.8 %shard_map.94 = f32[4608,128]{1,0:T(8,128)} custom-call(f32[4,72,1024]{2,1,0:T(8,128)S(1)} %get-tuple-element.36.keep, f32[4,72,1024]{2,1,0:T(8,128)S(1)} %collective-permute-done.9.got), custom_call_target="tpu_custom_call" | custom-call | bytes 4000000 | tf_op jit(solution)/shard_map/pallas_call | solution.py:378
  (39 shorter events, 0.8 us)
Async XLA Ops:
  0.6 1.7 %copy-start = (f32[72,8,1024]{2,1,0:T(8,128)S(1)}, f32[72,8,1024]{2,1,0:T(8,128)}, u32[]{:S(2)}) copy-start(f32[72,8,1024]{2,1,0:T(8,128)} %param.7) | copy-start | bytes 7077892
  5.8 6.0 %copy-start.6 = (s32[288]{0:T(512)S(1)}, s32[288]{0:T(512)}, u32[]{:S(2)}) copy-start(s32[288]{0:T(512)} %param.13) | copy-start | bytes 3460
  5.8 6.1 %copy-start.2 = (s32[1606]{0:T(1024)S(1)}, s32[1606]{0:T(1024)}, u32[]{:S(2)}) copy-start(s32[1606]{0:T(1024)} %param.9) | copy-start | bytes 19276
  5.8 6.1 %copy-start.3 = (s32[1606]{0:T(1024)S(1)}, s32[1606]{0:T(1024)}, u32[]{:S(2)}) copy-start(s32[1606]{0:T(1024)} %param.10) | copy-start | bytes 19276
  5.8 6.2 %copy-start.4 = (s32[1606]{0:T(1024)S(1)}, s32[1606]{0:T(1024)}, u32[]{:S(2)}) copy-start(s32[1606]{0:T(1024)} %param.11) | copy-start | bytes 19276
  5.8 6.2 %copy-start.5 = (bf16[1606]{0:T(1024)(128)(2,1)S(1)}, bf16[1606]{0:T(1024)(128)(2,1)}, u32[]{:S(2)}) copy-start(bf16[1606]{0:T(1024)(128)(2,1)} %param.12) | copy-start | bytes 9640
  5.8 3.6 %collective-permute-start = (f32[5,72,1024]{2,1,0:T(8,128)}, f32[5,72,1024]{2,1,0:T(8,128)S(1)}, u32[]{:S(2)}, u32[]{:S(2)}) collective-permute-start(f32[5,72,1024]{2,1,0:T(8,128)} %get-tuple-element.21), channel_id=1, source_target_pairs={{0,8},{8,0},{16,24},{24,16},{1,9},{9,1},{17,25},{25,17},{2,10},{10... | collective-permute-start | bytes 4423688 | tf_op jit(solution)/shard_map/ppermute | solution.py:308
  10.3 8.1 %collective-permute-start.1 = (f32[144,1024]{1,0:T(8,128)}, f32[144,1024]{1,0:T(8,128)}, u32[]{:S(2)}, u32[]{:S(2)}) collective-permute-start(f32[144,1024]{1,0:T(8,128)} %maximum_select_fusion), channel_id=1, source_target_pairs={{8,1},{1,8},{9,2},{2,9},{10,3},{3,10},{11,4},{4,11},{12,5},{5,12},... | collective-permute-start | bytes 1769480 | tf_op jit(solution)/shard_map/ppermute | solution.py:314
  12.1 6.3 %copy-start.1 = (f32[11,8,1024]{2,1,0:T(8,128)S(1)}, f32[11,8,1024]{2,1,0:T(8,128)}, u32[]{:S(2)}) copy-start(f32[11,8,1024]{2,1,0:T(8,128)} %stiff.7) | copy-start | bytes 1081348
  23.9 9.4 %collective-permute-start.2 = (bf16[4,56,1024]{2,1,0:T(8,128)(2,1)S(1)}, bf16[4,56,1024]{2,1,0:T(8,128)(2,1)S(1)}, u32[]{:S(2)}, u32[]{:S(2)}) collective-permute-start(bf16[4,56,1024]{2,1,0:T(8,128)(2,1)S(1)} %get-tuple-element.24), channel_id=1, source_target_pairs={{0,16},{8,24},{16,0},{24,8},{1,17},{9,25},{17,1},{25,9},{2,18},{10... | collective-permute-start | bytes 1376264 | tf_op jit(solution)/shard_map/ppermute | solution.py:311
  38.5 14.1 %collective-permute-start.3 = (bf16[2,144,1024]{2,1,0:T(8,128)(2,1)S(1)}, bf16[2,144,1024]{2,1,0:T(8,128)(2,1)S(1)}, u32[]{:S(2)}, u32[]{:S(2)}) collective-permute-start(bf16[2,144,1024]{2,1,0:T(8,128)(2,1)S(1)} %get-tuple-element.27), channel_id=1, source_target_pairs={{8,1},{1,8},{9,2},{2,9},{10,3},{3,10},{11,4},{4,11},{12,5},{5,12},... | collective-permute-start | bytes 1769480 | tf_op jit(solution)/shard_map/ppermute | solution.py:314
  39.4 14.8 %collective-permute-start.4 = (bf16[2,144,1024]{2,1,0:T(8,128)(2,1)S(1)}, bf16[2,144,1024]{2,1,0:T(8,128)(2,1)S(1)}, u32[]{:S(2)}, u32[]{:S(2)}) collective-permute-start(bf16[2,144,1024]{2,1,0:T(8,128)(2,1)S(1)} %get-tuple-element.28), channel_id=1, source_target_pairs={{0,8},{8,0},{16,24},{24,16},{1,9},{9,1},{17,25},{25,17},{2,10},{10... | collective-permute-start | bytes 1769480 | tf_op jit(solution)/shard_map/ppermute | solution.py:308
  61.3 8.5 %collective-permute-start.6 = (bf16[4,56,1024]{2,1,0:T(8,128)(2,1)S(1)}, bf16[4,56,1024]{2,1,0:T(8,128)(2,1)S(1)}, u32[]{:S(2)}, u32[]{:S(2)}) collective-permute-start(bf16[4,56,1024]{2,1,0:T(8,128)(2,1)S(1)} %get-tuple-element.32), channel_id=1, source_target_pairs={{0,16},{8,24},{16,0},{24,8},{1,17},{9,25},{17,1},{25,9},{2,18},{10... | collective-permute-start | bytes 1376264 | tf_op jit(solution)/shard_map/ppermute | solution.py:311
  73.7 10.9 %collective-permute-start.7 = (bf16[1,144,1024]{2,1,0:T(8,128)(2,1)S(1)}, bf16[1,144,1024]{2,1,0:T(8,128)(2,1)S(1)}, u32[]{:S(2)}, u32[]{:S(2)}) collective-permute-start(bf16[1,144,1024]{2,1,0:T(8,128)(2,1)S(1)} %get-tuple-element.34), channel_id=1, source_target_pairs={{8,1},{1,8},{9,2},{2,9},{10,3},{3,10},{11,4},{4,11},{12,5},{5,12},... | collective-permute-start | bytes 884744 | tf_op jit(solution)/shard_map/ppermute | solution.py:314
  74.4 11.3 %collective-permute-start.8 = (bf16[1,144,1024]{2,1,0:T(8,128)(2,1)S(1)}, bf16[1,144,1024]{2,1,0:T(8,128)(2,1)S(1)}, u32[]{:S(2)}, u32[]{:S(2)}) collective-permute-start(bf16[1,144,1024]{2,1,0:T(8,128)(2,1)S(1)} %get-tuple-element.35), channel_id=1, source_target_pairs={{0,8},{8,0},{16,24},{24,16},{1,9},{9,1},{17,25},{25,17},{2,10},{10... | collective-permute-start | bytes 884744 | tf_op jit(solution)/shard_map/ppermute | solution.py:308
  84.5 6.9 %collective-permute-start.5 = (f32[4,72,1024]{2,1,0:T(8,128)S(1)}, f32[4,72,1024]{2,1,0:T(8,128)S(1)}, u32[]{:S(2)}, u32[]{:S(2)}) collective-permute-start(f32[4,72,1024]{2,1,0:T(8,128)S(1)} %get-tuple-element.30), channel_id=1, source_target_pairs={{0,8},{8,0},{16,24},{24,16},{1,9},{9,1},{17,25},{25,17},{2,10},{10... | collective-permute-start | bytes 3538952 | tf_op jit(solution)/shard_map/ppermute | solution.py:308
  88.2 7.0 %collective-permute-start.9 = (f32[4,72,1024]{2,1,0:T(8,128)S(1)}, f32[4,72,1024]{2,1,0:T(8,128)S(1)}, u32[]{:S(2)}, u32[]{:S(2)}) collective-permute-start(f32[4,72,1024]{2,1,0:T(8,128)S(1)} %get-tuple-element.37), channel_id=1, source_target_pairs={{0,8},{8,0},{16,24},{24,16},{1,9},{9,1},{17,25},{25,17},{2,10},{10... | collective-permute-start | bytes 3538952 | tf_op jit(solution)/shard_map/ppermute | solution.py:308

commit v2 on v1

--- a/solution.py
+++ b/solution.py
@@ -8,18 +8,22 @@
 
 F32, BF16 = jnp.float32, jnp.bfloat16
 VMEM = pl.BlockSpec(memory_space=pltpu.VMEM)
-PARAMS = pltpu.CompilerParams(vmem_limit_bytes=48 * 1024 * 1024)
+TOKEN = jax.ShapeDtypeStruct((8, 128), jnp.float32)
 NT = (((1,), (1,)), ((), ()))
 STEP = 16
 
 
-def call(kernel, outs, scratch=(), flops=0, moved=0):
+def call(kernel, outs, scratch=(), us=1.0, specs=None, room=12):
+    extra = {} if specs is None else {"in_specs": specs}
     return pl.pallas_call(
         kernel,
         out_shape=outs,
         scratch_shapes=scratch,
-        compiler_params=PARAMS,
-        cost_estimate=pl.CostEstimate(flops=flops, bytes_accessed=moved, transcendentals=0),
+        compiler_params=pltpu.CompilerParams(vmem_limit_bytes=room * 1024 * 1024),
+        cost_estimate=pl.CostEstimate(
+            flops=int(us * 1e10), bytes_accessed=10, transcendentals=0
+        ),
+        **extra,
     )
 
 
@@ -31,7 +35,7 @@
     return lax.rem(lax.axis_index("chaos"), 2)
 
 
-def table_kernel(terms, pair, hubs, slot_total, entries, main_ref, send_ref, picks, cols):
+def table_kernel(terms, pair, hubs, slot_total, entries, unused, main_ref, send_ref, picks, cols):
     wide = entries.shape[1]
     modes = entries[0:1, :]
     rows = entries[1:2, :]
@@ -130,19 +134,6 @@
             send[i, :, cut] = field[pl.ds(j * rows + far, slots, stride=tiles * rows), :]
 
 
-def merge_kernel(slots, rows, half, keep, got, out):
-    side = core_side()
-    lanes = 128
-    tiles = keep.shape[2] // lanes
-    for i in range(half):
-        near = jnp.where(side == 0, i, rows - 1 - i)
-        far = rows - 1 - near
-        for j in range(tiles):
-            cut = slice(j * lanes, (j + 1) * lanes)
-            out[pl.ds(j * rows + near, slots, stride=tiles * rows), :] = keep[i, :, cut]
-            out[pl.ds(j * rows + far, slots, stride=tiles * rows), :] = got[i, :, cut]
-
-
 def five_point(above, center, below):
     width = center.shape[1]
     lane = lax.broadcasted_iota(jnp.int32, center.shape, 1)
@@ -151,16 +142,17 @@
     return above + below + left + right - 4.0 * center
 
 
-def fill_buffer(bent, stiff, send_table, buffer, row):
+def row_place(index, rows):
+    return jnp.where(core_side() == 0, index, rows - 1 - index)
+
+
+def fill_buffer(value_ref, stiff, send_table, buffer, row, place):
     hubs = buffer.shape[1]
-    width = bent.shape[2]
+    width = buffer.shape[2]
     terms = send_table.shape[0]
-    side = core_side()
-    half = bent.shape[0]
-    place = jnp.where(side == 0, row, 2 * half - 1 - row)
     for start in range(0, width, 256):
         cut = slice(start, start + 256)
-        value = bent[row, :, cut]
+        value = value_ref[row, :, cut]
         total = jnp.dot(send_table[0], value, preferred_element_type=F32)
         for mode in range(1, terms):
             part = jnp.dot(send_table[mode], value, preferred_element_type=F32)
@@ -168,41 +160,60 @@
         buffer[row, :, cut] = total[:hubs].astype(BF16)
 
 
-def first_bend_kernel(keep, got, halo, stiff, send_table, bent, buffer):
-    side = core_side()
-    half, pair, width = bent.shape
+def first_inner_kernel(keep, got, stiff, send_table, bent, buffer):
+    side = core_side()
+    count, pair, width = bent.shape
     own = keep.shape[1]
-
-    def load(row, at, group):
-        if row < 0:
-            return halo[pl.ds(group * own + at, 8), :]
-        mine = group == side
-        return jnp.where(mine, keep[row, pl.ds(at, 8), :], got[row, pl.ds(at, 8), :])
-
     for group in range(2):
 
         def chunk(k, carry):
             at = pl.multiple_of(k * 8, 8)
-            lines = [load(row, at, group) for row in range(-1, half + 1)]
-            for row in range(half):
+            cut = pl.ds(at, 8)
+            lines = [
+                jnp.where(side == group, keep[row, cut, :], got[row, cut, :])
+                for row in range(count + 2)
+            ]
+            for row in range(count):
                 value = five_point(lines[row], lines[row + 1], lines[row + 2])
                 bent[row, pl.ds(group * own + at, 8), :] = value.astype(BF16)
             return carry
 
         lax.fori_loop(0, own // 8, chunk, 0)
-    for row in range(half):
-        fill_buffer(bent, stiff, send_table, buffer, row)
-
-
-def couple_kernel(depth, bent, got, stiff, table, moment, outer, inner, stacked):
-    half, pair, width = bent.shape
+    for row in range(count):
+        fill_buffer(bent, stiff, send_table, buffer, row, row_place(row + 1, stiff.shape[1]))
+
+
+def first_outer_kernel(keep, got, halo, stiff, send_table, bent, buffer):
+    side = core_side()
+    own = keep.shape[1]
+    for group in range(2):
+
+        def chunk(k, carry):
+            at = pl.multiple_of(k * 8, 8)
+            cut = pl.ds(at, 8)
+            here, below = [
+                jnp.where(side == group, keep[row, cut, :], got[row, cut, :]) for row in range(2)
+            ]
+            far = pl.ds(group * own + at, 8)
+            bent[0, far, :] = five_point(halo[far, :], here, below).astype(BF16)
+            return carry
+
+        lax.fori_loop(0, own // 8, chunk, 0)
+    fill_buffer(bent, stiff, send_table, buffer, 0, row_place(0, stiff.shape[1]))
+
+
+def couple_kernel(first, outer_row, inner_rows, bent, got, stiff, table, moment, *rest):
+    stacked = rest[-1]
+    edges = list(rest[:-1])
+    outer = edges.pop(0) if outer_row is not None else None
+    inner = edges.pop(0) if inner_rows else None
+    count, pair, width = bent.shape
     hubs = got.shape[1]
     terms = stiff.shape[0]
-    side = core_side()
     room = stacked.shape[0]
     stacked[pair + hubs :, :] = jnp.zeros((room - pair - hubs, width), BF16)
-    for row in range(half):
-        place = jnp.where(side == 0, row, 2 * half - 1 - row)
+    for row in range(count):
+        place = row_place(first + row, stiff.shape[1])
         stacked[0:pair, :] = bent[row]
         stacked[pair : pair + hubs, :] = got[row]
         for start in range(0, width, 256):
@@ -213,74 +224,118 @@
                 part = jnp.dot(table[mode], value, preferred_element_type=F32)
                 total = total + stiff[mode, pl.ds(place, 1), cut] * part
             moment[row, :, cut] = total
-            if row < depth:
-                outer[row, :, cut] = total.astype(BF16)
-            if row >= half - depth:
-                inner[half - 1 - row, :, cut] = total.astype(BF16)
-
-
-def second_bend_kernel(moment, outer, inner, stiff, send_table, keep, send, bent, buffer, held):
-    half, pair, width = moment.shape
-    own = pair // 2
-    side = core_side()
+            if first + row == outer_row:
+                outer[0, :, cut] = total.astype(BF16)
+            if first + row in inner_rows:
+                inner[inner_rows.index(first + row), :, cut] = total.astype(BF16)
+
+
+def share(held, keep, send, rows, own):
+    side = core_side()
+    near = pl.multiple_of(side * own, 8)
+    far = pl.multiple_of((1 - side) * own, 8)
+    for target, row in enumerate(rows):
+        keep[target] = held[row, pl.ds(near, own), :]
+        send[target] = held[row, pl.ds(far, own), :]
+
+
+def second_inner_kernel(row_zero, others, inner, stiff, send_table, held, keep, send, bent, buffer):
+    count, pair, width = bent.shape
+
+    def chunk(k, carry):
+        cut = pl.ds(pl.multiple_of(k * STEP, STEP), STEP)
+        lines = [row_zero[0, cut, :]] + [others[row, cut, :] for row in range(3)]
+        lines += [inner[row, cut, :].astype(F32) for row in range(2)]
+        for row in range(4):
+            held[row, cut, :] = five_point(lines[row], lines[row + 1], lines[row + 2])
+        for row in range(2):
+            value = five_point(
+                held[row, cut, :], held[row + 1, cut, :], held[row + 2, cut, :]
+            )
+            bent[row, cut, :] = value.astype(BF16)
+        return carry
+
+    lax.fori_loop(0, pair // STEP, chunk, 0)
+    share(held, keep, send, (0, 1, 2), pair // 2)
+    for row in range(count):
+        fill_buffer(bent, stiff, send_table, buffer, row, row_place(row + 2, stiff.shape[1]))
+
+
+def second_outer_kernel(
+    row_zero, others, near, next_near, held, stiff, send_table, keep, send, bent, buffer, zero
+):
+    count, pair, width = bent.shape
     tile = lax.axis_index("tile")
     last = lax.axis_size("tile") - 1
-    at_edge = jnp.where(side == 0, tile == 0, tile == last)
+    at_edge = jnp.where(core_side() == 0, tile == 0, tile == last)
 
     def chunk(k, carry):
-        at = pl.multiple_of(k * STEP, STEP)
-        cut = pl.ds(at, STEP)
-
-        def load(row):
-            if row < 0:
-                return outer[-1 - row, cut, :].astype(F32)
-            if row >= half:
-                return inner[row - half, cut, :].astype(F32)
-            return moment[row, cut, :]
-
-        for row in range(-1, half + 1):
-            value = five_point(load(row - 1), load(row), load(row + 1))
-            if row < 0:
-                value = jnp.where(at_edge, 0.0, value)
-            held[row + 1, cut, :] = value
-        for row in range(half):
-            value = five_point(held[row, cut, :], held[row + 1, cut, :], held[row + 2, cut, :])
-            bent[row, cut, :] = value.astype(BF16)
+        cut = pl.ds(pl.multiple_of(k * STEP, STEP), STEP)
+        above = near[0, cut, :].astype(F32)
+        beyond = next_near[0, cut, :].astype(F32)
+        here = row_zero[0, cut, :]
+        outside = jnp.where(at_edge, 0.0, five_point(beyond, above, here))
+        zero[0, cut, :] = five_point(above, here, others[0, cut, :])
+        bent[0, cut, :] = five_point(outside, zero[0, cut, :], held[0, cut, :]).astype(BF16)
+        bent[1, cut, :] = five_point(
+            zero[0, cut, :], held[0, cut, :], held[1, cut, :]
+        ).astype(BF16)
         return carry
 
     lax.fori_loop(0, pair // STEP, chunk, 0)
-    near = pl.multiple_of(side * own, 8)
-    far = pl.multiple_of((1 - side) * own, 8)
-    for row in range(half):
-        keep[row] = held[row + 1, pl.ds(near, own), :]
-        send[row] = held[row + 1, pl.ds(far, own), :]
-    for row in range(half):
-        fill_buffer(bent, stiff, send_table, buffer, row)
-
-
-def last_kernel(moment, outer, inner, keep, send):
-    half, pair, width = moment.shape
-    own = pair // 2
-    side = core_side()
-
-    for target, group in ((keep, side), (send, 1 - side)):
+    share(zero, keep, send, (0,), pair // 2)
+    for row in range(count):
+        fill_buffer(bent, stiff, send_table, buffer, row, row_place(row, stiff.shape[1]))
+
+
+def last_kernel(rows, load, own, keep, send):
+    side = core_side()
+    for target, group in ((send, 1 - side), (keep, side)):
 
         def chunk(k, carry):
             at = pl.multiple_of(k * 8, 8)
             cut = pl.ds(pl.multiple_of(group * own + at, 8), 8)
-
-            def load(row):
-                if row < 0:
-                    return outer[0, cut, :].astype(F32)
-                if row >= half:
-                    return inner[0, cut, :].astype(F32)
-                return moment[row, cut, :]
-
-            for row in range(half):
-                target[row, pl.ds(at, 8), :] = five_point(load(row - 1), load(row), load(row + 1))
+            for place, row in enumerate(rows):
+                target[place, pl.ds(at, 8), :] = five_point(
+                    load(row - 1, cut), load(row, cut), load(row + 1, cut)
+                )
             return carry
 
         lax.fori_loop(0, own // 8, chunk, 0)
+
+
+def last_inner_kernel(outers, inners, inner, keep, send):
+    def load(row, cut):
+        if row < 2:
+            return outers[row, cut, :]
+        if row < 4:
+            return inners[row - 2, cut, :]
+        return inner[0, cut, :].astype(F32)
+
+    last_kernel((1, 2, 3), load, keep.shape[1], keep, send)
+
+
+def last_outer_kernel(outers, near, unused, keep, send):
+    def load(row, cut):
+        if row < 0:
+            return near[0, cut, :].astype(F32)
+        return outers[row, cut, :]
+
+    last_kernel((0,), load, keep.shape[1], keep, send)
+
+
+def merge_kernel(slots, rows, keep_zero, keep, got_zero, got, out, token):
+    token[...] = jnp.zeros_like(token)
+    lanes = 128
+    tiles = keep.shape[2] // lanes
+    for i in range(rows // 2):
+        near = row_place(i, rows)
+        far = rows - 1 - near
+        for source, place in (((keep_zero, keep), near), ((got_zero, got), far)):
+            ref, row = (source[0], 0) if i == 0 else (source[1], i - 1)
+            for j in range(tiles):
+                cut = slice(j * lanes, (j + 1) * lanes)
+                out[pl.ds(j * rows + place, slots, stride=tiles * rows), :] = ref[row, :, cut]
 
 
 def body(slot_field, stiffness, triple_modes, triple_rows, triple_cols, triple_weights, slot_of):
@@ -330,6 +385,16 @@
         ]
         + [jnp.zeros((wide,), F32)] * 3
     )
+    first_row, last_row = slot_field[:, 0, :], slot_field[:, rows - 1, :]
+    got_edge = by_core(jnp.where(side == 0, last_row, first_row))
+    own_edge = jnp.where(side == 0, first_row, last_row)
+    edge = jnp.where(
+        side == 0,
+        jnp.concatenate([own_edge, got_edge], axis=0),
+        jnp.concatenate([got_edge, own_edge], axis=0),
+    )
+    halo = by_tile(edge)
+
     main_table, send_table = call(
         functools.partial(table_kernel, terms, pair, hubs, slot_total),
         (shape((terms + 1, pair, room), BF16), shape((terms, 64, pair), BF16)),
@@ -337,68 +402,91 @@
             pltpu.VMEM((terms * pair + modes * 64, wide), BF16),
             pltpu.VMEM((room, wide), BF16),
         ],
-        4 * 10**9,
-        10**6,
-    )(entries)
+        6.0,
+        [VMEM, pl.BlockSpec(memory_space=pl.ANY)],
+        16,
+    )(entries, edge)
 
     lanes = width // 128
     flat = slot_field.reshape(own, rows, lanes, 128).transpose(0, 2, 1, 3).reshape(-1, 128)
     line_block = shape((half + 1, own, width), F32)
     keep, send = call(
-        functools.partial(split_kernel, own, rows, half), (line_block, line_block), (), 0, 4 * 10**6
+        functools.partial(split_kernel, own, rows, half), (line_block, line_block), (), 3.0
     )(flat)
     got = by_core(send)
-    edge = jnp.where(
-        side == 0,
-        jnp.concatenate([keep[0], got[0]], axis=0),
-        jnp.concatenate([got[0], keep[0]], axis=0),
-    )
-    halo = by_tile(edge)
-    bent_shape = shape((half, pair, width), BF16)
-    buffer_shape = shape((half, hubs, width), BF16)
-    moment_shape = shape((half, pair, width), F32)
-    out_block = shape((half, own, width), F32)
-    bent, buffer = call(first_bend_kernel, (bent_shape, buffer_shape), (), 2 * 10**9, 4 * 10**6)(
+
+    def bents(count):
+        return (shape((count, pair, width), BF16), shape((count, hubs, width), BF16))
+
+    def outs(count):
+        return (shape((count, own, width), F32),) * 2
+
+    def couple(bent, other, first, outer_row, inner_rows):
+        count = bent.shape[0]
+        out = [shape((count, pair, width), F32)]
+        if outer_row is not None:
+            out.append(shape((1, pair, width), BF16))
+        if inner_rows:
+            out.append(shape((len(inner_rows), pair, width), BF16))
+        return call(
+            functools.partial(couple_kernel, first, outer_row, inner_rows),
+            tuple(out),
+            [pltpu.VMEM((room, width), BF16)],
+            1.2 * count,
+        )(bent, other, stiffness, main_table)
+
+    bent_in, buffer_in = call(first_inner_kernel, bents(3), (), 4.0)(
+        keep, got, stiffness, send_table
+    )
+    cross_in = by_chip(buffer_in)
+    bent_out, buffer_out = call(first_outer_kernel, bents(1), (), 1.5)(
         keep, got, halo, stiffness, send_table
     )
-
-    def couple(bent, buffer, depth):
-        other = by_chip(buffer)
-        edge_shape = shape((depth, pair, width), BF16)
-        moment, outer, inner = call(
-            functools.partial(couple_kernel, depth),
-            (moment_shape, edge_shape, edge_shape),
-            [pltpu.VMEM((room, width), BF16)],
-            4 * 10**9,
-            4 * 10**6,
-        )(bent, other, stiffness, main_table)
-        return moment, by_tile(outer), by_core(inner)
-
-    def assemble(keep, send):
-        flat = call(
-            functools.partial(merge_kernel, own, rows, half),
-            shape((own * rows * lanes, 128), F32),
+    cross_out = by_chip(buffer_out)
+    moment_in, edge_one, inner = couple(bent_in, cross_in, 1, 1, (3, 2))
+    next_near = by_tile(edge_one)
+    inner = by_core(inner)
+    moment_out, edge_zero = couple(bent_out, cross_out, 0, 0, ())
+    near = by_tile(edge_zero)
+
+    held, keep_in, send_in, bent_in, buffer_in = call(
+        second_inner_kernel, (shape((4, pair, width), F32),) + outs(3) + bents(2), (), 4.0
+    )(moment_out, moment_in, inner, stiffness, send_table)
+    got_in = by_core(send_in)
+    cross_in = by_chip(buffer_in)
+    keep_out, send_out, bent_out, buffer_out = call(
+        second_outer_kernel,
+        outs(1) + bents(2),
+        [pltpu.VMEM((1, pair, width), F32)],
+        3.0,
+    )(moment_out, moment_in, near, next_near, held, stiffness, send_table)
+    cross_out = by_chip(buffer_out)
+    got_out = by_core(send_out)
+    moment_in, inner = couple(bent_in, cross_in, 2, None, (3,))
+    inner = by_core(inner)
+    moment_out, edge_zero = couple(bent_out, cross_out, 0, 0, ())
+    near = by_tile(edge_zero)
+
+    def assemble(*parts):
+        return call(
+            functools.partial(merge_kernel, own, rows),
+            (shape((own * rows * lanes, 128), F32), TOKEN),
             (),
-            0,
-            4 * 10**6,
-        )(keep, by_core(send))
+            3.5,
+        )(*parts)
+
+    def restore(flat):
         return flat.reshape(own, lanes, rows, 128).transpose(0, 2, 1, 3).reshape(own, rows, width)
 
-    moment, outer, inner = couple(bent, buffer, 2)
-    keep_one, send_one, bent, buffer = call(
-        second_bend_kernel,
-        (out_block, out_block, bent_shape, buffer_shape),
-        [pltpu.VMEM((half + 2, pair, width), F32)],
-        2 * 10**9,
-        8 * 10**6,
-    )(moment, outer, inner, stiffness, send_table)
-    first_apply = assemble(keep_one, send_one)
-    moment, outer, inner = couple(bent, buffer, 1)
-    keep_two, send_two = call(last_kernel, (out_block, out_block), (), 10**7, 4 * 10**6)(
-        moment, outer, inner
-    )
-    second_apply = assemble(keep_two, send_two)
-    return first_apply, second_apply
+    first_flat, token = assemble(keep_out, keep_in, got_out, got_in)
+    keep_in, send_in = call(last_inner_kernel, outs(3), (), 2.0)(moment_out, moment_in, inner)
+    got_in = by_core(send_in)
+    keep_out, send_out = call(
+        last_outer_kernel, outs(1), (), 1.0
+    )(moment_out, near, token)
+    got_out = by_core(send_out)
+    second_flat, unused = assemble(keep_out, keep_in, got_out, got_in)
+    return restore(first_flat), restore(second_flat)
 
 
 def solution(mesh):

time: 99.2 us -> 84.3 us (0.85)
  waiting for transfers between devices: 19.3 us -> 5.47 us
  starting transfers between devices: 34.6 us -> 30.9 us
  local copies, waits for them, and re-layouts: 1.88 us -> 4.43 us
    ppermute x2 -> x4, waiting for transfers between devices: 13.4 us -> 4.23 us  [by_chip(): return lax.ppermute(value, 'chaos', chip_swap)]
    ppermute x5 -> x8, starting transfers between devices: 27.1 us -> 22.4 us  [by_core(): return lax.ppermute(value, 'chaos', core_swap)]
    ppermute x5 -> x8, waiting for transfers between devices: 5.84 us -> 1.23 us  [by_core(): return lax.ppermute(value, 'chaos', core_swap)]
    slice x0 -> x1, local copies, waits for them, and re-layouts: none -> 3.13 us  [body(): first_row, last_row = (slot_field[:, 0, :], slot_field[:, rows - 1, :])]
    ppermute x2 -> x4, starting transfers between devices: 4.48 us -> 5.29 us  [by_chip(): return lax.ppermute(value, 'chaos', chip_swap)]
    pallas_call x7 -> x12, Pallas kernels: 31.6 us -> 32 us  [the longest x4 8.01 us: couple(): call(functools.partial(couple_kernel, first, outer_row, inner_rows), tupl...]
    ppermute x3 -> x4, starting transfers between devices: 3.08 us -> 3.27 us  [by_tile(): return lax.ppermute(value, ('chaos', 'tile'), tile_swap)]
  transfers between devices with their start and end apart: 10 -> 16, of which waited for: 5 -> 2; matrix products, arithmetic and copies ran while one was open for 0% -> 0% of each run, Pallas kernels for 13% -> 45%
where the time goes in v2:
time: 84.3 us; the launch traced here: 83.8 us
  Pallas kernels  41.7 us (49%)
  starting transfers between devices  30.9 us (37%)
  waiting for transfers between devices  5.47 us (6%)
  local copies, waits for them, and re-layouts  4.43 us (5%)
  between operations  1.02 us (1%)
    ppermute x8, starting transfers between devices, by_core(): return lax.ppermute(value, 'chaos', core_swap)  22.4 us
    pallas_call x4, Pallas kernels, couple(): call(functools.partial(couple_kernel, first, outer_row, inner_rows), tupl...  8.01 us
    pallas_call x2, Pallas kernels, assemble(): call(functools.partial(merge_kernel, own, rows), (shape((own * rows * lan...  7.52 us
    pallas_call x1, Pallas kernels, body(): call(functools.partial(table_kernel, terms, pair, hubs, slot_total), (sha...  6.26 us
    ppermute x4, starting transfers between devices, by_chip(): return lax.ppermute(value, 'chaos', chip_swap)  5.29 us
    ppermute x4, waiting for transfers between devices, by_chip(): return lax.ppermute(value, 'chaos', chip_swap)  4.23 us
    pallas_call x1, Pallas kernels, body(): call(first_inner_kernel, bents(3), (), 4.0)  3.65 us
    pallas_call x1, Pallas kernels, body(): call(second_inner_kernel, (shape((4, pair, width), F32),) + outs(3) + ben...  3.56 us
  transfers between devices with their start and end apart: 16, of which 2 were waited for; matrix products, arithmetic and copies ran while one was open for 0% of the time, Pallas kernels for 45%

profile of v2, /device:TPU:0, one launch (start us, length us, event | category | flops | bytes accessed | tf_op | source)
XLA Modules:
  0.0 83.8 jit_solution(10408744211641648349)
XLA Ops:
  0.6 3.1 %fusion = (f32[72,1,1024]{2,1,0:T(1,128)S(1)}, f32[72,1,1024]{2,1,0:T(1,128)S(1)}) fusion(f32[72,8,1024]{2,1,0:T(8,128)} %param.7), kind=kLoop, calls=%fused_computation.4 | loop fusion | bytes 1179648 | tf_op jit(solution)/shard_map/slice | solution.py:388
  4.4 3.5 %shard_map.86 = (f32[5,72,1024]{2,1,0:T(8,128)S(1)}, f32[5,72,1024]{2,1,0:T(8,128)}) custom-call(f32[4608,128]{1,0:T(8,128)S(1)} %bitcast.19), custom_call_target="tpu_custom_call" | custom-call | flops 30000001024 | bytes 10 | tf_op jit(solution)/shard_map/pallas_call | solution.py:413
  8.0 1.1 %copy-done.2 = f32[5,72,1024]{2,1,0:T(8,128)} copy-done((f32[5,72,1024]{2,1,0:T(8,128)}, f32[5,72,1024]{2,1,0:T(8,128)S(1)}, u32[]{:S(2)}) %copy-start.2) | copy-done | bytes 1474584
  9.5 1.0 %collective-permute-start.2 = (f32[144,1024]{1,0:T(8,128)S(1)}, f32[144,1024]{1,0:T(8,128)S(1)}, u32[]{:S(2)}, u32[]{:S(2)}) collective-permute-start(f32[144,1024]{1,0:T(8,128)S(1)} %maximum_select_fusion.unused), channel_id=1, source_target_pairs={{8,1},{1,8},{9,2},{2,9},{10,3},{3,10},{11,4},{4,11},{12,5},{5,12},... | collective-permute-start | bytes 1769480 | tf_op jit(solution)/shard_map/ppermute | solution.py:369
  10.5 6.3 %shard_map.87 = (bf16[12,144,208]{2,1,0:T(8,128)(2,1)S(1)}, bf16[11,64,144]{2,1,0:T(8,128)(2,1)S(1)}) custom-call(f32[8,1664]{1,0:T(8,128)S(1)} %stack.31.entries, f32[144,1024]{1,0:T(8,128)S(1)} %maximum_select_fusion.unused), custom_call_target="tpu_custom_call" | custom-call | flops 60000002048 | bytes 10 | tf_op jit(solution)/shard_map/pallas_call | solution.py:398
  16.8 3.7 %shard_map.90 = (bf16[3,144,1024]{2,1,0:T(8,128)(2,1)S(1)}, bf16[3,56,1024]{2,1,0:T(8,128)(2,1)S(1)}) custom-call(f32[5,72,1024]{2,1,0:T(8,128)S(1)} %copy-done.3, f32[5,72,1024]{2,1,0:T(8,128)S(1)} %collective-permute-done.got, f32[11,8,1024]{2,1,0:T(8,128)S(1)} %copy-done.1, bf16[11,64,144]{2,1,0:T(8,128)(2,1)S(1)} %get-tuple-element.37.send_table), custom_call_target="tpu_custom_call" | custom-call | flops 40000000000 | bytes 10 | tf_op jit(solution)/shard_map/pallas_call | solution.py:438
  20.5 3.0 %collective-permute-start.4 = (bf16[3,56,1024]{2,1,0:T(8,128)(2,1)S(1)}, bf16[3,56,1024]{2,1,0:T(8,128)(2,1)S(1)}, u32[]{:S(2)}, u32[]{:S(2)}) collective-permute-start(bf16[3,56,1024]{2,1,0:T(8,128)(2,1)S(1)} %get-tuple-element.43), channel_id=1, source_target_pairs={{0,16},{8,24},{16,0},{24,8},{1,17},{9,25},{17,1},{25,9},{2,18},{10... | collective-permute-start | bytes 1032200 | tf_op jit(solution)/shard_map/ppermute | solution.py:366
  23.5 2.2 %shard_map.88 = (bf16[1,144,1024]{2,1,0:T(8,128)(2,1)S(1)}, bf16[1,56,1024]{2,1,0:T(8,128)(2,1)S(1)}) custom-call(f32[5,72,1024]{2,1,0:T(8,128)S(1)} %copy-done.3, f32[5,72,1024]{2,1,0:T(8,128)S(1)} %collective-permute-done.got, f32[144,1024]{1,0:T(8,128)S(1)} %collective-permute-done.2.halo, f32[11,8,1024]{2,1,0:T(8,128)S(1)} %copy-done.1, ...), custom_call_target="tpu_custom_call" | custom-call | flops 15000000512 | bytes 10 | tf_op jit(solution)/shard_map/pallas_call | solution.py:442
  25.8 4.2 %collective-permute-done.4.got = bf16[3,56,1024]{2,1,0:T(8,128)(2,1)S(1)} collective-permute-done((bf16[3,56,1024]{2,1,0:T(8,128)(2,1)S(1)}, bf16[3,56,1024]{2,1,0:T(8,128)(2,1)S(1)}, u32[]{:S(2)}, u32[]{:S(2)}) %collective-permute-start.4) | collective-permute-done | bytes 344096 | tf_op jit(solution)/shard_map/ppermute | solution.py:366
  30.0 2.9 %shard_map.91 = (f32[3,144,1024]{2,1,0:T(8,128)S(1)}, bf16[1,144,1024]{2,1,0:T(8,128)(2,1)S(1)}, bf16[2,144,1024]{2,1,0:T(8,128)(2,1)S(1)}) custom-call(bf16[3,144,1024]{2,1,0:T(8,128)(2,1)S(1)} %get-tuple-element.42.bent, bf16[3,56,1024]{2,1,0:T(8,128)(2,1)S(1)} %collective-permute-done.4.got, f32[11,8,1024]{2,1,0:T(8,128)S(1)} %copy-done.1, ...), custom_call_target="tpu_custom_call" | custom-call | flops 35999997952 | bytes 10 | tf_op jit(solution)/shard_map/pallas_call | solution.py:431
  32.9 3.5 %collective-permute-start.7 = (bf16[2,144,1024]{2,1,0:T(8,128)(2,1)S(1)}, bf16[2,144,1024]{2,1,0:T(8,128)(2,1)S(1)}, u32[]{:S(2)}, u32[]{:S(2)}) collective-permute-start(bf16[2,144,1024]{2,1,0:T(8,128)(2,1)S(1)} %get-tuple-element.47), channel_id=1, source_target_pairs={{0,8},{8,0},{16,24},{24,16},{1,9},{9,1},{17,25},{25,17},{2,10},{10... | collective-permute-start | bytes 1769480 | tf_op jit(solution)/shard_map/ppermute | solution.py:363
  36.5 1.1 %shard_map.89 = (f32[1,144,1024]{2,1,0:T(8,128)S(1)}, bf16[1,144,1024]{2,1,0:T(8,128)(2,1)S(1)}) custom-call(bf16[1,144,1024]{2,1,0:T(8,128)(2,1)S(1)} %get-tuple-element.38.bent, bf16[1,56,1024]{2,1,0:T(8,128)(2,1)S(1)} %collective-permute-done.3.got, f32[11,8,1024]{2,1,0:T(8,128)S(1)} %copy-done.1, bf16[12,144,208]{2,1,0:T(8,128)(2,1)S(1)} %get-tuple-element.40.table), custom_call_target="tpu_custom_call" | custom-call | flops 12000000000 | bytes 10 | tf_op jit(solution)/shard_map/pallas_call | solution.py:431
  39.2 3.6 %shard_map.92 = (f32[4,144,1024]{2,1,0:T(8,128)S(1)}, f32[3,72,1024]{2,1,0:T(8,128)S(1)}, f32[3,72,1024]{2,1,0:T(8,128)S(1)}, bf16[2,144,1024]{2,1,0:T(8,128)(2,1)S(1)}, bf16[2,56,1024]{2,1,0:T(8,128)(2,1)S(1)}) custom-call(f32[1,144,1024]{2,1,0:T(8,128)S(1)} %get-tuple-element.41.row_zero, f32[3,144,1024]{2,1,0:T(8,128)S(1)} %get-tuple-element.44.others, ...), custom_call_target="tpu_custom_call" | custom-call | flops 40000000000 | bytes 10 | tf_op jit(solution)/shard_map/pallas_call | solution.py:452
  42.7 2.1 %collective-permute-start.12 = (bf16[2,56,1024]{2,1,0:T(8,128)(2,1)S(1)}, bf16[2,56,1024]{2,1,0:T(8,128)(2,1)S(1)}, u32[]{:S(2)}, u32[]{:S(2)}) collective-permute-start(bf16[2,56,1024]{2,1,0:T(8,128)(2,1)S(1)} %get-tuple-element.61), channel_id=1, source_target_pairs={{0,16},{8,24},{16,0},{24,8},{1,17},{9,25},{17,1},{25,9},{2,18},{10... | collective-permute-start | bytes 688136 | tf_op jit(solution)/shard_map/ppermute | solution.py:366
  44.8 3.3 %shard_map.93 = (f32[1,72,1024]{2,1,0:T(8,128)S(1)}, f32[1,72,1024]{2,1,0:T(8,128)S(1)}, bf16[2,144,1024]{2,1,0:T(8,128)(2,1)S(1)}, bf16[2,56,1024]{2,1,0:T(8,128)(2,1)S(1)}) custom-call(f32[1,144,1024]{2,1,0:T(8,128)S(1)} %get-tuple-element.41.row_zero, f32[3,144,1024]{2,1,0:T(8,128)S(1)} %get-tuple-element.44.others, ...), custom_call_target="tpu_custom_call" | custom-call | flops 30000001024 | bytes 10 | tf_op jit(solution)/shard_map/pallas_call | solution.py:457
  48.2 11.2 %collective-permute-start.8 = (f32[1,72,1024]{2,1,0:T(8,128)S(1)}, f32[1,72,1024]{2,1,0:T(8,128)S(1)}, u32[]{:S(2)}, u32[]{:S(2)}) collective-permute-start(f32[1,72,1024]{2,1,0:T(8,128)S(1)} %get-tuple-element.51), channel_id=1, source_target_pairs={{0,8},{8,0},{16,24},{24,16},{1,9},{9,1},{17,25},{25,17},{2,10},{10... | collective-permute-start | bytes 884744 | tf_op jit(solution)/shard_map/ppermute | solution.py:363
  59.5 2.0 %shard_map.97 = (f32[2,144,1024]{2,1,0:T(8,128)S(1)}, bf16[1,144,1024]{2,1,0:T(8,128)(2,1)S(1)}) custom-call(bf16[2,144,1024]{2,1,0:T(8,128)(2,1)S(1)} %get-tuple-element.60.bent, bf16[2,56,1024]{2,1,0:T(8,128)(2,1)S(1)} %collective-permute-done.12.got, f32[11,8,1024]{2,1,0:T(8,128)S(1)} %copy-done.1, bf16[12,144,208]{2,1,0:T(8,128)(2,1)S(1)} %get-tuple-element.40.table), custom_call_target="tpu_custom_call" | custom-call | flops 24000000000 | bytes 10 | tf_op jit(solution)/shard_map/pallas_call | solution.py:431
  62.1 2.0 %shard_map.95 = (f32[2,144,1024]{2,1,0:T(8,128)S(1)}, bf16[1,144,1024]{2,1,0:T(8,128)(2,1)S(1)}) custom-call(bf16[2,144,1024]{2,1,0:T(8,128)(2,1)S(1)} %get-tuple-element.54.bent, bf16[2,56,1024]{2,1,0:T(8,128)(2,1)S(1)} %collective-permute-done.10.got, f32[11,8,1024]{2,1,0:T(8,128)S(1)} %copy-done.1, bf16[12,144,208]{2,1,0:T(8,128)(2,1)S(1)} %get-tuple-element.40.table), custom_call_target="tpu_custom_call" | custom-call | flops 24000000000 | bytes 10 | tf_op jit(solution)/shard_map/pallas_call | solution.py:431
  64.8 2.2 %shard_map.98 = (f32[3,72,1024]{2,1,0:T(8,128)S(1)}, f32[3,72,1024]{2,1,0:T(8,128)S(1)}) custom-call(f32[2,144,1024]{2,1,0:T(8,128)S(1)} %get-tuple-element.56.outers, f32[2,144,1024]{2,1,0:T(8,128)S(1)} %get-tuple-element.62.inners, bf16[1,144,1024]{2,1,0:T(8,128)(2,1)S(1)} %collective-permute-done.13.inner), custom_call_target="tpu_custom_call" | custom-call | flops 20000000000 | bytes 10 | tf_op jit(solution)/shard_map/pallas_call | solution.py:482
  67.0 5.8 %collective-permute-start.15 = (f32[3,72,1024]{2,1,0:T(8,128)S(1)}, f32[3,72,1024]{2,1,0:T(8,128)S(1)}, u32[]{:S(2)}, u32[]{:S(2)}) collective-permute-start(f32[3,72,1024]{2,1,0:T(8,128)S(1)} %get-tuple-element.66), channel_id=1, source_target_pairs={{0,8},{8,0},{16,24},{24,16},{1,9},{9,1},{17,25},{25,17},{2,10},{10... | collective-permute-start | bytes 2654216 | tf_op jit(solution)/shard_map/ppermute | solution.py:363
  72.8 3.8 %shard_map.94 = (f32[4608,128]{1,0:T(8,128)}, f32[8,128]{1,0:T(8,128)S(1)}) custom-call(f32[1,72,1024]{2,1,0:T(8,128)S(1)} %get-tuple-element.49.keep_zero, f32[3,72,1024]{2,1,0:T(8,128)S(1)} %get-tuple-element.50.keep, f32[1,72,1024]{2,1,0:T(8,128)S(1)} %collective-permute-done.8.got_zero, f32[3,72,1024]{2,1,0:T(8,128)S(1)} %collective-permute-done.9.got), custom_call_target="tpu_custom_call" | custom-call | flops 35000000512 | bytes 10 | tf_op jit(solution)/shard_map/pallas_call | solution.py:471
  76.6 1.6 %shard_map.96 = (f32[1,72,1024]{2,1,0:T(8,128)S(1)}, f32[1,72,1024]{2,1,0:T(8,128)S(1)}) custom-call(f32[2,144,1024]{2,1,0:T(8,128)S(1)} %get-tuple-element.56.outers, bf16[1,144,1024]{2,1,0:T(8,128)(2,1)S(1)} %collective-permute-done.11.near, f32[8,128]{1,0:T(8,128)S(1)} %get-tuple-element.58.unused), custom_call_target="tpu_custom_call" | custom-call | flops 10000000000 | bytes 10 | tf_op jit(solution)/shard_map/pallas_call | solution.py:484
  78.8 1.2 %collective-permute-done.14.got_zero = f32[1,72,1024]{2,1,0:T(8,128)S(1)} collective-permute-done((f32[1,72,1024]{2,1,0:T(8,128)S(1)}, f32[1,72,1024]{2,1,0:T(8,128)S(1)}, u32[]{:S(2)}, u32[]{:S(2)}) %collective-permute-start.14) | collective-permute-done | bytes 294944 | tf_op jit(solution)/shard_map/ppermute | solution.py:363
  80.0 3.8 %shard_map.99 = (f32[4608,128]{1,0:T(8,128)}, f32[8,128]{1,0:T(8,128)}) custom-call(f32[1,72,1024]{2,1,0:T(8,128)S(1)} %get-tuple-element.59.keep_zero, f32[3,72,1024]{2,1,0:T(8,128)S(1)} %get-tuple-element.64.keep, f32[1,72,1024]{2,1,0:T(8,128)S(1)} %collective-permute-done.14.got_zero, f32[3,72,1024]{2,1,0:T(8,128)S(1)} %collective-permute-done.15.got), custom_call_target="tpu_custom_call" | custom-call | flops 35000000512 | bytes 10 | tf_op jit(solution)/shard_map/pallas_call | solution.py:471
  (60 shorter events, 4.7 us)
Async XLA Ops:
  0.6 3.8 %copy-start = (f32[72,8,1024]{2,1,0:T(8,128)S(1)}, f32[72,8,1024]{2,1,0:T(8,128)}, u32[]{:S(2)}) copy-start(f32[72,8,1024]{2,1,0:T(8,128)} %param.7) | copy-start | bytes 7077892
  3.9 5.5 %collective-permute-start.1 = (f32[72,1024]{1,0:T(8,128)S(1)}, f32[72,1024]{1,0:T(8,128)S(1)}, u32[]{:S(2)}, u32[]{:S(2)}) collective-permute-start(f32[72,1024]{1,0:T(8,128)S(1)} %get-tuple-element.71), channel_id=1, source_target_pairs={{0,8},{8,0},{16,24},{24,16},{1,9},{9,1},{17,25},{25,17},{2,10},{10... | collective-permute-start | bytes 884744 | tf_op jit(solution)/shard_map/ppermute | solution.py:363
  4.4 4.7 %copy-start.8 = (s32[288]{0:T(512)S(1)}, s32[288]{0:T(512)}, u32[]{:S(2)}) copy-start(s32[288]{0:T(512)} %param.13) | copy-start | bytes 3460
  4.4 4.7 %copy-start.4 = (s32[1606]{0:T(1024)S(1)}, s32[1606]{0:T(1024)}, u32[]{:S(2)}) copy-start(s32[1606]{0:T(1024)} %param.9) | copy-start | bytes 19276
  4.4 4.8 %copy-start.5 = (s32[1606]{0:T(1024)S(1)}, s32[1606]{0:T(1024)}, u32[]{:S(2)}) copy-start(s32[1606]{0:T(1024)} %param.10) | copy-start | bytes 19276
  4.4 4.8 %copy-start.6 = (s32[1606]{0:T(1024)S(1)}, s32[1606]{0:T(1024)}, u32[]{:S(2)}) copy-start(s32[1606]{0:T(1024)} %param.11) | copy-start | bytes 19276
  4.4 4.9 %copy-start.7 = (bf16[1606]{0:T(1024)(128)(2,1)S(1)}, bf16[1606]{0:T(1024)(128)(2,1)}, u32[]{:S(2)}) copy-start(bf16[1606]{0:T(1024)(128)(2,1)} %param.12) | copy-start | bytes 9640
  9.1 7.8 %collective-permute-start = (f32[5,72,1024]{2,1,0:T(8,128)}, f32[5,72,1024]{2,1,0:T(8,128)S(1)}, u32[]{:S(2)}, u32[]{:S(2)}) collective-permute-start(f32[5,72,1024]{2,1,0:T(8,128)} %get-tuple-element.36), channel_id=1, source_target_pairs={{0,8},{8,0},{16,24},{24,16},{1,9},{9,1},{17,25},{25,17},{2,10},{10... | collective-permute-start | bytes 4423688 | tf_op jit(solution)/shard_map/ppermute | solution.py:363
  9.5 7.3 %copy-start.1 = (f32[11,8,1024]{2,1,0:T(8,128)S(1)}, f32[11,8,1024]{2,1,0:T(8,128)}, u32[]{:S(2)}) copy-start(f32[11,8,1024]{2,1,0:T(8,128)} %stiff.15) | copy-start | bytes 1081348
  9.5 7.3 %copy-start.3 = (f32[5,72,1024]{2,1,0:T(8,128)S(1)}, f32[5,72,1024]{2,1,0:T(8,128)}, u32[]{:S(2)}) copy-start(f32[5,72,1024]{2,1,0:T(8,128)} %copy-done.2) | copy-start | bytes 4423684
  9.5 14.0 %collective-permute-start.2 = (f32[144,1024]{1,0:T(8,128)S(1)}, f32[144,1024]{1,0:T(8,128)S(1)}, u32[]{:S(2)}, u32[]{:S(2)}) collective-permute-start(f32[144,1024]{1,0:T(8,128)S(1)} %maximum_select_fusion.unused), channel_id=1, source_target_pairs={{8,1},{1,8},{9,2},{2,9},{10,3},{3,10},{11,4},{4,11},{12,5},{5,12},... | collective-permute-start | bytes 1769480 | tf_op jit(solution)/shard_map/ppermute | solution.py:369
  20.5 9.5 %collective-permute-start.4 = (bf16[3,56,1024]{2,1,0:T(8,128)(2,1)S(1)}, bf16[3,56,1024]{2,1,0:T(8,128)(2,1)S(1)}, u32[]{:S(2)}, u32[]{:S(2)}) collective-permute-start(bf16[3,56,1024]{2,1,0:T(8,128)(2,1)S(1)} %get-tuple-element.43), channel_id=1, source_target_pairs={{0,16},{8,24},{16,0},{24,8},{1,17},{9,25},{17,1},{25,9},{2,18},{10... | collective-permute-start | bytes 1032200 | tf_op jit(solution)/shard_map/ppermute | solution.py:366
  25.7 10.8 %collective-permute-start.3 = (bf16[1,56,1024]{2,1,0:T(8,128)(2,1)S(1)}, bf16[1,56,1024]{2,1,0:T(8,128)(2,1)S(1)}, u32[]{:S(2)}, u32[]{:S(2)}) collective-permute-start(bf16[1,56,1024]{2,1,0:T(8,128)(2,1)S(1)} %get-tuple-element.39), channel_id=1, source_target_pairs={{0,16},{8,24},{16,0},{24,8},{1,17},{9,25},{17,1},{25,9},{2,18},{10... | collective-permute-start | bytes 344072 | tf_op jit(solution)/shard_map/ppermute | solution.py:366
  32.9 6.2 %collective-permute-start.7 = (bf16[2,144,1024]{2,1,0:T(8,128)(2,1)S(1)}, bf16[2,144,1024]{2,1,0:T(8,128)(2,1)S(1)}, u32[]{:S(2)}, u32[]{:S(2)}) collective-permute-start(bf16[2,144,1024]{2,1,0:T(8,128)(2,1)S(1)} %get-tuple-element.47), channel_id=1, source_target_pairs={{0,8},{8,0},{16,24},{24,16},{1,9},{9,1},{17,25},{25,17},{2,10},{10... | collective-permute-start | bytes 1769480 | tf_op jit(solution)/shard_map/ppermute | solution.py:363
  37.6 7.3 %collective-permute-start.5 = (bf16[1,144,1024]{2,1,0:T(8,128)(2,1)S(1)}, bf16[1,144,1024]{2,1,0:T(8,128)(2,1)S(1)}, u32[]{:S(2)}, u32[]{:S(2)}) collective-permute-start(bf16[1,144,1024]{2,1,0:T(8,128)(2,1)S(1)} %get-tuple-element.45), channel_id=1, source_target_pairs={{8,1},{1,8},{9,2},{2,9},{10,3},{3,10},{11,4},{4,11},{12,5},{5,12},... | collective-permute-start | bytes 884744 | tf_op jit(solution)/shard_map/ppermute | solution.py:369
  38.2 6.6 %collective-permute-start.6 = (bf16[1,144,1024]{2,1,0:T(8,128)(2,1)S(1)}, bf16[1,144,1024]{2,1,0:T(8,128)(2,1)S(1)}, u32[]{:S(2)}, u32[]{:S(2)}) collective-permute-start(bf16[1,144,1024]{2,1,0:T(8,128)(2,1)S(1)} %get-tuple-element.46), channel_id=1, source_target_pairs={{8,1},{1,8},{9,2},{2,9},{10,3},{3,10},{11,4},{4,11},{12,5},{5,12},... | collective-permute-start | bytes 884744 | tf_op jit(solution)/shard_map/ppermute | solution.py:369
  42.7 16.8 %collective-permute-start.12 = (bf16[2,56,1024]{2,1,0:T(8,128)(2,1)S(1)}, bf16[2,56,1024]{2,1,0:T(8,128)(2,1)S(1)}, u32[]{:S(2)}, u32[]{:S(2)}) collective-permute-start(bf16[2,56,1024]{2,1,0:T(8,128)(2,1)S(1)} %get-tuple-element.61), channel_id=1, source_target_pairs={{0,16},{8,24},{16,0},{24,8},{1,17},{9,25},{17,1},{25,9},{2,18},{10... | collective-permute-start | bytes 688136 | tf_op jit(solution)/shard_map/ppermute | solution.py:366
  48.1 14.0 %collective-permute-start.10 = (bf16[2,56,1024]{2,1,0:T(8,128)(2,1)S(1)}, bf16[2,56,1024]{2,1,0:T(8,128)(2,1)S(1)}, u32[]{:S(2)}, u32[]{:S(2)}) collective-permute-start(bf16[2,56,1024]{2,1,0:T(8,128)(2,1)S(1)} %get-tuple-element.55), channel_id=1, source_target_pairs={{0,16},{8,24},{16,0},{24,8},{1,17},{9,25},{17,1},{25,9},{2,18},{10... | collective-permute-start | bytes 688136 | tf_op jit(solution)/shard_map/ppermute | solution.py:366
  48.2 24.6 %collective-permute-start.8 = (f32[1,72,1024]{2,1,0:T(8,128)S(1)}, f32[1,72,1024]{2,1,0:T(8,128)S(1)}, u32[]{:S(2)}, u32[]{:S(2)}) collective-permute-start(f32[1,72,1024]{2,1,0:T(8,128)S(1)} %get-tuple-element.51), channel_id=1, source_target_pairs={{0,8},{8,0},{16,24},{24,16},{1,9},{9,1},{17,25},{25,17},{2,10},{10... | collective-permute-start | bytes 884744 | tf_op jit(solution)/shard_map/ppermute | solution.py:363
  59.5 13.3 %collective-permute-start.9 = (f32[3,72,1024]{2,1,0:T(8,128)S(1)}, f32[3,72,1024]{2,1,0:T(8,128)S(1)}, u32[]{:S(2)}, u32[]{:S(2)}) collective-permute-start(f32[3,72,1024]{2,1,0:T(8,128)S(1)} %get-tuple-element.52), channel_id=1, source_target_pairs={{0,8},{8,0},{16,24},{24,16},{1,9},{9,1},{17,25},{25,17},{2,10},{10... | collective-permute-start | bytes 2654216 | tf_op jit(solution)/shard_map/ppermute | solution.py:363
  61.5 3.3 %collective-permute-start.13 = (bf16[1,144,1024]{2,1,0:T(8,128)(2,1)S(1)}, bf16[1,144,1024]{2,1,0:T(8,128)(2,1)S(1)}, u32[]{:S(2)}, u32[]{:S(2)}) collective-permute-start(bf16[1,144,1024]{2,1,0:T(8,128)(2,1)S(1)} %get-tuple-element.63), channel_id=1, source_target_pairs={{0,8},{8,0},{16,24},{24,16},{1,9},{9,1},{17,25},{25,17},{2,10},{10... | collective-permute-start | bytes 884744 | tf_op jit(solution)/shard_map/ppermute | solution.py:363
  64.1 12.5 %collective-permute-start.11 = (bf16[1,144,1024]{2,1,0:T(8,128)(2,1)S(1)}, bf16[1,144,1024]{2,1,0:T(8,128)(2,1)S(1)}, u32[]{:S(2)}, u32[]{:S(2)}) collective-permute-start(bf16[1,144,1024]{2,1,0:T(8,128)(2,1)S(1)} %get-tuple-element.57), channel_id=1, source_target_pairs={{8,1},{1,8},{9,2},{2,9},{10,3},{3,10},{11,4},{4,11},{12,5},{5,12},... | collective-permute-start | bytes 884744 | tf_op jit(solution)/shard_map/ppermute | solution.py:369
  67.0 13.0 %collective-permute-start.15 = (f32[3,72,1024]{2,1,0:T(8,128)S(1)}, f32[3,72,1024]{2,1,0:T(8,128)S(1)}, u32[]{:S(2)}, u32[]{:S(2)}) collective-permute-start(f32[3,72,1024]{2,1,0:T(8,128)S(1)} %get-tuple-element.66), channel_id=1, source_target_pairs={{0,8},{8,0},{16,24},{24,16},{1,9},{9,1},{17,25},{25,17},{2,10},{10... | collective-permute-start | bytes 2654216 | tf_op jit(solution)/shard_map/ppermute | solution.py:363
  78.2 1.8 %collective-permute-start.14 = (f32[1,72,1024]{2,1,0:T(8,128)S(1)}, f32[1,72,1024]{2,1,0:T(8,128)S(1)}, u32[]{:S(2)}, u32[]{:S(2)}) collective-permute-start(f32[1,72,1024]{2,1,0:T(8,128)S(1)} %get-tuple-element.65), channel_id=1, source_target_pairs={{0,8},{8,0},{16,24},{24,16},{1,9},{9,1},{17,25},{25,17},{2,10},{10... | collective-permute-start | bytes 884744 | tf_op jit(solution)/shard_map/ppermute | solution.py:363
  (1 other events, 1.1 us)

commit v3 on v2

--- a/solution.py
+++ b/solution.py
@@ -8,7 +8,8 @@
 
 F32, BF16 = jnp.float32, jnp.bfloat16
 VMEM = pl.BlockSpec(memory_space=pltpu.VMEM)
-TOKEN = jax.ShapeDtypeStruct((8, 128), jnp.float32)
+TOKEN = jax.ShapeDtypeStruct((8, 128), jnp.int32)
+ANY = pl.BlockSpec(memory_space=pl.ANY)
 NT = (((1,), (1,)), ((), ()))
 STEP = 16
 
@@ -121,17 +122,29 @@
     ).astype(BF16)
 
 
-def split_kernel(slots, rows, half, field, keep, send):
-    side = core_side()
-    lanes = 128
-    tiles = keep.shape[2] // lanes
-    for i in range(half + 1):
-        near = jnp.where(side == 0, i, rows - 1 - i)
-        far = rows - 1 - near
-        for j in range(tiles):
-            cut = slice(j * lanes, (j + 1) * lanes)
-            keep[i, :, cut] = field[pl.ds(j * rows + near, slots, stride=tiles * rows), :]
-            send[i, :, cut] = field[pl.ds(j * rows + far, slots, stride=tiles * rows), :]
+def edge_kernel(field, near, far, lines, arrived):
+    rows = field.shape[1]
+    copies = [
+        pltpu.make_async_copy(field.at[:, row, :], lines.at[k], arrived.at[k])
+        for k, row in enumerate((0, rows - 1))
+    ]
+    for copy in copies:
+        copy.start()
+    for copy in copies:
+        copy.wait()
+    first = core_side() == 0
+    near[...] = jnp.where(first, lines[0], lines[1])
+    far[...] = jnp.where(first, lines[1], lines[0])
+
+
+def split_kernel(field, unused, keep, send):
+    slots, rows, width = field.shape
+    first = core_side() == 0
+    for at in range(0, slots, 8):
+        lines = jnp.swapaxes(field[at : at + 8], 0, 1)
+        for i in range(keep.shape[0]):
+            keep[i, at : at + 8, :] = jnp.where(first, lines[i], lines[rows - 1 - i])
+            send[i, at : at + 8, :] = jnp.where(first, lines[rows - 1 - i], lines[i])
 
 
 def five_point(above, center, below):
@@ -160,7 +173,9 @@
         buffer[row, :, cut] = total[:hubs].astype(BF16)
 
 
-def first_inner_kernel(keep, got, stiff, send_table, bent, buffer):
+def first_kernel(first_row, keep, got, *rest):
+    halo = rest[0] if first_row == 0 else None
+    stiff, send_table, unused, bent, buffer = rest[-5:]
     side = core_side()
     count, pair, width = bent.shape
     own = keep.shape[1]
@@ -169,37 +184,21 @@
         def chunk(k, carry):
             at = pl.multiple_of(k * 8, 8)
             cut = pl.ds(at, 8)
+            far = pl.ds(group * own + at, 8)
             lines = [
-                jnp.where(side == group, keep[row, cut, :], got[row, cut, :])
-                for row in range(count + 2)
+                halo[far, :]
+                if row < 0
+                else jnp.where(side == group, keep[row, cut, :], got[row, cut, :])
+                for row in range(first_row - 1, first_row + count + 1)
             ]
             for row in range(count):
                 value = five_point(lines[row], lines[row + 1], lines[row + 2])
-                bent[row, pl.ds(group * own + at, 8), :] = value.astype(BF16)
+                bent[row, far, :] = value.astype(BF16)
             return carry
 
-        lax.fori_loop(0, own // 8, chunk, 0)
+        lax.fori_loop(0, own // 8, chunk, 0, unroll=3)
     for row in range(count):
-        fill_buffer(bent, stiff, send_table, buffer, row, row_place(row + 1, stiff.shape[1]))
-
-
-def first_outer_kernel(keep, got, halo, stiff, send_table, bent, buffer):
-    side = core_side()
-    own = keep.shape[1]
-    for group in range(2):
-
-        def chunk(k, carry):
-            at = pl.multiple_of(k * 8, 8)
-            cut = pl.ds(at, 8)
-            here, below = [
-                jnp.where(side == group, keep[row, cut, :], got[row, cut, :]) for row in range(2)
-            ]
-            far = pl.ds(group * own + at, 8)
-            bent[0, far, :] = five_point(halo[far, :], here, below).astype(BF16)
-            return carry
-
-        lax.fori_loop(0, own // 8, chunk, 0)
-    fill_buffer(bent, stiff, send_table, buffer, 0, row_place(0, stiff.shape[1]))
+        fill_buffer(bent, stiff, send_table, buffer, row, row_place(first_row + row, stiff.shape[1]))
 
 
 def couple_kernel(first, outer_row, inner_rows, bent, got, stiff, table, moment, *rest):
@@ -239,12 +238,14 @@
         send[target] = held[row, pl.ds(far, own), :]
 
 
-def second_inner_kernel(row_zero, others, inner, stiff, send_table, held, keep, send, bent, buffer):
+def second_inner_kernel(
+    row_zero, row_one, others, inner, stiff, send_table, held, keep, send, bent, buffer
+):
     count, pair, width = bent.shape
 
     def chunk(k, carry):
         cut = pl.ds(pl.multiple_of(k * STEP, STEP), STEP)
-        lines = [row_zero[0, cut, :]] + [others[row, cut, :] for row in range(3)]
+        lines = [row_zero[0, cut, :], row_one[0, cut, :]] + [others[row, cut, :] for row in range(2)]
         lines += [inner[row, cut, :].astype(F32) for row in range(2)]
         for row in range(4):
             held[row, cut, :] = five_point(lines[row], lines[row + 1], lines[row + 2])
@@ -255,16 +256,16 @@
             bent[row, cut, :] = value.astype(BF16)
         return carry
 
-    lax.fori_loop(0, pair // STEP, chunk, 0)
+    lax.fori_loop(0, pair // STEP, chunk, 0, unroll=3)
     share(held, keep, send, (0, 1, 2), pair // 2)
     for row in range(count):
         fill_buffer(bent, stiff, send_table, buffer, row, row_place(row + 2, stiff.shape[1]))
 
 
-def second_outer_kernel(
-    row_zero, others, near, next_near, held, stiff, send_table, keep, send, bent, buffer, zero
+def second_edge_kernel(
+    row_zero, others, near, next_near, held, stiff, send_table, unused, zero, keep, send, bent, buffer
 ):
-    count, pair, width = bent.shape
+    pair = bent.shape[1]
     tile = lax.axis_index("tile")
     last = lax.axis_size("tile") - 1
     at_edge = jnp.where(core_side() == 0, tile == 0, tile == last)
@@ -275,67 +276,73 @@
         beyond = next_near[0, cut, :].astype(F32)
         here = row_zero[0, cut, :]
         outside = jnp.where(at_edge, 0.0, five_point(beyond, above, here))
-        zero[0, cut, :] = five_point(above, here, others[0, cut, :])
-        bent[0, cut, :] = five_point(outside, zero[0, cut, :], held[0, cut, :]).astype(BF16)
-        bent[1, cut, :] = five_point(
-            zero[0, cut, :], held[0, cut, :], held[1, cut, :]
-        ).astype(BF16)
+        value = five_point(above, here, others[0, cut, :])
+        zero[0, cut, :] = value
+        bent[0, cut, :] = five_point(outside, value, held[0, cut, :]).astype(BF16)
         return carry
 
-    lax.fori_loop(0, pair // STEP, chunk, 0)
+    lax.fori_loop(0, pair // STEP, chunk, 0, unroll=3)
+    fill_buffer(bent, stiff, send_table, buffer, 0, row_place(0, stiff.shape[1]))
     share(zero, keep, send, (0,), pair // 2)
-    for row in range(count):
-        fill_buffer(bent, stiff, send_table, buffer, row, row_place(row, stiff.shape[1]))
-
-
-def last_kernel(rows, load, own, keep, send):
+
+
+def second_next_kernel(zero, held, stiff, send_table, bent, buffer):
+    pair = bent.shape[1]
+
+    def chunk(k, carry):
+        cut = pl.ds(pl.multiple_of(k * STEP, STEP), STEP)
+        value = five_point(zero[0, cut, :], held[0, cut, :], held[1, cut, :])
+        bent[0, cut, :] = value.astype(BF16)
+        return carry
+
+    lax.fori_loop(0, pair // STEP, chunk, 0, unroll=3)
+    fill_buffer(bent, stiff, send_table, buffer, 0, row_place(1, stiff.shape[1]))
+
+
+def last_kernel(zero, one, inners, inner, keep, send):
     side = core_side()
+    count, own, width = keep.shape
     for target, group in ((send, 1 - side), (keep, side)):
 
         def chunk(k, carry):
             at = pl.multiple_of(k * 8, 8)
             cut = pl.ds(pl.multiple_of(group * own + at, 8), 8)
-            for place, row in enumerate(rows):
-                target[place, pl.ds(at, 8), :] = five_point(
-                    load(row - 1, cut), load(row, cut), load(row + 1, cut)
+            lines = [jnp.zeros((8, width), F32), zero[0, cut, :], one[0, cut, :]]
+            lines += [inners[row, cut, :] for row in range(2)]
+            lines += [inner[0, cut, :].astype(F32)]
+            for row in range(count):
+                target[row, pl.ds(at, 8), :] = five_point(
+                    lines[row], lines[row + 1], lines[row + 2]
                 )
             return carry
 
-        lax.fori_loop(0, own // 8, chunk, 0)
-
-
-def last_inner_kernel(outers, inners, inner, keep, send):
-    def load(row, cut):
-        if row < 2:
-            return outers[row, cut, :]
-        if row < 4:
-            return inners[row - 2, cut, :]
-        return inner[0, cut, :].astype(F32)
-
-    last_kernel((1, 2, 3), load, keep.shape[1], keep, send)
-
-
-def last_outer_kernel(outers, near, unused, keep, send):
-    def load(row, cut):
-        if row < 0:
-            return near[0, cut, :].astype(F32)
-        return outers[row, cut, :]
-
-    last_kernel((0,), load, keep.shape[1], keep, send)
-
-
-def merge_kernel(slots, rows, keep_zero, keep, got_zero, got, out, token):
+        lax.fori_loop(0, own // 8, chunk, 0, unroll=3)
+
+
+def write_tiles(out, at, near, far):
+    first = core_side() == 0
+    lines = [jnp.where(first, a, b) for a, b in zip(near, far)]
+    lines += [jnp.where(first, b, a) for a, b in zip(near[::-1], far[::-1])]
+    out[at : at + 8] = jnp.swapaxes(jnp.stack(lines, axis=0), 0, 1)
+
+
+def merge_kernel(keep_zero, keep, got_zero, got, unused, out, token):
     token[...] = jnp.zeros_like(token)
-    lanes = 128
-    tiles = keep.shape[2] // lanes
-    for i in range(rows // 2):
-        near = row_place(i, rows)
-        far = rows - 1 - near
-        for source, place in (((keep_zero, keep), near), ((got_zero, got), far)):
-            ref, row = (source[0], 0) if i == 0 else (source[1], i - 1)
-            for j in range(tiles):
-                cut = slice(j * lanes, (j + 1) * lanes)
-                out[pl.ds(j * rows + place, slots, stride=tiles * rows), :] = ref[row, :, cut]
+    for at in range(0, out.shape[0], 8):
+        cut = slice(at, at + 8)
+        near = [keep_zero[0, cut, :]] + [keep[i, cut, :] for i in range(keep.shape[0])]
+        far = [got_zero[0, cut, :]] + [got[i, cut, :] for i in range(keep.shape[0])]
+        write_tiles(out, at, near, far)
+
+
+def last_merge_kernel(keep, got, near_halo, far_halo, out):
+    for at in range(0, out.shape[0], 8):
+        cut = slice(at, at + 8)
+        near = [keep[i, cut, :] for i in range(keep.shape[0])]
+        far = [got[i, cut, :] for i in range(keep.shape[0])]
+        near[0] = near[0] + near_halo[cut, :].astype(F32)
+        far[0] = far[0] + far_halo[cut, :].astype(F32)
+        write_tiles(out, at, near, far)
 
 
 def body(slot_field, stiffness, triple_modes, triple_rows, triple_cols, triple_weights, slot_of):
@@ -385,13 +392,20 @@
         ]
         + [jnp.zeros((wide,), F32)] * 3
     )
-    first_row, last_row = slot_field[:, 0, :], slot_field[:, rows - 1, :]
-    got_edge = by_core(jnp.where(side == 0, last_row, first_row))
-    own_edge = jnp.where(side == 0, first_row, last_row)
+    row_block = shape((own, width), F32)
+    near_edge, far_edge = call(
+        edge_kernel,
+        (row_block, row_block),
+        [pltpu.VMEM((2, own, width), F32), pltpu.SemaphoreType.DMA((2,))],
+        2.0,
+        [ANY],
+        60,
+    )(slot_field)
+    got_edge = by_core(far_edge)
     edge = jnp.where(
         side == 0,
-        jnp.concatenate([own_edge, got_edge], axis=0),
-        jnp.concatenate([got_edge, own_edge], axis=0),
+        jnp.concatenate([near_edge, got_edge], axis=0),
+        jnp.concatenate([got_edge, near_edge], axis=0),
     )
     halo = by_tile(edge)
 
@@ -403,16 +417,14 @@
             pltpu.VMEM((room, wide), BF16),
         ],
         6.0,
-        [VMEM, pl.BlockSpec(memory_space=pl.ANY)],
-        16,
+        [VMEM, ANY],
+        24,
     )(entries, edge)
 
-    lanes = width // 128
-    flat = slot_field.reshape(own, rows, lanes, 128).transpose(0, 2, 1, 3).reshape(-1, 128)
     line_block = shape((half + 1, own, width), F32)
-    keep, send = call(
-        functools.partial(split_kernel, own, rows, half), (line_block, line_block), (), 3.0
-    )(flat)
+    keep, send = call(split_kernel, (line_block, line_block), (), 2.5, [VMEM, ANY])(
+        slot_field, edge
+    )
     got = by_core(send)
 
     def bents(count):
@@ -421,7 +433,17 @@
     def outs(count):
         return (shape((count, own, width), F32),) * 2
 
-    def couple(bent, other, first, outer_row, inner_rows):
+    def bend(first, count, after, *halo):
+        bent, buffer = call(
+            functools.partial(first_kernel, first),
+            bents(count),
+            (),
+            0.9 * count,
+            [VMEM] * (4 + len(halo)) + [ANY],
+        )(keep, got, *halo, stiffness, send_table, after)
+        return bent, buffer, by_chip(buffer)
+
+    def couple(bent, other, first, outer_row, inner_rows, weight=1.0):
         count = bent.shape[0]
         out = [shape((count, pair, width), F32)]
         if outer_row is not None:
@@ -432,61 +454,58 @@
             functools.partial(couple_kernel, first, outer_row, inner_rows),
             tuple(out),
             [pltpu.VMEM((room, width), BF16)],
-            1.2 * count,
+            weight * count,
         )(bent, other, stiffness, main_table)
 
-    bent_in, buffer_in = call(first_inner_kernel, bents(3), (), 4.0)(
-        keep, got, stiffness, send_table
-    )
-    cross_in = by_chip(buffer_in)
-    bent_out, buffer_out = call(first_outer_kernel, bents(1), (), 1.5)(
-        keep, got, halo, stiffness, send_table
-    )
-    cross_out = by_chip(buffer_out)
-    moment_in, edge_one, inner = couple(bent_in, cross_in, 1, 1, (3, 2))
+    bent_one, sent, cross_one = bend(1, 1, got)
+    bent_in, sent, cross_in = bend(2, 2, sent)
+    moment_one, edge_one = couple(bent_one, cross_one, 1, 1, ())
     next_near = by_tile(edge_one)
+    bent_out, sent, cross_out = bend(0, 1, edge_one, halo)
+    moment_in, inner = couple(bent_in, cross_in, 2, None, (3, 2))
     inner = by_core(inner)
     moment_out, edge_zero = couple(bent_out, cross_out, 0, 0, ())
     near = by_tile(edge_zero)
 
     held, keep_in, send_in, bent_in, buffer_in = call(
-        second_inner_kernel, (shape((4, pair, width), F32),) + outs(3) + bents(2), (), 4.0
-    )(moment_out, moment_in, inner, stiffness, send_table)
+        second_inner_kernel, (shape((4, pair, width), F32),) + outs(3) + bents(2), (), 3.5
+    )(moment_out, moment_one, moment_in, inner, stiffness, send_table)
     got_in = by_core(send_in)
     cross_in = by_chip(buffer_in)
-    keep_out, send_out, bent_out, buffer_out = call(
-        second_outer_kernel,
-        outs(1) + bents(2),
-        [pltpu.VMEM((1, pair, width), F32)],
-        3.0,
-    )(moment_out, moment_in, near, next_near, held, stiffness, send_table)
+    zero, keep_out, send_out, bent_out, buffer_out = call(
+        second_edge_kernel,
+        (shape((1, pair, width), F32),) + outs(1) + bents(1),
+        (),
+        1.6,
+        [VMEM] * 7 + [ANY],
+    )(moment_out, moment_one, near, next_near, held, stiffness, send_table, cross_in)
     cross_out = by_chip(buffer_out)
+    bent_one, buffer_one = call(second_next_kernel, bents(1), (), 0.01)(
+        zero, held, stiffness, send_table
+    )
+    cross_one = by_chip(buffer_one)
     got_out = by_core(send_out)
-    moment_in, inner = couple(bent_in, cross_in, 2, None, (3,))
+    moment_in, inner = couple(bent_in, cross_in, 2, None, (3,), 0.01)
     inner = by_core(inner)
     moment_out, edge_zero = couple(bent_out, cross_out, 0, 0, ())
     near = by_tile(edge_zero)
-
-    def assemble(*parts):
-        return call(
-            functools.partial(merge_kernel, own, rows),
-            (shape((own * rows * lanes, 128), F32), TOKEN),
-            (),
-            3.5,
-        )(*parts)
-
-    def restore(flat):
-        return flat.reshape(own, lanes, rows, 128).transpose(0, 2, 1, 3).reshape(own, rows, width)
-
-    first_flat, token = assemble(keep_out, keep_in, got_out, got_in)
-    keep_in, send_in = call(last_inner_kernel, outs(3), (), 2.0)(moment_out, moment_in, inner)
-    got_in = by_core(send_in)
-    keep_out, send_out = call(
-        last_outer_kernel, outs(1), (), 1.0
-    )(moment_out, near, token)
-    got_out = by_core(send_out)
-    second_flat, unused = assemble(keep_out, keep_in, got_out, got_in)
-    return restore(first_flat), restore(second_flat)
+    (moment_one,) = couple(bent_one, cross_one, 1, None, ())
+
+    keep, send = call(last_kernel, outs(half), (), 2.5)(
+        moment_out, moment_one, moment_in, inner
+    )
+    got = by_core(send)
+    first_apply, token = call(
+        merge_kernel, (shape(slot_field.shape, F32), TOKEN), (), 1.9, [VMEM] * 4 + [ANY]
+    )(keep_out, keep_in, got_out, got_in, keep)
+    late_side = side + token[0, 0]
+    lower, upper = near[0, :own], near[0, own:]
+    near_halo = jnp.where(late_side == 0, lower, upper)
+    far_halo = by_core(jnp.where(late_side == 0, upper, lower))
+    second_apply = call(last_merge_kernel, shape(slot_field.shape, F32), (), 1.9)(
+        keep, got, near_halo, far_halo
+    )
+    return first_apply, second_apply
 
 
 def solution(mesh):

time: 84.3 us -> 73.8 us (0.88)
  the two profiles are of different devices: /device:TPU:0 before, /device:TPU:11 now
where the time goes in v3:
time: 73.8 us; the launch traced here: 73.6 us
  Pallas kernels  33.9 us (46%)
  starting transfers between devices  20.9 us (28%)
  waiting for transfers between devices  13.9 us (19%)
  local copies, waits for them, and re-layouts  2 us (3%)
  between operations  1.74 us (2%)
  other arithmetic  1.15 us (2%)
    ppermute x4, starting transfers between devices, by_tile(): return lax.ppermute(value, ('chaos', 'tile'), tile_swap)  14 us
    pallas_call x6, Pallas kernels, couple(): call(functools.partial(couple_kernel, first, outer_row, inner_rows), tupl...  8.48 us
    ppermute x4, waiting for transfers between devices, by_tile(): return lax.ppermute(value, ('chaos', 'tile'), tile_swap)  7.26 us
    pallas_call x1, Pallas kernels, body(): call(functools.partial(table_kernel, terms, pair, hubs, slot_total), (sha...  6.24 us
    pallas_call x3, Pallas kernels, bend(): call(functools.partial(first_kernel, first), bents(count), (), 0.9 * coun...  4.76 us
    ppermute x6, waiting for transfers between devices, by_chip(): return lax.ppermute(value, 'chaos', chip_swap)  4.17 us
    ppermute x6, starting transfers between devices, by_chip(): return lax.ppermute(value, 'chaos', chip_swap)  3.51 us
    ppermute x8, starting transfers between devices, by_core(): return lax.ppermute(value, 'chaos', core_swap)  3.34 us
  transfers between devices with their start and end apart: 18, of which 7 were waited for; matrix products, arithmetic and copies ran while one was open for 1% of the time, Pallas kernels for 38%

profile of v3, /device:TPU:11, one launch (start us, length us, event | category | flops | bytes accessed | tf_op | source)
XLA Modules:
  0.0 73.6 jit_solution(8539187948773034451)
XLA Ops:
  0.7 2.1 %shard_map.86 = (f32[72,1024]{1,0:T(8,128)}, f32[72,1024]{1,0:T(8,128)}) custom-call(f32[72,8,1024]{2,1,0:T(8,128)} %field.3), custom_call_target="tpu_custom_call" | custom-call | flops 20000000000 | bytes 10 | tf_op jit(solution)/shard_map/pallas_call | solution.py:396
  6.1 3.4 %collective-permute-start.2 = (f32[144,1024]{1,0:T(8,128)S(1)}, f32[144,1024]{1,0:T(8,128)S(1)}, u32[]{:S(2)}, u32[]{:S(2)}) collective-permute-start(f32[144,1024]{1,0:T(8,128)S(1)} %maximum_select_fusion.unused), channel_id=1, source_target_pairs={{8,1},{1,8},{9,2},{2,9},{10,3},{3,10},{11,4},{4,11},{12,5},{5,12},... | collective-permute-start | bytes 1769480 | tf_op jit(solution)/shard_map/ppermute | solution.py:376
  10.2 6.2 %shard_map.88 = (bf16[12,144,208]{2,1,0:T(8,128)(2,1)S(1)}, bf16[11,64,144]{2,1,0:T(8,128)(2,1)S(1)}) custom-call(f32[8,1664]{1,0:T(8,128)S(1)} %stack.31.entries, f32[144,1024]{1,0:T(8,128)S(1)} %maximum_select_fusion.unused), custom_call_target="tpu_custom_call" | custom-call | flops 60000002048 | bytes 10 | tf_op jit(solution)/shard_map/pallas_call | solution.py:412
  16.4 1.3 %shard_map.89 = (bf16[1,144,1024]{2,1,0:T(8,128)(2,1)S(1)}, bf16[1,56,1024]{2,1,0:T(8,128)(2,1)S(1)}) custom-call(f32[5,72,1024]{2,1,0:T(8,128)S(1)} %get-tuple-element.42.keep, f32[5,72,1024]{2,1,0:T(8,128)S(1)} %collective-permute-done.1.got.rest_2_, f32[11,8,1024]{2,1,0:T(8,128)S(1)} %copy-done, ...), custom_call_target="tpu_custom_call" | custom-call | flops 8999999488 | bytes 10 | tf_op jit(solution)/shard_map/pallas_call | solution.py:437
  18.1 2.1 %shard_map.93 = (bf16[2,144,1024]{2,1,0:T(8,128)(2,1)S(1)}, bf16[2,56,1024]{2,1,0:T(8,128)(2,1)S(1)}) custom-call(f32[5,72,1024]{2,1,0:T(8,128)S(1)} %get-tuple-element.42.keep, f32[5,72,1024]{2,1,0:T(8,128)S(1)} %collective-permute-done.1.got.rest_2_, f32[11,8,1024]{2,1,0:T(8,128)S(1)} %copy-done, ...), custom_call_target="tpu_custom_call" | custom-call | flops 17999998976 | bytes 10 | tf_op jit(solution)/shard_map/pallas_call | solution.py:437
  23.2 4.4 %collective-permute-start.6 = (bf16[1,144,1024]{2,1,0:T(8,128)(2,1)S(1)}, bf16[1,144,1024]{2,1,0:T(8,128)(2,1)S(1)}, u32[]{:S(2)}, u32[]{:S(2)}) collective-permute-start(bf16[1,144,1024]{2,1,0:T(8,128)(2,1)S(1)} %get-tuple-element.48.rest_3_), channel_id=1, source_target_pairs={{8,1},{1,8},{9,2},{2,9},{10,3},{3,10},{11,4},{4,11},{12,5},{5,12},... | collective-permute-start | bytes 884744 | tf_op jit(solution)/shard_map/ppermute | solution.py:376
  27.6 1.4 %shard_map.91 = (bf16[1,144,1024]{2,1,0:T(8,128)(2,1)S(1)}, bf16[1,56,1024]{2,1,0:T(8,128)(2,1)S(1)}) custom-call(f32[5,72,1024]{2,1,0:T(8,128)S(1)} %get-tuple-element.42.keep, f32[5,72,1024]{2,1,0:T(8,128)S(1)} %collective-permute-done.1.got.rest_2_, f32[144,1024]{1,0:T(8,128)S(1)} %collective-permute-done.2.rest_0_, f32[11,8,1024]{2,1,0:T(8,128)S(1)} %copy-done, ...), custom_call_target="tpu_custom_call" | custom-call | flops 8999999488 | bytes 10 | tf_op jit(solution)/shard_map/pallas_call | solution.py:437
  29.2 2.0 %shard_map.94 = (f32[2,144,1024]{2,1,0:T(8,128)S(1)}, bf16[2,144,1024]{2,1,0:T(8,128)(2,1)S(1)}) custom-call(bf16[2,144,1024]{2,1,0:T(8,128)(2,1)S(1)} %get-tuple-element.54.bent, bf16[2,56,1024]{2,1,0:T(8,128)(2,1)S(1)} %collective-permute-done.7.got, f32[11,8,1024]{2,1,0:T(8,128)S(1)} %copy-done, bf16[12,144,208]{2,1,0:T(8,128)(2,1)S(1)} %get-tuple-element.47.table), custom_call_target="tpu_custom_call" | custom-call | flops 20000000000 | bytes 10 | tf_op jit(solution)/shard_map/pallas_call | solution.py:453
  31.4 2.0 %collective-permute-done.4.got = bf16[1,56,1024]{2,1,0:T(8,128)(2,1)S(1)} collective-permute-done((bf16[1,56,1024]{2,1,0:T(8,128)(2,1)S(1)}, bf16[1,56,1024]{2,1,0:T(8,128)(2,1)S(1)}, u32[]{:S(2)}, u32[]{:S(2)}) %collective-permute-start.4) | collective-permute-done | bytes 114720 | tf_op jit(solution)/shard_map/ppermute | solution.py:373
  34.5 3.2 %collective-permute-start.5 = (bf16[1,144,1024]{2,1,0:T(8,128)(2,1)S(1)}, bf16[1,144,1024]{2,1,0:T(8,128)(2,1)S(1)}, u32[]{:S(2)}, u32[]{:S(2)}) collective-permute-start(bf16[1,144,1024]{2,1,0:T(8,128)(2,1)S(1)} %get-tuple-element.53), channel_id=1, source_target_pairs={{8,1},{1,8},{9,2},{2,9},{10,3},{3,10},{11,4},{4,11},{12,5},{5,12},... | collective-permute-start | bytes 884744 | tf_op jit(solution)/shard_map/ppermute | solution.py:376
  37.8 3.0 %shard_map.95 = (f32[4,144,1024]{2,1,0:T(8,128)S(1)}, f32[3,72,1024]{2,1,0:T(8,128)S(1)}, f32[3,72,1024]{2,1,0:T(8,128)S(1)}, bf16[2,144,1024]{2,1,0:T(8,128)(2,1)S(1)}, bf16[2,56,1024]{2,1,0:T(8,128)(2,1)S(1)}) custom-call(f32[1,144,1024]{2,1,0:T(8,128)S(1)} %get-tuple-element.51.row_zero, f32[1,144,1024]{2,1,0:T(8,128)S(1)} %get-tuple-element.52.row_one.others, ...), custom_call_target="tpu_custom_call" | custom-call | flops 35000000512 | bytes 10 | tf_op jit(solution)/shard_map/pallas_call | solution.py:470
  41.0 5.0 %collective-permute-done.5.near = bf16[1,144,1024]{2,1,0:T(8,128)(2,1)S(1)} collective-permute-done((bf16[1,144,1024]{2,1,0:T(8,128)(2,1)S(1)}, bf16[1,144,1024]{2,1,0:T(8,128)(2,1)S(1)}, u32[]{:S(2)}, u32[]{:S(2)}) %collective-permute-start.5) | collective-permute-done | bytes 294944 | tf_op jit(solution)/shard_map/ppermute | solution.py:376
  46.0 1.5 %collective-permute-done.9.unused.got = bf16[2,56,1024]{2,1,0:T(8,128)(2,1)S(1)} collective-permute-done((bf16[2,56,1024]{2,1,0:T(8,128)(2,1)S(1)}, bf16[2,56,1024]{2,1,0:T(8,128)(2,1)S(1)}, u32[]{:S(2)}, u32[]{:S(2)}) %collective-permute-start.9) | collective-permute-done | bytes 229408 | tf_op jit(solution)/shard_map/ppermute | solution.py:373
  47.5 2.1 %shard_map.96 = (f32[1,144,1024]{2,1,0:T(8,128)S(1)}, f32[1,72,1024]{2,1,0:T(8,128)S(1)}, f32[1,72,1024]{2,1,0:T(8,128)S(1)}, bf16[1,144,1024]{2,1,0:T(8,128)(2,1)S(1)}, bf16[1,56,1024]{2,1,0:T(8,128)(2,1)S(1)}) custom-call(f32[1,144,1024]{2,1,0:T(8,128)S(1)} %get-tuple-element.51.row_zero, f32[1,144,1024]{2,1,0:T(8,128)S(1)} %get-tuple-element.52.row_one.others, ...), custom_call_target="tpu_custom_call" | custom-call | flops 16000000000 | bytes 10 | tf_op jit(solution)/shard_map/pallas_call | solution.py:475
  49.7 1.7 %collective-permute-start.11 = (f32[3,72,1024]{2,1,0:T(8,128)S(1)}, f32[3,72,1024]{2,1,0:T(8,128)S(1)}, u32[]{:S(2)}, u32[]{:S(2)}) collective-permute-start(f32[3,72,1024]{2,1,0:T(8,128)S(1)} %get-tuple-element.63), channel_id=1, source_target_pairs={{0,8},{8,0},{16,24},{24,16},{1,9},{9,1},{17,25},{25,17},{2,10},{10... | collective-permute-start | bytes 2654216 | tf_op jit(solution)/shard_map/ppermute | solution.py:370
  52.5 1.5 %collective-permute-start.13 = (bf16[1,56,1024]{2,1,0:T(8,128)(2,1)S(1)}, bf16[1,56,1024]{2,1,0:T(8,128)(2,1)S(1)}, u32[]{:S(2)}, u32[]{:S(2)}) collective-permute-start(bf16[1,56,1024]{2,1,0:T(8,128)(2,1)S(1)} %get-tuple-element.69), channel_id=1, source_target_pairs={{0,16},{8,24},{16,0},{24,8},{1,17},{9,25},{17,1},{25,9},{2,18},{10... | collective-permute-start | bytes 344072 | tf_op jit(solution)/shard_map/ppermute | solution.py:373
  54.2 2.0 %shard_map.100 = (f32[2,144,1024]{2,1,0:T(8,128)S(1)}, bf16[1,144,1024]{2,1,0:T(8,128)(2,1)S(1)}) custom-call(bf16[2,144,1024]{2,1,0:T(8,128)(2,1)S(1)} %get-tuple-element.70.bent, bf16[2,56,1024]{2,1,0:T(8,128)(2,1)S(1)} %collective-permute-done.9.unused.got, f32[11,8,1024]{2,1,0:T(8,128)S(1)} %copy-done, bf16[12,144,208]{2,1,0:T(8,128)(2,1)S(1)} %get-tuple-element.47.table), custom_call_target="tpu_custom_call" | custom-call | flops 200000000 | bytes 10 | tf_op jit(solution)/shard_map/pallas_call | solution.py:453
  57.7 3.0 %collective-permute-start.16 = (bf16[1,144,1024]{2,1,0:T(8,128)(2,1)S(1)}, bf16[1,144,1024]{2,1,0:T(8,128)(2,1)S(1)}, u32[]{:S(2)}, u32[]{:S(2)}) collective-permute-start(bf16[1,144,1024]{2,1,0:T(8,128)(2,1)S(1)} %get-tuple-element.77), channel_id=1, source_target_pairs={{8,1},{1,8},{9,2},{2,9},{10,3},{3,10},{11,4},{4,11},{12,5},{5,12},... | collective-permute-start | bytes 884744 | tf_op jit(solution)/shard_map/ppermute | solution.py:376
  61.8 1.7 %shard_map.101 = (f32[4,72,1024]{2,1,0:T(8,128)S(1)}, f32[4,72,1024]{2,1,0:T(8,128)S(1)}) custom-call(f32[1,144,1024]{2,1,0:T(8,128)S(1)} %get-tuple-element.66.zero, f32[1,144,1024]{2,1,0:T(8,128)S(1)} %shard_map.99.one, f32[2,144,1024]{2,1,0:T(8,128)S(1)} %get-tuple-element.71.inners, bf16[1,144,1024]{2,1,0:T(8,128)(2,1)S(1)} %collective-permute-done.14.inner), custom_call_target="tpu_custom_call" | custom-call | flops 24999999488 | bytes 10 | tf_op jit(solution)/shard_map/pallas_call | solution.py:494
  63.6 1.9 %shard_map.102 = (f32[72,8,1024]{2,1,0:T(8,128)}, s32[8,128]{1,0:T(8,128)S(1)}) custom-call(f32[1,72,1024]{2,1,0:T(8,128)S(1)} %get-tuple-element.60.keep_zero, f32[3,72,1024]{2,1,0:T(8,128)S(1)} %get-tuple-element.61.keep, f32[1,72,1024]{2,1,0:T(8,128)S(1)} %collective-permute-done.10.got_zero, f32[3,72,1024]{2,1,0:T(8,128)S(1)} %collective-permute-done.11.got, ...), custom_call_target="tpu_custom_call" | custom-call | flops 19000000512 | bytes 10 | tf_op jit(solution)/shard_map/pallas_call | solution.py:498
  66.7 2.2 %collective-permute-done.16 = bf16[1,144,1024]{2,1,0:T(8,128)(2,1)S(1)} collective-permute-done((bf16[1,144,1024]{2,1,0:T(8,128)(2,1)S(1)}, bf16[1,144,1024]{2,1,0:T(8,128)(2,1)S(1)}, u32[]{:S(2)}, u32[]{:S(2)}) %collective-permute-start.16) | collective-permute-done | bytes 294944 | tf_op jit(solution)/shard_map/ppermute | solution.py:376
  69.0 1.4 %collective-permute-done.17.far_halo = bf16[72,1024]{1,0:T(8,128)(2,1)S(1)} collective-permute-done((bf16[72,1024]{1,0:T(8,128)(2,1)S(1)}, bf16[72,1024]{1,0:T(8,128)(2,1)S(1)}, u32[]{:S(2)}, u32[]{:S(2)}) %collective-permute-start.17) | collective-permute-done | bytes 147488 | tf_op jit(solution)/shard_map/ppermute | solution.py:370
  70.4 1.3 %copy-done.3 = f32[4,72,1024]{2,1,0:T(8,128)S(1)} copy-done((f32[4,72,1024]{2,1,0:T(8,128)S(1)}, f32[4,72,1024]{2,1,0:T(8,128)}, u32[]{:S(2)}) %copy-start.3) | copy-done | bytes 1179672
  71.6 1.9 %shard_map.103 = f32[72,8,1024]{2,1,0:T(8,128)} custom-call(f32[4,72,1024]{2,1,0:T(8,128)S(1)} %copy-done.3, f32[4,72,1024]{2,1,0:T(8,128)S(1)} %collective-permute-done.15.got, bf16[72,1024]{1,0:T(8,128)(2,1)S(1)} %get-tuple-element.79.near_halo, bf16[72,1024]{1,0:T(8,128)(2,1)S(1)} %collective-permute-done.17.far_halo), custom_call_target="tpu_custom_call" | custom-call | flops 19000000512 | bytes 10 | tf_op jit(solution)/shard_map/pallas_call | solution.py:505
  (68 shorter events, 13.3 us)
Async XLA Ops:
  0.6 3.0 %copy-start.4 = (s32[1606]{0:T(1024)S(1)}, s32[1606]{0:T(1024)}, u32[]{:S(2)}) copy-start(s32[1606]{0:T(1024)} %param.9) | copy-start | bytes 19276
  0.7 3.0 %copy-start.5 = (s32[1606]{0:T(1024)S(1)}, s32[1606]{0:T(1024)}, u32[]{:S(2)}) copy-start(s32[1606]{0:T(1024)} %param.10) | copy-start | bytes 19276
  0.7 3.0 %copy-start.6 = (s32[1606]{0:T(1024)S(1)}, s32[1606]{0:T(1024)}, u32[]{:S(2)}) copy-start(s32[1606]{0:T(1024)} %param.11) | copy-start | bytes 19276
  0.7 3.1 %copy-start.7 = (bf16[1606]{0:T(1024)(128)(2,1)S(1)}, bf16[1606]{0:T(1024)(128)(2,1)}, u32[]{:S(2)}) copy-start(bf16[1606]{0:T(1024)(128)(2,1)} %param.12) | copy-start | bytes 9640
  0.7 8.8 %copy-start.1 = (f32[72,8,1024]{2,1,0:T(8,128)S(1)}, f32[72,8,1024]{2,1,0:T(8,128)}, u32[]{:S(2)}) copy-start(f32[72,8,1024]{2,1,0:T(8,128)} %field.3) | copy-start | bytes 7077892
  2.8 2.2 %collective-permute-start = (f32[72,1024]{1,0:T(8,128)}, f32[72,1024]{1,0:T(8,128)S(1)}, u32[]{:S(2)}, u32[]{:S(2)}) collective-permute-start(f32[72,1024]{1,0:T(8,128)} %get-tuple-element.41), channel_id=1, source_target_pairs={{0,8},{8,0},{16,24},{24,16},{1,9},{9,1},{17,25},{25,17},{2,10},{10... | collective-permute-start | bytes 884744 | tf_op jit(solution)/shard_map/ppermute | solution.py:370
  6.1 21.5 %collective-permute-start.2 = (f32[144,1024]{1,0:T(8,128)S(1)}, f32[144,1024]{1,0:T(8,128)S(1)}, u32[]{:S(2)}, u32[]{:S(2)}) collective-permute-start(f32[144,1024]{1,0:T(8,128)S(1)} %maximum_select_fusion.unused), channel_id=1, source_target_pairs={{8,1},{1,8},{9,2},{2,9},{10,3},{3,10},{11,4},{4,11},{12,5},{5,12},... | collective-permute-start | bytes 1769480 | tf_op jit(solution)/shard_map/ppermute | solution.py:376
  10.1 6.4 %copy-start = (f32[11,8,1024]{2,1,0:T(8,128)S(1)}, f32[11,8,1024]{2,1,0:T(8,128)}, u32[]{:S(2)}) copy-start(f32[11,8,1024]{2,1,0:T(8,128)} %stiff.17) | copy-start | bytes 1081348
  10.1 6.3 %collective-permute-start.1 = (f32[5,72,1024]{2,1,0:T(8,128)S(1)}, f32[5,72,1024]{2,1,0:T(8,128)S(1)}, u32[]{:S(2)}, u32[]{:S(2)}) collective-permute-start(f32[5,72,1024]{2,1,0:T(8,128)S(1)} %get-tuple-element.43), channel_id=1, source_target_pairs={{0,8},{8,0},{16,24},{24,16},{1,9},{9,1},{17,25},{25,17},{2,10},{10... | collective-permute-start | bytes 4423688 | tf_op jit(solution)/shard_map/ppermute | solution.py:370
  17.8 4.3 %collective-permute-start.3 = (bf16[1,56,1024]{2,1,0:T(8,128)(2,1)S(1)}, bf16[1,56,1024]{2,1,0:T(8,128)(2,1)S(1)}, u32[]{:S(2)}, u32[]{:S(2)}) collective-permute-start(bf16[1,56,1024]{2,1,0:T(8,128)(2,1)S(1)} %get-tuple-element.46.rest_2_), channel_id=1, source_target_pairs={{0,16},{8,24},{16,0},{24,8},{1,17},{9,25},{17,1},{25,9},{2,18},{10... | collective-permute-start | bytes 344072 | tf_op jit(solution)/shard_map/ppermute | solution.py:373
  20.2 9.1 %collective-permute-start.7 = (bf16[2,56,1024]{2,1,0:T(8,128)(2,1)S(1)}, bf16[2,56,1024]{2,1,0:T(8,128)(2,1)S(1)}, u32[]{:S(2)}, u32[]{:S(2)}) collective-permute-start(bf16[2,56,1024]{2,1,0:T(8,128)(2,1)S(1)} %get-tuple-element.55), channel_id=1, source_target_pairs={{0,16},{8,24},{16,0},{24,8},{1,17},{9,25},{17,1},{25,9},{2,18},{10... | collective-permute-start | bytes 688136 | tf_op jit(solution)/shard_map/ppermute | solution.py:373
  23.2 17.8 %collective-permute-start.6 = (bf16[1,144,1024]{2,1,0:T(8,128)(2,1)S(1)}, bf16[1,144,1024]{2,1,0:T(8,128)(2,1)S(1)}, u32[]{:S(2)}, u32[]{:S(2)}) collective-permute-start(bf16[1,144,1024]{2,1,0:T(8,128)(2,1)S(1)} %get-tuple-element.48.rest_3_), channel_id=1, source_target_pairs={{8,1},{1,8},{9,2},{2,9},{10,3},{3,10},{11,4},{4,11},{12,5},{5,12},... | collective-permute-start | bytes 884744 | tf_op jit(solution)/shard_map/ppermute | solution.py:376
  29.0 4.4 %collective-permute-start.4 = (bf16[1,56,1024]{2,1,0:T(8,128)(2,1)S(1)}, bf16[1,56,1024]{2,1,0:T(8,128)(2,1)S(1)}, u32[]{:S(2)}, u32[]{:S(2)}) collective-permute-start(bf16[1,56,1024]{2,1,0:T(8,128)(2,1)S(1)} %get-tuple-element.50), channel_id=1, source_target_pairs={{0,16},{8,24},{16,0},{24,8},{1,17},{9,25},{17,1},{25,9},{2,18},{10... | collective-permute-start | bytes 344072 | tf_op jit(solution)/shard_map/ppermute | solution.py:373
  31.3 6.5 %collective-permute-start.8 = (bf16[2,144,1024]{2,1,0:T(8,128)(2,1)S(1)}, bf16[2,144,1024]{2,1,0:T(8,128)(2,1)S(1)}, u32[]{:S(2)}, u32[]{:S(2)}) collective-permute-start(bf16[2,144,1024]{2,1,0:T(8,128)(2,1)S(1)} %get-tuple-element.57), channel_id=1, source_target_pairs={{0,8},{8,0},{16,24},{24,16},{1,9},{9,1},{17,25},{25,17},{2,10},{10... | collective-permute-start | bytes 1769480 | tf_op jit(solution)/shard_map/ppermute | solution.py:370
  34.5 11.5 %collective-permute-start.5 = (bf16[1,144,1024]{2,1,0:T(8,128)(2,1)S(1)}, bf16[1,144,1024]{2,1,0:T(8,128)(2,1)S(1)}, u32[]{:S(2)}, u32[]{:S(2)}) collective-permute-start(bf16[1,144,1024]{2,1,0:T(8,128)(2,1)S(1)} %get-tuple-element.53), channel_id=1, source_target_pairs={{8,1},{1,8},{9,2},{2,9},{10,3},{3,10},{11,4},{4,11},{12,5},{5,12},... | collective-permute-start | bytes 884744 | tf_op jit(solution)/shard_map/ppermute | solution.py:376
  40.8 6.7 %collective-permute-start.9 = (bf16[2,56,1024]{2,1,0:T(8,128)(2,1)S(1)}, bf16[2,56,1024]{2,1,0:T(8,128)(2,1)S(1)}, u32[]{:S(2)}, u32[]{:S(2)}) collective-permute-start(bf16[2,56,1024]{2,1,0:T(8,128)(2,1)S(1)} %get-tuple-element.59), channel_id=1, source_target_pairs={{0,16},{8,24},{16,0},{24,8},{1,17},{9,25},{17,1},{25,9},{2,18},{10... | collective-permute-start | bytes 688136 | tf_op jit(solution)/shard_map/ppermute | solution.py:373
  49.6 7.0 %collective-permute-start.12 = (bf16[1,56,1024]{2,1,0:T(8,128)(2,1)S(1)}, bf16[1,56,1024]{2,1,0:T(8,128)(2,1)S(1)}, u32[]{:S(2)}, u32[]{:S(2)}) collective-permute-start(bf16[1,56,1024]{2,1,0:T(8,128)(2,1)S(1)} %get-tuple-element.65), channel_id=1, source_target_pairs={{0,16},{8,24},{16,0},{24,8},{1,17},{9,25},{17,1},{25,9},{2,18},{10... | collective-permute-start | bytes 344072 | tf_op jit(solution)/shard_map/ppermute | solution.py:373
  49.7 13.9 %collective-permute-start.11 = (f32[3,72,1024]{2,1,0:T(8,128)S(1)}, f32[3,72,1024]{2,1,0:T(8,128)S(1)}, u32[]{:S(2)}, u32[]{:S(2)}) collective-permute-start(f32[3,72,1024]{2,1,0:T(8,128)S(1)} %get-tuple-element.63), channel_id=1, source_target_pairs={{0,8},{8,0},{16,24},{24,16},{1,9},{9,1},{17,25},{25,17},{2,10},{10... | collective-permute-start | bytes 2654216 | tf_op jit(solution)/shard_map/ppermute | solution.py:370
  52.5 8.2 %collective-permute-start.13 = (bf16[1,56,1024]{2,1,0:T(8,128)(2,1)S(1)}, bf16[1,56,1024]{2,1,0:T(8,128)(2,1)S(1)}, u32[]{:S(2)}, u32[]{:S(2)}) collective-permute-start(bf16[1,56,1024]{2,1,0:T(8,128)(2,1)S(1)} %get-tuple-element.69), channel_id=1, source_target_pairs={{0,16},{8,24},{16,0},{24,8},{1,17},{9,25},{17,1},{25,9},{2,18},{10... | collective-permute-start | bytes 344072 | tf_op jit(solution)/shard_map/ppermute | solution.py:373
  54.0 9.6 %collective-permute-start.10 = (f32[1,72,1024]{2,1,0:T(8,128)S(1)}, f32[1,72,1024]{2,1,0:T(8,128)S(1)}, u32[]{:S(2)}, u32[]{:S(2)}) collective-permute-start(f32[1,72,1024]{2,1,0:T(8,128)S(1)} %get-tuple-element.62), channel_id=1, source_target_pairs={{0,8},{8,0},{16,24},{24,16},{1,9},{9,1},{17,25},{25,17},{2,10},{10... | collective-permute-start | bytes 884744 | tf_op jit(solution)/shard_map/ppermute | solution.py:370
  56.3 5.5 %collective-permute-start.14 = (bf16[1,144,1024]{2,1,0:T(8,128)(2,1)S(1)}, bf16[1,144,1024]{2,1,0:T(8,128)(2,1)S(1)}, u32[]{:S(2)}, u32[]{:S(2)}) collective-permute-start(bf16[1,144,1024]{2,1,0:T(8,128)(2,1)S(1)} %get-tuple-element.72), channel_id=1, source_target_pairs={{0,8},{8,0},{16,24},{24,16},{1,9},{9,1},{17,25},{25,17},{2,10},{10... | collective-permute-start | bytes 884744 | tf_op jit(solution)/shard_map/ppermute | solution.py:370
  57.7 11.2 %collective-permute-start.16 = (bf16[1,144,1024]{2,1,0:T(8,128)(2,1)S(1)}, bf16[1,144,1024]{2,1,0:T(8,128)(2,1)S(1)}, u32[]{:S(2)}, u32[]{:S(2)}) collective-permute-start(bf16[1,144,1024]{2,1,0:T(8,128)(2,1)S(1)} %get-tuple-element.77), channel_id=1, source_target_pairs={{8,1},{1,8},{9,2},{2,9},{10,3},{3,10},{11,4},{4,11},{12,5},{5,12},... | collective-permute-start | bytes 884744 | tf_op jit(solution)/shard_map/ppermute | solution.py:376
  63.5 6.9 %collective-permute-start.15 = (f32[4,72,1024]{2,1,0:T(8,128)S(1)}, f32[4,72,1024]{2,1,0:T(8,128)S(1)}, u32[]{:S(2)}, u32[]{:S(2)}) collective-permute-start(f32[4,72,1024]{2,1,0:T(8,128)S(1)} %get-tuple-element.75), channel_id=1, source_target_pairs={{0,8},{8,0},{16,24},{24,16},{1,9},{9,1},{17,25},{25,17},{2,10},{10... | collective-permute-start | bytes 3538952 | tf_op jit(solution)/shard_map/ppermute | solution.py:370
  68.9 1.4 %collective-permute-start.17 = (bf16[72,1024]{1,0:T(8,128)(2,1)S(1)}, bf16[72,1024]{1,0:T(8,128)(2,1)S(1)}, u32[]{:S(2)}, u32[]{:S(2)}) collective-permute-start(bf16[72,1024]{1,0:T(8,128)(2,1)S(1)} %get-tuple-element.78), channel_id=1, source_target_pairs={{0,8},{8,0},{16,24},{24,16},{1,9},{9,1},{17,25},{25,17},{2,10},{10... | collective-permute-start | bytes 442376 | tf_op jit(solution)/shard_map/ppermute | solution.py:370
  (3 other events, 6.3 us)

commit v4 on v3

--- a/solution.py
+++ b/solution.py
@@ -14,8 +14,10 @@
 STEP = 16
 
 
-def call(kernel, outs, scratch=(), us=1.0, specs=None, room=12):
+def call(kernel, outs, scratch=(), us=1.0, specs=None, room=12, into=None):
     extra = {} if specs is None else {"in_specs": specs}
+    if into is not None:
+        extra["out_specs"] = into
     return pl.pallas_call(
         kernel,
         out_shape=outs,
@@ -36,7 +38,9 @@
     return lax.rem(lax.axis_index("chaos"), 2)
 
 
-def table_kernel(terms, pair, hubs, slot_total, entries, unused, main_ref, send_ref, picks, cols):
+def table_kernel(
+    terms, pair, hubs, slot_total, entries, unused, main_ref, send_ref, picks, codes, cols
+):
     wide = entries.shape[1]
     modes = entries[0:1, :]
     rows = entries[1:2, :]
@@ -79,32 +83,23 @@
     lanes = lax.broadcasted_iota(jnp.int32, (pair, slot_total), 1).astype(F32)
     own_index = jnp.sum(jnp.where(place == slots, lanes, 0.0), axis=1, keepdims=True)
 
+    tail = cols.shape[0] - pair
+    far_cols = jnp.concatenate([hub_far, jnp.full((tail - hubs, 1), -5.0, F32)], axis=0)
+    far_rows = jnp.concatenate([hub_far, jnp.full((64 - hubs, 1), -5.0, F32)], axis=0)
     cols[0:pair, :] = jnp.where(own_index == colv, 1.0, 0.0).astype(BF16)
-    tail = cols.shape[0] - pair
-    far_pad = jnp.concatenate([hub_far, jnp.full((tail - hubs, 1), -5.0, F32)], axis=0)
-    cols[pair:, :] = jnp.where(far_pad == colv, 1.0, 0.0).astype(BF16)
-
+    cols[pair:, :] = jnp.where(far_cols == colv, 1.0, 0.0).astype(BF16)
+    coded = modes + 1.0
+    for index, start, stop in ((own_index, 0, pair), (far_rows, pair, pair + 64)):
+        hit = index == rows
+        picks[start:stop, :] = jnp.where(hit, weights, 0.0).astype(BF16)
+        codes[start:stop, :] = jnp.where(hit, coded, 0.0).astype(BF16)
+    weight = lax.dot_general(picks[...], cols[...], NT, preferred_element_type=F32)
+    code = lax.dot_general(codes[...], cols[...], NT, preferred_element_type=F32)
     for mode in range(terms):
-        keyed = jnp.where(modes == float(mode), rows, -1.0)
-        picks[mode * pair : (mode + 1) * pair, :] = jnp.where(
-            own_index == keyed, weights, 0.0
-        ).astype(BF16)
-    start = terms * pair
-    far16 = jnp.concatenate([hub_far, jnp.full((64 - hubs, 1), -5.0, F32)], axis=0)
-    for mode in range(1, terms):
-        keyed = jnp.where(modes == float(mode), rows, -1.0)
-        at = start + (mode - 1) * 64
-        picks[at : at + 64, :] = jnp.where(far16 == keyed, weights, 0.0).astype(BF16)
-
-    for mode in range(terms):
-        main_ref[mode] = lax.dot_general(
-            picks[mode * pair : (mode + 1) * pair, :], cols[...], NT, preferred_element_type=F32
-        ).astype(BF16)
-    for mode in range(1, terms):
-        at = start + (mode - 1) * 64
-        send_ref[mode] = lax.dot_general(
-            picks[at : at + 64, :], cols[0:pair, :], NT, preferred_element_type=F32
-        ).astype(BF16)
+        table = jnp.where(code == float(mode + 1), weight, 0.0).astype(BF16)
+        main_ref[mode] = table[:pair]
+        if mode > 0:
+            send_ref[mode] = table[pair:, :pair]
     hub_lane = lax.broadcasted_iota(jnp.int32, (pair, cols.shape[0]), 1).astype(F32) - float(pair)
     own_rank = jnp.sum(
         jnp.where(lanes == own_index, rank, 0.0), axis=1, keepdims=True
@@ -201,7 +196,7 @@
         fill_buffer(bent, stiff, send_table, buffer, row, row_place(first_row + row, stiff.shape[1]))
 
 
-def couple_kernel(first, outer_row, inner_rows, bent, got, stiff, table, moment, *rest):
+def couple_kernel(first, outer_row, inner_rows, bent, got, stiff, table, unused, moment, *rest):
     stacked = rest[-1]
     edges = list(rest[:-1])
     outer = edges.pop(0) if outer_row is not None else None
@@ -263,7 +258,7 @@
 
 
 def second_edge_kernel(
-    row_zero, others, near, next_near, held, stiff, send_table, unused, zero, keep, send, bent, buffer
+    row_zero, others, near, next_near, held, stiff, send_table, zero, keep, send, bent, buffer
 ):
     pair = bent.shape[1]
     tile = lax.axis_index("tile")
@@ -286,7 +281,7 @@
     share(zero, keep, send, (0,), pair // 2)
 
 
-def second_next_kernel(zero, held, stiff, send_table, bent, buffer):
+def second_next_kernel(zero, held, stiff, send_table, unused, bent, buffer):
     pair = bent.shape[1]
 
     def chunk(k, carry):
@@ -319,30 +314,51 @@
         lax.fori_loop(0, own // 8, chunk, 0, unroll=3)
 
 
-def write_tiles(out, at, near, far):
+def write_tiles(near, far, out, lines, done):
     first = core_side() == 0
-    lines = [jnp.where(first, a, b) for a, b in zip(near, far)]
-    lines += [jnp.where(first, b, a) for a, b in zip(near[::-1], far[::-1])]
-    out[at : at + 8] = jnp.swapaxes(jnp.stack(lines, axis=0), 0, 1)
-
-
-def merge_kernel(keep_zero, keep, got_zero, got, unused, out, token):
+    half = out.shape[1] // 2
+    step = 24
+    copies = []
+    for k, at in enumerate(range(0, out.shape[0], step)):
+        for start in range(at, at + step, 8):
+            ours = [near(i, slice(start, start + 8)) for i in range(half)]
+            theirs = [far(i, slice(start, start + 8)) for i in range(half)]
+            rows = [jnp.where(first, a, b) for a, b in zip(ours, theirs)]
+            rows += [jnp.where(first, b, a) for a, b in zip(ours[::-1], theirs[::-1])]
+            lines[start : start + 8] = jnp.swapaxes(jnp.stack(rows, axis=0), 0, 1)
+        cut = pl.ds(at, step)
+        copies.append(pltpu.make_async_copy(lines.at[cut], out.at[cut], done.at[k]))
+        copies[-1].start()
+    for copy in copies:
+        copy.wait()
+
+
+def merge_kernel(keep_zero, keep, got_zero, got, unused, out, token, lines, done):
     token[...] = jnp.zeros_like(token)
-    for at in range(0, out.shape[0], 8):
-        cut = slice(at, at + 8)
-        near = [keep_zero[0, cut, :]] + [keep[i, cut, :] for i in range(keep.shape[0])]
-        far = [got_zero[0, cut, :]] + [got[i, cut, :] for i in range(keep.shape[0])]
-        write_tiles(out, at, near, far)
-
-
-def last_merge_kernel(keep, got, near_halo, far_halo, out):
-    for at in range(0, out.shape[0], 8):
-        cut = slice(at, at + 8)
-        near = [keep[i, cut, :] for i in range(keep.shape[0])]
-        far = [got[i, cut, :] for i in range(keep.shape[0])]
-        near[0] = near[0] + near_halo[cut, :].astype(F32)
-        far[0] = far[0] + far_halo[cut, :].astype(F32)
-        write_tiles(out, at, near, far)
+
+    def near(i, cut):
+        return keep_zero[0, cut, :] if i == 0 else keep[i - 1, cut, :]
+
+    def far(i, cut):
+        return got_zero[0, cut, :] if i == 0 else got[i - 1, cut, :]
+
+    write_tiles(near, far, out, lines, done)
+
+
+def last_merge_kernel(keep, got, halo, far_halo, out, lines, done):
+    own = keep.shape[1]
+    first = core_side() == 0
+    halos = halo[0].astype(F32)
+    near_line = jnp.where(first, halos[:own], halos[own:])
+    far_line = far_halo[...].astype(F32)
+
+    def near(i, cut):
+        return keep[0, cut, :] + near_line[cut] if i == 0 else keep[i, cut, :]
+
+    def far(i, cut):
+        return got[0, cut, :] + far_line[cut] if i == 0 else got[i, cut, :]
+
+    write_tiles(near, far, out, lines, done)
 
 
 def body(slot_field, stiffness, triple_modes, triple_rows, triple_cols, triple_weights, slot_of):
@@ -413,12 +429,13 @@
         functools.partial(table_kernel, terms, pair, hubs, slot_total),
         (shape((terms + 1, pair, room), BF16), shape((terms, 64, pair), BF16)),
         [
-            pltpu.VMEM((terms * pair + modes * 64, wide), BF16),
+            pltpu.VMEM((pair + 64, wide), BF16),
+            pltpu.VMEM((pair + 64, wide), BF16),
             pltpu.VMEM((room, wide), BF16),
         ],
-        6.0,
+        3.0,
         [VMEM, ANY],
-        24,
+        12,
     )(entries, edge)
 
     line_block = shape((half + 1, own, width), F32)
@@ -443,7 +460,7 @@
         )(keep, got, *halo, stiffness, send_table, after)
         return bent, buffer, by_chip(buffer)
 
-    def couple(bent, other, first, outer_row, inner_rows, weight=1.0):
+    def couple(bent, other, first, outer_row, inner_rows, after, weight=1.0):
         count = bent.shape[0]
         out = [shape((count, pair, width), F32)]
         if outer_row is not None:
@@ -455,16 +472,17 @@
             tuple(out),
             [pltpu.VMEM((room, width), BF16)],
             weight * count,
-        )(bent, other, stiffness, main_table)
+            [VMEM] * 4 + [ANY],
+        )(bent, other, stiffness, main_table, after)
 
     bent_one, sent, cross_one = bend(1, 1, got)
     bent_in, sent, cross_in = bend(2, 2, sent)
-    moment_one, edge_one = couple(bent_one, cross_one, 1, 1, ())
+    moment_one, edge_one = couple(bent_one, cross_one, 1, 1, (), sent)
     next_near = by_tile(edge_one)
     bent_out, sent, cross_out = bend(0, 1, edge_one, halo)
-    moment_in, inner = couple(bent_in, cross_in, 2, None, (3, 2))
-    inner = by_core(inner)
-    moment_out, edge_zero = couple(bent_out, cross_out, 0, 0, ())
+    moment_in, edge_in = couple(bent_in, cross_in, 2, None, (3, 2), sent)
+    inner = by_core(edge_in)
+    moment_out, edge_zero = couple(bent_out, cross_out, 0, 0, (), edge_in)
     near = by_tile(edge_zero)
 
     held, keep_in, send_in, bent_in, buffer_in = call(
@@ -476,34 +494,33 @@
         second_edge_kernel,
         (shape((1, pair, width), F32),) + outs(1) + bents(1),
         (),
-        1.6,
-        [VMEM] * 7 + [ANY],
-    )(moment_out, moment_one, near, next_near, held, stiffness, send_table, cross_in)
+        0.01,
+    )(moment_out, moment_one, near, next_near, held, stiffness, send_table)
     cross_out = by_chip(buffer_out)
-    bent_one, buffer_one = call(second_next_kernel, bents(1), (), 0.01)(
-        zero, held, stiffness, send_table
+    bent_one, buffer_one = call(second_next_kernel, bents(1), (), 0.01, [VMEM] * 4 + [ANY])(
+        zero, held, stiffness, send_table, cross_in
     )
     cross_one = by_chip(buffer_one)
     got_out = by_core(send_out)
-    moment_in, inner = couple(bent_in, cross_in, 2, None, (3,), 0.01)
+    moment_out, edge_zero = couple(bent_out, cross_out, 0, 0, (), buffer_one)
+    near = by_tile(edge_zero)
+    moment_in, inner = couple(bent_in, cross_in, 2, None, (3,), edge_zero)
     inner = by_core(inner)
-    moment_out, edge_zero = couple(bent_out, cross_out, 0, 0, ())
-    near = by_tile(edge_zero)
-    (moment_one,) = couple(bent_one, cross_one, 1, None, ())
+    (moment_one,) = couple(bent_one, cross_one, 1, None, (), edge_zero)
 
     keep, send = call(last_kernel, outs(half), (), 2.5)(
         moment_out, moment_one, moment_in, inner
     )
     got = by_core(send)
+    whole = shape(slot_field.shape, F32)
+    writers = [pltpu.VMEM(slot_field.shape, F32), pltpu.SemaphoreType.DMA((own // 24,))]
     first_apply, token = call(
-        merge_kernel, (shape(slot_field.shape, F32), TOKEN), (), 1.9, [VMEM] * 4 + [ANY]
+        merge_kernel, (whole, TOKEN), writers, 1.9, [VMEM] * 4 + [ANY], 6, (ANY, VMEM)
     )(keep_out, keep_in, got_out, got_in, keep)
     late_side = side + token[0, 0]
-    lower, upper = near[0, :own], near[0, own:]
-    near_halo = jnp.where(late_side == 0, lower, upper)
-    far_halo = by_core(jnp.where(late_side == 0, upper, lower))
-    second_apply = call(last_merge_kernel, shape(slot_field.shape, F32), (), 1.9)(
-        keep, got, near_halo, far_halo
+    far_halo = by_core(jnp.where(late_side == 0, near[0, own:], near[0, :own]))
+    second_apply = call(last_merge_kernel, whole, writers, 1.9, [VMEM] * 4, 6, ANY)(
+        keep, got, near, far_halo
     )
     return first_apply, second_apply
 

time: 73.8 us -> 68.9 us (0.934)
  the two profiles are of different devices: /device:TPU:11 before, /device:TPU:0 now
where the time goes in v4:
time: 68.9 us; the launch traced here: 68.7 us
  starting transfers between devices  29.3 us (43%)
  Pallas kernels  29.1 us (42%)
  waiting for transfers between devices  5.43 us (8%)
  local copies, waits for them, and re-layouts  1.98 us (3%)
  between operations  1.8 us (3%)
  other arithmetic  1.15 us (2%)
    ppermute x8, starting transfers between devices, by_core(): return lax.ppermute(value, 'chaos', core_swap)  19.8 us
    pallas_call x6, Pallas kernels, couple(): call(functools.partial(couple_kernel, first, outer_row, inner_rows), tupl...  8.34 us
    ppermute x6, starting transfers between devices, by_chip(): return lax.ppermute(value, 'chaos', chip_swap)  6.54 us
    pallas_call x3, Pallas kernels, bend(): call(functools.partial(first_kernel, first), bents(count), (), 0.9 * coun...  4.69 us
    ppermute x8, waiting for transfers between devices, by_core(): return lax.ppermute(value, 'chaos', core_swap)  3.06 us
    pallas_call x1, Pallas kernels, body(): call(second_inner_kernel, (shape((4, pair, width), F32),) + outs(3) + ben...  3.03 us
    ppermute x4, starting transfers between devices, by_tile(): return lax.ppermute(value, ('chaos', 'tile'), tile_swap)  2.92 us
    ppermute x6, waiting for transfers between devices, by_chip(): return lax.ppermute(value, 'chaos', chip_swap)  2.36 us
  transfers between devices with their start and end apart: 18, of which 6 were waited for; matrix products, arithmetic and copies ran while one was open for 1% of the time, Pallas kernels for 37%

profile of v4, /device:TPU:0, one launch (start us, length us, event | category | flops | bytes accessed | tf_op | source)
XLA Modules:
  0.0 68.7 jit_solution(3232091960052724219)
XLA Ops:
  0.7 2.1 %shard_map.86 = (f32[72,1024]{1,0:T(8,128)}, f32[72,1024]{1,0:T(8,128)}) custom-call(f32[72,8,1024]{2,1,0:T(8,128)} %field.3), custom_call_target="tpu_custom_call" | custom-call | flops 20000000000 | bytes 10 | tf_op jit(solution)/shard_map/pallas_call | solution.py:412
  3.7 1.1 %collective-permute-done = f32[72,1024]{1,0:T(8,128)S(1)} collective-permute-done((f32[72,1024]{1,0:T(8,128)}, f32[72,1024]{1,0:T(8,128)S(1)}, u32[]{:S(2)}, u32[]{:S(2)}) %collective-permute-start) | collective-permute-done | bytes 294944 | tf_op jit(solution)/shard_map/ppermute | solution.py:386
  4.8 1.1 %maximum_select_fusion.unused = f32[144,1024]{1,0:T(8,128)S(1)} fusion(f32[72,1024]{1,0:T(8,128)S(1)} %collective-permute-done, f32[72,1024]{1,0:T(8,128)} %get-tuple-element.40, pred[]{:T(512)S(6)} %eq.6), kind=kLoop, calls=%fused_computation | loop fusion | flops 442368 | bytes 1179649 | tf_op jit(solution)/shard_map/jit(_where)/select_n | solution.py:421
  7.1 4.3 %collective-permute-start.1 = (f32[5,72,1024]{2,1,0:T(8,128)S(1)}, f32[5,72,1024]{2,1,0:T(8,128)S(1)}, u32[]{:S(2)}, u32[]{:S(2)}) collective-permute-start(f32[5,72,1024]{2,1,0:T(8,128)S(1)} %get-tuple-element.43), channel_id=1, source_target_pairs={{0,8},{8,0},{16,24},{24,16},{1,9},{9,1},{17,25},{25,17},{2,10},{10... | collective-permute-start | bytes 4423688 | tf_op jit(solution)/shard_map/ppermute | solution.py:386
  11.4 2.3 %shard_map.88 = (bf16[12,144,208]{2,1,0:T(8,128)(2,1)S(1)}, bf16[11,64,144]{2,1,0:T(8,128)(2,1)S(1)}) custom-call(f32[8,1664]{1,0:T(8,128)S(1)} %stack.31.entries, f32[144,1024]{1,0:T(8,128)S(1)} %maximum_select_fusion.unused), custom_call_target="tpu_custom_call" | custom-call | flops 30000001024 | bytes 10 | tf_op jit(solution)/shard_map/pallas_call | solution.py:428
  14.3 1.3 %shard_map.89 = (bf16[1,144,1024]{2,1,0:T(8,128)(2,1)S(1)}, bf16[1,56,1024]{2,1,0:T(8,128)(2,1)S(1)}) custom-call(f32[5,72,1024]{2,1,0:T(8,128)S(1)} %get-tuple-element.42.keep, f32[5,72,1024]{2,1,0:T(8,128)S(1)} %collective-permute-done.1.got.rest_2_, f32[11,8,1024]{2,1,0:T(8,128)S(1)} %copy-done, ...), custom_call_target="tpu_custom_call" | custom-call | flops 8999999488 | bytes 10 | tf_op jit(solution)/shard_map/pallas_call | solution.py:454
  15.6 1.6 %collective-permute-start.3 = (bf16[1,56,1024]{2,1,0:T(8,128)(2,1)S(1)}, bf16[1,56,1024]{2,1,0:T(8,128)(2,1)S(1)}, u32[]{:S(2)}, u32[]{:S(2)}) collective-permute-start(bf16[1,56,1024]{2,1,0:T(8,128)(2,1)S(1)} %get-tuple-element.46.rest_2_), channel_id=1, source_target_pairs={{0,16},{8,24},{16,0},{24,8},{1,17},{9,25},{17,1},{25,9},{2,18},{10... | collective-permute-start | bytes 344072 | tf_op jit(solution)/shard_map/ppermute | solution.py:389
  17.2 2.0 %shard_map.90 = (bf16[2,144,1024]{2,1,0:T(8,128)(2,1)S(1)}, bf16[2,56,1024]{2,1,0:T(8,128)(2,1)S(1)}) custom-call(f32[5,72,1024]{2,1,0:T(8,128)S(1)} %get-tuple-element.42.keep, f32[5,72,1024]{2,1,0:T(8,128)S(1)} %collective-permute-done.1.got.rest_2_, f32[11,8,1024]{2,1,0:T(8,128)S(1)} %copy-done, ...), custom_call_target="tpu_custom_call" | custom-call | flops 17999998976 | bytes 10 | tf_op jit(solution)/shard_map/pallas_call | solution.py:454
  19.9 1.3 %collective-permute-done.3.got = bf16[1,56,1024]{2,1,0:T(8,128)(2,1)S(1)} collective-permute-done((bf16[1,56,1024]{2,1,0:T(8,128)(2,1)S(1)}, bf16[1,56,1024]{2,1,0:T(8,128)(2,1)S(1)}, u32[]{:S(2)}, u32[]{:S(2)}) %collective-permute-start.3) | collective-permute-done | bytes 114720 | tf_op jit(solution)/shard_map/ppermute | solution.py:389
  22.9 1.3 %shard_map.92 = (bf16[1,144,1024]{2,1,0:T(8,128)(2,1)S(1)}, bf16[1,56,1024]{2,1,0:T(8,128)(2,1)S(1)}) custom-call(f32[5,72,1024]{2,1,0:T(8,128)S(1)} %get-tuple-element.42.keep, f32[5,72,1024]{2,1,0:T(8,128)S(1)} %collective-permute-done.1.got.rest_2_, f32[144,1024]{1,0:T(8,128)S(1)} %collective-permute-done.2.rest_0_, f32[11,8,1024]{2,1,0:T(8,128)S(1)} %copy-done, ...), custom_call_target="tpu_custom_call" | custom-call | flops 8999999488 | bytes 10 | tf_op jit(solution)/shard_map/pallas_call | solution.py:454
  24.3 1.6 %collective-permute-start.4 = (bf16[1,56,1024]{2,1,0:T(8,128)(2,1)S(1)}, bf16[1,56,1024]{2,1,0:T(8,128)(2,1)S(1)}, u32[]{:S(2)}, u32[]{:S(2)}) collective-permute-start(bf16[1,56,1024]{2,1,0:T(8,128)(2,1)S(1)} %get-tuple-element.51.unused), channel_id=1, source_target_pairs={{0,16},{8,24},{16,0},{24,8},{1,17},{9,25},{17,1},{25,9},{2,18},{10... | collective-permute-start | bytes 344072 | tf_op jit(solution)/shard_map/ppermute | solution.py:389
  26.9 2.0 %shard_map.93 = (f32[2,144,1024]{2,1,0:T(8,128)S(1)}, bf16[2,144,1024]{2,1,0:T(8,128)(2,1)S(1)}) custom-call(bf16[2,144,1024]{2,1,0:T(8,128)(2,1)S(1)} %get-tuple-element.52.bent, bf16[2,56,1024]{2,1,0:T(8,128)(2,1)S(1)} %collective-permute-done.5.got, f32[11,8,1024]{2,1,0:T(8,128)S(1)} %copy-done, bf16[12,144,208]{2,1,0:T(8,128)(2,1)S(1)} %get-tuple-element.47.table, ...), custom_call_target="tpu_custom_call" | custom-call | flops 20000000000 | bytes 10 | tf_op jit(solution)/shard_map/pallas_call | solution.py:470
  28.9 1.6 %collective-permute-start.8 = (bf16[2,144,1024]{2,1,0:T(8,128)(2,1)S(1)}, bf16[2,144,1024]{2,1,0:T(8,128)(2,1)S(1)}, u32[]{:S(2)}, u32[]{:S(2)}) collective-permute-start(bf16[2,144,1024]{2,1,0:T(8,128)(2,1)S(1)} %get-tuple-element.53.unused), channel_id=1, source_target_pairs={{0,8},{8,0},{16,24},{24,16},{1,9},{9,1},{17,25},{25,17},{2,10},{10... | collective-permute-start | bytes 1769480 | tf_op jit(solution)/shard_map/ppermute | solution.py:386
  32.5 3.0 %shard_map.95 = (f32[4,144,1024]{2,1,0:T(8,128)S(1)}, f32[3,72,1024]{2,1,0:T(8,128)S(1)}, f32[3,72,1024]{2,1,0:T(8,128)S(1)}, bf16[2,144,1024]{2,1,0:T(8,128)(2,1)S(1)}, bf16[2,56,1024]{2,1,0:T(8,128)(2,1)S(1)}) custom-call(f32[1,144,1024]{2,1,0:T(8,128)S(1)} %get-tuple-element.54.row_zero, f32[1,144,1024]{2,1,0:T(8,128)S(1)} %get-tuple-element.55.row_one.others, ...), custom_call_target="tpu_custom_call" | custom-call | flops 35000000512 | bytes 10 | tf_op jit(solution)/shard_map/pallas_call | solution.py:488
  36.1 2.1 %shard_map.96 = (f32[1,144,1024]{2,1,0:T(8,128)S(1)}, f32[1,72,1024]{2,1,0:T(8,128)S(1)}, f32[1,72,1024]{2,1,0:T(8,128)S(1)}, bf16[1,144,1024]{2,1,0:T(8,128)(2,1)S(1)}, bf16[1,56,1024]{2,1,0:T(8,128)(2,1)S(1)}) custom-call(f32[1,144,1024]{2,1,0:T(8,128)S(1)} %get-tuple-element.54.row_zero, f32[1,144,1024]{2,1,0:T(8,128)S(1)} %get-tuple-element.55.row_one.others, ...), custom_call_target="tpu_custom_call" | custom-call | flops 100000000 | bytes 10 | tf_op jit(solution)/shard_map/pallas_call | solution.py:493
  38.2 1.6 %collective-permute-start.11 = (bf16[1,56,1024]{2,1,0:T(8,128)(2,1)S(1)}, bf16[1,56,1024]{2,1,0:T(8,128)(2,1)S(1)}, u32[]{:S(2)}, u32[]{:S(2)}) collective-permute-start(bf16[1,56,1024]{2,1,0:T(8,128)(2,1)S(1)} %get-tuple-element.64), channel_id=1, source_target_pairs={{0,16},{8,24},{16,0},{24,8},{1,17},{9,25},{17,1},{25,9},{2,18},{10... | collective-permute-start | bytes 344072 | tf_op jit(solution)/shard_map/ppermute | solution.py:389
  39.8 7.1 %collective-permute-start.9 = (f32[1,72,1024]{2,1,0:T(8,128)S(1)}, f32[1,72,1024]{2,1,0:T(8,128)S(1)}, u32[]{:S(2)}, u32[]{:S(2)}) collective-permute-start(f32[1,72,1024]{2,1,0:T(8,128)S(1)} %get-tuple-element.61), channel_id=1, source_target_pairs={{0,8},{8,0},{16,24},{24,16},{1,9},{9,1},{17,25},{25,17},{2,10},{10... | collective-permute-start | bytes 884744 | tf_op jit(solution)/shard_map/ppermute | solution.py:386
  50.4 2.0 %shard_map.100 = (f32[2,144,1024]{2,1,0:T(8,128)S(1)}, bf16[1,144,1024]{2,1,0:T(8,128)(2,1)S(1)}) custom-call(bf16[2,144,1024]{2,1,0:T(8,128)(2,1)S(1)} %get-tuple-element.71.bent, bf16[2,56,1024]{2,1,0:T(8,128)(2,1)S(1)} %collective-permute-done.12.unused.got, f32[11,8,1024]{2,1,0:T(8,128)S(1)} %copy-done, ...), custom_call_target="tpu_custom_call" | custom-call | flops 20000000000 | bytes 10 | tf_op jit(solution)/shard_map/pallas_call | solution.py:470
  52.4 5.6 %collective-permute-start.14 = (bf16[1,144,1024]{2,1,0:T(8,128)(2,1)S(1)}, bf16[1,144,1024]{2,1,0:T(8,128)(2,1)S(1)}, u32[]{:S(2)}, u32[]{:S(2)}) collective-permute-start(bf16[1,144,1024]{2,1,0:T(8,128)(2,1)S(1)} %get-tuple-element.73), channel_id=1, source_target_pairs={{0,8},{8,0},{16,24},{24,16},{1,9},{9,1},{17,25},{25,17},{2,10},{10... | collective-permute-start | bytes 884744 | tf_op jit(solution)/shard_map/ppermute | solution.py:386
  59.3 1.6 %shard_map.101 = (f32[4,72,1024]{2,1,0:T(8,128)S(1)}, f32[4,72,1024]{2,1,0:T(8,128)S(1)}) custom-call(f32[1,144,1024]{2,1,0:T(8,128)S(1)} %get-tuple-element.68.zero, f32[1,144,1024]{2,1,0:T(8,128)S(1)} %shard_map.99.one, f32[2,144,1024]{2,1,0:T(8,128)S(1)} %get-tuple-element.72.inners, bf16[1,144,1024]{2,1,0:T(8,128)(2,1)S(1)} %collective-permute-done.14.inner), custom_call_target="tpu_custom_call" | custom-call | flops 24999999488 | bytes 10 | tf_op jit(solution)/shard_map/pallas_call | solution.py:511
  61.4 1.6 %shard_map.102 = (f32[72,8,1024]{2,1,0:T(8,128)}, s32[8,128]{1,0:T(8,128)S(1)}) custom-call(f32[1,72,1024]{2,1,0:T(8,128)S(1)} %get-tuple-element.59.keep_zero, f32[3,72,1024]{2,1,0:T(8,128)S(1)} %get-tuple-element.60.keep, f32[1,72,1024]{2,1,0:T(8,128)S(1)} %collective-permute-done.9.got_zero, f32[3,72,1024]{2,1,0:T(8,128)S(1)} %collective-permute-done.10.got, ...), custom_call_target="tpu_custom_call" | custom-call | flops 19000000512 | bytes 10 | tf_op jit(solution)/shard_map/pallas_call | solution.py:517
  64.4 1.2 %collective-permute-done.17.far_halo = bf16[72,1024]{1,0:T(8,128)(2,1)S(1)} collective-permute-done((bf16[72,1024]{1,0:T(8,128)(2,1)S(1)}, bf16[72,1024]{1,0:T(8,128)(2,1)S(1)}, u32[]{:S(2)}, u32[]{:S(2)}) %collective-permute-start.17) | collective-permute-done | bytes 147488 | tf_op jit(solution)/shard_map/ppermute | solution.py:386
  65.6 1.3 %copy-done.3 = f32[4,72,1024]{2,1,0:T(8,128)S(1)} copy-done((f32[4,72,1024]{2,1,0:T(8,128)S(1)}, f32[4,72,1024]{2,1,0:T(8,128)}, u32[]{:S(2)}) %copy-start.3) | copy-done | bytes 1179672
  66.9 1.6 %shard_map.103 = f32[72,8,1024]{2,1,0:T(8,128)} custom-call(f32[4,72,1024]{2,1,0:T(8,128)S(1)} %copy-done.3, f32[4,72,1024]{2,1,0:T(8,128)S(1)} %collective-permute-done.15.got, bf16[1,144,1024]{2,1,0:T(8,128)(2,1)S(1)} %collective-permute-done.16.halo, bf16[72,1024]{1,0:T(8,128)(2,1)S(1)} %collective-permute-done.17.far_halo), custom_call_target="tpu_custom_call" | custom-call | flops 19000000512 | bytes 10 | tf_op jit(solution)/shard_map/pallas_call | solution.py:522
  (68 shorter events, 14.4 us)
Async XLA Ops:
  0.6 2.7 %copy-start.4 = (s32[1606]{0:T(1024)S(1)}, s32[1606]{0:T(1024)}, u32[]{:S(2)}) copy-start(s32[1606]{0:T(1024)} %param.9) | copy-start | bytes 19276
  0.7 2.8 %copy-start.5 = (s32[1606]{0:T(1024)S(1)}, s32[1606]{0:T(1024)}, u32[]{:S(2)}) copy-start(s32[1606]{0:T(1024)} %param.10) | copy-start | bytes 19276
  0.7 2.8 %copy-start.6 = (s32[1606]{0:T(1024)S(1)}, s32[1606]{0:T(1024)}, u32[]{:S(2)}) copy-start(s32[1606]{0:T(1024)} %param.11) | copy-start | bytes 19276
  0.7 2.8 %copy-start.7 = (bf16[1606]{0:T(1024)(128)(2,1)S(1)}, bf16[1606]{0:T(1024)(128)(2,1)}, u32[]{:S(2)}) copy-start(bf16[1606]{0:T(1024)(128)(2,1)} %param.12) | copy-start | bytes 9640
  0.7 5.9 %copy-start.1 = (f32[72,8,1024]{2,1,0:T(8,128)S(1)}, f32[72,8,1024]{2,1,0:T(8,128)}, u32[]{:S(2)}) copy-start(f32[72,8,1024]{2,1,0:T(8,128)} %field.3) | copy-start | bytes 7077892
  2.8 1.9 %collective-permute-start = (f32[72,1024]{1,0:T(8,128)}, f32[72,1024]{1,0:T(8,128)S(1)}, u32[]{:S(2)}, u32[]{:S(2)}) collective-permute-start(f32[72,1024]{1,0:T(8,128)} %get-tuple-element.41), channel_id=1, source_target_pairs={{0,8},{8,0},{16,24},{24,16},{1,9},{9,1},{17,25},{25,17},{2,10},{10... | collective-permute-start | bytes 884744 | tf_op jit(solution)/shard_map/ppermute | solution.py:386
  5.9 17.0 %collective-permute-start.2 = (f32[144,1024]{1,0:T(8,128)S(1)}, f32[144,1024]{1,0:T(8,128)S(1)}, u32[]{:S(2)}, u32[]{:S(2)}) collective-permute-start(f32[144,1024]{1,0:T(8,128)S(1)} %maximum_select_fusion.unused), channel_id=1, source_target_pairs={{8,1},{1,8},{9,2},{2,9},{10,3},{3,10},{11,4},{4,11},{12,5},{5,12},... | collective-permute-start | bytes 1769480 | tf_op jit(solution)/shard_map/ppermute | solution.py:392
  7.1 7.2 %copy-start = (f32[11,8,1024]{2,1,0:T(8,128)S(1)}, f32[11,8,1024]{2,1,0:T(8,128)}, u32[]{:S(2)}) copy-start(f32[11,8,1024]{2,1,0:T(8,128)} %stiff.17) | copy-start | bytes 1081348
  7.1 7.2 %collective-permute-start.1 = (f32[5,72,1024]{2,1,0:T(8,128)S(1)}, f32[5,72,1024]{2,1,0:T(8,128)S(1)}, u32[]{:S(2)}, u32[]{:S(2)}) collective-permute-start(f32[5,72,1024]{2,1,0:T(8,128)S(1)} %get-tuple-element.43), channel_id=1, source_target_pairs={{0,8},{8,0},{16,24},{24,16},{1,9},{9,1},{17,25},{25,17},{2,10},{10... | collective-permute-start | bytes 4423688 | tf_op jit(solution)/shard_map/ppermute | solution.py:386
  15.6 5.5 %collective-permute-start.3 = (bf16[1,56,1024]{2,1,0:T(8,128)(2,1)S(1)}, bf16[1,56,1024]{2,1,0:T(8,128)(2,1)S(1)}, u32[]{:S(2)}, u32[]{:S(2)}) collective-permute-start(bf16[1,56,1024]{2,1,0:T(8,128)(2,1)S(1)} %get-tuple-element.46.rest_2_), channel_id=1, source_target_pairs={{0,16},{8,24},{16,0},{24,8},{1,17},{9,25},{17,1},{25,9},{2,18},{10... | collective-permute-start | bytes 344072 | tf_op jit(solution)/shard_map/ppermute | solution.py:389
  19.3 7.7 %collective-permute-start.5 = (bf16[2,56,1024]{2,1,0:T(8,128)(2,1)S(1)}, bf16[2,56,1024]{2,1,0:T(8,128)(2,1)S(1)}, u32[]{:S(2)}, u32[]{:S(2)}) collective-permute-start(bf16[2,56,1024]{2,1,0:T(8,128)(2,1)S(1)} %get-tuple-element.48.unused), channel_id=1, source_target_pairs={{0,16},{8,24},{16,0},{24,8},{1,17},{9,25},{17,1},{25,9},{2,18},{10... | collective-permute-start | bytes 688136 | tf_op jit(solution)/shard_map/ppermute | solution.py:389
  22.2 13.9 %collective-permute-start.7 = (bf16[1,144,1024]{2,1,0:T(8,128)(2,1)S(1)}, bf16[1,144,1024]{2,1,0:T(8,128)(2,1)S(1)}, u32[]{:S(2)}, u32[]{:S(2)}) collective-permute-start(bf16[1,144,1024]{2,1,0:T(8,128)(2,1)S(1)} %get-tuple-element.49.rest_3_), channel_id=1, source_target_pairs={{8,1},{1,8},{9,2},{2,9},{10,3},{3,10},{11,4},{4,11},{12,5},{5,12},... | collective-permute-start | bytes 884744 | tf_op jit(solution)/shard_map/ppermute | solution.py:392
  24.3 6.3 %collective-permute-start.4 = (bf16[1,56,1024]{2,1,0:T(8,128)(2,1)S(1)}, bf16[1,56,1024]{2,1,0:T(8,128)(2,1)S(1)}, u32[]{:S(2)}, u32[]{:S(2)}) collective-permute-start(bf16[1,56,1024]{2,1,0:T(8,128)(2,1)S(1)} %get-tuple-element.51.unused), channel_id=1, source_target_pairs={{0,16},{8,24},{16,0},{24,8},{1,17},{9,25},{17,1},{25,9},{2,18},{10... | collective-permute-start | bytes 344072 | tf_op jit(solution)/shard_map/ppermute | solution.py:389
  28.9 3.5 %collective-permute-start.8 = (bf16[2,144,1024]{2,1,0:T(8,128)(2,1)S(1)}, bf16[2,144,1024]{2,1,0:T(8,128)(2,1)S(1)}, u32[]{:S(2)}, u32[]{:S(2)}) collective-permute-start(bf16[2,144,1024]{2,1,0:T(8,128)(2,1)S(1)} %get-tuple-element.53.unused), channel_id=1, source_target_pairs={{0,8},{8,0},{16,24},{24,16},{1,9},{9,1},{17,25},{25,17},{2,10},{10... | collective-permute-start | bytes 1769480 | tf_op jit(solution)/shard_map/ppermute | solution.py:386
  31.6 4.5 %collective-permute-start.6 = (bf16[1,144,1024]{2,1,0:T(8,128)(2,1)S(1)}, bf16[1,144,1024]{2,1,0:T(8,128)(2,1)S(1)}, u32[]{:S(2)}, u32[]{:S(2)}) collective-permute-start(bf16[1,144,1024]{2,1,0:T(8,128)(2,1)S(1)} %get-tuple-element.56), channel_id=1, source_target_pairs={{8,1},{1,8},{9,2},{2,9},{10,3},{3,10},{11,4},{4,11},{12,5},{5,12},... | collective-permute-start | bytes 884744 | tf_op jit(solution)/shard_map/ppermute | solution.py:392
  35.5 11.4 %collective-permute-start.12 = (bf16[2,56,1024]{2,1,0:T(8,128)(2,1)S(1)}, bf16[2,56,1024]{2,1,0:T(8,128)(2,1)S(1)}, u32[]{:S(2)}, u32[]{:S(2)}) collective-permute-start(bf16[2,56,1024]{2,1,0:T(8,128)(2,1)S(1)} %get-tuple-element.66), channel_id=1, source_target_pairs={{0,16},{8,24},{16,0},{24,8},{1,17},{9,25},{17,1},{25,9},{2,18},{10... | collective-permute-start | bytes 688136 | tf_op jit(solution)/shard_map/ppermute | solution.py:389
  38.2 10.5 %collective-permute-start.11 = (bf16[1,56,1024]{2,1,0:T(8,128)(2,1)S(1)}, bf16[1,56,1024]{2,1,0:T(8,128)(2,1)S(1)}, u32[]{:S(2)}, u32[]{:S(2)}) collective-permute-start(bf16[1,56,1024]{2,1,0:T(8,128)(2,1)S(1)} %get-tuple-element.64), channel_id=1, source_target_pairs={{0,16},{8,24},{16,0},{24,8},{1,17},{9,25},{17,1},{25,9},{2,18},{10... | collective-permute-start | bytes 344072 | tf_op jit(solution)/shard_map/ppermute | solution.py:389
  39.8 21.6 %collective-permute-start.9 = (f32[1,72,1024]{2,1,0:T(8,128)S(1)}, f32[1,72,1024]{2,1,0:T(8,128)S(1)}, u32[]{:S(2)}, u32[]{:S(2)}) collective-permute-start(f32[1,72,1024]{2,1,0:T(8,128)S(1)} %get-tuple-element.61), channel_id=1, source_target_pairs={{0,8},{8,0},{16,24},{24,16},{1,9},{9,1},{17,25},{25,17},{2,10},{10... | collective-permute-start | bytes 884744 | tf_op jit(solution)/shard_map/ppermute | solution.py:386
  46.9 14.5 %collective-permute-start.10 = (f32[3,72,1024]{2,1,0:T(8,128)S(1)}, f32[3,72,1024]{2,1,0:T(8,128)S(1)}, u32[]{:S(2)}, u32[]{:S(2)}) collective-permute-start(f32[3,72,1024]{2,1,0:T(8,128)S(1)} %get-tuple-element.62), channel_id=1, source_target_pairs={{0,8},{8,0},{16,24},{24,16},{1,9},{9,1},{17,25},{25,17},{2,10},{10... | collective-permute-start | bytes 2654216 | tf_op jit(solution)/shard_map/ppermute | solution.py:386
  48.0 10.1 %collective-permute-start.13 = (bf16[1,56,1024]{2,1,0:T(8,128)(2,1)S(1)}, bf16[1,56,1024]{2,1,0:T(8,128)(2,1)S(1)}, u32[]{:S(2)}, u32[]{:S(2)}) collective-permute-start(bf16[1,56,1024]{2,1,0:T(8,128)(2,1)S(1)} %get-tuple-element.67.unused), channel_id=1, source_target_pairs={{0,16},{8,24},{16,0},{24,8},{1,17},{9,25},{17,1},{25,9},{2,18},{10... | collective-permute-start | bytes 344072 | tf_op jit(solution)/shard_map/ppermute | solution.py:389
  49.7 14.4 %collective-permute-start.16 = (bf16[1,144,1024]{2,1,0:T(8,128)(2,1)S(1)}, bf16[1,144,1024]{2,1,0:T(8,128)(2,1)S(1)}, u32[]{:S(2)}, u32[]{:S(2)}) collective-permute-start(bf16[1,144,1024]{2,1,0:T(8,128)(2,1)S(1)} %get-tuple-element.70.unused), channel_id=1, source_target_pairs={{8,1},{1,8},{9,2},{2,9},{10,3},{3,10},{11,4},{4,11},{12,5},{5,12},... | collective-permute-start | bytes 884744 | tf_op jit(solution)/shard_map/ppermute | solution.py:392
  52.4 6.8 %collective-permute-start.14 = (bf16[1,144,1024]{2,1,0:T(8,128)(2,1)S(1)}, bf16[1,144,1024]{2,1,0:T(8,128)(2,1)S(1)}, u32[]{:S(2)}, u32[]{:S(2)}) collective-permute-start(bf16[1,144,1024]{2,1,0:T(8,128)(2,1)S(1)} %get-tuple-element.73), channel_id=1, source_target_pairs={{0,8},{8,0},{16,24},{24,16},{1,9},{9,1},{17,25},{25,17},{2,10},{10... | collective-permute-start | bytes 884744 | tf_op jit(solution)/shard_map/ppermute | solution.py:386
  60.9 4.7 %collective-permute-start.15 = (f32[4,72,1024]{2,1,0:T(8,128)S(1)}, f32[4,72,1024]{2,1,0:T(8,128)S(1)}, u32[]{:S(2)}, u32[]{:S(2)}) collective-permute-start(f32[4,72,1024]{2,1,0:T(8,128)S(1)} %get-tuple-element.76), channel_id=1, source_target_pairs={{0,8},{8,0},{16,24},{24,16},{1,9},{9,1},{17,25},{25,17},{2,10},{10... | collective-permute-start | bytes 3538952 | tf_op jit(solution)/shard_map/ppermute | solution.py:386
  64.2 1.4 %collective-permute-start.17 = (bf16[72,1024]{1,0:T(8,128)(2,1)S(1)}, bf16[72,1024]{1,0:T(8,128)(2,1)S(1)}, u32[]{:S(2)}, u32[]{:S(2)}) collective-permute-start(bf16[72,1024]{1,0:T(8,128)(2,1)S(1)} %fusion), channel_id=1, source_target_pairs={{0,8},{8,0},{16,24},{24,16},{1,9},{9,1},{17,25},{25,17},{2,10},{10... | collective-permute-start | bytes 442376 | tf_op jit(solution)/shard_map/ppermute | solution.py:386
  (3 other events, 6.1 us)

commit v5 on v4

--- a/solution.py
+++ b/solution.py
@@ -169,7 +169,7 @@
 
 
 def first_kernel(first_row, keep, got, *rest):
-    halo = rest[0] if first_row == 0 else None
+    halos = rest[:2] if first_row == 0 else None
     stiff, send_table, unused, bent, buffer = rest[-5:]
     side = core_side()
     count, pair, width = bent.shape
@@ -181,7 +181,7 @@
             cut = pl.ds(at, 8)
             far = pl.ds(group * own + at, 8)
             lines = [
-                halo[far, :]
+                jnp.where(side == group, halos[0][cut, :], halos[1][cut, :])
                 if row < 0
                 else jnp.where(side == group, keep[row, cut, :], got[row, cut, :])
                 for row in range(first_row - 1, first_row + count + 1)
@@ -348,9 +348,9 @@
 def last_merge_kernel(keep, got, halo, far_halo, out, lines, done):
     own = keep.shape[1]
     first = core_side() == 0
-    halos = halo[0].astype(F32)
+    halos, others = halo[0].astype(F32), far_halo[0].astype(F32)
     near_line = jnp.where(first, halos[:own], halos[own:])
-    far_line = far_halo[...].astype(F32)
+    far_line = jnp.where(first, others[:own], others[own:])
 
     def near(i, cut):
         return keep[0, cut, :] + near_line[cut] if i == 0 else keep[i, cut, :]
@@ -417,13 +417,9 @@
         [ANY],
         60,
     )(slot_field)
+    halo_far = by_tile(near_edge)
     got_edge = by_core(far_edge)
-    edge = jnp.where(
-        side == 0,
-        jnp.concatenate([near_edge, got_edge], axis=0),
-        jnp.concatenate([got_edge, near_edge], axis=0),
-    )
-    halo = by_tile(edge)
+    halo_near = by_tile(got_edge)
 
     main_table, send_table = call(
         functools.partial(table_kernel, terms, pair, hubs, slot_total),
@@ -436,11 +432,11 @@
         3.0,
         [VMEM, ANY],
         12,
-    )(entries, edge)
+    )(entries, got_edge)
 
     line_block = shape((half + 1, own, width), F32)
     keep, send = call(split_kernel, (line_block, line_block), (), 2.5, [VMEM, ANY])(
-        slot_field, edge
+        slot_field, got_edge
     )
     got = by_core(send)
 
@@ -479,7 +475,7 @@
     bent_in, sent, cross_in = bend(2, 2, sent)
     moment_one, edge_one = couple(bent_one, cross_one, 1, 1, (), sent)
     next_near = by_tile(edge_one)
-    bent_out, sent, cross_out = bend(0, 1, edge_one, halo)
+    bent_out, sent, cross_out = bend(0, 1, edge_one, halo_near, halo_far)
     moment_in, edge_in = couple(bent_in, cross_in, 2, None, (3, 2), sent)
     inner = by_core(edge_in)
     moment_out, edge_zero = couple(bent_out, cross_out, 0, 0, (), edge_in)
@@ -517,8 +513,7 @@
     first_apply, token = call(
         merge_kernel, (whole, TOKEN), writers, 1.9, [VMEM] * 4 + [ANY], 6, (ANY, VMEM)
     )(keep_out, keep_in, got_out, got_in, keep)
-    late_side = side + token[0, 0]
-    far_halo = by_core(jnp.where(late_side == 0, near[0, own:], near[0, :own]))
+    far_halo = by_core(jnp.where(token[0, 0] == 0, near, jnp.zeros_like(near)))
     second_apply = call(last_merge_kernel, whole, writers, 1.9, [VMEM] * 4, 6, ANY)(
         keep, got, near, far_halo
     )

time: 68.9 us -> 66.4 us (0.964)
  waiting for transfers between devices: 5.43 us -> 3.5 us
  starting transfers between devices: 29.3 us -> 30.9 us
  local copies, waits for them, and re-layouts: 1.98 us -> 0.69 us
  other arithmetic: 1.15 us -> 0.04 us
    unnamed x18 -> x14, local copies, waits for them, and re-layouts: 1.31 us -> 0.03 us
    select_n x2 -> x1, other arithmetic: 1.13 us -> 0.03 us  [body(): far_halo = by_core(jnp.where(token[0, 0] == 0, near, jnp.zeros_like(near)))]
    ppermute x8, waiting for transfers between devices: 3.06 us -> 1.97 us  [by_core(): return lax.ppermute(value, 'chaos', core_swap)]
    ppermute x6, waiting for transfers between devices: 2.36 us -> 1.52 us  [by_chip(): return lax.ppermute(value, 'chaos', chip_swap)]
    ppermute x4 -> x5, starting transfers between devices: 2.92 us -> 3.55 us  [by_tile(): return lax.ppermute(value, ('chaos', 'tile'), tile_swap)]
  transfers between devices with their start and end apart: 18 -> 19, of which waited for: 6 -> 5; matrix products, arithmetic and copies ran while one was open for 1% -> 1% of each run, Pallas kernels for 37% -> 38%
where the time goes in v5:
time: 66.4 us; the launch traced here: 66.2 us
  starting transfers between devices  30.9 us (47%)
  Pallas kernels  29.2 us (44%)
  waiting for transfers between devices  3.5 us (5%)
  between operations  1.89 us (3%)
  local copies, waits for them, and re-layouts  0.69 us (1%)
    ppermute x8, starting transfers between devices, by_core(): return lax.ppermute(value, 'chaos', core_swap)  20.2 us
    pallas_call x6, Pallas kernels, couple(): call(functools.partial(couple_kernel, first, outer_row, inner_rows), tupl...  8.45 us
    ppermute x6, starting transfers between devices, by_chip(): return lax.ppermute(value, 'chaos', chip_swap)  7.13 us
    pallas_call x3, Pallas kernels, bend(): call(functools.partial(first_kernel, first), bents(count), (), 0.9 * coun...  4.72 us
    ppermute x5, starting transfers between devices, by_tile(): return lax.ppermute(value, ('chaos', 'tile'), tile_swap)  3.55 us
    pallas_call x1, Pallas kernels, body(): call(second_inner_kernel, (shape((4, pair, width), F32),) + outs(3) + ben...  3.03 us
    pallas_call x1, Pallas kernels, body(): call(functools.partial(table_kernel, terms, pair, hubs, slot_total), (sha...  2.29 us
    pallas_call x1, Pallas kernels, body(): call(edge_kernel, (row_block, row_block), [pltpu.VMEM((2, own, width), F3...  2.13 us
  transfers between devices with their start and end apart: 19, of which 5 were waited for; matrix products, arithmetic and copies ran while one was open for 1% of the time, Pallas kernels for 38%

profile of v5, /device:TPU:0, one launch (start us, length us, event | category | flops | bytes accessed | tf_op | source)
XLA Modules:
  0.0 66.2 jit_solution(42360030248311475)
XLA Ops:
  0.7 2.1 %shard_map.86 = (f32[72,1024]{1,0:T(8,128)}, f32[72,1024]{1,0:T(8,128)}) custom-call(f32[72,8,1024]{2,1,0:T(8,128)} %field.3), custom_call_target="tpu_custom_call" | custom-call | flops 20000000000 | bytes 10 | tf_op jit(solution)/shard_map/pallas_call | solution.py:412
  5.3 3.6 %collective-permute-start.1 = (f32[5,72,1024]{2,1,0:T(8,128)S(1)}, f32[5,72,1024]{2,1,0:T(8,128)S(1)}, u32[]{:S(2)}, u32[]{:S(2)}) collective-permute-start(f32[5,72,1024]{2,1,0:T(8,128)S(1)} %get-tuple-element.42), channel_id=1, source_target_pairs={{0,8},{8,0},{16,24},{24,16},{1,9},{9,1},{17,25},{25,17},{2,10},{10... | collective-permute-start | bytes 4423688 | tf_op jit(solution)/shard_map/ppermute | solution.py:386
  9.6 2.3 %shard_map.88 = (bf16[12,144,208]{2,1,0:T(8,128)(2,1)S(1)}, bf16[11,64,144]{2,1,0:T(8,128)(2,1)S(1)}) custom-call(f32[8,1664]{1,0:T(8,128)S(1)} %stack.31.entries, f32[72,1024]{1,0:T(8,128)S(1)} %collective-permute-done.unused), custom_call_target="tpu_custom_call" | custom-call | flops 30000001024 | bytes 10 | tf_op jit(solution)/shard_map/pallas_call | solution.py:424
  11.9 1.3 %shard_map.89 = (bf16[1,144,1024]{2,1,0:T(8,128)(2,1)S(1)}, bf16[1,56,1024]{2,1,0:T(8,128)(2,1)S(1)}) custom-call(f32[5,72,1024]{2,1,0:T(8,128)S(1)} %get-tuple-element.41.keep, f32[5,72,1024]{2,1,0:T(8,128)S(1)} %collective-permute-done.1.got.rest_2_, f32[11,8,1024]{2,1,0:T(8,128)S(1)} %copy-done, ...), custom_call_target="tpu_custom_call" | custom-call | flops 8999999488 | bytes 10 | tf_op jit(solution)/shard_map/pallas_call | solution.py:450
  13.2 1.6 %collective-permute-start.4 = (bf16[1,56,1024]{2,1,0:T(8,128)(2,1)S(1)}, bf16[1,56,1024]{2,1,0:T(8,128)(2,1)S(1)}, u32[]{:S(2)}, u32[]{:S(2)}) collective-permute-start(bf16[1,56,1024]{2,1,0:T(8,128)(2,1)S(1)} %get-tuple-element.46.rest_2_), channel_id=1, source_target_pairs={{0,16},{8,24},{16,0},{24,8},{1,17},{9,25},{17,1},{25,9},{2,18},{10... | collective-permute-start | bytes 344072 | tf_op jit(solution)/shard_map/ppermute | solution.py:389
  14.8 2.0 %shard_map.90 = (bf16[2,144,1024]{2,1,0:T(8,128)(2,1)S(1)}, bf16[2,56,1024]{2,1,0:T(8,128)(2,1)S(1)}) custom-call(f32[5,72,1024]{2,1,0:T(8,128)S(1)} %get-tuple-element.41.keep, f32[5,72,1024]{2,1,0:T(8,128)S(1)} %collective-permute-done.1.got.rest_2_, f32[11,8,1024]{2,1,0:T(8,128)S(1)} %copy-done, ...), custom_call_target="tpu_custom_call" | custom-call | flops 17999998976 | bytes 10 | tf_op jit(solution)/shard_map/pallas_call | solution.py:450
  18.1 1.1 %shard_map.91 = (f32[1,144,1024]{2,1,0:T(8,128)S(1)}, bf16[1,144,1024]{2,1,0:T(8,128)(2,1)S(1)}) custom-call(bf16[1,144,1024]{2,1,0:T(8,128)(2,1)S(1)} %get-tuple-element.45.bent, bf16[1,56,1024]{2,1,0:T(8,128)(2,1)S(1)} %collective-permute-done.4.got, f32[11,8,1024]{2,1,0:T(8,128)S(1)} %copy-done, bf16[12,144,208]{2,1,0:T(8,128)(2,1)S(1)} %get-tuple-element.47.table, ...), custom_call_target="tpu_custom_call" | custom-call | flops 10000000000 | bytes 10 | tf_op jit(solution)/shard_map/pallas_call | solution.py:466
  19.9 1.4 %shard_map.92 = (bf16[1,144,1024]{2,1,0:T(8,128)(2,1)S(1)}, bf16[1,56,1024]{2,1,0:T(8,128)(2,1)S(1)}) custom-call(f32[5,72,1024]{2,1,0:T(8,128)S(1)} %get-tuple-element.41.keep, f32[5,72,1024]{2,1,0:T(8,128)S(1)} %collective-permute-done.1.got.rest_2_, f32[72,1024]{1,0:T(8,128)S(1)} %collective-permute-done.2.rest_0_, ...), custom_call_target="tpu_custom_call" | custom-call | flops 8999999488 | bytes 10 | tf_op jit(solution)/shard_map/pallas_call | solution.py:450
  21.2 1.6 %collective-permute-start.5 = (bf16[1,56,1024]{2,1,0:T(8,128)(2,1)S(1)}, bf16[1,56,1024]{2,1,0:T(8,128)(2,1)S(1)}, u32[]{:S(2)}, u32[]{:S(2)}) collective-permute-start(bf16[1,56,1024]{2,1,0:T(8,128)(2,1)S(1)} %get-tuple-element.51.unused), channel_id=1, source_target_pairs={{0,16},{8,24},{16,0},{24,8},{1,17},{9,25},{17,1},{25,9},{2,18},{10... | collective-permute-start | bytes 344072 | tf_op jit(solution)/shard_map/ppermute | solution.py:389
  23.6 2.0 %shard_map.93 = (f32[2,144,1024]{2,1,0:T(8,128)S(1)}, bf16[2,144,1024]{2,1,0:T(8,128)(2,1)S(1)}) custom-call(bf16[2,144,1024]{2,1,0:T(8,128)(2,1)S(1)} %get-tuple-element.52.bent, bf16[2,56,1024]{2,1,0:T(8,128)(2,1)S(1)} %collective-permute-done.6.got, f32[11,8,1024]{2,1,0:T(8,128)S(1)} %copy-done, bf16[12,144,208]{2,1,0:T(8,128)(2,1)S(1)} %get-tuple-element.47.table, ...), custom_call_target="tpu_custom_call" | custom-call | flops 20000000000 | bytes 10 | tf_op jit(solution)/shard_map/pallas_call | solution.py:466
  25.7 4.2 %collective-permute-start.9 = (bf16[2,144,1024]{2,1,0:T(8,128)(2,1)S(1)}, bf16[2,144,1024]{2,1,0:T(8,128)(2,1)S(1)}, u32[]{:S(2)}, u32[]{:S(2)}) collective-permute-start(bf16[2,144,1024]{2,1,0:T(8,128)(2,1)S(1)} %get-tuple-element.53.unused), channel_id=1, source_target_pairs={{0,8},{8,0},{16,24},{24,16},{1,9},{9,1},{17,25},{25,17},{2,10},{10... | collective-permute-start | bytes 1769480 | tf_op jit(solution)/shard_map/ppermute | solution.py:386
  29.9 1.1 %shard_map.94 = (f32[1,144,1024]{2,1,0:T(8,128)S(1)}, bf16[1,144,1024]{2,1,0:T(8,128)(2,1)S(1)}) custom-call(bf16[1,144,1024]{2,1,0:T(8,128)(2,1)S(1)} %get-tuple-element.50.bent, bf16[1,56,1024]{2,1,0:T(8,128)(2,1)S(1)} %collective-permute-done.5.got, f32[11,8,1024]{2,1,0:T(8,128)S(1)} %copy-done, bf16[12,144,208]{2,1,0:T(8,128)(2,1)S(1)} %get-tuple-element.47.table, ...), custom_call_target="tpu_custom_call" | custom-call | flops 10000000000 | bytes 10 | tf_op jit(solution)/shard_map/pallas_call | solution.py:466
  31.9 3.0 %shard_map.95 = (f32[4,144,1024]{2,1,0:T(8,128)S(1)}, f32[3,72,1024]{2,1,0:T(8,128)S(1)}, f32[3,72,1024]{2,1,0:T(8,128)S(1)}, bf16[2,144,1024]{2,1,0:T(8,128)(2,1)S(1)}, bf16[2,56,1024]{2,1,0:T(8,128)(2,1)S(1)}) custom-call(f32[1,144,1024]{2,1,0:T(8,128)S(1)} %get-tuple-element.54.row_zero, f32[1,144,1024]{2,1,0:T(8,128)S(1)} %get-tuple-element.55.row_one.others, ...), custom_call_target="tpu_custom_call" | custom-call | flops 35000000512 | bytes 10 | tf_op jit(solution)/shard_map/pallas_call | solution.py:484
  35.5 2.1 %shard_map.96 = (f32[1,144,1024]{2,1,0:T(8,128)S(1)}, f32[1,72,1024]{2,1,0:T(8,128)S(1)}, f32[1,72,1024]{2,1,0:T(8,128)S(1)}, bf16[1,144,1024]{2,1,0:T(8,128)(2,1)S(1)}, bf16[1,56,1024]{2,1,0:T(8,128)(2,1)S(1)}) custom-call(f32[1,144,1024]{2,1,0:T(8,128)S(1)} %get-tuple-element.54.row_zero, f32[1,144,1024]{2,1,0:T(8,128)S(1)} %get-tuple-element.55.row_one.others, ...), custom_call_target="tpu_custom_call" | custom-call | flops 100000000 | bytes 10 | tf_op jit(solution)/shard_map/pallas_call | solution.py:489
  37.6 1.6 %collective-permute-start.12 = (bf16[1,56,1024]{2,1,0:T(8,128)(2,1)S(1)}, bf16[1,56,1024]{2,1,0:T(8,128)(2,1)S(1)}, u32[]{:S(2)}, u32[]{:S(2)}) collective-permute-start(bf16[1,56,1024]{2,1,0:T(8,128)(2,1)S(1)} %get-tuple-element.64), channel_id=1, source_target_pairs={{0,16},{8,24},{16,0},{24,8},{1,17},{9,25},{17,1},{25,9},{2,18},{10... | collective-permute-start | bytes 344072 | tf_op jit(solution)/shard_map/ppermute | solution.py:389
  39.2 5.6 %collective-permute-start.10 = (f32[1,72,1024]{2,1,0:T(8,128)S(1)}, f32[1,72,1024]{2,1,0:T(8,128)S(1)}, u32[]{:S(2)}, u32[]{:S(2)}) collective-permute-start(f32[1,72,1024]{2,1,0:T(8,128)S(1)} %get-tuple-element.61), channel_id=1, source_target_pairs={{0,8},{8,0},{16,24},{24,16},{1,9},{9,1},{17,25},{25,17},{2,10},{10... | collective-permute-start | bytes 884744 | tf_op jit(solution)/shard_map/ppermute | solution.py:386
  45.9 1.3 %collective-permute-start.14 = (bf16[1,56,1024]{2,1,0:T(8,128)(2,1)S(1)}, bf16[1,56,1024]{2,1,0:T(8,128)(2,1)S(1)}, u32[]{:S(2)}, u32[]{:S(2)}) collective-permute-start(bf16[1,56,1024]{2,1,0:T(8,128)(2,1)S(1)} %get-tuple-element.67.unused), channel_id=1, source_target_pairs={{0,16},{8,24},{16,0},{24,8},{1,17},{9,25},{17,1},{25,9},{2,18},{10... | collective-permute-start | bytes 344072 | tf_op jit(solution)/shard_map/ppermute | solution.py:389
  47.2 1.1 %shard_map.98 = (f32[1,144,1024]{2,1,0:T(8,128)S(1)}, bf16[1,144,1024]{2,1,0:T(8,128)(2,1)S(1)}) custom-call(bf16[1,144,1024]{2,1,0:T(8,128)(2,1)S(1)} %get-tuple-element.63.bent, bf16[1,56,1024]{2,1,0:T(8,128)(2,1)S(1)} %collective-permute-done.12.got, f32[11,8,1024]{2,1,0:T(8,128)S(1)} %copy-done, bf16[12,144,208]{2,1,0:T(8,128)(2,1)S(1)} %get-tuple-element.47.table, ...), custom_call_target="tpu_custom_call" | custom-call | flops 10000000000 | bytes 10 | tf_op jit(solution)/shard_map/pallas_call | solution.py:466
  49.0 2.0 %shard_map.100 = (f32[2,144,1024]{2,1,0:T(8,128)S(1)}, bf16[1,144,1024]{2,1,0:T(8,128)(2,1)S(1)}) custom-call(bf16[2,144,1024]{2,1,0:T(8,128)(2,1)S(1)} %get-tuple-element.71.bent, bf16[2,56,1024]{2,1,0:T(8,128)(2,1)S(1)} %collective-permute-done.13.unused.got, f32[11,8,1024]{2,1,0:T(8,128)S(1)} %copy-done, ...), custom_call_target="tpu_custom_call" | custom-call | flops 20000000000 | bytes 10 | tf_op jit(solution)/shard_map/pallas_call | solution.py:466
  51.0 5.7 %collective-permute-start.15 = (bf16[1,144,1024]{2,1,0:T(8,128)(2,1)S(1)}, bf16[1,144,1024]{2,1,0:T(8,128)(2,1)S(1)}, u32[]{:S(2)}, u32[]{:S(2)}) collective-permute-start(bf16[1,144,1024]{2,1,0:T(8,128)(2,1)S(1)} %get-tuple-element.73), channel_id=1, source_target_pairs={{0,8},{8,0},{16,24},{24,16},{1,9},{9,1},{17,25},{25,17},{2,10},{10... | collective-permute-start | bytes 884744 | tf_op jit(solution)/shard_map/ppermute | solution.py:386
  57.9 1.6 %shard_map.101 = (f32[4,72,1024]{2,1,0:T(8,128)S(1)}, f32[4,72,1024]{2,1,0:T(8,128)S(1)}) custom-call(f32[1,144,1024]{2,1,0:T(8,128)S(1)} %get-tuple-element.68.zero, f32[1,144,1024]{2,1,0:T(8,128)S(1)} %shard_map.99.one, f32[2,144,1024]{2,1,0:T(8,128)S(1)} %get-tuple-element.72.inners, bf16[1,144,1024]{2,1,0:T(8,128)(2,1)S(1)} %collective-permute-done.15.inner), custom_call_target="tpu_custom_call" | custom-call | flops 24999999488 | bytes 10 | tf_op jit(solution)/shard_map/pallas_call | solution.py:507
  59.9 1.6 %shard_map.102 = (f32[72,8,1024]{2,1,0:T(8,128)}, s32[8,128]{1,0:T(8,128)S(1)}) custom-call(f32[1,72,1024]{2,1,0:T(8,128)S(1)} %get-tuple-element.59.keep_zero, f32[3,72,1024]{2,1,0:T(8,128)S(1)} %get-tuple-element.60.keep, f32[1,72,1024]{2,1,0:T(8,128)S(1)} %collective-permute-done.10.got_zero, f32[3,72,1024]{2,1,0:T(8,128)S(1)} %collective-permute-done.11.got, ...), custom_call_target="tpu_custom_call" | custom-call | flops 19000000512 | bytes 10 | tf_op jit(solution)/shard_map/pallas_call | solution.py:513
  63.0 1.4 %collective-permute-done.18.far_halo = bf16[1,144,1024]{2,1,0:T(8,128)(2,1)S(1)} collective-permute-done((bf16[1,144,1024]{2,1,0:T(8,128)(2,1)S(1)}, bf16[1,144,1024]{2,1,0:T(8,128)(2,1)S(1)}, u32[]{:S(2)}, u32[]{:S(2)}) %collective-permute-start.18) | collective-permute-done | bytes 294944 | tf_op jit(solution)/shard_map/ppermute | solution.py:386
  64.4 1.6 %shard_map.103 = f32[72,8,1024]{2,1,0:T(8,128)} custom-call(f32[4,72,1024]{2,1,0:T(8,128)S(1)} %get-tuple-element.74.unused.keep, f32[4,72,1024]{2,1,0:T(8,128)S(1)} %collective-permute-done.16.got, bf16[1,144,1024]{2,1,0:T(8,128)(2,1)S(1)} %collective-permute-done.17.halo, bf16[1,144,1024]{2,1,0:T(8,128)(2,1)S(1)} %collective-permute-done.18.far_halo), custom_call_target="tpu_custom_call" | custom-call | flops 19000000512 | bytes 10 | tf_op jit(solution)/shard_map/pallas_call | solution.py:517
  (65 shorter events, 11.4 us)
Async XLA Ops:
  0.6 4.1 %copy-start.1 = (f32[72,8,1024]{2,1,0:T(8,128)S(1)}, f32[72,8,1024]{2,1,0:T(8,128)}, u32[]{:S(2)}) copy-start(f32[72,8,1024]{2,1,0:T(8,128)} %field.3) | copy-start | bytes 7077892
  0.7 3.5 %copy-start.3 = (s32[1606]{0:T(1024)S(1)}, s32[1606]{0:T(1024)}, u32[]{:S(2)}) copy-start(s32[1606]{0:T(1024)} %param.10) | copy-start | bytes 19276
  0.7 3.5 %copy-start.4 = (s32[1606]{0:T(1024)S(1)}, s32[1606]{0:T(1024)}, u32[]{:S(2)}) copy-start(s32[1606]{0:T(1024)} %param.11) | copy-start | bytes 19276
  0.7 3.5 %copy-start.5 = (bf16[1606]{0:T(1024)(128)(2,1)S(1)}, bf16[1606]{0:T(1024)(128)(2,1)}, u32[]{:S(2)}) copy-start(bf16[1606]{0:T(1024)(128)(2,1)} %param.12) | copy-start | bytes 9640
  2.8 1.9 %collective-permute-start = (f32[72,1024]{1,0:T(8,128)}, f32[72,1024]{1,0:T(8,128)S(1)}, u32[]{:S(2)}, u32[]{:S(2)}) collective-permute-start(f32[72,1024]{1,0:T(8,128)} %get-tuple-element.40), channel_id=1, source_target_pairs={{0,8},{8,0},{16,24},{24,16},{1,9},{9,1},{17,25},{25,17},{2,10},{10... | collective-permute-start | bytes 884744 | tf_op jit(solution)/shard_map/ppermute | solution.py:386
  3.3 16.5 %collective-permute-start.3 = (f32[72,1024]{1,0:T(8,128)}, f32[72,1024]{1,0:T(8,128)S(1)}, u32[]{:S(2)}, u32[]{:S(2)}) collective-permute-start(f32[72,1024]{1,0:T(8,128)} %get-tuple-element.43), channel_id=1, source_target_pairs={{8,1},{1,8},{9,2},{2,9},{10,3},{3,10},{11,4},{4,11},{12,5},{5,12},... | collective-permute-start | bytes 884744 | tf_op jit(solution)/shard_map/ppermute | solution.py:392
  5.3 6.6 %copy-start = (f32[11,8,1024]{2,1,0:T(8,128)S(1)}, f32[11,8,1024]{2,1,0:T(8,128)}, u32[]{:S(2)}) copy-start(f32[11,8,1024]{2,1,0:T(8,128)} %stiff.17) | copy-start | bytes 1081348
  5.3 6.5 %collective-permute-start.1 = (f32[5,72,1024]{2,1,0:T(8,128)S(1)}, f32[5,72,1024]{2,1,0:T(8,128)S(1)}, u32[]{:S(2)}, u32[]{:S(2)}) collective-permute-start(f32[5,72,1024]{2,1,0:T(8,128)S(1)} %get-tuple-element.42), channel_id=1, source_target_pairs={{0,8},{8,0},{16,24},{24,16},{1,9},{9,1},{17,25},{25,17},{2,10},{10... | collective-permute-start | bytes 4423688 | tf_op jit(solution)/shard_map/ppermute | solution.py:386
  8.9 11.0 %collective-permute-start.2 = (f32[72,1024]{1,0:T(8,128)S(1)}, f32[72,1024]{1,0:T(8,128)S(1)}, u32[]{:S(2)}, u32[]{:S(2)}) collective-permute-start(f32[72,1024]{1,0:T(8,128)S(1)} %collective-permute-done.unused), channel_id=1, source_target_pairs={{8,1},{1,8},{9,2},{2,9},{10,3},{3,10},{11,4},{4,11},{12,5},{5,12},... | collective-permute-start | bytes 884744 | tf_op jit(solution)/shard_map/ppermute | solution.py:392
  13.2 4.9 %collective-permute-start.4 = (bf16[1,56,1024]{2,1,0:T(8,128)(2,1)S(1)}, bf16[1,56,1024]{2,1,0:T(8,128)(2,1)S(1)}, u32[]{:S(2)}, u32[]{:S(2)}) collective-permute-start(bf16[1,56,1024]{2,1,0:T(8,128)(2,1)S(1)} %get-tuple-element.46.rest_2_), channel_id=1, source_target_pairs={{0,16},{8,24},{16,0},{24,8},{1,17},{9,25},{17,1},{25,9},{2,18},{10... | collective-permute-start | bytes 344072 | tf_op jit(solution)/shard_map/ppermute | solution.py:389
  16.8 6.8 %collective-permute-start.6 = (bf16[2,56,1024]{2,1,0:T(8,128)(2,1)S(1)}, bf16[2,56,1024]{2,1,0:T(8,128)(2,1)S(1)}, u32[]{:S(2)}, u32[]{:S(2)}) collective-permute-start(bf16[2,56,1024]{2,1,0:T(8,128)(2,1)S(1)} %get-tuple-element.48.unused), channel_id=1, source_target_pairs={{0,16},{8,24},{16,0},{24,8},{1,17},{9,25},{17,1},{25,9},{2,18},{10... | collective-permute-start | bytes 688136 | tf_op jit(solution)/shard_map/ppermute | solution.py:389
  19.2 16.3 %collective-permute-start.8 = (bf16[1,144,1024]{2,1,0:T(8,128)(2,1)S(1)}, bf16[1,144,1024]{2,1,0:T(8,128)(2,1)S(1)}, u32[]{:S(2)}, u32[]{:S(2)}) collective-permute-start(bf16[1,144,1024]{2,1,0:T(8,128)(2,1)S(1)} %get-tuple-element.49.rest_4_), channel_id=1, source_target_pairs={{8,1},{1,8},{9,2},{2,9},{10,3},{3,10},{11,4},{4,11},{12,5},{5,12},... | collective-permute-start | bytes 884744 | tf_op jit(solution)/shard_map/ppermute | solution.py:392
  21.2 8.7 %collective-permute-start.5 = (bf16[1,56,1024]{2,1,0:T(8,128)(2,1)S(1)}, bf16[1,56,1024]{2,1,0:T(8,128)(2,1)S(1)}, u32[]{:S(2)}, u32[]{:S(2)}) collective-permute-start(bf16[1,56,1024]{2,1,0:T(8,128)(2,1)S(1)} %get-tuple-element.51.unused), channel_id=1, source_target_pairs={{0,16},{8,24},{16,0},{24,8},{1,17},{9,25},{17,1},{25,9},{2,18},{10... | collective-permute-start | bytes 344072 | tf_op jit(solution)/shard_map/ppermute | solution.py:389
  25.7 6.2 %collective-permute-start.9 = (bf16[2,144,1024]{2,1,0:T(8,128)(2,1)S(1)}, bf16[2,144,1024]{2,1,0:T(8,128)(2,1)S(1)}, u32[]{:S(2)}, u32[]{:S(2)}) collective-permute-start(bf16[2,144,1024]{2,1,0:T(8,128)(2,1)S(1)} %get-tuple-element.53.unused), channel_id=1, source_target_pairs={{0,8},{8,0},{16,24},{24,16},{1,9},{9,1},{17,25},{25,17},{2,10},{10... | collective-permute-start | bytes 1769480 | tf_op jit(solution)/shard_map/ppermute | solution.py:386
  31.0 4.5 %collective-permute-start.7 = (bf16[1,144,1024]{2,1,0:T(8,128)(2,1)S(1)}, bf16[1,144,1024]{2,1,0:T(8,128)(2,1)S(1)}, u32[]{:S(2)}, u32[]{:S(2)}) collective-permute-start(bf16[1,144,1024]{2,1,0:T(8,128)(2,1)S(1)} %get-tuple-element.56), channel_id=1, source_target_pairs={{8,1},{1,8},{9,2},{2,9},{10,3},{3,10},{11,4},{4,11},{12,5},{5,12},... | collective-permute-start | bytes 884744 | tf_op jit(solution)/shard_map/ppermute | solution.py:392
  34.9 9.9 %collective-permute-start.13 = (bf16[2,56,1024]{2,1,0:T(8,128)(2,1)S(1)}, bf16[2,56,1024]{2,1,0:T(8,128)(2,1)S(1)}, u32[]{:S(2)}, u32[]{:S(2)}) collective-permute-start(bf16[2,56,1024]{2,1,0:T(8,128)(2,1)S(1)} %get-tuple-element.66), channel_id=1, source_target_pairs={{0,16},{8,24},{16,0},{24,8},{1,17},{9,25},{17,1},{25,9},{2,18},{10... | collective-permute-start | bytes 688136 | tf_op jit(solution)/shard_map/ppermute | solution.py:389
  37.6 9.6 %collective-permute-start.12 = (bf16[1,56,1024]{2,1,0:T(8,128)(2,1)S(1)}, bf16[1,56,1024]{2,1,0:T(8,128)(2,1)S(1)}, u32[]{:S(2)}, u32[]{:S(2)}) collective-permute-start(bf16[1,56,1024]{2,1,0:T(8,128)(2,1)S(1)} %get-tuple-element.64), channel_id=1, source_target_pairs={{0,16},{8,24},{16,0},{24,8},{1,17},{9,25},{17,1},{25,9},{2,18},{10... | collective-permute-start | bytes 344072 | tf_op jit(solution)/shard_map/ppermute | solution.py:389
  39.2 20.8 %collective-permute-start.10 = (f32[1,72,1024]{2,1,0:T(8,128)S(1)}, f32[1,72,1024]{2,1,0:T(8,128)S(1)}, u32[]{:S(2)}, u32[]{:S(2)}) collective-permute-start(f32[1,72,1024]{2,1,0:T(8,128)S(1)} %get-tuple-element.61), channel_id=1, source_target_pairs={{0,8},{8,0},{16,24},{24,16},{1,9},{9,1},{17,25},{25,17},{2,10},{10... | collective-permute-start | bytes 884744 | tf_op jit(solution)/shard_map/ppermute | solution.py:386
  44.8 15.1 %collective-permute-start.11 = (f32[3,72,1024]{2,1,0:T(8,128)S(1)}, f32[3,72,1024]{2,1,0:T(8,128)S(1)}, u32[]{:S(2)}, u32[]{:S(2)}) collective-permute-start(f32[3,72,1024]{2,1,0:T(8,128)S(1)} %get-tuple-element.62), channel_id=1, source_target_pairs={{0,8},{8,0},{16,24},{24,16},{1,9},{9,1},{17,25},{25,17},{2,10},{10... | collective-permute-start | bytes 2654216 | tf_op jit(solution)/shard_map/ppermute | solution.py:386
  45.9 10.7 %collective-permute-start.14 = (bf16[1,56,1024]{2,1,0:T(8,128)(2,1)S(1)}, bf16[1,56,1024]{2,1,0:T(8,128)(2,1)S(1)}, u32[]{:S(2)}, u32[]{:S(2)}) collective-permute-start(bf16[1,56,1024]{2,1,0:T(8,128)(2,1)S(1)} %get-tuple-element.67.unused), channel_id=1, source_target_pairs={{0,16},{8,24},{16,0},{24,8},{1,17},{9,25},{17,1},{25,9},{2,18},{10... | collective-permute-start | bytes 344072 | tf_op jit(solution)/shard_map/ppermute | solution.py:389
  48.3 14.5 %collective-permute-start.17 = (bf16[1,144,1024]{2,1,0:T(8,128)(2,1)S(1)}, bf16[1,144,1024]{2,1,0:T(8,128)(2,1)S(1)}, u32[]{:S(2)}, u32[]{:S(2)}) collective-permute-start(bf16[1,144,1024]{2,1,0:T(8,128)(2,1)S(1)} %get-tuple-element.70.unused), channel_id=1, source_target_pairs={{8,1},{1,8},{9,2},{2,9},{10,3},{3,10},{11,4},{4,11},{12,5},{5,12},... | collective-permute-start | bytes 884744 | tf_op jit(solution)/shard_map/ppermute | solution.py:392
  51.0 6.9 %collective-permute-start.15 = (bf16[1,144,1024]{2,1,0:T(8,128)(2,1)S(1)}, bf16[1,144,1024]{2,1,0:T(8,128)(2,1)S(1)}, u32[]{:S(2)}, u32[]{:S(2)}) collective-permute-start(bf16[1,144,1024]{2,1,0:T(8,128)(2,1)S(1)} %get-tuple-element.73), channel_id=1, source_target_pairs={{0,8},{8,0},{16,24},{24,16},{1,9},{9,1},{17,25},{25,17},{2,10},{10... | collective-permute-start | bytes 884744 | tf_op jit(solution)/shard_map/ppermute | solution.py:386
  59.5 4.9 %collective-permute-start.16 = (f32[4,72,1024]{2,1,0:T(8,128)S(1)}, f32[4,72,1024]{2,1,0:T(8,128)S(1)}, u32[]{:S(2)}, u32[]{:S(2)}) collective-permute-start(f32[4,72,1024]{2,1,0:T(8,128)S(1)} %get-tuple-element.76), channel_id=1, source_target_pairs={{0,8},{8,0},{16,24},{24,16},{1,9},{9,1},{17,25},{25,17},{2,10},{10... | collective-permute-start | bytes 3538952 | tf_op jit(solution)/shard_map/ppermute | solution.py:386
  62.8 1.6 %collective-permute-start.18 = (bf16[1,144,1024]{2,1,0:T(8,128)(2,1)S(1)}, bf16[1,144,1024]{2,1,0:T(8,128)(2,1)S(1)}, u32[]{:S(2)}, u32[]{:S(2)}) collective-permute-start(bf16[1,144,1024]{2,1,0:T(8,128)(2,1)S(1)} %broadcast_select_fusion), channel_id=1, source_target_pairs={{0,8},{8,0},{16,24},{24,16},{1,9},{9,1},{17,25},{25,17},{2,10},{10... | collective-permute-start | bytes 884744 | tf_op jit(solution)/shard_map/ppermute | solution.py:386
  (2 other events, 6.8 us)

commit v6 on v5

--- a/solution.py
+++ b/solution.py
@@ -345,12 +345,20 @@
     write_tiles(near, far, out, lines, done)
 
 
+def halves(halo, own):
+    whole = halo[0].astype(F32)
+    first = core_side() == 0
+    lower, upper = whole[:own], whole[own:]
+    return jnp.where(first, lower, upper), jnp.where(first, upper, lower)
+
+
+def cut_kernel(halo, unused, part):
+    part[...] = halves(halo, part.shape[0])[1].astype(BF16)
+
+
 def last_merge_kernel(keep, got, halo, far_halo, out, lines, done):
-    own = keep.shape[1]
-    first = core_side() == 0
-    halos, others = halo[0].astype(F32), far_halo[0].astype(F32)
-    near_line = jnp.where(first, halos[:own], halos[own:])
-    far_line = jnp.where(first, others[:own], others[own:])
+    near_line = halves(halo, keep.shape[1])[0]
+    far_line = far_halo[...].astype(F32)
 
     def near(i, cut):
         return keep[0, cut, :] + near_line[cut] if i == 0 else keep[i, cut, :]
@@ -473,10 +481,10 @@
 
     bent_one, sent, cross_one = bend(1, 1, got)
     bent_in, sent, cross_in = bend(2, 2, sent)
+    bent_out, sent, cross_out = bend(0, 1, sent, halo_near, halo_far)
     moment_one, edge_one = couple(bent_one, cross_one, 1, 1, (), sent)
     next_near = by_tile(edge_one)
-    bent_out, sent, cross_out = bend(0, 1, edge_one, halo_near, halo_far)
-    moment_in, edge_in = couple(bent_in, cross_in, 2, None, (3, 2), sent)
+    moment_in, edge_in = couple(bent_in, cross_in, 2, None, (3, 2), edge_one)
     inner = by_core(edge_in)
     moment_out, edge_zero = couple(bent_out, cross_out, 0, 0, (), edge_in)
     near = by_tile(edge_zero)
@@ -513,7 +521,9 @@
     first_apply, token = call(
         merge_kernel, (whole, TOKEN), writers, 1.9, [VMEM] * 4 + [ANY], 6, (ANY, VMEM)
     )(keep_out, keep_in, got_out, got_in, keep)
-    far_halo = by_core(jnp.where(token[0, 0] == 0, near, jnp.zeros_like(near)))
+    far_halo = by_core(
+        call(cut_kernel, shape((own, width), BF16), (), 0.3, [VMEM, ANY])(near, token)
+    )
     second_apply = call(last_merge_kernel, whole, writers, 1.9, [VMEM] * 4, 6, ANY)(
         keep, got, near, far_halo
     )

time: 66.4 us -> 64.7 us (0.974)
  starting transfers between devices: 30.9 us -> 29.4 us
  waiting for transfers between devices: 3.5 us -> 4.35 us
    ppermute x6, waiting for transfers between devices: 1.52 us -> 2.58 us  [by_chip(): return lax.ppermute(value, 'chaos', chip_swap)]
    ppermute x8, starting transfers between devices: 20.2 us -> 19.4 us  [by_core(): return lax.ppermute(value, 'chaos', core_swap)]
    ppermute x6, starting transfers between devices: 7.13 us -> 6.46 us  [by_chip(): return lax.ppermute(value, 'chaos', chip_swap)]
  transfers between devices with their start and end apart: 19 -> 19, of which waited for: 5 -> 5; matrix products, arithmetic and copies ran while one was open for 1% -> 0% of each run, Pallas kernels for 38% -> 39%
where the time goes in v6:
time: 64.7 us; the launch traced here: 64.4 us
  starting transfers between devices  29.4 us (45%)
  Pallas kernels  29.2 us (45%)
  waiting for transfers between devices  4.35 us (7%)
  between operations  1.23 us (2%)
    ppermute x8, starting transfers between devices, by_core(): return lax.ppermute(value, 'chaos', core_swap)  19.4 us
    pallas_call x6, Pallas kernels, couple(): call(functools.partial(couple_kernel, first, outer_row, inner_rows), tupl...  8.45 us
    ppermute x6, starting transfers between devices, by_chip(): return lax.ppermute(value, 'chaos', chip_swap)  6.46 us
    pallas_call x3, Pallas kernels, bend(): call(functools.partial(first_kernel, first), bents(count), (), 0.9 * coun...  4.7 us
    ppermute x5, starting transfers between devices, by_tile(): return lax.ppermute(value, ('chaos', 'tile'), tile_swap)  3.55 us
    pallas_call x1, Pallas kernels, body(): call(second_inner_kernel, (shape((4, pair, width), F32),) + outs(3) + ben...  3.03 us
    ppermute x6, waiting for transfers between devices, by_chip(): return lax.ppermute(value, 'chaos', chip_swap)  2.58 us
    pallas_call x1, Pallas kernels, body(): call(functools.partial(table_kernel, terms, pair, hubs, slot_total), (sha...  2.29 us
  transfers between devices with their start and end apart: 19, of which 5 were waited for; matrix products, arithmetic and copies ran while one was open for 0% of the time, Pallas kernels for 39%

profile of v6, /device:TPU:0, one launch (start us, length us, event | category | flops | bytes accessed | tf_op | source)
XLA Modules:
  0.0 64.4 jit_solution(15306374519951051566)
XLA Ops:
  0.7 2.1 %shard_map.86 = (f32[72,1024]{1,0:T(8,128)}, f32[72,1024]{1,0:T(8,128)}) custom-call(f32[72,8,1024]{2,1,0:T(8,128)} %field.3), custom_call_target="tpu_custom_call" | custom-call | flops 20000000000 | bytes 10 | tf_op jit(solution)/shard_map/pallas_call | solution.py:420
  5.3 3.6 %collective-permute-start.1 = (f32[5,72,1024]{2,1,0:T(8,128)S(1)}, f32[5,72,1024]{2,1,0:T(8,128)S(1)}, u32[]{:S(2)}, u32[]{:S(2)}) collective-permute-start(f32[5,72,1024]{2,1,0:T(8,128)S(1)} %get-tuple-element.42), channel_id=1, source_target_pairs={{0,8},{8,0},{16,24},{24,16},{1,9},{9,1},{17,25},{25,17},{2,10},{10... | collective-permute-start | bytes 4423688 | tf_op jit(solution)/shard_map/ppermute | solution.py:394
  9.6 2.3 %shard_map.88 = (bf16[12,144,208]{2,1,0:T(8,128)(2,1)S(1)}, bf16[11,64,144]{2,1,0:T(8,128)(2,1)S(1)}) custom-call(f32[8,1664]{1,0:T(8,128)S(1)} %stack.31.entries, f32[72,1024]{1,0:T(8,128)S(1)} %collective-permute-done.unused), custom_call_target="tpu_custom_call" | custom-call | flops 30000001024 | bytes 10 | tf_op jit(solution)/shard_map/pallas_call | solution.py:432
  11.9 1.3 %shard_map.89 = (bf16[1,144,1024]{2,1,0:T(8,128)(2,1)S(1)}, bf16[1,56,1024]{2,1,0:T(8,128)(2,1)S(1)}) custom-call(f32[5,72,1024]{2,1,0:T(8,128)S(1)} %get-tuple-element.41.keep, f32[5,72,1024]{2,1,0:T(8,128)S(1)} %collective-permute-done.1.got.rest_2_, f32[11,8,1024]{2,1,0:T(8,128)S(1)} %copy-done, ...), custom_call_target="tpu_custom_call" | custom-call | flops 8999999488 | bytes 10 | tf_op jit(solution)/shard_map/pallas_call | solution.py:458
  13.2 1.6 %collective-permute-start.6 = (bf16[1,56,1024]{2,1,0:T(8,128)(2,1)S(1)}, bf16[1,56,1024]{2,1,0:T(8,128)(2,1)S(1)}, u32[]{:S(2)}, u32[]{:S(2)}) collective-permute-start(bf16[1,56,1024]{2,1,0:T(8,128)(2,1)S(1)} %get-tuple-element.45.rest_2_), channel_id=1, source_target_pairs={{0,16},{8,24},{16,0},{24,8},{1,17},{9,25},{17,1},{25,9},{2,18},{10... | collective-permute-start | bytes 344072 | tf_op jit(solution)/shard_map/ppermute | solution.py:397
  14.8 2.0 %shard_map.90 = (bf16[2,144,1024]{2,1,0:T(8,128)(2,1)S(1)}, bf16[2,56,1024]{2,1,0:T(8,128)(2,1)S(1)}) custom-call(f32[5,72,1024]{2,1,0:T(8,128)S(1)} %get-tuple-element.41.keep, f32[5,72,1024]{2,1,0:T(8,128)S(1)} %collective-permute-done.1.got.rest_2_, f32[11,8,1024]{2,1,0:T(8,128)S(1)} %copy-done, ...), custom_call_target="tpu_custom_call" | custom-call | flops 17999998976 | bytes 10 | tf_op jit(solution)/shard_map/pallas_call | solution.py:458
  17.4 1.3 %shard_map.91 = (bf16[1,144,1024]{2,1,0:T(8,128)(2,1)S(1)}, bf16[1,56,1024]{2,1,0:T(8,128)(2,1)S(1)}) custom-call(f32[5,72,1024]{2,1,0:T(8,128)S(1)} %get-tuple-element.41.keep, f32[5,72,1024]{2,1,0:T(8,128)S(1)} %collective-permute-done.1.got.rest_2_, f32[72,1024]{1,0:T(8,128)S(1)} %collective-permute-done.2.rest_0_, ...), custom_call_target="tpu_custom_call" | custom-call | flops 8999999488 | bytes 10 | tf_op jit(solution)/shard_map/pallas_call | solution.py:458
  18.8 1.5 %collective-permute-start.4 = (bf16[1,56,1024]{2,1,0:T(8,128)(2,1)S(1)}, bf16[1,56,1024]{2,1,0:T(8,128)(2,1)S(1)}, u32[]{:S(2)}, u32[]{:S(2)}) collective-permute-start(bf16[1,56,1024]{2,1,0:T(8,128)(2,1)S(1)} %get-tuple-element.48.unused), channel_id=1, source_target_pairs={{0,16},{8,24},{16,0},{24,8},{1,17},{9,25},{17,1},{25,9},{2,18},{10... | collective-permute-start | bytes 344072 | tf_op jit(solution)/shard_map/ppermute | solution.py:397
  20.3 1.1 %shard_map.92 = (f32[1,144,1024]{2,1,0:T(8,128)S(1)}, bf16[1,144,1024]{2,1,0:T(8,128)(2,1)S(1)}) custom-call(bf16[1,144,1024]{2,1,0:T(8,128)(2,1)S(1)} %get-tuple-element.51.bent, bf16[1,56,1024]{2,1,0:T(8,128)(2,1)S(1)} %collective-permute-done.6.got, f32[11,8,1024]{2,1,0:T(8,128)S(1)} %copy-done, bf16[12,144,208]{2,1,0:T(8,128)(2,1)S(1)} %get-tuple-element.49.table, ...), custom_call_target="tpu_custom_call" | custom-call | flops 10000000000 | bytes 10 | tf_op jit(solution)/shard_map/pallas_call | solution.py:474
  22.1 1.5 %collective-permute-done.5.got = bf16[2,56,1024]{2,1,0:T(8,128)(2,1)S(1)} collective-permute-done((bf16[2,56,1024]{2,1,0:T(8,128)(2,1)S(1)}, bf16[2,56,1024]{2,1,0:T(8,128)(2,1)S(1)}, u32[]{:S(2)}, u32[]{:S(2)}) %collective-permute-start.5) | collective-permute-done | bytes 229408 | tf_op jit(solution)/shard_map/ppermute | solution.py:397
  23.6 2.0 %shard_map.93 = (f32[2,144,1024]{2,1,0:T(8,128)S(1)}, bf16[2,144,1024]{2,1,0:T(8,128)(2,1)S(1)}) custom-call(bf16[2,144,1024]{2,1,0:T(8,128)(2,1)S(1)} %get-tuple-element.50.bent, bf16[2,56,1024]{2,1,0:T(8,128)(2,1)S(1)} %collective-permute-done.5.got, f32[11,8,1024]{2,1,0:T(8,128)S(1)} %copy-done, bf16[12,144,208]{2,1,0:T(8,128)(2,1)S(1)} %get-tuple-element.49.table, ...), custom_call_target="tpu_custom_call" | custom-call | flops 20000000000 | bytes 10 | tf_op jit(solution)/shard_map/pallas_call | solution.py:474
  25.7 6.1 %collective-permute-start.9 = (bf16[2,144,1024]{2,1,0:T(8,128)(2,1)S(1)}, bf16[2,144,1024]{2,1,0:T(8,128)(2,1)S(1)}, u32[]{:S(2)}, u32[]{:S(2)}) collective-permute-start(bf16[2,144,1024]{2,1,0:T(8,128)(2,1)S(1)} %get-tuple-element.53.unused), channel_id=1, source_target_pairs={{0,8},{8,0},{16,24},{24,16},{1,9},{9,1},{17,25},{25,17},{2,10},{10... | collective-permute-start | bytes 1769480 | tf_op jit(solution)/shard_map/ppermute | solution.py:394
  31.8 1.1 %shard_map.94 = (f32[1,144,1024]{2,1,0:T(8,128)S(1)}, bf16[1,144,1024]{2,1,0:T(8,128)(2,1)S(1)}) custom-call(bf16[1,144,1024]{2,1,0:T(8,128)(2,1)S(1)} %get-tuple-element.47.bent, bf16[1,56,1024]{2,1,0:T(8,128)(2,1)S(1)} %collective-permute-done.4.got, f32[11,8,1024]{2,1,0:T(8,128)S(1)} %copy-done, bf16[12,144,208]{2,1,0:T(8,128)(2,1)S(1)} %get-tuple-element.49.table, ...), custom_call_target="tpu_custom_call" | custom-call | flops 10000000000 | bytes 10 | tf_op jit(solution)/shard_map/pallas_call | solution.py:474
  33.8 3.0 %shard_map.95 = (f32[4,144,1024]{2,1,0:T(8,128)S(1)}, f32[3,72,1024]{2,1,0:T(8,128)S(1)}, f32[3,72,1024]{2,1,0:T(8,128)S(1)}, bf16[2,144,1024]{2,1,0:T(8,128)(2,1)S(1)}, bf16[2,56,1024]{2,1,0:T(8,128)(2,1)S(1)}) custom-call(f32[1,144,1024]{2,1,0:T(8,128)S(1)} %get-tuple-element.54.row_zero, f32[1,144,1024]{2,1,0:T(8,128)S(1)} %get-tuple-element.55.row_one.others, ...), custom_call_target="tpu_custom_call" | custom-call | flops 35000000512 | bytes 10 | tf_op jit(solution)/shard_map/pallas_call | solution.py:492
  37.4 2.1 %shard_map.96 = (f32[1,144,1024]{2,1,0:T(8,128)S(1)}, f32[1,72,1024]{2,1,0:T(8,128)S(1)}, f32[1,72,1024]{2,1,0:T(8,128)S(1)}, bf16[1,144,1024]{2,1,0:T(8,128)(2,1)S(1)}, bf16[1,56,1024]{2,1,0:T(8,128)(2,1)S(1)}) custom-call(f32[1,144,1024]{2,1,0:T(8,128)S(1)} %get-tuple-element.54.row_zero, f32[1,144,1024]{2,1,0:T(8,128)S(1)} %get-tuple-element.55.row_one.others, ...), custom_call_target="tpu_custom_call" | custom-call | flops 100000000 | bytes 10 | tf_op jit(solution)/shard_map/pallas_call | solution.py:497
  39.5 1.6 %collective-permute-start.12 = (bf16[1,56,1024]{2,1,0:T(8,128)(2,1)S(1)}, bf16[1,56,1024]{2,1,0:T(8,128)(2,1)S(1)}, u32[]{:S(2)}, u32[]{:S(2)}) collective-permute-start(bf16[1,56,1024]{2,1,0:T(8,128)(2,1)S(1)} %get-tuple-element.64), channel_id=1, source_target_pairs={{0,16},{8,24},{16,0},{24,8},{1,17},{9,25},{17,1},{25,9},{2,18},{10... | collective-permute-start | bytes 344072 | tf_op jit(solution)/shard_map/ppermute | solution.py:397
  41.0 3.0 %collective-permute-start.10 = (f32[1,72,1024]{2,1,0:T(8,128)S(1)}, f32[1,72,1024]{2,1,0:T(8,128)S(1)}, u32[]{:S(2)}, u32[]{:S(2)}) collective-permute-start(f32[1,72,1024]{2,1,0:T(8,128)S(1)} %get-tuple-element.61), channel_id=1, source_target_pairs={{0,8},{8,0},{16,24},{24,16},{1,9},{9,1},{17,25},{25,17},{2,10},{10... | collective-permute-start | bytes 884744 | tf_op jit(solution)/shard_map/ppermute | solution.py:394
  46.7 1.1 %shard_map.98 = (f32[1,144,1024]{2,1,0:T(8,128)S(1)}, bf16[1,144,1024]{2,1,0:T(8,128)(2,1)S(1)}) custom-call(bf16[1,144,1024]{2,1,0:T(8,128)(2,1)S(1)} %get-tuple-element.63.bent, bf16[1,56,1024]{2,1,0:T(8,128)(2,1)S(1)} %collective-permute-done.12.got, f32[11,8,1024]{2,1,0:T(8,128)S(1)} %copy-done, bf16[12,144,208]{2,1,0:T(8,128)(2,1)S(1)} %get-tuple-element.49.table, ...), custom_call_target="tpu_custom_call" | custom-call | flops 10000000000 | bytes 10 | tf_op jit(solution)/shard_map/pallas_call | solution.py:474
  48.5 2.0 %shard_map.100 = (f32[2,144,1024]{2,1,0:T(8,128)S(1)}, bf16[1,144,1024]{2,1,0:T(8,128)(2,1)S(1)}) custom-call(bf16[2,144,1024]{2,1,0:T(8,128)(2,1)S(1)} %get-tuple-element.71.bent, bf16[2,56,1024]{2,1,0:T(8,128)(2,1)S(1)} %collective-permute-done.13.unused.got, f32[11,8,1024]{2,1,0:T(8,128)S(1)} %copy-done, ...), custom_call_target="tpu_custom_call" | custom-call | flops 20000000000 | bytes 10 | tf_op jit(solution)/shard_map/pallas_call | solution.py:474
  50.6 5.6 %collective-permute-start.15 = (bf16[1,144,1024]{2,1,0:T(8,128)(2,1)S(1)}, bf16[1,144,1024]{2,1,0:T(8,128)(2,1)S(1)}, u32[]{:S(2)}, u32[]{:S(2)}) collective-permute-start(bf16[1,144,1024]{2,1,0:T(8,128)(2,1)S(1)} %get-tuple-element.73), channel_id=1, source_target_pairs={{0,8},{8,0},{16,24},{24,16},{1,9},{9,1},{17,25},{25,17},{2,10},{10... | collective-permute-start | bytes 884744 | tf_op jit(solution)/shard_map/ppermute | solution.py:394
  57.4 1.6 %shard_map.101 = (f32[4,72,1024]{2,1,0:T(8,128)S(1)}, f32[4,72,1024]{2,1,0:T(8,128)S(1)}) custom-call(f32[1,144,1024]{2,1,0:T(8,128)S(1)} %get-tuple-element.68.zero, f32[1,144,1024]{2,1,0:T(8,128)S(1)} %shard_map.99.one, f32[2,144,1024]{2,1,0:T(8,128)S(1)} %get-tuple-element.72.inners, bf16[1,144,1024]{2,1,0:T(8,128)(2,1)S(1)} %collective-permute-done.15.inner), custom_call_target="tpu_custom_call" | custom-call | flops 24999999488 | bytes 10 | tf_op jit(solution)/shard_map/pallas_call | solution.py:515
  59.5 1.6 %shard_map.102 = (f32[72,8,1024]{2,1,0:T(8,128)}, s32[8,128]{1,0:T(8,128)S(1)}) custom-call(f32[1,72,1024]{2,1,0:T(8,128)S(1)} %get-tuple-element.59.keep_zero, f32[3,72,1024]{2,1,0:T(8,128)S(1)} %get-tuple-element.60.keep, f32[1,72,1024]{2,1,0:T(8,128)S(1)} %collective-permute-done.10.got_zero, f32[3,72,1024]{2,1,0:T(8,128)S(1)} %collective-permute-done.11.got, ...), custom_call_target="tpu_custom_call" | custom-call | flops 19000000512 | bytes 10 | tf_op jit(solution)/shard_map/pallas_call | solution.py:521
  61.4 1.2 %collective-permute-done.18.far_halo = bf16[72,1024]{1,0:T(8,128)(2,1)S(1)} collective-permute-done((bf16[72,1024]{1,0:T(8,128)(2,1)S(1)}, bf16[72,1024]{1,0:T(8,128)(2,1)S(1)}, u32[]{:S(2)}, u32[]{:S(2)}) %collective-permute-start.18) | collective-permute-done | bytes 147488 | tf_op jit(solution)/shard_map/ppermute | solution.py:394
  62.6 1.6 %shard_map.104 = f32[72,8,1024]{2,1,0:T(8,128)} custom-call(f32[4,72,1024]{2,1,0:T(8,128)S(1)} %get-tuple-element.74.unused.keep, f32[4,72,1024]{2,1,0:T(8,128)S(1)} %collective-permute-done.16.got, bf16[1,144,1024]{2,1,0:T(8,128)(2,1)S(1)} %collective-permute-done.17.halo, bf16[72,1024]{1,0:T(8,128)(2,1)S(1)} %collective-permute-done.18.far_halo), custom_call_target="tpu_custom_call" | custom-call | flops 19000000512 | bytes 10 | tf_op jit(solution)/shard_map/pallas_call | solution.py:527
  (64 shorter events, 11.0 us)
Async XLA Ops:
  0.6 4.1 %copy-start.1 = (f32[72,8,1024]{2,1,0:T(8,128)S(1)}, f32[72,8,1024]{2,1,0:T(8,128)}, u32[]{:S(2)}) copy-start(f32[72,8,1024]{2,1,0:T(8,128)} %field.3) | copy-start | bytes 7077892
  0.7 3.5 %copy-start.3 = (s32[1606]{0:T(1024)S(1)}, s32[1606]{0:T(1024)}, u32[]{:S(2)}) copy-start(s32[1606]{0:T(1024)} %param.10) | copy-start | bytes 19276
  0.7 3.5 %copy-start.4 = (s32[1606]{0:T(1024)S(1)}, s32[1606]{0:T(1024)}, u32[]{:S(2)}) copy-start(s32[1606]{0:T(1024)} %param.11) | copy-start | bytes 19276
  0.7 3.5 %copy-start.5 = (bf16[1606]{0:T(1024)(128)(2,1)S(1)}, bf16[1606]{0:T(1024)(128)(2,1)}, u32[]{:S(2)}) copy-start(bf16[1606]{0:T(1024)(128)(2,1)} %param.12) | copy-start | bytes 9640
  2.8 1.9 %collective-permute-start = (f32[72,1024]{1,0:T(8,128)}, f32[72,1024]{1,0:T(8,128)S(1)}, u32[]{:S(2)}, u32[]{:S(2)}) collective-permute-start(f32[72,1024]{1,0:T(8,128)} %get-tuple-element.40), channel_id=1, source_target_pairs={{0,8},{8,0},{16,24},{24,16},{1,9},{9,1},{17,25},{25,17},{2,10},{10... | collective-permute-start | bytes 884744 | tf_op jit(solution)/shard_map/ppermute | solution.py:394
  3.3 14.1 %collective-permute-start.3 = (f32[72,1024]{1,0:T(8,128)}, f32[72,1024]{1,0:T(8,128)S(1)}, u32[]{:S(2)}, u32[]{:S(2)}) collective-permute-start(f32[72,1024]{1,0:T(8,128)} %get-tuple-element.43), channel_id=1, source_target_pairs={{8,1},{1,8},{9,2},{2,9},{10,3},{3,10},{11,4},{4,11},{12,5},{5,12},... | collective-permute-start | bytes 884744 | tf_op jit(solution)/shard_map/ppermute | solution.py:400
  5.3 6.6 %copy-start = (f32[11,8,1024]{2,1,0:T(8,128)S(1)}, f32[11,8,1024]{2,1,0:T(8,128)}, u32[]{:S(2)}) copy-start(f32[11,8,1024]{2,1,0:T(8,128)} %stiff.17) | copy-start | bytes 1081348
  5.3 6.5 %collective-permute-start.1 = (f32[5,72,1024]{2,1,0:T(8,128)S(1)}, f32[5,72,1024]{2,1,0:T(8,128)S(1)}, u32[]{:S(2)}, u32[]{:S(2)}) collective-permute-start(f32[5,72,1024]{2,1,0:T(8,128)S(1)} %get-tuple-element.42), channel_id=1, source_target_pairs={{0,8},{8,0},{16,24},{24,16},{1,9},{9,1},{17,25},{25,17},{2,10},{10... | collective-permute-start | bytes 4423688 | tf_op jit(solution)/shard_map/ppermute | solution.py:394
  8.9 8.5 %collective-permute-start.2 = (f32[72,1024]{1,0:T(8,128)S(1)}, f32[72,1024]{1,0:T(8,128)S(1)}, u32[]{:S(2)}, u32[]{:S(2)}) collective-permute-start(f32[72,1024]{1,0:T(8,128)S(1)} %collective-permute-done.unused), channel_id=1, source_target_pairs={{8,1},{1,8},{9,2},{2,9},{10,3},{3,10},{11,4},{4,11},{12,5},{5,12},... | collective-permute-start | bytes 884744 | tf_op jit(solution)/shard_map/ppermute | solution.py:400
  13.2 7.1 %collective-permute-start.6 = (bf16[1,56,1024]{2,1,0:T(8,128)(2,1)S(1)}, bf16[1,56,1024]{2,1,0:T(8,128)(2,1)S(1)}, u32[]{:S(2)}, u32[]{:S(2)}) collective-permute-start(bf16[1,56,1024]{2,1,0:T(8,128)(2,1)S(1)} %get-tuple-element.45.rest_2_), channel_id=1, source_target_pairs={{0,16},{8,24},{16,0},{24,8},{1,17},{9,25},{17,1},{25,9},{2,18},{10... | collective-permute-start | bytes 344072 | tf_op jit(solution)/shard_map/ppermute | solution.py:397
  16.8 6.8 %collective-permute-start.5 = (bf16[2,56,1024]{2,1,0:T(8,128)(2,1)S(1)}, bf16[2,56,1024]{2,1,0:T(8,128)(2,1)S(1)}, u32[]{:S(2)}, u32[]{:S(2)}) collective-permute-start(bf16[2,56,1024]{2,1,0:T(8,128)(2,1)S(1)} %get-tuple-element.46.rest_4_), channel_id=1, source_target_pairs={{0,16},{8,24},{16,0},{24,8},{1,17},{9,25},{17,1},{25,9},{2,18},{10... | collective-permute-start | bytes 688136 | tf_op jit(solution)/shard_map/ppermute | solution.py:397
  18.8 13.0 %collective-permute-start.4 = (bf16[1,56,1024]{2,1,0:T(8,128)(2,1)S(1)}, bf16[1,56,1024]{2,1,0:T(8,128)(2,1)S(1)}, u32[]{:S(2)}, u32[]{:S(2)}) collective-permute-start(bf16[1,56,1024]{2,1,0:T(8,128)(2,1)S(1)} %get-tuple-element.48.unused), channel_id=1, source_target_pairs={{0,16},{8,24},{16,0},{24,8},{1,17},{9,25},{17,1},{25,9},{2,18},{10... | collective-permute-start | bytes 344072 | tf_op jit(solution)/shard_map/ppermute | solution.py:397
  21.4 16.0 %collective-permute-start.8 = (bf16[1,144,1024]{2,1,0:T(8,128)(2,1)S(1)}, bf16[1,144,1024]{2,1,0:T(8,128)(2,1)S(1)}, u32[]{:S(2)}, u32[]{:S(2)}) collective-permute-start(bf16[1,144,1024]{2,1,0:T(8,128)(2,1)S(1)} %get-tuple-element.52.unused), channel_id=1, source_target_pairs={{8,1},{1,8},{9,2},{2,9},{10,3},{3,10},{11,4},{4,11},{12,5},{5,12},... | collective-permute-start | bytes 884744 | tf_op jit(solution)/shard_map/ppermute | solution.py:400
  25.7 8.1 %collective-permute-start.9 = (bf16[2,144,1024]{2,1,0:T(8,128)(2,1)S(1)}, bf16[2,144,1024]{2,1,0:T(8,128)(2,1)S(1)}, u32[]{:S(2)}, u32[]{:S(2)}) collective-permute-start(bf16[2,144,1024]{2,1,0:T(8,128)(2,1)S(1)} %get-tuple-element.53.unused), channel_id=1, source_target_pairs={{0,8},{8,0},{16,24},{24,16},{1,9},{9,1},{17,25},{25,17},{2,10},{10... | collective-permute-start | bytes 1769480 | tf_op jit(solution)/shard_map/ppermute | solution.py:394
  32.9 4.5 %collective-permute-start.7 = (bf16[1,144,1024]{2,1,0:T(8,128)(2,1)S(1)}, bf16[1,144,1024]{2,1,0:T(8,128)(2,1)S(1)}, u32[]{:S(2)}, u32[]{:S(2)}) collective-permute-start(bf16[1,144,1024]{2,1,0:T(8,128)(2,1)S(1)} %get-tuple-element.56), channel_id=1, source_target_pairs={{8,1},{1,8},{9,2},{2,9},{10,3},{3,10},{11,4},{4,11},{12,5},{5,12},... | collective-permute-start | bytes 884744 | tf_op jit(solution)/shard_map/ppermute | solution.py:400
  36.8 8.2 %collective-permute-start.13 = (bf16[2,56,1024]{2,1,0:T(8,128)(2,1)S(1)}, bf16[2,56,1024]{2,1,0:T(8,128)(2,1)S(1)}, u32[]{:S(2)}, u32[]{:S(2)}) collective-permute-start(bf16[2,56,1024]{2,1,0:T(8,128)(2,1)S(1)} %get-tuple-element.66), channel_id=1, source_target_pairs={{0,16},{8,24},{16,0},{24,8},{1,17},{9,25},{17,1},{25,9},{2,18},{10... | collective-permute-start | bytes 688136 | tf_op jit(solution)/shard_map/ppermute | solution.py:397
  39.5 7.3 %collective-permute-start.12 = (bf16[1,56,1024]{2,1,0:T(8,128)(2,1)S(1)}, bf16[1,56,1024]{2,1,0:T(8,128)(2,1)S(1)}, u32[]{:S(2)}, u32[]{:S(2)}) collective-permute-start(bf16[1,56,1024]{2,1,0:T(8,128)(2,1)S(1)} %get-tuple-element.64), channel_id=1, source_target_pairs={{0,16},{8,24},{16,0},{24,8},{1,17},{9,25},{17,1},{25,9},{2,18},{10... | collective-permute-start | bytes 344072 | tf_op jit(solution)/shard_map/ppermute | solution.py:397
  41.0 18.4 %collective-permute-start.10 = (f32[1,72,1024]{2,1,0:T(8,128)S(1)}, f32[1,72,1024]{2,1,0:T(8,128)S(1)}, u32[]{:S(2)}, u32[]{:S(2)}) collective-permute-start(f32[1,72,1024]{2,1,0:T(8,128)S(1)} %get-tuple-element.61), channel_id=1, source_target_pairs={{0,8},{8,0},{16,24},{24,16},{1,9},{9,1},{17,25},{25,17},{2,10},{10... | collective-permute-start | bytes 884744 | tf_op jit(solution)/shard_map/ppermute | solution.py:394
  44.0 15.4 %collective-permute-start.11 = (f32[3,72,1024]{2,1,0:T(8,128)S(1)}, f32[3,72,1024]{2,1,0:T(8,128)S(1)}, u32[]{:S(2)}, u32[]{:S(2)}) collective-permute-start(f32[3,72,1024]{2,1,0:T(8,128)S(1)} %get-tuple-element.62), channel_id=1, source_target_pairs={{0,8},{8,0},{16,24},{24,16},{1,9},{9,1},{17,25},{25,17},{2,10},{10... | collective-permute-start | bytes 2654216 | tf_op jit(solution)/shard_map/ppermute | solution.py:394
  46.1 10.0 %collective-permute-start.14 = (bf16[1,56,1024]{2,1,0:T(8,128)(2,1)S(1)}, bf16[1,56,1024]{2,1,0:T(8,128)(2,1)S(1)}, u32[]{:S(2)}, u32[]{:S(2)}) collective-permute-start(bf16[1,56,1024]{2,1,0:T(8,128)(2,1)S(1)} %get-tuple-element.67.unused), channel_id=1, source_target_pairs={{0,16},{8,24},{16,0},{24,8},{1,17},{9,25},{17,1},{25,9},{2,18},{10... | collective-permute-start | bytes 344072 | tf_op jit(solution)/shard_map/ppermute | solution.py:397
  47.9 13.2 %collective-permute-start.17 = (bf16[1,144,1024]{2,1,0:T(8,128)(2,1)S(1)}, bf16[1,144,1024]{2,1,0:T(8,128)(2,1)S(1)}, u32[]{:S(2)}, u32[]{:S(2)}) collective-permute-start(bf16[1,144,1024]{2,1,0:T(8,128)(2,1)S(1)} %get-tuple-element.70.unused), channel_id=1, source_target_pairs={{8,1},{1,8},{9,2},{2,9},{10,3},{3,10},{11,4},{4,11},{12,5},{5,12},... | collective-permute-start | bytes 884744 | tf_op jit(solution)/shard_map/ppermute | solution.py:400
  50.6 6.8 %collective-permute-start.15 = (bf16[1,144,1024]{2,1,0:T(8,128)(2,1)S(1)}, bf16[1,144,1024]{2,1,0:T(8,128)(2,1)S(1)}, u32[]{:S(2)}, u32[]{:S(2)}) collective-permute-start(bf16[1,144,1024]{2,1,0:T(8,128)(2,1)S(1)} %get-tuple-element.73), channel_id=1, source_target_pairs={{0,8},{8,0},{16,24},{24,16},{1,9},{9,1},{17,25},{25,17},{2,10},{10... | collective-permute-start | bytes 884744 | tf_op jit(solution)/shard_map/ppermute | solution.py:394
  59.0 3.6 %collective-permute-start.16 = (f32[4,72,1024]{2,1,0:T(8,128)S(1)}, f32[4,72,1024]{2,1,0:T(8,128)S(1)}, u32[]{:S(2)}, u32[]{:S(2)}) collective-permute-start(f32[4,72,1024]{2,1,0:T(8,128)S(1)} %get-tuple-element.76), channel_id=1, source_target_pairs={{0,8},{8,0},{16,24},{24,16},{1,9},{9,1},{17,25},{25,17},{2,10},{10... | collective-permute-start | bytes 3538952 | tf_op jit(solution)/shard_map/ppermute | solution.py:394
  61.1 1.4 %collective-permute-start.18 = (bf16[72,1024]{1,0:T(8,128)(2,1)S(1)}, bf16[72,1024]{1,0:T(8,128)(2,1)S(1)}, u32[]{:S(2)}, u32[]{:S(2)}) collective-permute-start(bf16[72,1024]{1,0:T(8,128)(2,1)S(1)} %shard_map.103), channel_id=1, source_target_pairs={{0,8},{8,0},{16,24},{24,16},{1,9},{9,1},{17,25},{25,17},{2,10},{10... | collective-permute-start | bytes 442376 | tf_op jit(solution)/shard_map/ppermute | solution.py:394
  (2 other events, 6.8 us)

commit v7 on v6

--- a/solution.py
+++ b/solution.py
@@ -12,6 +12,7 @@
 ANY = pl.BlockSpec(memory_space=pl.ANY)
 NT = (((1,), (1,)), ((), ()))
 STEP = 16
+EARLY = 0.01
 
 
 def call(kernel, outs, scratch=(), us=1.0, specs=None, room=12, into=None):
@@ -142,6 +143,10 @@
             send[i, at : at + 8, :] = jnp.where(first, lines[rows - 1 - i], lines[i])
 
 
+def across(center):
+    return five_point(0.0, center, 0.0)
+
+
 def five_point(above, center, below):
     width = center.shape[1]
     lane = lax.broadcasted_iota(jnp.int32, center.shape, 1)
@@ -168,9 +173,7 @@
         buffer[row, :, cut] = total[:hubs].astype(BF16)
 
 
-def first_kernel(first_row, keep, got, *rest):
-    halos = rest[:2] if first_row == 0 else None
-    stiff, send_table, unused, bent, buffer = rest[-5:]
+def first_kernel(first_row, keep, got, stiff, send_table, unused, bent, buffer):
     side = core_side()
     count, pair, width = bent.shape
     own = keep.shape[1]
@@ -181,9 +184,7 @@
             cut = pl.ds(at, 8)
             far = pl.ds(group * own + at, 8)
             lines = [
-                jnp.where(side == group, halos[0][cut, :], halos[1][cut, :])
-                if row < 0
-                else jnp.where(side == group, keep[row, cut, :], got[row, cut, :])
+                jnp.where(side == group, keep[row, cut, :], got[row, cut, :])
                 for row in range(first_row - 1, first_row + count + 1)
             ]
             for row in range(count):
@@ -194,6 +195,36 @@
         lax.fori_loop(0, own // 8, chunk, 0, unroll=3)
     for row in range(count):
         fill_buffer(bent, stiff, send_table, buffer, row, row_place(first_row + row, stiff.shape[1]))
+
+
+def first_base_kernel(keep, got, unused, base):
+    side = core_side()
+    own = keep.shape[1]
+    for group in range(2):
+
+        def chunk(k, carry):
+            at = pl.multiple_of(k * 8, 8)
+            cut = pl.ds(at, 8)
+            here, below = [
+                jnp.where(side == group, keep[row, cut, :], got[row, cut, :]) for row in range(2)
+            ]
+            base[pl.ds(group * own + at, 8), :] = across(here) + below
+            return carry
+
+        lax.fori_loop(0, own // 8, chunk, 0, unroll=3)
+
+
+def first_outer_kernel(base, halo_near, halo_far, stiff, send_table, unused, bent, buffer):
+    first = core_side() == 0
+    own = halo_near.shape[0]
+    near, far = halo_near[...], halo_far[...]
+    halo = jnp.concatenate([jnp.where(first, near, far), jnp.where(first, far, near)], axis=0)
+    bent[0] = (base[...] + halo).astype(BF16)
+    fill_buffer(bent, stiff, send_table, buffer, 0, row_place(0, stiff.shape[1]))
+
+
+def pass_kernel(value, unused, out):
+    out[...] = value[...]
 
 
 def couple_kernel(first, outer_row, inner_rows, bent, got, stiff, table, unused, moment, *rest):
@@ -234,9 +265,13 @@
 
 
 def second_inner_kernel(
-    row_zero, row_one, others, inner, stiff, send_table, held, keep, send, bent, buffer
+    row_zero, row_one, others, inner, stiff, send_table,
+    held, base, ahead, keep, send, bent, buffer,
 ):
     count, pair, width = bent.shape
+    tile = lax.axis_index("tile")
+    last = lax.axis_size("tile") - 1
+    at_edge = jnp.where(core_side() == 0, tile == 0, tile == last)
 
     def chunk(k, carry):
         cut = pl.ds(pl.multiple_of(k * STEP, STEP), STEP)
@@ -249,39 +284,34 @@
                 held[row, cut, :], held[row + 1, cut, :], held[row + 2, cut, :]
             )
             bent[row, cut, :] = value.astype(BF16)
+        partial = across(lines[0]) + lines[1]
+        base[0, cut, :] = partial
+        outside = jnp.where(at_edge, 0.0, lines[0])
+        ahead[0, cut, :] = five_point(outside, partial, held[0, cut, :])
         return carry
 
     lax.fori_loop(0, pair // STEP, chunk, 0, unroll=3)
-    share(held, keep, send, (0, 1, 2), pair // 2)
     for row in range(count):
         fill_buffer(bent, stiff, send_table, buffer, row, row_place(row + 2, stiff.shape[1]))
-
-
-def second_edge_kernel(
-    row_zero, others, near, next_near, held, stiff, send_table, zero, keep, send, bent, buffer
-):
+    share(held, keep, send, (0, 1, 2), pair // 2)
+
+
+def second_edge_kernel(base, ahead, near, next_near, stiff, send_table, zero, bent, buffer):
     pair = bent.shape[1]
-    tile = lax.axis_index("tile")
-    last = lax.axis_size("tile") - 1
-    at_edge = jnp.where(core_side() == 0, tile == 0, tile == last)
 
     def chunk(k, carry):
         cut = pl.ds(pl.multiple_of(k * STEP, STEP), STEP)
         above = near[0, cut, :].astype(F32)
-        beyond = next_near[0, cut, :].astype(F32)
-        here = row_zero[0, cut, :]
-        outside = jnp.where(at_edge, 0.0, five_point(beyond, above, here))
-        value = five_point(above, here, others[0, cut, :])
-        zero[0, cut, :] = value
-        bent[0, cut, :] = five_point(outside, value, held[0, cut, :]).astype(BF16)
+        zero[0, cut, :] = base[0, cut, :] + above
+        value = ahead[0, cut, :] + next_near[0, cut, :].astype(F32) + 2.0 * across(above)
+        bent[0, cut, :] = value.astype(BF16)
         return carry
 
     lax.fori_loop(0, pair // STEP, chunk, 0, unroll=3)
     fill_buffer(bent, stiff, send_table, buffer, 0, row_place(0, stiff.shape[1]))
-    share(zero, keep, send, (0,), pair // 2)
-
-
-def second_next_kernel(zero, held, stiff, send_table, unused, bent, buffer):
+
+
+def second_next_kernel(zero, held, stiff, send_table, unused, keep, send, bent, buffer):
     pair = bent.shape[1]
 
     def chunk(k, carry):
@@ -292,6 +322,7 @@
 
     lax.fori_loop(0, pair // STEP, chunk, 0, unroll=3)
     fill_buffer(bent, stiff, send_table, buffer, 0, row_place(1, stiff.shape[1]))
+    share(zero, keep, send, (0,), pair // 2)
 
 
 def last_kernel(zero, one, inners, inner, keep, send):
@@ -454,14 +485,10 @@
     def outs(count):
         return (shape((count, own, width), F32),) * 2
 
-    def bend(first, count, after, *halo):
+    def bend(first, count, after):
         bent, buffer = call(
-            functools.partial(first_kernel, first),
-            bents(count),
-            (),
-            0.9 * count,
-            [VMEM] * (4 + len(halo)) + [ANY],
-        )(keep, got, *halo, stiffness, send_table, after)
+            functools.partial(first_kernel, first), bents(count), (), 0.9 * count, [VMEM] * 4 + [ANY]
+        )(keep, got, stiffness, send_table, after)
         return bent, buffer, by_chip(buffer)
 
     def couple(bent, other, first, outer_row, inner_rows, after, weight=1.0):
@@ -481,29 +508,37 @@
 
     bent_one, sent, cross_one = bend(1, 1, got)
     bent_in, sent, cross_in = bend(2, 2, sent)
-    bent_out, sent, cross_out = bend(0, 1, sent, halo_near, halo_far)
-    moment_one, edge_one = couple(bent_one, cross_one, 1, 1, (), sent)
+    base = call(first_base_kernel, shape((pair, width), F32), (), 0.4, [VMEM] * 2 + [ANY])(
+        keep, got, sent
+    )
+    moment_one, edge_one = couple(bent_one, cross_one, 1, 1, (), base)
+    bent_out, sent = call(first_outer_kernel, bents(1), (), 0.9, [VMEM] * 5 + [ANY])(
+        base, halo_near, halo_far, stiffness, send_table, edge_one
+    )
+    cross_out = by_chip(sent)
+    edge_one = call(pass_kernel, shape(edge_one.shape, BF16), (), 0.1, [VMEM, ANY])(edge_one, sent)
     next_near = by_tile(edge_one)
     moment_in, edge_in = couple(bent_in, cross_in, 2, None, (3, 2), edge_one)
     inner = by_core(edge_in)
     moment_out, edge_zero = couple(bent_out, cross_out, 0, 0, (), edge_in)
     near = by_tile(edge_zero)
 
-    held, keep_in, send_in, bent_in, buffer_in = call(
-        second_inner_kernel, (shape((4, pair, width), F32),) + outs(3) + bents(2), (), 3.5
+    row_shape = shape((1, pair, width), F32)
+    held, base, ahead, keep_in, send_in, bent_in, buffer_in = call(
+        second_inner_kernel,
+        (shape((4, pair, width), F32), row_shape, row_shape) + outs(3) + bents(2),
+        (),
+        3.5,
     )(moment_out, moment_one, moment_in, inner, stiffness, send_table)
     got_in = by_core(send_in)
     cross_in = by_chip(buffer_in)
-    zero, keep_out, send_out, bent_out, buffer_out = call(
-        second_edge_kernel,
-        (shape((1, pair, width), F32),) + outs(1) + bents(1),
-        (),
-        0.01,
-    )(moment_out, moment_one, near, next_near, held, stiffness, send_table)
+    zero, bent_out, buffer_out = call(second_edge_kernel, (row_shape,) + bents(1), (), EARLY)(
+        base, ahead, near, next_near, stiffness, send_table
+    )
     cross_out = by_chip(buffer_out)
-    bent_one, buffer_one = call(second_next_kernel, bents(1), (), 0.01, [VMEM] * 4 + [ANY])(
-        zero, held, stiffness, send_table, cross_in
-    )
+    keep_out, send_out, bent_one, buffer_one = call(
+        second_next_kernel, outs(1) + bents(1), (), EARLY, [VMEM] * 4 + [ANY]
+    )(zero, held, stiffness, send_table, cross_in)
     cross_one = by_chip(buffer_one)
     got_out = by_core(send_out)
     moment_out, edge_zero = couple(bent_out, cross_out, 0, 0, (), buffer_one)

time: 64.7 us -> 63.8 us (0.986)
  waiting for transfers between devices: 4.35 us -> 3.24 us
    pallas_call x3 -> x6, Pallas kernels: 6.18 us -> 7.55 us  [the longest x1 4.08 us: body(): call(second_inner_kernel, (shape((4, pair, width), F32), row_shape, row_s...]
    pallas_call x3 -> x2, Pallas kernels: 4.7 us -> 3.37 us  [bend(): call(functools.partial(first_kernel, first), bents(count), (), 0.9 * coun...]
    ppermute x6, waiting for transfers between devices: 2.58 us -> 1.47 us  [by_chip(): return lax.ppermute(value, 'chaos', chip_swap)]
    ppermute x6, starting transfers between devices: 6.46 us -> 7.46 us  [by_chip(): return lax.ppermute(value, 'chaos', chip_swap)]
    ppermute x8, starting transfers between devices: 19.4 us -> 18.6 us  [by_core(): return lax.ppermute(value, 'chaos', core_swap)]
  transfers between devices with their start and end apart: 19 -> 19, of which waited for: 5 -> 4; matrix products, arithmetic and copies ran while one was open for 0% -> 0% of each run, Pallas kernels for 39% -> 40%
where the time goes in v7:
time: 63.8 us; the launch traced here: 63.5 us
  starting transfers between devices  29.6 us (46%)
  Pallas kernels  29.2 us (46%)
  waiting for transfers between devices  3.24 us (5%)
  between operations  1.26 us (2%)
    ppermute x8, starting transfers between devices, by_core(): return lax.ppermute(value, 'chaos', core_swap)  18.6 us
    pallas_call x6, Pallas kernels, couple(): call(functools.partial(couple_kernel, first, outer_row, inner_rows), tupl...  8.46 us
    ppermute x6, starting transfers between devices, by_chip(): return lax.ppermute(value, 'chaos', chip_swap)  7.46 us
    pallas_call x1, Pallas kernels, body(): call(second_inner_kernel, (shape((4, pair, width), F32), row_shape, row_s...  4.08 us
    ppermute x5, starting transfers between devices, by_tile(): return lax.ppermute(value, ('chaos', 'tile'), tile_swap)  3.55 us
    pallas_call x2, Pallas kernels, bend(): call(functools.partial(first_kernel, first), bents(count), (), 0.9 * coun...  3.37 us
    pallas_call x1, Pallas kernels, body(): call(functools.partial(table_kernel, terms, pair, hubs, slot_total), (sha...  2.29 us
    pallas_call x1, Pallas kernels, body(): call(edge_kernel, (row_block, row_block), [pltpu.VMEM((2, own, width), F3...  2.13 us
  transfers between devices with their start and end apart: 19, of which 4 were waited for; matrix products, arithmetic and copies ran while one was open for 0% of the time, Pallas kernels for 40%

profile of v7, /device:TPU:0, one launch (start us, length us, event | category | flops | bytes accessed | tf_op | source)
XLA Modules:
  0.0 63.5 jit_solution(16040819571472655677)
XLA Ops:
  0.7 2.1 %shard_map.86 = (f32[72,1024]{1,0:T(8,128)}, f32[72,1024]{1,0:T(8,128)}) custom-call(f32[72,8,1024]{2,1,0:T(8,128)} %field.3), custom_call_target="tpu_custom_call" | custom-call | flops 20000000000 | bytes 10 | tf_op jit(solution)/shard_map/pallas_call | solution.py:451
  5.3 3.6 %collective-permute-start.1 = (f32[5,72,1024]{2,1,0:T(8,128)S(1)}, f32[5,72,1024]{2,1,0:T(8,128)S(1)}, u32[]{:S(2)}, u32[]{:S(2)}) collective-permute-start(f32[5,72,1024]{2,1,0:T(8,128)S(1)} %get-tuple-element.44), channel_id=1, source_target_pairs={{0,8},{8,0},{16,24},{24,16},{1,9},{9,1},{17,25},{25,17},{2,10},{10... | collective-permute-start | bytes 4423688 | tf_op jit(solution)/shard_map/ppermute | solution.py:425
  9.6 2.3 %shard_map.88 = (bf16[12,144,208]{2,1,0:T(8,128)(2,1)S(1)}, bf16[11,64,144]{2,1,0:T(8,128)(2,1)S(1)}) custom-call(f32[8,1664]{1,0:T(8,128)S(1)} %stack.31.entries, f32[72,1024]{1,0:T(8,128)S(1)} %collective-permute-done.unused), custom_call_target="tpu_custom_call" | custom-call | flops 30000001024 | bytes 10 | tf_op jit(solution)/shard_map/pallas_call | solution.py:463
  11.9 1.3 %shard_map.89 = (bf16[1,144,1024]{2,1,0:T(8,128)(2,1)S(1)}, bf16[1,56,1024]{2,1,0:T(8,128)(2,1)S(1)}) custom-call(f32[5,72,1024]{2,1,0:T(8,128)S(1)} %get-tuple-element.43.keep, f32[5,72,1024]{2,1,0:T(8,128)S(1)} %collective-permute-done.1.got.unused, f32[11,8,1024]{2,1,0:T(8,128)S(1)} %copy-done, bf16[11,64,144]{2,1,0:T(8,128)(2,1)S(1)} %get-tuple-element.45.send_table, ...), custom_call_target="tpu_custom_call" | custom-call | flops 8999999488 | bytes 10 | tf_op jit(solution)/shard_map/pallas_call | solution.py:489
  13.2 1.6 %collective-permute-start.4 = (bf16[1,56,1024]{2,1,0:T(8,128)(2,1)S(1)}, bf16[1,56,1024]{2,1,0:T(8,128)(2,1)S(1)}, u32[]{:S(2)}, u32[]{:S(2)}) collective-permute-start(bf16[1,56,1024]{2,1,0:T(8,128)(2,1)S(1)} %get-tuple-element.46.unused), channel_id=1, source_target_pairs={{0,16},{8,24},{16,0},{24,8},{1,17},{9,25},{17,1},{25,9},{2,18},{10... | collective-permute-start | bytes 344072 | tf_op jit(solution)/shard_map/ppermute | solution.py:428
  14.8 2.0 %shard_map.90 = (bf16[2,144,1024]{2,1,0:T(8,128)(2,1)S(1)}, bf16[2,56,1024]{2,1,0:T(8,128)(2,1)S(1)}) custom-call(f32[5,72,1024]{2,1,0:T(8,128)S(1)} %get-tuple-element.43.keep, f32[5,72,1024]{2,1,0:T(8,128)S(1)} %collective-permute-done.1.got.unused, f32[11,8,1024]{2,1,0:T(8,128)S(1)} %copy-done, bf16[11,64,144]{2,1,0:T(8,128)(2,1)S(1)} %get-tuple-element.45.send_table, ...), custom_call_target="tpu_custom_call" | custom-call | flops 17999998976 | bytes 10 | tf_op jit(solution)/shard_map/pallas_call | solution.py:489
  18.2 1.1 %shard_map.92 = (f32[1,144,1024]{2,1,0:T(8,128)S(1)}, bf16[1,144,1024]{2,1,0:T(8,128)(2,1)S(1)}) custom-call(bf16[1,144,1024]{2,1,0:T(8,128)(2,1)S(1)} %get-tuple-element.49.bent, bf16[1,56,1024]{2,1,0:T(8,128)(2,1)S(1)} %collective-permute-done.4.got, f32[11,8,1024]{2,1,0:T(8,128)S(1)} %copy-done, bf16[12,144,208]{2,1,0:T(8,128)(2,1)S(1)} %get-tuple-element.50.table, ...), custom_call_target="tpu_custom_call" | custom-call | flops 10000000000 | bytes 10 | tf_op jit(solution)/shard_map/pallas_call | solution.py:501
  19.9 1.6 %collective-permute-start.5 = (bf16[1,56,1024]{2,1,0:T(8,128)(2,1)S(1)}, bf16[1,56,1024]{2,1,0:T(8,128)(2,1)S(1)}, u32[]{:S(2)}, u32[]{:S(2)}) collective-permute-start(bf16[1,56,1024]{2,1,0:T(8,128)(2,1)S(1)} %get-tuple-element.53.unused), channel_id=1, source_target_pairs={{0,16},{8,24},{16,0},{24,8},{1,17},{9,25},{17,1},{25,9},{2,18},{10... | collective-permute-start | bytes 344072 | tf_op jit(solution)/shard_map/ppermute | solution.py:428
  22.2 1.5 %collective-permute-done.6.got = bf16[2,56,1024]{2,1,0:T(8,128)(2,1)S(1)} collective-permute-done((bf16[2,56,1024]{2,1,0:T(8,128)(2,1)S(1)}, bf16[2,56,1024]{2,1,0:T(8,128)(2,1)S(1)}, u32[]{:S(2)}, u32[]{:S(2)}) %collective-permute-start.6) | collective-permute-done | bytes 229408 | tf_op jit(solution)/shard_map/ppermute | solution.py:428
  23.6 2.0 %shard_map.95 = (f32[2,144,1024]{2,1,0:T(8,128)S(1)}, bf16[2,144,1024]{2,1,0:T(8,128)(2,1)S(1)}) custom-call(bf16[2,144,1024]{2,1,0:T(8,128)(2,1)S(1)} %get-tuple-element.54.bent, bf16[2,56,1024]{2,1,0:T(8,128)(2,1)S(1)} %collective-permute-done.6.got, f32[11,8,1024]{2,1,0:T(8,128)S(1)} %copy-done, bf16[12,144,208]{2,1,0:T(8,128)(2,1)S(1)} %get-tuple-element.50.table, ...), custom_call_target="tpu_custom_call" | custom-call | flops 20000000000 | bytes 10 | tf_op jit(solution)/shard_map/pallas_call | solution.py:501
  25.7 4.3 %collective-permute-start.7 = (bf16[2,144,1024]{2,1,0:T(8,128)(2,1)S(1)}, bf16[2,144,1024]{2,1,0:T(8,128)(2,1)S(1)}, u32[]{:S(2)}, u32[]{:S(2)}) collective-permute-start(bf16[2,144,1024]{2,1,0:T(8,128)(2,1)S(1)} %get-tuple-element.55.unused), channel_id=1, source_target_pairs={{0,8},{8,0},{16,24},{24,16},{1,9},{9,1},{17,25},{25,17},{2,10},{10... | collective-permute-start | bytes 1769480 | tf_op jit(solution)/shard_map/ppermute | solution.py:425
  30.0 1.1 %shard_map.96 = (f32[1,144,1024]{2,1,0:T(8,128)S(1)}, bf16[1,144,1024]{2,1,0:T(8,128)(2,1)S(1)}) custom-call(bf16[1,144,1024]{2,1,0:T(8,128)(2,1)S(1)} %get-tuple-element.52.bent, bf16[1,56,1024]{2,1,0:T(8,128)(2,1)S(1)} %collective-permute-done.5.got, f32[11,8,1024]{2,1,0:T(8,128)S(1)} %copy-done, bf16[12,144,208]{2,1,0:T(8,128)(2,1)S(1)} %get-tuple-element.50.table, ...), custom_call_target="tpu_custom_call" | custom-call | flops 10000000000 | bytes 10 | tf_op jit(solution)/shard_map/pallas_call | solution.py:501
  32.0 4.1 %shard_map.97 = (f32[4,144,1024]{2,1,0:T(8,128)S(1)}, f32[1,144,1024]{2,1,0:T(8,128)S(1)}, f32[1,144,1024]{2,1,0:T(8,128)S(1)}, f32[3,72,1024]{2,1,0:T(8,128)S(1...) custom-call(f32[1,144,1024]{2,1,0:T(8,128)S(1)} %get-tuple-element.56.row_zero, ...), custom_call_target="tpu_custom_call" | custom-call | flops 35000000512 | bytes 10 | tf_op jit(solution)/shard_map/pallas_call | solution.py:527
  37.7 1.5 %collective-permute-start.13 = (bf16[1,56,1024]{2,1,0:T(8,128)(2,1)S(1)}, bf16[1,56,1024]{2,1,0:T(8,128)(2,1)S(1)}, u32[]{:S(2)}, u32[]{:S(2)}) collective-permute-start(bf16[1,56,1024]{2,1,0:T(8,128)(2,1)S(1)} %get-tuple-element.70), channel_id=1, source_target_pairs={{0,16},{8,24},{16,0},{24,8},{1,17},{9,25},{17,1},{25,9},{2,18},{10... | collective-permute-start | bytes 344072 | tf_op jit(solution)/shard_map/ppermute | solution.py:428
  39.2 3.8 %collective-permute-start.12 = (f32[3,72,1024]{2,1,0:T(8,128)S(1)}, f32[3,72,1024]{2,1,0:T(8,128)S(1)}, u32[]{:S(2)}, u32[]{:S(2)}) collective-permute-start(f32[3,72,1024]{2,1,0:T(8,128)S(1)} %get-tuple-element.68), channel_id=1, source_target_pairs={{0,8},{8,0},{16,24},{24,16},{1,9},{9,1},{17,25},{25,17},{2,10},{10... | collective-permute-start | bytes 2654216 | tf_op jit(solution)/shard_map/ppermute | solution.py:425
  44.1 1.6 %collective-permute-start.14 = (bf16[1,56,1024]{2,1,0:T(8,128)(2,1)S(1)}, bf16[1,56,1024]{2,1,0:T(8,128)(2,1)S(1)}, u32[]{:S(2)}, u32[]{:S(2)}) collective-permute-start(bf16[1,56,1024]{2,1,0:T(8,128)(2,1)S(1)} %get-tuple-element.71.unused), channel_id=1, source_target_pairs={{0,16},{8,24},{16,0},{24,8},{1,17},{9,25},{17,1},{25,9},{2,18},{10... | collective-permute-start | bytes 344072 | tf_op jit(solution)/shard_map/ppermute | solution.py:428
  45.7 1.4 %collective-permute-start.11 = (f32[1,72,1024]{2,1,0:T(8,128)S(1)}, f32[1,72,1024]{2,1,0:T(8,128)S(1)}, u32[]{:S(2)}, u32[]{:S(2)}) collective-permute-start(f32[1,72,1024]{2,1,0:T(8,128)S(1)} %get-tuple-element.67), channel_id=1, source_target_pairs={{0,8},{8,0},{16,24},{24,16},{1,9},{9,1},{17,25},{25,17},{2,10},{10... | collective-permute-start | bytes 884744 | tf_op jit(solution)/shard_map/ppermute | solution.py:425
  48.9 2.0 %shard_map.102 = (f32[2,144,1024]{2,1,0:T(8,128)S(1)}, bf16[1,144,1024]{2,1,0:T(8,128)(2,1)S(1)}) custom-call(bf16[2,144,1024]{2,1,0:T(8,128)(2,1)S(1)} %get-tuple-element.75.bent, bf16[2,56,1024]{2,1,0:T(8,128)(2,1)S(1)} %collective-permute-done.10.unused.got, f32[11,8,1024]{2,1,0:T(8,128)S(1)} %copy-done, ...), custom_call_target="tpu_custom_call" | custom-call | flops 20000000000 | bytes 10 | tf_op jit(solution)/shard_map/pallas_call | solution.py:501
  50.9 4.4 %collective-permute-start.15 = (bf16[1,144,1024]{2,1,0:T(8,128)(2,1)S(1)}, bf16[1,144,1024]{2,1,0:T(8,128)(2,1)S(1)}, u32[]{:S(2)}, u32[]{:S(2)}) collective-permute-start(bf16[1,144,1024]{2,1,0:T(8,128)(2,1)S(1)} %get-tuple-element.77), channel_id=1, source_target_pairs={{0,8},{8,0},{16,24},{24,16},{1,9},{9,1},{17,25},{25,17},{2,10},{10... | collective-permute-start | bytes 884744 | tf_op jit(solution)/shard_map/ppermute | solution.py:425
  55.3 1.1 %shard_map.101.one = f32[1,144,1024]{2,1,0:T(8,128)S(1)} custom-call(bf16[1,144,1024]{2,1,0:T(8,128)(2,1)S(1)} %get-tuple-element.73.bent, bf16[1,56,1024]{2,1,0:T(8,128)(2,1)S(1)} %collective-permute-done.14.got, f32[11,8,1024]{2,1,0:T(8,128)S(1)} %copy-done, bf16[12,144,208]{2,1,0:T(8,128)(2,1)S(1)} %get-tuple-element.50.table, ...), custom_call_target="tpu_custom_call" | custom-call | flops 10000000000 | bytes 10 | tf_op jit(solution)/shard_map/pallas_call | solution.py:501
  56.5 1.6 %shard_map.103 = (f32[4,72,1024]{2,1,0:T(8,128)S(1)}, f32[4,72,1024]{2,1,0:T(8,128)S(1)}) custom-call(f32[1,144,1024]{2,1,0:T(8,128)S(1)} %get-tuple-element.72.zero, f32[1,144,1024]{2,1,0:T(8,128)S(1)} %shard_map.101.one, f32[2,144,1024]{2,1,0:T(8,128)S(1)} %get-tuple-element.76.inners, bf16[1,144,1024]{2,1,0:T(8,128)(2,1)S(1)} %collective-permute-done.15.inner), custom_call_target="tpu_custom_call" | custom-call | flops 24999999488 | bytes 10 | tf_op jit(solution)/shard_map/pallas_call | solution.py:550
  58.6 1.6 %shard_map.104 = (f32[72,8,1024]{2,1,0:T(8,128)}, s32[8,128]{1,0:T(8,128)S(1)}) custom-call(f32[1,72,1024]{2,1,0:T(8,128)S(1)} %get-tuple-element.65.keep_zero, f32[3,72,1024]{2,1,0:T(8,128)S(1)} %get-tuple-element.66.keep, f32[1,72,1024]{2,1,0:T(8,128)S(1)} %collective-permute-done.11.got_zero, f32[3,72,1024]{2,1,0:T(8,128)S(1)} %collective-permute-done.12.got, ...), custom_call_target="tpu_custom_call" | custom-call | flops 19000000512 | bytes 10 | tf_op jit(solution)/shard_map/pallas_call | solution.py:556
  60.5 1.2 %collective-permute-done.18.far_halo = bf16[72,1024]{1,0:T(8,128)(2,1)S(1)} collective-permute-done((bf16[72,1024]{1,0:T(8,128)(2,1)S(1)}, bf16[72,1024]{1,0:T(8,128)(2,1)S(1)}, u32[]{:S(2)}, u32[]{:S(2)}) %collective-permute-start.18) | collective-permute-done | bytes 147488 | tf_op jit(solution)/shard_map/ppermute | solution.py:425
  61.7 1.6 %shard_map.106 = f32[72,8,1024]{2,1,0:T(8,128)} custom-call(f32[4,72,1024]{2,1,0:T(8,128)S(1)} %get-tuple-element.78.unused.keep, f32[4,72,1024]{2,1,0:T(8,128)S(1)} %collective-permute-done.16.got, bf16[1,144,1024]{2,1,0:T(8,128)(2,1)S(1)} %collective-permute-done.17.halo, bf16[72,1024]{1,0:T(8,128)(2,1)S(1)} %collective-permute-done.18.far_halo), custom_call_target="tpu_custom_call" | custom-call | flops 19000000512 | bytes 10 | tf_op jit(solution)/shard_map/pallas_call | solution.py:562
  (66 shorter events, 11.8 us)
Async XLA Ops:
  0.6 4.1 %copy-start.1 = (f32[72,8,1024]{2,1,0:T(8,128)S(1)}, f32[72,8,1024]{2,1,0:T(8,128)}, u32[]{:S(2)}) copy-start(f32[72,8,1024]{2,1,0:T(8,128)} %field.3) | copy-start | bytes 7077892
  0.7 3.5 %copy-start.3 = (s32[1606]{0:T(1024)S(1)}, s32[1606]{0:T(1024)}, u32[]{:S(2)}) copy-start(s32[1606]{0:T(1024)} %param.10) | copy-start | bytes 19276
  0.7 3.5 %copy-start.4 = (s32[1606]{0:T(1024)S(1)}, s32[1606]{0:T(1024)}, u32[]{:S(2)}) copy-start(s32[1606]{0:T(1024)} %param.11) | copy-start | bytes 19276
  0.7 3.5 %copy-start.5 = (bf16[1606]{0:T(1024)(128)(2,1)S(1)}, bf16[1606]{0:T(1024)(128)(2,1)}, u32[]{:S(2)}) copy-start(bf16[1606]{0:T(1024)(128)(2,1)} %param.12) | copy-start | bytes 9640
  2.8 1.9 %collective-permute-start = (f32[72,1024]{1,0:T(8,128)}, f32[72,1024]{1,0:T(8,128)S(1)}, u32[]{:S(2)}, u32[]{:S(2)}) collective-permute-start(f32[72,1024]{1,0:T(8,128)} %get-tuple-element.42), channel_id=1, source_target_pairs={{0,8},{8,0},{16,24},{24,16},{1,9},{9,1},{17,25},{25,17},{2,10},{10... | collective-permute-start | bytes 884744 | tf_op jit(solution)/shard_map/ppermute | solution.py:425
  3.3 15.9 %collective-permute-start.3 = (f32[72,1024]{1,0:T(8,128)}, f32[72,1024]{1,0:T(8,128)S(1)}, u32[]{:S(2)}, u32[]{:S(2)}) collective-permute-start(f32[72,1024]{1,0:T(8,128)} %get-tuple-element.48), channel_id=1, source_target_pairs={{8,1},{1,8},{9,2},{2,9},{10,3},{3,10},{11,4},{4,11},{12,5},{5,12},... | collective-permute-start | bytes 884744 | tf_op jit(solution)/shard_map/ppermute | solution.py:431
  5.3 6.6 %copy-start = (f32[11,8,1024]{2,1,0:T(8,128)S(1)}, f32[11,8,1024]{2,1,0:T(8,128)}, u32[]{:S(2)}) copy-start(f32[11,8,1024]{2,1,0:T(8,128)} %stiff.23) | copy-start | bytes 1081348
  5.3 6.5 %collective-permute-start.1 = (f32[5,72,1024]{2,1,0:T(8,128)S(1)}, f32[5,72,1024]{2,1,0:T(8,128)S(1)}, u32[]{:S(2)}, u32[]{:S(2)}) collective-permute-start(f32[5,72,1024]{2,1,0:T(8,128)S(1)} %get-tuple-element.44), channel_id=1, source_target_pairs={{0,8},{8,0},{16,24},{24,16},{1,9},{9,1},{17,25},{25,17},{2,10},{10... | collective-permute-start | bytes 4423688 | tf_op jit(solution)/shard_map/ppermute | solution.py:425
  8.9 10.4 %collective-permute-start.2 = (f32[72,1024]{1,0:T(8,128)S(1)}, f32[72,1024]{1,0:T(8,128)S(1)}, u32[]{:S(2)}, u32[]{:S(2)}) collective-permute-start(f32[72,1024]{1,0:T(8,128)S(1)} %collective-permute-done.unused), channel_id=1, source_target_pairs={{8,1},{1,8},{9,2},{2,9},{10,3},{3,10},{11,4},{4,11},{12,5},{5,12},... | collective-permute-start | bytes 884744 | tf_op jit(solution)/shard_map/ppermute | solution.py:431
  13.2 5.0 %collective-permute-start.4 = (bf16[1,56,1024]{2,1,0:T(8,128)(2,1)S(1)}, bf16[1,56,1024]{2,1,0:T(8,128)(2,1)S(1)}, u32[]{:S(2)}, u32[]{:S(2)}) collective-permute-start(bf16[1,56,1024]{2,1,0:T(8,128)(2,1)S(1)} %get-tuple-element.46.unused), channel_id=1, source_target_pairs={{0,16},{8,24},{16,0},{24,8},{1,17},{9,25},{17,1},{25,9},{2,18},{10... | collective-permute-start | bytes 344072 | tf_op jit(solution)/shard_map/ppermute | solution.py:428
  16.8 6.8 %collective-permute-start.6 = (bf16[2,56,1024]{2,1,0:T(8,128)(2,1)S(1)}, bf16[2,56,1024]{2,1,0:T(8,128)(2,1)S(1)}, u32[]{:S(2)}, u32[]{:S(2)}) collective-permute-start(bf16[2,56,1024]{2,1,0:T(8,128)(2,1)S(1)} %get-tuple-element.47.unused), channel_id=1, source_target_pairs={{0,16},{8,24},{16,0},{24,8},{1,17},{9,25},{17,1},{25,9},{2,18},{10... | collective-permute-start | bytes 688136 | tf_op jit(solution)/shard_map/ppermute | solution.py:428
  19.9 10.1 %collective-permute-start.5 = (bf16[1,56,1024]{2,1,0:T(8,128)(2,1)S(1)}, bf16[1,56,1024]{2,1,0:T(8,128)(2,1)S(1)}, u32[]{:S(2)}, u32[]{:S(2)}) collective-permute-start(bf16[1,56,1024]{2,1,0:T(8,128)(2,1)S(1)} %get-tuple-element.53.unused), channel_id=1, source_target_pairs={{0,16},{8,24},{16,0},{24,8},{1,17},{9,25},{17,1},{25,9},{2,18},{10... | collective-permute-start | bytes 344072 | tf_op jit(solution)/shard_map/ppermute | solution.py:428
  21.5 15.2 %collective-permute-start.9 = (bf16[1,144,1024]{2,1,0:T(8,128)(2,1)S(1)}, bf16[1,144,1024]{2,1,0:T(8,128)(2,1)S(1)}, u32[]{:S(2)}, u32[]{:S(2)}) collective-permute-start(bf16[1,144,1024]{2,1,0:T(8,128)(2,1)S(1)} %shard_map.94.unused), channel_id=1, source_target_pairs={{8,1},{1,8},{9,2},{2,9},{10,3},{3,10},{11,4},{4,11},{12,5},{5,12},... | collective-permute-start | bytes 884744 | tf_op jit(solution)/shard_map/ppermute | solution.py:431
  25.7 6.3 %collective-permute-start.7 = (bf16[2,144,1024]{2,1,0:T(8,128)(2,1)S(1)}, bf16[2,144,1024]{2,1,0:T(8,128)(2,1)S(1)}, u32[]{:S(2)}, u32[]{:S(2)}) collective-permute-start(bf16[2,144,1024]{2,1,0:T(8,128)(2,1)S(1)} %get-tuple-element.55.unused), channel_id=1, source_target_pairs={{0,8},{8,0},{16,24},{24,16},{1,9},{9,1},{17,25},{25,17},{2,10},{10... | collective-permute-start | bytes 1769480 | tf_op jit(solution)/shard_map/ppermute | solution.py:425
  31.1 5.6 %collective-permute-start.8 = (bf16[1,144,1024]{2,1,0:T(8,128)(2,1)S(1)}, bf16[1,144,1024]{2,1,0:T(8,128)(2,1)S(1)}, u32[]{:S(2)}, u32[]{:S(2)}) collective-permute-start(bf16[1,144,1024]{2,1,0:T(8,128)(2,1)S(1)} %get-tuple-element.61), channel_id=1, source_target_pairs={{8,1},{1,8},{9,2},{2,9},{10,3},{3,10},{11,4},{4,11},{12,5},{5,12},... | collective-permute-start | bytes 884744 | tf_op jit(solution)/shard_map/ppermute | solution.py:431
  36.0 7.0 %collective-permute-start.10 = (bf16[2,56,1024]{2,1,0:T(8,128)(2,1)S(1)}, bf16[2,56,1024]{2,1,0:T(8,128)(2,1)S(1)}, u32[]{:S(2)}, u32[]{:S(2)}) collective-permute-start(bf16[2,56,1024]{2,1,0:T(8,128)(2,1)S(1)} %get-tuple-element.64), channel_id=1, source_target_pairs={{0,16},{8,24},{16,0},{24,8},{1,17},{9,25},{17,1},{25,9},{2,18},{10... | collective-permute-start | bytes 688136 | tf_op jit(solution)/shard_map/ppermute | solution.py:428
  37.7 9.4 %collective-permute-start.13 = (bf16[1,56,1024]{2,1,0:T(8,128)(2,1)S(1)}, bf16[1,56,1024]{2,1,0:T(8,128)(2,1)S(1)}, u32[]{:S(2)}, u32[]{:S(2)}) collective-permute-start(bf16[1,56,1024]{2,1,0:T(8,128)(2,1)S(1)} %get-tuple-element.70), channel_id=1, source_target_pairs={{0,16},{8,24},{16,0},{24,8},{1,17},{9,25},{17,1},{25,9},{2,18},{10... | collective-permute-start | bytes 344072 | tf_op jit(solution)/shard_map/ppermute | solution.py:428
  39.2 19.4 %collective-permute-start.12 = (f32[3,72,1024]{2,1,0:T(8,128)S(1)}, f32[3,72,1024]{2,1,0:T(8,128)S(1)}, u32[]{:S(2)}, u32[]{:S(2)}) collective-permute-start(f32[3,72,1024]{2,1,0:T(8,128)S(1)} %get-tuple-element.68), channel_id=1, source_target_pairs={{0,8},{8,0},{16,24},{24,16},{1,9},{9,1},{17,25},{25,17},{2,10},{10... | collective-permute-start | bytes 2654216 | tf_op jit(solution)/shard_map/ppermute | solution.py:425
  44.1 11.2 %collective-permute-start.14 = (bf16[1,56,1024]{2,1,0:T(8,128)(2,1)S(1)}, bf16[1,56,1024]{2,1,0:T(8,128)(2,1)S(1)}, u32[]{:S(2)}, u32[]{:S(2)}) collective-permute-start(bf16[1,56,1024]{2,1,0:T(8,128)(2,1)S(1)} %get-tuple-element.71.unused), channel_id=1, source_target_pairs={{0,16},{8,24},{16,0},{24,8},{1,17},{9,25},{17,1},{25,9},{2,18},{10... | collective-permute-start | bytes 344072 | tf_op jit(solution)/shard_map/ppermute | solution.py:428
  45.7 12.9 %collective-permute-start.11 = (f32[1,72,1024]{2,1,0:T(8,128)S(1)}, f32[1,72,1024]{2,1,0:T(8,128)S(1)}, u32[]{:S(2)}, u32[]{:S(2)}) collective-permute-start(f32[1,72,1024]{2,1,0:T(8,128)S(1)} %get-tuple-element.67), channel_id=1, source_target_pairs={{0,8},{8,0},{16,24},{24,16},{1,9},{9,1},{17,25},{25,17},{2,10},{10... | collective-permute-start | bytes 884744 | tf_op jit(solution)/shard_map/ppermute | solution.py:425
  48.2 12.0 %collective-permute-start.17 = (bf16[1,144,1024]{2,1,0:T(8,128)(2,1)S(1)}, bf16[1,144,1024]{2,1,0:T(8,128)(2,1)S(1)}, u32[]{:S(2)}, u32[]{:S(2)}) collective-permute-start(bf16[1,144,1024]{2,1,0:T(8,128)(2,1)S(1)} %get-tuple-element.74.unused), channel_id=1, source_target_pairs={{8,1},{1,8},{9,2},{2,9},{10,3},{3,10},{11,4},{4,11},{12,5},{5,12},... | collective-permute-start | bytes 884744 | tf_op jit(solution)/shard_map/ppermute | solution.py:431
  50.9 5.6 %collective-permute-start.15 = (bf16[1,144,1024]{2,1,0:T(8,128)(2,1)S(1)}, bf16[1,144,1024]{2,1,0:T(8,128)(2,1)S(1)}, u32[]{:S(2)}, u32[]{:S(2)}) collective-permute-start(bf16[1,144,1024]{2,1,0:T(8,128)(2,1)S(1)} %get-tuple-element.77), channel_id=1, source_target_pairs={{0,8},{8,0},{16,24},{24,16},{1,9},{9,1},{17,25},{25,17},{2,10},{10... | collective-permute-start | bytes 884744 | tf_op jit(solution)/shard_map/ppermute | solution.py:425
  58.2 3.6 %collective-permute-start.16 = (f32[4,72,1024]{2,1,0:T(8,128)S(1)}, f32[4,72,1024]{2,1,0:T(8,128)S(1)}, u32[]{:S(2)}, u32[]{:S(2)}) collective-permute-start(f32[4,72,1024]{2,1,0:T(8,128)S(1)} %get-tuple-element.80), channel_id=1, source_target_pairs={{0,8},{8,0},{16,24},{24,16},{1,9},{9,1},{17,25},{25,17},{2,10},{10... | collective-permute-start | bytes 3538952 | tf_op jit(solution)/shard_map/ppermute | solution.py:425
  60.3 1.4 %collective-permute-start.18 = (bf16[72,1024]{1,0:T(8,128)(2,1)S(1)}, bf16[72,1024]{1,0:T(8,128)(2,1)S(1)}, u32[]{:S(2)}, u32[]{:S(2)}) collective-permute-start(bf16[72,1024]{1,0:T(8,128)(2,1)S(1)} %shard_map.105), channel_id=1, source_target_pairs={{0,8},{8,0},{16,24},{24,16},{1,9},{9,1},{17,25},{25,17},{2,10},{10... | collective-permute-start | bytes 442376 | tf_op jit(solution)/shard_map/ppermute | solution.py:425
  (2 other events, 6.8 us)

commit v8 on v7

--- a/solution.py
+++ b/solution.py
@@ -264,14 +264,8 @@
         send[target] = held[row, pl.ds(far, own), :]
 
 
-def second_inner_kernel(
-    row_zero, row_one, others, inner, stiff, send_table,
-    held, base, ahead, keep, send, bent, buffer,
-):
+def second_inner_kernel(row_zero, row_one, others, inner, stiff, send_table, held, bent, buffer):
     count, pair, width = bent.shape
-    tile = lax.axis_index("tile")
-    last = lax.axis_size("tile") - 1
-    at_edge = jnp.where(core_side() == 0, tile == 0, tile == last)
 
     def chunk(k, carry):
         cut = pl.ds(pl.multiple_of(k * STEP, STEP), STEP)
@@ -284,15 +278,29 @@
                 held[row, cut, :], held[row + 1, cut, :], held[row + 2, cut, :]
             )
             bent[row, cut, :] = value.astype(BF16)
-        partial = across(lines[0]) + lines[1]
-        base[0, cut, :] = partial
-        outside = jnp.where(at_edge, 0.0, lines[0])
-        ahead[0, cut, :] = five_point(outside, partial, held[0, cut, :])
         return carry
 
     lax.fori_loop(0, pair // STEP, chunk, 0, unroll=3)
     for row in range(count):
         fill_buffer(bent, stiff, send_table, buffer, row, row_place(row + 2, stiff.shape[1]))
+
+
+def second_base_kernel(row_zero, row_one, held, base, ahead, keep, send):
+    pair = row_zero.shape[1]
+    tile = lax.axis_index("tile")
+    last = lax.axis_size("tile") - 1
+    at_edge = jnp.where(core_side() == 0, tile == 0, tile == last)
+
+    def chunk(k, carry):
+        cut = pl.ds(pl.multiple_of(k * STEP, STEP), STEP)
+        here = row_zero[0, cut, :]
+        partial = across(here) + row_one[0, cut, :]
+        base[0, cut, :] = partial
+        outside = jnp.where(at_edge, 0.0, here)
+        ahead[0, cut, :] = five_point(outside, partial, held[0, cut, :])
+        return carry
+
+    lax.fori_loop(0, pair // STEP, chunk, 0, unroll=3)
     share(held, keep, send, (0, 1, 2), pair // 2)
 
 
@@ -524,12 +532,12 @@
     near = by_tile(edge_zero)
 
     row_shape = shape((1, pair, width), F32)
-    held, base, ahead, keep_in, send_in, bent_in, buffer_in = call(
-        second_inner_kernel,
-        (shape((4, pair, width), F32), row_shape, row_shape) + outs(3) + bents(2),
-        (),
-        3.5,
+    held, bent_in, buffer_in = call(
+        second_inner_kernel, (shape((4, pair, width), F32),) + bents(2), (), 2.7
     )(moment_out, moment_one, moment_in, inner, stiffness, send_table)
+    base, ahead, keep_in, send_in = call(
+        second_base_kernel, (row_shape, row_shape) + outs(3), (), 3.0
+    )(moment_out, moment_one, held)
     got_in = by_core(send_in)
     cross_in = by_chip(buffer_in)
     zero, bent_out, buffer_out = call(second_edge_kernel, (row_shape,) + bents(1), (), EARLY)(

time: 63.8 us -> 63.6 us (level)
    pallas_call x1 -> x2, Pallas kernels: 4.08 us -> 4.41 us  [the longest x1 3 us: body(): call(second_inner_kernel, (shape((4, pair, width), F32),) + bents(2), (),...]
  transfers between devices with their start and end apart: 19 -> 19, of which waited for: 4 -> 4; matrix products, arithmetic and copies ran while one was open for 0% -> 0% of each run, Pallas kernels for 40% -> 41%
where the time goes in v8:
time: 63.6 us; the launch traced here: 63.4 us
  Pallas kernels  29.6 us (47%)
  starting transfers between devices  29 us (46%)
  waiting for transfers between devices  3.27 us (5%)
  between operations  1.28 us (2%)
    ppermute x8, starting transfers between devices, by_core(): return lax.ppermute(value, 'chaos', core_swap)  18.1 us
    pallas_call x6, Pallas kernels, couple(): call(functools.partial(couple_kernel, first, outer_row, inner_rows), tupl...  8.46 us
    ppermute x6, starting transfers between devices, by_chip(): return lax.ppermute(value, 'chaos', chip_swap)  7.43 us
    ppermute x5, starting transfers between devices, by_tile(): return lax.ppermute(value, ('chaos', 'tile'), tile_swap)  3.55 us
    pallas_call x2, Pallas kernels, bend(): call(functools.partial(first_kernel, first), bents(count), (), 0.9 * coun...  3.37 us
    pallas_call x1, Pallas kernels, body(): call(second_inner_kernel, (shape((4, pair, width), F32),) + bents(2), (),...  3 us
    pallas_call x1, Pallas kernels, body(): call(functools.partial(table_kernel, terms, pair, hubs, slot_total), (sha...  2.29 us
    pallas_call x1, Pallas kernels, body(): call(edge_kernel, (row_block, row_block), [pltpu.VMEM((2, own, width), F3...  2.13 us
  transfers between devices with their start and end apart: 19, of which 4 were waited for; matrix products, arithmetic and copies ran while one was open for 0% of the time, Pallas kernels for 41%

profile of v8, /device:TPU:0, one launch (start us, length us, event | category | flops | bytes accessed | tf_op | source)
XLA Modules:
  0.0 63.4 jit_solution(8979657553799883690)
XLA Ops:
  0.7 2.1 %shard_map.86 = (f32[72,1024]{1,0:T(8,128)}, f32[72,1024]{1,0:T(8,128)}) custom-call(f32[72,8,1024]{2,1,0:T(8,128)} %field.3), custom_call_target="tpu_custom_call" | custom-call | flops 20000000000 | bytes 10 | tf_op jit(solution)/shard_map/pallas_call | solution.py:459
  5.3 3.6 %collective-permute-start.1 = (f32[5,72,1024]{2,1,0:T(8,128)S(1)}, f32[5,72,1024]{2,1,0:T(8,128)S(1)}, u32[]{:S(2)}, u32[]{:S(2)}) collective-permute-start(f32[5,72,1024]{2,1,0:T(8,128)S(1)} %get-tuple-element.44), channel_id=1, source_target_pairs={{0,8},{8,0},{16,24},{24,16},{1,9},{9,1},{17,25},{25,17},{2,10},{10... | collective-permute-start | bytes 4423688 | tf_op jit(solution)/shard_map/ppermute | solution.py:433
  9.6 2.3 %shard_map.88 = (bf16[12,144,208]{2,1,0:T(8,128)(2,1)S(1)}, bf16[11,64,144]{2,1,0:T(8,128)(2,1)S(1)}) custom-call(f32[8,1664]{1,0:T(8,128)S(1)} %stack.31.entries, f32[72,1024]{1,0:T(8,128)S(1)} %collective-permute-done.unused), custom_call_target="tpu_custom_call" | custom-call | flops 30000001024 | bytes 10 | tf_op jit(solution)/shard_map/pallas_call | solution.py:471
  11.9 1.3 %shard_map.89 = (bf16[1,144,1024]{2,1,0:T(8,128)(2,1)S(1)}, bf16[1,56,1024]{2,1,0:T(8,128)(2,1)S(1)}) custom-call(f32[5,72,1024]{2,1,0:T(8,128)S(1)} %get-tuple-element.43.keep, f32[5,72,1024]{2,1,0:T(8,128)S(1)} %collective-permute-done.1.got.unused, f32[11,8,1024]{2,1,0:T(8,128)S(1)} %copy-done, bf16[11,64,144]{2,1,0:T(8,128)(2,1)S(1)} %get-tuple-element.45.send_table, ...), custom_call_target="tpu_custom_call" | custom-call | flops 8999999488 | bytes 10 | tf_op jit(solution)/shard_map/pallas_call | solution.py:497
  13.2 1.6 %collective-permute-start.4 = (bf16[1,56,1024]{2,1,0:T(8,128)(2,1)S(1)}, bf16[1,56,1024]{2,1,0:T(8,128)(2,1)S(1)}, u32[]{:S(2)}, u32[]{:S(2)}) collective-permute-start(bf16[1,56,1024]{2,1,0:T(8,128)(2,1)S(1)} %get-tuple-element.46.unused), channel_id=1, source_target_pairs={{0,16},{8,24},{16,0},{24,8},{1,17},{9,25},{17,1},{25,9},{2,18},{10... | collective-permute-start | bytes 344072 | tf_op jit(solution)/shard_map/ppermute | solution.py:436
  14.8 2.0 %shard_map.90 = (bf16[2,144,1024]{2,1,0:T(8,128)(2,1)S(1)}, bf16[2,56,1024]{2,1,0:T(8,128)(2,1)S(1)}) custom-call(f32[5,72,1024]{2,1,0:T(8,128)S(1)} %get-tuple-element.43.keep, f32[5,72,1024]{2,1,0:T(8,128)S(1)} %collective-permute-done.1.got.unused, f32[11,8,1024]{2,1,0:T(8,128)S(1)} %copy-done, bf16[11,64,144]{2,1,0:T(8,128)(2,1)S(1)} %get-tuple-element.45.send_table, ...), custom_call_target="tpu_custom_call" | custom-call | flops 17999998976 | bytes 10 | tf_op jit(solution)/shard_map/pallas_call | solution.py:497
  18.2 1.1 %shard_map.92 = (f32[1,144,1024]{2,1,0:T(8,128)S(1)}, bf16[1,144,1024]{2,1,0:T(8,128)(2,1)S(1)}) custom-call(bf16[1,144,1024]{2,1,0:T(8,128)(2,1)S(1)} %get-tuple-element.49.bent, bf16[1,56,1024]{2,1,0:T(8,128)(2,1)S(1)} %collective-permute-done.4.got, f32[11,8,1024]{2,1,0:T(8,128)S(1)} %copy-done, bf16[12,144,208]{2,1,0:T(8,128)(2,1)S(1)} %get-tuple-element.50.table, ...), custom_call_target="tpu_custom_call" | custom-call | flops 10000000000 | bytes 10 | tf_op jit(solution)/shard_map/pallas_call | solution.py:509
  19.9 1.5 %collective-permute-start.5 = (bf16[1,56,1024]{2,1,0:T(8,128)(2,1)S(1)}, bf16[1,56,1024]{2,1,0:T(8,128)(2,1)S(1)}, u32[]{:S(2)}, u32[]{:S(2)}) collective-permute-start(bf16[1,56,1024]{2,1,0:T(8,128)(2,1)S(1)} %get-tuple-element.53.unused), channel_id=1, source_target_pairs={{0,16},{8,24},{16,0},{24,8},{1,17},{9,25},{17,1},{25,9},{2,18},{10... | collective-permute-start | bytes 344072 | tf_op jit(solution)/shard_map/ppermute | solution.py:436
  22.2 1.5 %collective-permute-done.6.got = bf16[2,56,1024]{2,1,0:T(8,128)(2,1)S(1)} collective-permute-done((bf16[2,56,1024]{2,1,0:T(8,128)(2,1)S(1)}, bf16[2,56,1024]{2,1,0:T(8,128)(2,1)S(1)}, u32[]{:S(2)}, u32[]{:S(2)}) %collective-permute-start.6) | collective-permute-done | bytes 229408 | tf_op jit(solution)/shard_map/ppermute | solution.py:436
  23.7 2.0 %shard_map.95 = (f32[2,144,1024]{2,1,0:T(8,128)S(1)}, bf16[2,144,1024]{2,1,0:T(8,128)(2,1)S(1)}) custom-call(bf16[2,144,1024]{2,1,0:T(8,128)(2,1)S(1)} %get-tuple-element.54.bent, bf16[2,56,1024]{2,1,0:T(8,128)(2,1)S(1)} %collective-permute-done.6.got, f32[11,8,1024]{2,1,0:T(8,128)S(1)} %copy-done, bf16[12,144,208]{2,1,0:T(8,128)(2,1)S(1)} %get-tuple-element.50.table, ...), custom_call_target="tpu_custom_call" | custom-call | flops 20000000000 | bytes 10 | tf_op jit(solution)/shard_map/pallas_call | solution.py:509
  25.7 4.3 %collective-permute-start.7 = (bf16[2,144,1024]{2,1,0:T(8,128)(2,1)S(1)}, bf16[2,144,1024]{2,1,0:T(8,128)(2,1)S(1)}, u32[]{:S(2)}, u32[]{:S(2)}) collective-permute-start(bf16[2,144,1024]{2,1,0:T(8,128)(2,1)S(1)} %get-tuple-element.55.unused), channel_id=1, source_target_pairs={{0,8},{8,0},{16,24},{24,16},{1,9},{9,1},{17,25},{25,17},{2,10},{10... | collective-permute-start | bytes 1769480 | tf_op jit(solution)/shard_map/ppermute | solution.py:433
  30.0 1.1 %shard_map.96 = (f32[1,144,1024]{2,1,0:T(8,128)S(1)}, bf16[1,144,1024]{2,1,0:T(8,128)(2,1)S(1)}) custom-call(bf16[1,144,1024]{2,1,0:T(8,128)(2,1)S(1)} %get-tuple-element.52.bent, bf16[1,56,1024]{2,1,0:T(8,128)(2,1)S(1)} %collective-permute-done.5.got, f32[11,8,1024]{2,1,0:T(8,128)S(1)} %copy-done, bf16[12,144,208]{2,1,0:T(8,128)(2,1)S(1)} %get-tuple-element.50.table, ...), custom_call_target="tpu_custom_call" | custom-call | flops 10000000000 | bytes 10 | tf_op jit(solution)/shard_map/pallas_call | solution.py:509
  31.9 3.0 %shard_map.97 = (f32[4,144,1024]{2,1,0:T(8,128)S(1)}, bf16[2,144,1024]{2,1,0:T(8,128)(2,1)S(1)}, bf16[2,56,1024]{2,1,0:T(8,128)(2,1)S(1)}) custom-call(f32[1,144,1024]{2,1,0:T(8,128)S(1)} %get-tuple-element.56.row_zero, f32[1,144,1024]{2,1,0:T(8,128)S(1)} %get-tuple-element.57.row_one, f32[2,144,1024]{2,1,0:T(8,128)S(1)} %get-tuple-element.58.others, ...), custom_call_target="tpu_custom_call" | custom-call | flops 27000000512 | bytes 10 | tf_op jit(solution)/shard_map/pallas_call | solution.py:535
  35.6 1.4 %shard_map.98 = (f32[1,144,1024]{2,1,0:T(8,128)S(1)}, f32[1,144,1024]{2,1,0:T(8,128)S(1)}, f32[3,72,1024]{2,1,0:T(8,128)S(1)}, f32[3,72,1024]{2,1,0:T(8,128)S(1)}) custom-call(f32[1,144,1024]{2,1,0:T(8,128)S(1)} %get-tuple-element.56.row_zero, f32[1,144,1024]{2,1,0:T(8,128)S(1)} %get-tuple-element.57.row_one, f32[4,144,1024]{2,1,0:T(8,128)S(1)} %get-tuple-element.59.held), custom_call_target="tpu_custom_call" | custom-call | flops 30000001024 | bytes 10 | tf_op jit(solution)/shard_map/pallas_call | solution.py:538
  38.0 1.5 %collective-permute-start.13 = (bf16[1,56,1024]{2,1,0:T(8,128)(2,1)S(1)}, bf16[1,56,1024]{2,1,0:T(8,128)(2,1)S(1)}, u32[]{:S(2)}, u32[]{:S(2)}) collective-permute-start(bf16[1,56,1024]{2,1,0:T(8,128)(2,1)S(1)} %get-tuple-element.70), channel_id=1, source_target_pairs={{0,16},{8,24},{16,0},{24,8},{1,17},{9,25},{17,1},{25,9},{2,18},{10... | collective-permute-start | bytes 344072 | tf_op jit(solution)/shard_map/ppermute | solution.py:436
  39.6 3.4 %collective-permute-start.12 = (f32[3,72,1024]{2,1,0:T(8,128)S(1)}, f32[3,72,1024]{2,1,0:T(8,128)S(1)}, u32[]{:S(2)}, u32[]{:S(2)}) collective-permute-start(f32[3,72,1024]{2,1,0:T(8,128)S(1)} %get-tuple-element.68), channel_id=1, source_target_pairs={{0,8},{8,0},{16,24},{24,16},{1,9},{9,1},{17,25},{25,17},{2,10},{10... | collective-permute-start | bytes 2654216 | tf_op jit(solution)/shard_map/ppermute | solution.py:433
  44.1 1.6 %collective-permute-start.14 = (bf16[1,56,1024]{2,1,0:T(8,128)(2,1)S(1)}, bf16[1,56,1024]{2,1,0:T(8,128)(2,1)S(1)}, u32[]{:S(2)}, u32[]{:S(2)}) collective-permute-start(bf16[1,56,1024]{2,1,0:T(8,128)(2,1)S(1)} %get-tuple-element.71.unused), channel_id=1, source_target_pairs={{0,16},{8,24},{16,0},{24,8},{1,17},{9,25},{17,1},{25,9},{2,18},{10... | collective-permute-start | bytes 344072 | tf_op jit(solution)/shard_map/ppermute | solution.py:436
  45.9 1.1 %shard_map.101 = (f32[1,144,1024]{2,1,0:T(8,128)S(1)}, bf16[1,144,1024]{2,1,0:T(8,128)(2,1)S(1)}) custom-call(bf16[1,144,1024]{2,1,0:T(8,128)(2,1)S(1)} %get-tuple-element.69.bent, bf16[1,56,1024]{2,1,0:T(8,128)(2,1)S(1)} %collective-permute-done.13.got, f32[11,8,1024]{2,1,0:T(8,128)S(1)} %copy-done, bf16[12,144,208]{2,1,0:T(8,128)(2,1)S(1)} %get-tuple-element.50.table, ...), custom_call_target="tpu_custom_call" | custom-call | flops 10000000000 | bytes 10 | tf_op jit(solution)/shard_map/pallas_call | solution.py:509
  47.7 2.0 %shard_map.103 = (f32[2,144,1024]{2,1,0:T(8,128)S(1)}, bf16[1,144,1024]{2,1,0:T(8,128)(2,1)S(1)}) custom-call(bf16[2,144,1024]{2,1,0:T(8,128)(2,1)S(1)} %get-tuple-element.75.bent, bf16[2,56,1024]{2,1,0:T(8,128)(2,1)S(1)} %collective-permute-done.10.unused.got, f32[11,8,1024]{2,1,0:T(8,128)S(1)} %copy-done, ...), custom_call_target="tpu_custom_call" | custom-call | flops 20000000000 | bytes 10 | tf_op jit(solution)/shard_map/pallas_call | solution.py:509
  49.7 5.4 %collective-permute-start.15 = (bf16[1,144,1024]{2,1,0:T(8,128)(2,1)S(1)}, bf16[1,144,1024]{2,1,0:T(8,128)(2,1)S(1)}, u32[]{:S(2)}, u32[]{:S(2)}) collective-permute-start(bf16[1,144,1024]{2,1,0:T(8,128)(2,1)S(1)} %get-tuple-element.77), channel_id=1, source_target_pairs={{0,8},{8,0},{16,24},{24,16},{1,9},{9,1},{17,25},{25,17},{2,10},{10... | collective-permute-start | bytes 884744 | tf_op jit(solution)/shard_map/ppermute | solution.py:433
  56.4 1.6 %shard_map.104 = (f32[4,72,1024]{2,1,0:T(8,128)S(1)}, f32[4,72,1024]{2,1,0:T(8,128)S(1)}) custom-call(f32[1,144,1024]{2,1,0:T(8,128)S(1)} %get-tuple-element.72.zero, f32[1,144,1024]{2,1,0:T(8,128)S(1)} %shard_map.102.one, f32[2,144,1024]{2,1,0:T(8,128)S(1)} %get-tuple-element.76.inners, bf16[1,144,1024]{2,1,0:T(8,128)(2,1)S(1)} %collective-permute-done.15.inner), custom_call_target="tpu_custom_call" | custom-call | flops 24999999488 | bytes 10 | tf_op jit(solution)/shard_map/pallas_call | solution.py:558
  58.5 1.6 %shard_map.105 = (f32[72,8,1024]{2,1,0:T(8,128)}, s32[8,128]{1,0:T(8,128)S(1)}) custom-call(f32[1,72,1024]{2,1,0:T(8,128)S(1)} %get-tuple-element.65.keep_zero, f32[3,72,1024]{2,1,0:T(8,128)S(1)} %get-tuple-element.66.keep, f32[1,72,1024]{2,1,0:T(8,128)S(1)} %collective-permute-done.11.got_zero, f32[3,72,1024]{2,1,0:T(8,128)S(1)} %collective-permute-done.12.got, ...), custom_call_target="tpu_custom_call" | custom-call | flops 19000000512 | bytes 10 | tf_op jit(solution)/shard_map/pallas_call | solution.py:564
  60.3 1.2 %collective-permute-done.18.far_halo = bf16[72,1024]{1,0:T(8,128)(2,1)S(1)} collective-permute-done((bf16[72,1024]{1,0:T(8,128)(2,1)S(1)}, bf16[72,1024]{1,0:T(8,128)(2,1)S(1)}, u32[]{:S(2)}, u32[]{:S(2)}) %collective-permute-start.18) | collective-permute-done | bytes 147488 | tf_op jit(solution)/shard_map/ppermute | solution.py:433
  61.6 1.6 %shard_map.107 = f32[72,8,1024]{2,1,0:T(8,128)} custom-call(f32[4,72,1024]{2,1,0:T(8,128)S(1)} %get-tuple-element.78.unused.keep, f32[4,72,1024]{2,1,0:T(8,128)S(1)} %collective-permute-done.16.got, bf16[1,144,1024]{2,1,0:T(8,128)(2,1)S(1)} %collective-permute-done.17.halo, bf16[72,1024]{1,0:T(8,128)(2,1)S(1)} %collective-permute-done.18.far_halo), custom_call_target="tpu_custom_call" | custom-call | flops 19000000512 | bytes 10 | tf_op jit(solution)/shard_map/pallas_call | solution.py:570
  (67 shorter events, 12.1 us)
Async XLA Ops:
  0.6 4.1 %copy-start.1 = (f32[72,8,1024]{2,1,0:T(8,128)S(1)}, f32[72,8,1024]{2,1,0:T(8,128)}, u32[]{:S(2)}) copy-start(f32[72,8,1024]{2,1,0:T(8,128)} %field.3) | copy-start | bytes 7077892
  0.7 3.5 %copy-start.3 = (s32[1606]{0:T(1024)S(1)}, s32[1606]{0:T(1024)}, u32[]{:S(2)}) copy-start(s32[1606]{0:T(1024)} %param.10) | copy-start | bytes 19276
  0.7 3.5 %copy-start.4 = (s32[1606]{0:T(1024)S(1)}, s32[1606]{0:T(1024)}, u32[]{:S(2)}) copy-start(s32[1606]{0:T(1024)} %param.11) | copy-start | bytes 19276
  0.7 3.5 %copy-start.5 = (bf16[1606]{0:T(1024)(128)(2,1)S(1)}, bf16[1606]{0:T(1024)(128)(2,1)}, u32[]{:S(2)}) copy-start(bf16[1606]{0:T(1024)(128)(2,1)} %param.12) | copy-start | bytes 9640
  2.8 1.9 %collective-permute-start = (f32[72,1024]{1,0:T(8,128)}, f32[72,1024]{1,0:T(8,128)S(1)}, u32[]{:S(2)}, u32[]{:S(2)}) collective-permute-start(f32[72,1024]{1,0:T(8,128)} %get-tuple-element.42), channel_id=1, source_target_pairs={{0,8},{8,0},{16,24},{24,16},{1,9},{9,1},{17,25},{25,17},{2,10},{10... | collective-permute-start | bytes 884744 | tf_op jit(solution)/shard_map/ppermute | solution.py:433
  3.3 15.9 %collective-permute-start.3 = (f32[72,1024]{1,0:T(8,128)}, f32[72,1024]{1,0:T(8,128)S(1)}, u32[]{:S(2)}, u32[]{:S(2)}) collective-permute-start(f32[72,1024]{1,0:T(8,128)} %get-tuple-element.48), channel_id=1, source_target_pairs={{8,1},{1,8},{9,2},{2,9},{10,3},{3,10},{11,4},{4,11},{12,5},{5,12},... | collective-permute-start | bytes 884744 | tf_op jit(solution)/shard_map/ppermute | solution.py:439
  5.3 6.6 %copy-start = (f32[11,8,1024]{2,1,0:T(8,128)S(1)}, f32[11,8,1024]{2,1,0:T(8,128)}, u32[]{:S(2)}) copy-start(f32[11,8,1024]{2,1,0:T(8,128)} %stiff.23) | copy-start | bytes 1081348
  5.3 6.5 %collective-permute-start.1 = (f32[5,72,1024]{2,1,0:T(8,128)S(1)}, f32[5,72,1024]{2,1,0:T(8,128)S(1)}, u32[]{:S(2)}, u32[]{:S(2)}) collective-permute-start(f32[5,72,1024]{2,1,0:T(8,128)S(1)} %get-tuple-element.44), channel_id=1, source_target_pairs={{0,8},{8,0},{16,24},{24,16},{1,9},{9,1},{17,25},{25,17},{2,10},{10... | collective-permute-start | bytes 4423688 | tf_op jit(solution)/shard_map/ppermute | solution.py:433
  8.9 10.4 %collective-permute-start.2 = (f32[72,1024]{1,0:T(8,128)S(1)}, f32[72,1024]{1,0:T(8,128)S(1)}, u32[]{:S(2)}, u32[]{:S(2)}) collective-permute-start(f32[72,1024]{1,0:T(8,128)S(1)} %collective-permute-done.unused), channel_id=1, source_target_pairs={{8,1},{1,8},{9,2},{2,9},{10,3},{3,10},{11,4},{4,11},{12,5},{5,12},... | collective-permute-start | bytes 884744 | tf_op jit(solution)/shard_map/ppermute | solution.py:439
  13.2 5.0 %collective-permute-start.4 = (bf16[1,56,1024]{2,1,0:T(8,128)(2,1)S(1)}, bf16[1,56,1024]{2,1,0:T(8,128)(2,1)S(1)}, u32[]{:S(2)}, u32[]{:S(2)}) collective-permute-start(bf16[1,56,1024]{2,1,0:T(8,128)(2,1)S(1)} %get-tuple-element.46.unused), channel_id=1, source_target_pairs={{0,16},{8,24},{16,0},{24,8},{1,17},{9,25},{17,1},{25,9},{2,18},{10... | collective-permute-start | bytes 344072 | tf_op jit(solution)/shard_map/ppermute | solution.py:436
  16.8 6.9 %collective-permute-start.6 = (bf16[2,56,1024]{2,1,0:T(8,128)(2,1)S(1)}, bf16[2,56,1024]{2,1,0:T(8,128)(2,1)S(1)}, u32[]{:S(2)}, u32[]{:S(2)}) collective-permute-start(bf16[2,56,1024]{2,1,0:T(8,128)(2,1)S(1)} %get-tuple-element.47.unused), channel_id=1, source_target_pairs={{0,16},{8,24},{16,0},{24,8},{1,17},{9,25},{17,1},{25,9},{2,18},{10... | collective-permute-start | bytes 688136 | tf_op jit(solution)/shard_map/ppermute | solution.py:436
  19.9 10.0 %collective-permute-start.5 = (bf16[1,56,1024]{2,1,0:T(8,128)(2,1)S(1)}, bf16[1,56,1024]{2,1,0:T(8,128)(2,1)S(1)}, u32[]{:S(2)}, u32[]{:S(2)}) collective-permute-start(bf16[1,56,1024]{2,1,0:T(8,128)(2,1)S(1)} %get-tuple-element.53.unused), channel_id=1, source_target_pairs={{0,16},{8,24},{16,0},{24,8},{1,17},{9,25},{17,1},{25,9},{2,18},{10... | collective-permute-start | bytes 344072 | tf_op jit(solution)/shard_map/ppermute | solution.py:436
  21.5 15.5 %collective-permute-start.9 = (bf16[1,144,1024]{2,1,0:T(8,128)(2,1)S(1)}, bf16[1,144,1024]{2,1,0:T(8,128)(2,1)S(1)}, u32[]{:S(2)}, u32[]{:S(2)}) collective-permute-start(bf16[1,144,1024]{2,1,0:T(8,128)(2,1)S(1)} %shard_map.94.unused), channel_id=1, source_target_pairs={{8,1},{1,8},{9,2},{2,9},{10,3},{3,10},{11,4},{4,11},{12,5},{5,12},... | collective-permute-start | bytes 884744 | tf_op jit(solution)/shard_map/ppermute | solution.py:439
  25.7 6.2 %collective-permute-start.7 = (bf16[2,144,1024]{2,1,0:T(8,128)(2,1)S(1)}, bf16[2,144,1024]{2,1,0:T(8,128)(2,1)S(1)}, u32[]{:S(2)}, u32[]{:S(2)}) collective-permute-start(bf16[2,144,1024]{2,1,0:T(8,128)(2,1)S(1)} %get-tuple-element.55.unused), channel_id=1, source_target_pairs={{0,8},{8,0},{16,24},{24,16},{1,9},{9,1},{17,25},{25,17},{2,10},{10... | collective-permute-start | bytes 1769480 | tf_op jit(solution)/shard_map/ppermute | solution.py:433
  31.1 5.9 %collective-permute-start.8 = (bf16[1,144,1024]{2,1,0:T(8,128)(2,1)S(1)}, bf16[1,144,1024]{2,1,0:T(8,128)(2,1)S(1)}, u32[]{:S(2)}, u32[]{:S(2)}) collective-permute-start(bf16[1,144,1024]{2,1,0:T(8,128)(2,1)S(1)} %get-tuple-element.62), channel_id=1, source_target_pairs={{8,1},{1,8},{9,2},{2,9},{10,3},{3,10},{11,4},{4,11},{12,5},{5,12},... | collective-permute-start | bytes 884744 | tf_op jit(solution)/shard_map/ppermute | solution.py:439
  35.0 8.0 %collective-permute-start.10 = (bf16[2,56,1024]{2,1,0:T(8,128)(2,1)S(1)}, bf16[2,56,1024]{2,1,0:T(8,128)(2,1)S(1)}, u32[]{:S(2)}, u32[]{:S(2)}) collective-permute-start(bf16[2,56,1024]{2,1,0:T(8,128)(2,1)S(1)} %get-tuple-element.64), channel_id=1, source_target_pairs={{0,16},{8,24},{16,0},{24,8},{1,17},{9,25},{17,1},{25,9},{2,18},{10... | collective-permute-start | bytes 688136 | tf_op jit(solution)/shard_map/ppermute | solution.py:436
  38.0 7.9 %collective-permute-start.13 = (bf16[1,56,1024]{2,1,0:T(8,128)(2,1)S(1)}, bf16[1,56,1024]{2,1,0:T(8,128)(2,1)S(1)}, u32[]{:S(2)}, u32[]{:S(2)}) collective-permute-start(bf16[1,56,1024]{2,1,0:T(8,128)(2,1)S(1)} %get-tuple-element.70), channel_id=1, source_target_pairs={{0,16},{8,24},{16,0},{24,8},{1,17},{9,25},{17,1},{25,9},{2,18},{10... | collective-permute-start | bytes 344072 | tf_op jit(solution)/shard_map/ppermute | solution.py:436
  39.6 18.9 %collective-permute-start.12 = (f32[3,72,1024]{2,1,0:T(8,128)S(1)}, f32[3,72,1024]{2,1,0:T(8,128)S(1)}, u32[]{:S(2)}, u32[]{:S(2)}) collective-permute-start(f32[3,72,1024]{2,1,0:T(8,128)S(1)} %get-tuple-element.68), channel_id=1, source_target_pairs={{0,8},{8,0},{16,24},{24,16},{1,9},{9,1},{17,25},{25,17},{2,10},{10... | collective-permute-start | bytes 2654216 | tf_op jit(solution)/shard_map/ppermute | solution.py:433
  44.1 11.1 %collective-permute-start.14 = (bf16[1,56,1024]{2,1,0:T(8,128)(2,1)S(1)}, bf16[1,56,1024]{2,1,0:T(8,128)(2,1)S(1)}, u32[]{:S(2)}, u32[]{:S(2)}) collective-permute-start(bf16[1,56,1024]{2,1,0:T(8,128)(2,1)S(1)} %get-tuple-element.71.unused), channel_id=1, source_target_pairs={{0,16},{8,24},{16,0},{24,8},{1,17},{9,25},{17,1},{25,9},{2,18},{10... | collective-permute-start | bytes 344072 | tf_op jit(solution)/shard_map/ppermute | solution.py:436
  45.7 12.8 %collective-permute-start.11 = (f32[1,72,1024]{2,1,0:T(8,128)S(1)}, f32[1,72,1024]{2,1,0:T(8,128)S(1)}, u32[]{:S(2)}, u32[]{:S(2)}) collective-permute-start(f32[1,72,1024]{2,1,0:T(8,128)S(1)} %get-tuple-element.67), channel_id=1, source_target_pairs={{0,8},{8,0},{16,24},{24,16},{1,9},{9,1},{17,25},{25,17},{2,10},{10... | collective-permute-start | bytes 884744 | tf_op jit(solution)/shard_map/ppermute | solution.py:433
  47.0 13.1 %collective-permute-start.17 = (bf16[1,144,1024]{2,1,0:T(8,128)(2,1)S(1)}, bf16[1,144,1024]{2,1,0:T(8,128)(2,1)S(1)}, u32[]{:S(2)}, u32[]{:S(2)}) collective-permute-start(bf16[1,144,1024]{2,1,0:T(8,128)(2,1)S(1)} %get-tuple-element.74.unused), channel_id=1, source_target_pairs={{8,1},{1,8},{9,2},{2,9},{10,3},{3,10},{11,4},{4,11},{12,5},{5,12},... | collective-permute-start | bytes 884744 | tf_op jit(solution)/shard_map/ppermute | solution.py:439
  49.7 6.6 %collective-permute-start.15 = (bf16[1,144,1024]{2,1,0:T(8,128)(2,1)S(1)}, bf16[1,144,1024]{2,1,0:T(8,128)(2,1)S(1)}, u32[]{:S(2)}, u32[]{:S(2)}) collective-permute-start(bf16[1,144,1024]{2,1,0:T(8,128)(2,1)S(1)} %get-tuple-element.77), channel_id=1, source_target_pairs={{0,8},{8,0},{16,24},{24,16},{1,9},{9,1},{17,25},{25,17},{2,10},{10... | collective-permute-start | bytes 884744 | tf_op jit(solution)/shard_map/ppermute | solution.py:433
  58.0 3.6 %collective-permute-start.16 = (f32[4,72,1024]{2,1,0:T(8,128)S(1)}, f32[4,72,1024]{2,1,0:T(8,128)S(1)}, u32[]{:S(2)}, u32[]{:S(2)}) collective-permute-start(f32[4,72,1024]{2,1,0:T(8,128)S(1)} %get-tuple-element.80), channel_id=1, source_target_pairs={{0,8},{8,0},{16,24},{24,16},{1,9},{9,1},{17,25},{25,17},{2,10},{10... | collective-permute-start | bytes 3538952 | tf_op jit(solution)/shard_map/ppermute | solution.py:433
  60.1 1.4 %collective-permute-start.18 = (bf16[72,1024]{1,0:T(8,128)(2,1)S(1)}, bf16[72,1024]{1,0:T(8,128)(2,1)S(1)}, u32[]{:S(2)}, u32[]{:S(2)}) collective-permute-start(bf16[72,1024]{1,0:T(8,128)(2,1)S(1)} %shard_map.106), channel_id=1, source_target_pairs={{0,8},{8,0},{16,24},{24,16},{1,9},{9,1},{17,25},{25,17},{2,10},{10... | collective-permute-start | bytes 442376 | tf_op jit(solution)/shard_map/ppermute | solution.py:433
  (2 other events, 6.8 us)

commit v9 on v8

--- a/solution.py
+++ b/solution.py
@@ -12,6 +12,7 @@
 ANY = pl.BlockSpec(memory_space=pl.ANY)
 NT = (((1,), (1,)), ((), ()))
 STEP = 16
+CHUNK = 8
 EARLY = 0.01
 
 
@@ -356,16 +357,15 @@
 def write_tiles(near, far, out, lines, done):
     first = core_side() == 0
     half = out.shape[1] // 2
-    step = 24
     copies = []
-    for k, at in enumerate(range(0, out.shape[0], step)):
-        for start in range(at, at + step, 8):
+    for k, at in enumerate(range(0, out.shape[0], CHUNK)):
+        for start in range(at, at + CHUNK, 8):
             ours = [near(i, slice(start, start + 8)) for i in range(half)]
             theirs = [far(i, slice(start, start + 8)) for i in range(half)]
             rows = [jnp.where(first, a, b) for a, b in zip(ours, theirs)]
             rows += [jnp.where(first, b, a) for a, b in zip(ours[::-1], theirs[::-1])]
             lines[start : start + 8] = jnp.swapaxes(jnp.stack(rows, axis=0), 0, 1)
-        cut = pl.ds(at, step)
+        cut = pl.ds(at, CHUNK)
         copies.append(pltpu.make_async_copy(lines.at[cut], out.at[cut], done.at[k]))
         copies[-1].start()
     for copy in copies:
@@ -546,7 +546,7 @@
     cross_out = by_chip(buffer_out)
     keep_out, send_out, bent_one, buffer_one = call(
         second_next_kernel, outs(1) + bents(1), (), EARLY, [VMEM] * 4 + [ANY]
-    )(zero, held, stiffness, send_table, cross_in)
+    )(zero, held, stiffness, send_table, buffer_out)
     cross_one = by_chip(buffer_one)
     got_out = by_core(send_out)
     moment_out, edge_zero = couple(bent_out, cross_out, 0, 0, (), buffer_one)
@@ -560,7 +560,7 @@
     )
     got = by_core(send)
     whole = shape(slot_field.shape, F32)
-    writers = [pltpu.VMEM(slot_field.shape, F32), pltpu.SemaphoreType.DMA((own // 24,))]
+    writers = [pltpu.VMEM(slot_field.shape, F32), pltpu.SemaphoreType.DMA((own // CHUNK,))]
     first_apply, token = call(
         merge_kernel, (whole, TOKEN), writers, 1.9, [VMEM] * 4 + [ANY], 6, (ANY, VMEM)
     )(keep_out, keep_in, got_out, got_in, keep)

time: 63.6 us -> 64.8 us (1.019)
  starting transfers between devices: 29 us -> 30.3 us
    ppermute x8, starting transfers between devices: 18.1 us -> 20.4 us  [by_core(): return lax.ppermute(value, 'chaos', core_swap)]
    ppermute x6, starting transfers between devices: 7.43 us -> 6.39 us  [by_chip(): return lax.ppermute(value, 'chaos', chip_swap)]
  transfers between devices with their start and end apart: 19 -> 19, of which waited for: 4 -> 4; matrix products, arithmetic and copies ran while one was open for 0% -> 0% of each run, Pallas kernels for 41% -> 38%
where the time goes in v9:
time: 64.8 us; the launch traced here: 64.5 us
  starting transfers between devices  30.3 us (47%)
  Pallas kernels  29.5 us (46%)
  waiting for transfers between devices  3.26 us (5%)
  between operations  1.29 us (2%)
    ppermute x8, starting transfers between devices, by_core(): return lax.ppermute(value, 'chaos', core_swap)  20.4 us
    pallas_call x6, Pallas kernels, couple(): call(functools.partial(couple_kernel, first, outer_row, inner_rows), tupl...  8.46 us
    ppermute x6, starting transfers between devices, by_chip(): return lax.ppermute(value, 'chaos', chip_swap)  6.39 us
    ppermute x5, starting transfers between devices, by_tile(): return lax.ppermute(value, ('chaos', 'tile'), tile_swap)  3.55 us
    pallas_call x2, Pallas kernels, bend(): call(functools.partial(first_kernel, first), bents(count), (), 0.9 * coun...  3.37 us
    pallas_call x1, Pallas kernels, body(): call(second_inner_kernel, (shape((4, pair, width), F32),) + bents(2), (),...  3 us
    pallas_call x1, Pallas kernels, body(): call(functools.partial(table_kernel, terms, pair, hubs, slot_total), (sha...  2.29 us
    pallas_call x1, Pallas kernels, body(): call(edge_kernel, (row_block, row_block), [pltpu.VMEM((2, own, width), F3...  2.13 us
  transfers between devices with their start and end apart: 19, of which 4 were waited for; matrix products, arithmetic and copies ran while one was open for 0% of the time, Pallas kernels for 38%

profile of v9, /device:TPU:0, one launch (start us, length us, event | category | flops | bytes accessed | tf_op | source)
XLA Modules:
  0.0 64.5 jit_solution(17287179243686320212)
XLA Ops:
  0.7 2.1 %shard_map.86 = (f32[72,1024]{1,0:T(8,128)}, f32[72,1024]{1,0:T(8,128)}) custom-call(f32[72,8,1024]{2,1,0:T(8,128)} %field.3), custom_call_target="tpu_custom_call" | custom-call | flops 20000000000 | bytes 10 | tf_op jit(solution)/shard_map/pallas_call | solution.py:459
  5.3 3.6 %collective-permute-start.1 = (f32[5,72,1024]{2,1,0:T(8,128)S(1)}, f32[5,72,1024]{2,1,0:T(8,128)S(1)}, u32[]{:S(2)}, u32[]{:S(2)}) collective-permute-start(f32[5,72,1024]{2,1,0:T(8,128)S(1)} %get-tuple-element.44), channel_id=1, source_target_pairs={{0,8},{8,0},{16,24},{24,16},{1,9},{9,1},{17,25},{25,17},{2,10},{10... | collective-permute-start | bytes 4423688 | tf_op jit(solution)/shard_map/ppermute | solution.py:433
  9.6 2.3 %shard_map.88 = (bf16[12,144,208]{2,1,0:T(8,128)(2,1)S(1)}, bf16[11,64,144]{2,1,0:T(8,128)(2,1)S(1)}) custom-call(f32[8,1664]{1,0:T(8,128)S(1)} %stack.31.entries, f32[72,1024]{1,0:T(8,128)S(1)} %collective-permute-done.unused), custom_call_target="tpu_custom_call" | custom-call | flops 30000001024 | bytes 10 | tf_op jit(solution)/shard_map/pallas_call | solution.py:471
  11.9 1.3 %shard_map.89 = (bf16[1,144,1024]{2,1,0:T(8,128)(2,1)S(1)}, bf16[1,56,1024]{2,1,0:T(8,128)(2,1)S(1)}) custom-call(f32[5,72,1024]{2,1,0:T(8,128)S(1)} %get-tuple-element.43.keep, f32[5,72,1024]{2,1,0:T(8,128)S(1)} %collective-permute-done.1.got.unused, f32[11,8,1024]{2,1,0:T(8,128)S(1)} %copy-done, bf16[11,64,144]{2,1,0:T(8,128)(2,1)S(1)} %get-tuple-element.45.send_table, ...), custom_call_target="tpu_custom_call" | custom-call | flops 8999999488 | bytes 10 | tf_op jit(solution)/shard_map/pallas_call | solution.py:497
  13.2 1.6 %collective-permute-start.4 = (bf16[1,56,1024]{2,1,0:T(8,128)(2,1)S(1)}, bf16[1,56,1024]{2,1,0:T(8,128)(2,1)S(1)}, u32[]{:S(2)}, u32[]{:S(2)}) collective-permute-start(bf16[1,56,1024]{2,1,0:T(8,128)(2,1)S(1)} %get-tuple-element.46.unused), channel_id=1, source_target_pairs={{0,16},{8,24},{16,0},{24,8},{1,17},{9,25},{17,1},{25,9},{2,18},{10... | collective-permute-start | bytes 344072 | tf_op jit(solution)/shard_map/ppermute | solution.py:436
  14.8 2.0 %shard_map.90 = (bf16[2,144,1024]{2,1,0:T(8,128)(2,1)S(1)}, bf16[2,56,1024]{2,1,0:T(8,128)(2,1)S(1)}) custom-call(f32[5,72,1024]{2,1,0:T(8,128)S(1)} %get-tuple-element.43.keep, f32[5,72,1024]{2,1,0:T(8,128)S(1)} %collective-permute-done.1.got.unused, f32[11,8,1024]{2,1,0:T(8,128)S(1)} %copy-done, bf16[11,64,144]{2,1,0:T(8,128)(2,1)S(1)} %get-tuple-element.45.send_table, ...), custom_call_target="tpu_custom_call" | custom-call | flops 17999998976 | bytes 10 | tf_op jit(solution)/shard_map/pallas_call | solution.py:497
  18.2 1.1 %shard_map.92 = (f32[1,144,1024]{2,1,0:T(8,128)S(1)}, bf16[1,144,1024]{2,1,0:T(8,128)(2,1)S(1)}) custom-call(bf16[1,144,1024]{2,1,0:T(8,128)(2,1)S(1)} %get-tuple-element.49.bent, bf16[1,56,1024]{2,1,0:T(8,128)(2,1)S(1)} %collective-permute-done.4.got, f32[11,8,1024]{2,1,0:T(8,128)S(1)} %copy-done, bf16[12,144,208]{2,1,0:T(8,128)(2,1)S(1)} %get-tuple-element.50.table, ...), custom_call_target="tpu_custom_call" | custom-call | flops 10000000000 | bytes 10 | tf_op jit(solution)/shard_map/pallas_call | solution.py:509
  19.9 1.5 %collective-permute-start.5 = (bf16[1,56,1024]{2,1,0:T(8,128)(2,1)S(1)}, bf16[1,56,1024]{2,1,0:T(8,128)(2,1)S(1)}, u32[]{:S(2)}, u32[]{:S(2)}) collective-permute-start(bf16[1,56,1024]{2,1,0:T(8,128)(2,1)S(1)} %get-tuple-element.53.unused), channel_id=1, source_target_pairs={{0,16},{8,24},{16,0},{24,8},{1,17},{9,25},{17,1},{25,9},{2,18},{10... | collective-permute-start | bytes 344072 | tf_op jit(solution)/shard_map/ppermute | solution.py:436
  22.2 1.5 %collective-permute-done.6.got = bf16[2,56,1024]{2,1,0:T(8,128)(2,1)S(1)} collective-permute-done((bf16[2,56,1024]{2,1,0:T(8,128)(2,1)S(1)}, bf16[2,56,1024]{2,1,0:T(8,128)(2,1)S(1)}, u32[]{:S(2)}, u32[]{:S(2)}) %collective-permute-start.6) | collective-permute-done | bytes 229408 | tf_op jit(solution)/shard_map/ppermute | solution.py:436
  23.7 2.0 %shard_map.95 = (f32[2,144,1024]{2,1,0:T(8,128)S(1)}, bf16[2,144,1024]{2,1,0:T(8,128)(2,1)S(1)}) custom-call(bf16[2,144,1024]{2,1,0:T(8,128)(2,1)S(1)} %get-tuple-element.54.bent, bf16[2,56,1024]{2,1,0:T(8,128)(2,1)S(1)} %collective-permute-done.6.got, f32[11,8,1024]{2,1,0:T(8,128)S(1)} %copy-done, bf16[12,144,208]{2,1,0:T(8,128)(2,1)S(1)} %get-tuple-element.50.table, ...), custom_call_target="tpu_custom_call" | custom-call | flops 20000000000 | bytes 10 | tf_op jit(solution)/shard_map/pallas_call | solution.py:509
  25.7 4.3 %collective-permute-start.7 = (bf16[2,144,1024]{2,1,0:T(8,128)(2,1)S(1)}, bf16[2,144,1024]{2,1,0:T(8,128)(2,1)S(1)}, u32[]{:S(2)}, u32[]{:S(2)}) collective-permute-start(bf16[2,144,1024]{2,1,0:T(8,128)(2,1)S(1)} %get-tuple-element.55.unused), channel_id=1, source_target_pairs={{0,8},{8,0},{16,24},{24,16},{1,9},{9,1},{17,25},{25,17},{2,10},{10... | collective-permute-start | bytes 1769480 | tf_op jit(solution)/shard_map/ppermute | solution.py:433
  30.0 1.1 %shard_map.96 = (f32[1,144,1024]{2,1,0:T(8,128)S(1)}, bf16[1,144,1024]{2,1,0:T(8,128)(2,1)S(1)}) custom-call(bf16[1,144,1024]{2,1,0:T(8,128)(2,1)S(1)} %get-tuple-element.52.bent, bf16[1,56,1024]{2,1,0:T(8,128)(2,1)S(1)} %collective-permute-done.5.got, f32[11,8,1024]{2,1,0:T(8,128)S(1)} %copy-done, bf16[12,144,208]{2,1,0:T(8,128)(2,1)S(1)} %get-tuple-element.50.table, ...), custom_call_target="tpu_custom_call" | custom-call | flops 10000000000 | bytes 10 | tf_op jit(solution)/shard_map/pallas_call | solution.py:509
  31.9 3.0 %shard_map.97 = (f32[4,144,1024]{2,1,0:T(8,128)S(1)}, bf16[2,144,1024]{2,1,0:T(8,128)(2,1)S(1)}, bf16[2,56,1024]{2,1,0:T(8,128)(2,1)S(1)}) custom-call(f32[1,144,1024]{2,1,0:T(8,128)S(1)} %get-tuple-element.56.row_zero, f32[1,144,1024]{2,1,0:T(8,128)S(1)} %get-tuple-element.57.row_one, f32[2,144,1024]{2,1,0:T(8,128)S(1)} %get-tuple-element.58.others, ...), custom_call_target="tpu_custom_call" | custom-call | flops 27000000512 | bytes 10 | tf_op jit(solution)/shard_map/pallas_call | solution.py:535
  35.0 1.4 %shard_map.98 = (f32[1,144,1024]{2,1,0:T(8,128)S(1)}, f32[1,144,1024]{2,1,0:T(8,128)S(1)}, f32[3,72,1024]{2,1,0:T(8,128)S(1)}, f32[3,72,1024]{2,1,0:T(8,128)S(1)}) custom-call(f32[1,144,1024]{2,1,0:T(8,128)S(1)} %get-tuple-element.56.row_zero, f32[1,144,1024]{2,1,0:T(8,128)S(1)} %get-tuple-element.57.row_one, f32[4,144,1024]{2,1,0:T(8,128)S(1)} %get-tuple-element.59.held), custom_call_target="tpu_custom_call" | custom-call | flops 30000001024 | bytes 10 | tf_op jit(solution)/shard_map/pallas_call | solution.py:538
  38.0 1.5 %collective-permute-start.14 = (bf16[2,56,1024]{2,1,0:T(8,128)(2,1)S(1)}, bf16[2,56,1024]{2,1,0:T(8,128)(2,1)S(1)}, u32[]{:S(2)}, u32[]{:S(2)}) collective-permute-start(bf16[2,56,1024]{2,1,0:T(8,128)(2,1)S(1)} %get-tuple-element.75), channel_id=1, source_target_pairs={{0,16},{8,24},{16,0},{24,8},{1,17},{9,25},{17,1},{25,9},{2,18},{10... | collective-permute-start | bytes 688136 | tf_op jit(solution)/shard_map/ppermute | solution.py:436
  41.2 4.4 %collective-permute-start.10 = (f32[1,72,1024]{2,1,0:T(8,128)S(1)}, f32[1,72,1024]{2,1,0:T(8,128)S(1)}, u32[]{:S(2)}, u32[]{:S(2)}) collective-permute-start(f32[1,72,1024]{2,1,0:T(8,128)S(1)} %get-tuple-element.67), channel_id=1, source_target_pairs={{0,8},{8,0},{16,24},{24,16},{1,9},{9,1},{17,25},{25,17},{2,10},{10... | collective-permute-start | bytes 884744 | tf_op jit(solution)/shard_map/ppermute | solution.py:433
  45.6 1.1 %shard_map.101 = (f32[1,144,1024]{2,1,0:T(8,128)S(1)}, bf16[1,144,1024]{2,1,0:T(8,128)(2,1)S(1)}) custom-call(bf16[1,144,1024]{2,1,0:T(8,128)(2,1)S(1)} %get-tuple-element.69.bent, bf16[1,56,1024]{2,1,0:T(8,128)(2,1)S(1)} %collective-permute-done.12.got, f32[11,8,1024]{2,1,0:T(8,128)S(1)} %copy-done, bf16[12,144,208]{2,1,0:T(8,128)(2,1)S(1)} %get-tuple-element.50.table, ...), custom_call_target="tpu_custom_call" | custom-call | flops 10000000000 | bytes 10 | tf_op jit(solution)/shard_map/pallas_call | solution.py:509
  47.4 2.0 %shard_map.103 = (f32[2,144,1024]{2,1,0:T(8,128)S(1)}, bf16[1,144,1024]{2,1,0:T(8,128)(2,1)S(1)}) custom-call(bf16[2,144,1024]{2,1,0:T(8,128)(2,1)S(1)} %get-tuple-element.74.bent, bf16[2,56,1024]{2,1,0:T(8,128)(2,1)S(1)} %collective-permute-done.14.got, f32[11,8,1024]{2,1,0:T(8,128)S(1)} %copy-done, bf16[12,144,208]{2,1,0:T(8,128)(2,1)S(1)} %get-tuple-element.50.table, ...), custom_call_target="tpu_custom_call" | custom-call | flops 20000000000 | bytes 10 | tf_op jit(solution)/shard_map/pallas_call | solution.py:509
  49.5 7.0 %collective-permute-start.15 = (bf16[1,144,1024]{2,1,0:T(8,128)(2,1)S(1)}, bf16[1,144,1024]{2,1,0:T(8,128)(2,1)S(1)}, u32[]{:S(2)}, u32[]{:S(2)}) collective-permute-start(bf16[1,144,1024]{2,1,0:T(8,128)(2,1)S(1)} %get-tuple-element.77), channel_id=1, source_target_pairs={{0,8},{8,0},{16,24},{24,16},{1,9},{9,1},{17,25},{25,17},{2,10},{10... | collective-permute-start | bytes 884744 | tf_op jit(solution)/shard_map/ppermute | solution.py:433
  56.5 1.1 %shard_map.102.one = f32[1,144,1024]{2,1,0:T(8,128)S(1)} custom-call(bf16[1,144,1024]{2,1,0:T(8,128)(2,1)S(1)} %get-tuple-element.72.bent, bf16[1,56,1024]{2,1,0:T(8,128)(2,1)S(1)} %collective-permute-done.13.got, f32[11,8,1024]{2,1,0:T(8,128)S(1)} %copy-done, bf16[12,144,208]{2,1,0:T(8,128)(2,1)S(1)} %get-tuple-element.50.table, ...), custom_call_target="tpu_custom_call" | custom-call | flops 10000000000 | bytes 10 | tf_op jit(solution)/shard_map/pallas_call | solution.py:509
  57.7 1.6 %shard_map.104 = (f32[4,72,1024]{2,1,0:T(8,128)S(1)}, f32[4,72,1024]{2,1,0:T(8,128)S(1)}) custom-call(f32[1,144,1024]{2,1,0:T(8,128)S(1)} %get-tuple-element.71.zero, f32[1,144,1024]{2,1,0:T(8,128)S(1)} %shard_map.102.one, f32[2,144,1024]{2,1,0:T(8,128)S(1)} %get-tuple-element.76.inners, bf16[1,144,1024]{2,1,0:T(8,128)(2,1)S(1)} %collective-permute-done.15.inner), custom_call_target="tpu_custom_call" | custom-call | flops 24999999488 | bytes 10 | tf_op jit(solution)/shard_map/pallas_call | solution.py:558
  59.8 1.5 %shard_map.105 = (f32[72,8,1024]{2,1,0:T(8,128)}, s32[8,128]{1,0:T(8,128)S(1)}) custom-call(f32[1,72,1024]{2,1,0:T(8,128)S(1)} %get-tuple-element.65.keep_zero, f32[3,72,1024]{2,1,0:T(8,128)S(1)} %get-tuple-element.66.keep, f32[1,72,1024]{2,1,0:T(8,128)S(1)} %collective-permute-done.10.got_zero, f32[3,72,1024]{2,1,0:T(8,128)S(1)} %collective-permute-done.11.got, ...), custom_call_target="tpu_custom_call" | custom-call | flops 19000000512 | bytes 10 | tf_op jit(solution)/shard_map/pallas_call | solution.py:564
  61.6 1.2 %collective-permute-done.18.far_halo = bf16[72,1024]{1,0:T(8,128)(2,1)S(1)} collective-permute-done((bf16[72,1024]{1,0:T(8,128)(2,1)S(1)}, bf16[72,1024]{1,0:T(8,128)(2,1)S(1)}, u32[]{:S(2)}, u32[]{:S(2)}) %collective-permute-start.18) | collective-permute-done | bytes 147488 | tf_op jit(solution)/shard_map/ppermute | solution.py:433
  62.8 1.5 %shard_map.107 = f32[72,8,1024]{2,1,0:T(8,128)} custom-call(f32[4,72,1024]{2,1,0:T(8,128)S(1)} %get-tuple-element.78.unused.keep, f32[4,72,1024]{2,1,0:T(8,128)S(1)} %collective-permute-done.16.got, bf16[1,144,1024]{2,1,0:T(8,128)(2,1)S(1)} %collective-permute-done.17.halo, bf16[72,1024]{1,0:T(8,128)(2,1)S(1)} %collective-permute-done.18.far_halo), custom_call_target="tpu_custom_call" | custom-call | flops 19000000512 | bytes 10 | tf_op jit(solution)/shard_map/pallas_call | solution.py:570
  (67 shorter events, 11.3 us)
Async XLA Ops:
  0.6 4.1 %copy-start.1 = (f32[72,8,1024]{2,1,0:T(8,128)S(1)}, f32[72,8,1024]{2,1,0:T(8,128)}, u32[]{:S(2)}) copy-start(f32[72,8,1024]{2,1,0:T(8,128)} %field.3) | copy-start | bytes 7077892
  0.7 3.5 %copy-start.3 = (s32[1606]{0:T(1024)S(1)}, s32[1606]{0:T(1024)}, u32[]{:S(2)}) copy-start(s32[1606]{0:T(1024)} %param.10) | copy-start | bytes 19276
  0.7 3.5 %copy-start.4 = (s32[1606]{0:T(1024)S(1)}, s32[1606]{0:T(1024)}, u32[]{:S(2)}) copy-start(s32[1606]{0:T(1024)} %param.11) | copy-start | bytes 19276
  0.7 3.5 %copy-start.5 = (bf16[1606]{0:T(1024)(128)(2,1)S(1)}, bf16[1606]{0:T(1024)(128)(2,1)}, u32[]{:S(2)}) copy-start(bf16[1606]{0:T(1024)(128)(2,1)} %param.12) | copy-start | bytes 9640
  2.8 1.9 %collective-permute-start = (f32[72,1024]{1,0:T(8,128)}, f32[72,1024]{1,0:T(8,128)S(1)}, u32[]{:S(2)}, u32[]{:S(2)}) collective-permute-start(f32[72,1024]{1,0:T(8,128)} %get-tuple-element.42), channel_id=1, source_target_pairs={{0,8},{8,0},{16,24},{24,16},{1,9},{9,1},{17,25},{25,17},{2,10},{10... | collective-permute-start | bytes 884744 | tf_op jit(solution)/shard_map/ppermute | solution.py:433
  3.3 15.9 %collective-permute-start.3 = (f32[72,1024]{1,0:T(8,128)}, f32[72,1024]{1,0:T(8,128)S(1)}, u32[]{:S(2)}, u32[]{:S(2)}) collective-permute-start(f32[72,1024]{1,0:T(8,128)} %get-tuple-element.48), channel_id=1, source_target_pairs={{8,1},{1,8},{9,2},{2,9},{10,3},{3,10},{11,4},{4,11},{12,5},{5,12},... | collective-permute-start | bytes 884744 | tf_op jit(solution)/shard_map/ppermute | solution.py:439
  5.3 6.6 %copy-start = (f32[11,8,1024]{2,1,0:T(8,128)S(1)}, f32[11,8,1024]{2,1,0:T(8,128)}, u32[]{:S(2)}) copy-start(f32[11,8,1024]{2,1,0:T(8,128)} %stiff.23) | copy-start | bytes 1081348
  5.3 6.5 %collective-permute-start.1 = (f32[5,72,1024]{2,1,0:T(8,128)S(1)}, f32[5,72,1024]{2,1,0:T(8,128)S(1)}, u32[]{:S(2)}, u32[]{:S(2)}) collective-permute-start(f32[5,72,1024]{2,1,0:T(8,128)S(1)} %get-tuple-element.44), channel_id=1, source_target_pairs={{0,8},{8,0},{16,24},{24,16},{1,9},{9,1},{17,25},{25,17},{2,10},{10... | collective-permute-start | bytes 4423688 | tf_op jit(solution)/shard_map/ppermute | solution.py:433
  8.9 10.4 %collective-permute-start.2 = (f32[72,1024]{1,0:T(8,128)S(1)}, f32[72,1024]{1,0:T(8,128)S(1)}, u32[]{:S(2)}, u32[]{:S(2)}) collective-permute-start(f32[72,1024]{1,0:T(8,128)S(1)} %collective-permute-done.unused), channel_id=1, source_target_pairs={{8,1},{1,8},{9,2},{2,9},{10,3},{3,10},{11,4},{4,11},{12,5},{5,12},... | collective-permute-start | bytes 884744 | tf_op jit(solution)/shard_map/ppermute | solution.py:439
  13.2 5.0 %collective-permute-start.4 = (bf16[1,56,1024]{2,1,0:T(8,128)(2,1)S(1)}, bf16[1,56,1024]{2,1,0:T(8,128)(2,1)S(1)}, u32[]{:S(2)}, u32[]{:S(2)}) collective-permute-start(bf16[1,56,1024]{2,1,0:T(8,128)(2,1)S(1)} %get-tuple-element.46.unused), channel_id=1, source_target_pairs={{0,16},{8,24},{16,0},{24,8},{1,17},{9,25},{17,1},{25,9},{2,18},{10... | collective-permute-start | bytes 344072 | tf_op jit(solution)/shard_map/ppermute | solution.py:436
  16.8 6.9 %collective-permute-start.6 = (bf16[2,56,1024]{2,1,0:T(8,128)(2,1)S(1)}, bf16[2,56,1024]{2,1,0:T(8,128)(2,1)S(1)}, u32[]{:S(2)}, u32[]{:S(2)}) collective-permute-start(bf16[2,56,1024]{2,1,0:T(8,128)(2,1)S(1)} %get-tuple-element.47.unused), channel_id=1, source_target_pairs={{0,16},{8,24},{16,0},{24,8},{1,17},{9,25},{17,1},{25,9},{2,18},{10... | collective-permute-start | bytes 688136 | tf_op jit(solution)/shard_map/ppermute | solution.py:436
  19.9 10.0 %collective-permute-start.5 = (bf16[1,56,1024]{2,1,0:T(8,128)(2,1)S(1)}, bf16[1,56,1024]{2,1,0:T(8,128)(2,1)S(1)}, u32[]{:S(2)}, u32[]{:S(2)}) collective-permute-start(bf16[1,56,1024]{2,1,0:T(8,128)(2,1)S(1)} %get-tuple-element.53.unused), channel_id=1, source_target_pairs={{0,16},{8,24},{16,0},{24,8},{1,17},{9,25},{17,1},{25,9},{2,18},{10... | collective-permute-start | bytes 344072 | tf_op jit(solution)/shard_map/ppermute | solution.py:436
  21.5 14.9 %collective-permute-start.9 = (bf16[1,144,1024]{2,1,0:T(8,128)(2,1)S(1)}, bf16[1,144,1024]{2,1,0:T(8,128)(2,1)S(1)}, u32[]{:S(2)}, u32[]{:S(2)}) collective-permute-start(bf16[1,144,1024]{2,1,0:T(8,128)(2,1)S(1)} %shard_map.94.unused), channel_id=1, source_target_pairs={{8,1},{1,8},{9,2},{2,9},{10,3},{3,10},{11,4},{4,11},{12,5},{5,12},... | collective-permute-start | bytes 884744 | tf_op jit(solution)/shard_map/ppermute | solution.py:439
  25.7 6.2 %collective-permute-start.7 = (bf16[2,144,1024]{2,1,0:T(8,128)(2,1)S(1)}, bf16[2,144,1024]{2,1,0:T(8,128)(2,1)S(1)}, u32[]{:S(2)}, u32[]{:S(2)}) collective-permute-start(bf16[2,144,1024]{2,1,0:T(8,128)(2,1)S(1)} %get-tuple-element.55.unused), channel_id=1, source_target_pairs={{0,8},{8,0},{16,24},{24,16},{1,9},{9,1},{17,25},{25,17},{2,10},{10... | collective-permute-start | bytes 1769480 | tf_op jit(solution)/shard_map/ppermute | solution.py:433
  31.1 5.3 %collective-permute-start.8 = (bf16[1,144,1024]{2,1,0:T(8,128)(2,1)S(1)}, bf16[1,144,1024]{2,1,0:T(8,128)(2,1)S(1)}, u32[]{:S(2)}, u32[]{:S(2)}) collective-permute-start(bf16[1,144,1024]{2,1,0:T(8,128)(2,1)S(1)} %get-tuple-element.62), channel_id=1, source_target_pairs={{8,1},{1,8},{9,2},{2,9},{10,3},{3,10},{11,4},{4,11},{12,5},{5,12},... | collective-permute-start | bytes 884744 | tf_op jit(solution)/shard_map/ppermute | solution.py:439
  37.4 8.2 %collective-permute-start.12 = (bf16[1,56,1024]{2,1,0:T(8,128)(2,1)S(1)}, bf16[1,56,1024]{2,1,0:T(8,128)(2,1)S(1)}, u32[]{:S(2)}, u32[]{:S(2)}) collective-permute-start(bf16[1,56,1024]{2,1,0:T(8,128)(2,1)S(1)} %get-tuple-element.64.unused), channel_id=1, source_target_pairs={{0,16},{8,24},{16,0},{24,8},{1,17},{9,25},{17,1},{25,9},{2,18},{10... | collective-permute-start | bytes 344072 | tf_op jit(solution)/shard_map/ppermute | solution.py:436
  38.0 9.4 %collective-permute-start.14 = (bf16[2,56,1024]{2,1,0:T(8,128)(2,1)S(1)}, bf16[2,56,1024]{2,1,0:T(8,128)(2,1)S(1)}, u32[]{:S(2)}, u32[]{:S(2)}) collective-permute-start(bf16[2,56,1024]{2,1,0:T(8,128)(2,1)S(1)} %get-tuple-element.75), channel_id=1, source_target_pairs={{0,16},{8,24},{16,0},{24,8},{1,17},{9,25},{17,1},{25,9},{2,18},{10... | collective-permute-start | bytes 688136 | tf_op jit(solution)/shard_map/ppermute | solution.py:436
  40.6 15.8 %collective-permute-start.13 = (bf16[1,56,1024]{2,1,0:T(8,128)(2,1)S(1)}, bf16[1,56,1024]{2,1,0:T(8,128)(2,1)S(1)}, u32[]{:S(2)}, u32[]{:S(2)}) collective-permute-start(bf16[1,56,1024]{2,1,0:T(8,128)(2,1)S(1)} %get-tuple-element.70.unused), channel_id=1, source_target_pairs={{0,16},{8,24},{16,0},{24,8},{1,17},{9,25},{17,1},{25,9},{2,18},{10... | collective-permute-start | bytes 344072 | tf_op jit(solution)/shard_map/ppermute | solution.py:436
  41.2 18.5 %collective-permute-start.10 = (f32[1,72,1024]{2,1,0:T(8,128)S(1)}, f32[1,72,1024]{2,1,0:T(8,128)S(1)}, u32[]{:S(2)}, u32[]{:S(2)}) collective-permute-start(f32[1,72,1024]{2,1,0:T(8,128)S(1)} %get-tuple-element.67), channel_id=1, source_target_pairs={{0,8},{8,0},{16,24},{24,16},{1,9},{9,1},{17,25},{25,17},{2,10},{10... | collective-permute-start | bytes 884744 | tf_op jit(solution)/shard_map/ppermute | solution.py:433
  45.6 14.1 %collective-permute-start.11 = (f32[3,72,1024]{2,1,0:T(8,128)S(1)}, f32[3,72,1024]{2,1,0:T(8,128)S(1)}, u32[]{:S(2)}, u32[]{:S(2)}) collective-permute-start(f32[3,72,1024]{2,1,0:T(8,128)S(1)} %get-tuple-element.68), channel_id=1, source_target_pairs={{0,8},{8,0},{16,24},{24,16},{1,9},{9,1},{17,25},{25,17},{2,10},{10... | collective-permute-start | bytes 2654216 | tf_op jit(solution)/shard_map/ppermute | solution.py:433
  46.7 14.6 %collective-permute-start.17 = (bf16[1,144,1024]{2,1,0:T(8,128)(2,1)S(1)}, bf16[1,144,1024]{2,1,0:T(8,128)(2,1)S(1)}, u32[]{:S(2)}, u32[]{:S(2)}) collective-permute-start(bf16[1,144,1024]{2,1,0:T(8,128)(2,1)S(1)} %get-tuple-element.73.unused), channel_id=1, source_target_pairs={{8,1},{1,8},{9,2},{2,9},{10,3},{3,10},{11,4},{4,11},{12,5},{5,12},... | collective-permute-start | bytes 884744 | tf_op jit(solution)/shard_map/ppermute | solution.py:439
  49.5 8.2 %collective-permute-start.15 = (bf16[1,144,1024]{2,1,0:T(8,128)(2,1)S(1)}, bf16[1,144,1024]{2,1,0:T(8,128)(2,1)S(1)}, u32[]{:S(2)}, u32[]{:S(2)}) collective-permute-start(bf16[1,144,1024]{2,1,0:T(8,128)(2,1)S(1)} %get-tuple-element.77), channel_id=1, source_target_pairs={{0,8},{8,0},{16,24},{24,16},{1,9},{9,1},{17,25},{25,17},{2,10},{10... | collective-permute-start | bytes 884744 | tf_op jit(solution)/shard_map/ppermute | solution.py:433
  59.3 3.5 %collective-permute-start.16 = (f32[4,72,1024]{2,1,0:T(8,128)S(1)}, f32[4,72,1024]{2,1,0:T(8,128)S(1)}, u32[]{:S(2)}, u32[]{:S(2)}) collective-permute-start(f32[4,72,1024]{2,1,0:T(8,128)S(1)} %get-tuple-element.80), channel_id=1, source_target_pairs={{0,8},{8,0},{16,24},{24,16},{1,9},{9,1},{17,25},{25,17},{2,10},{10... | collective-permute-start | bytes 3538952 | tf_op jit(solution)/shard_map/ppermute | solution.py:433
  61.4 1.4 %collective-permute-start.18 = (bf16[72,1024]{1,0:T(8,128)(2,1)S(1)}, bf16[72,1024]{1,0:T(8,128)(2,1)S(1)}, u32[]{:S(2)}, u32[]{:S(2)}) collective-permute-start(bf16[72,1024]{1,0:T(8,128)(2,1)S(1)} %shard_map.106), channel_id=1, source_target_pairs={{0,8},{8,0},{16,24},{24,16},{1,9},{9,1},{17,25},{25,17},{2,10},{10... | collective-permute-start | bytes 442376 | tf_op jit(solution)/shard_map/ppermute | solution.py:433
  (2 other events, 6.8 us)

commit v10 on v9

--- a/solution.py
+++ b/solution.py
@@ -13,6 +13,7 @@
 NT = (((1,), (1,)), ((), ()))
 STEP = 16
 CHUNK = 8
+PIECES = 3
 EARLY = 0.01
 
 
@@ -121,10 +122,16 @@
 
 def edge_kernel(field, near, far, lines, arrived):
     rows = field.shape[1]
-    copies = [
-        pltpu.make_async_copy(field.at[:, row, :], lines.at[k], arrived.at[k])
-        for k, row in enumerate((0, rows - 1))
-    ]
+    step = field.shape[0] // PIECES
+    copies = []
+    for k, row in enumerate((0, rows - 1)):
+        for piece in range(PIECES):
+            cut = pl.ds(piece * step, step)
+            copies.append(
+                pltpu.make_async_copy(
+                    field.at[cut, row, :], lines.at[k, cut, :], arrived.at[k * PIECES + piece]
+                )
+            )
     for copy in copies:
         copy.start()
     for copy in copies:
@@ -316,7 +323,7 @@
         bent[0, cut, :] = value.astype(BF16)
         return carry
 
-    lax.fori_loop(0, pair // STEP, chunk, 0, unroll=3)
+    lax.fori_loop(0, pair // STEP, chunk, 0, unroll=9)
     fill_buffer(bent, stiff, send_table, buffer, 0, row_place(0, stiff.shape[1]))
 
 
@@ -459,7 +466,7 @@
     near_edge, far_edge = call(
         edge_kernel,
         (row_block, row_block),
-        [pltpu.VMEM((2, own, width), F32), pltpu.SemaphoreType.DMA((2,))],
+        [pltpu.VMEM((2, own, width), F32), pltpu.SemaphoreType.DMA((2 * PIECES,))],
         2.0,
         [ANY],
         60,
@@ -546,7 +553,7 @@
     cross_out = by_chip(buffer_out)
     keep_out, send_out, bent_one, buffer_one = call(
         second_next_kernel, outs(1) + bents(1), (), EARLY, [VMEM] * 4 + [ANY]
-    )(zero, held, stiffness, send_table, buffer_out)
+    )(zero, held, stiffness, send_table, cross_in)
     cross_one = by_chip(buffer_one)
     got_out = by_core(send_out)
     moment_out, edge_zero = couple(bent_out, cross_out, 0, 0, (), buffer_one)

time: 64.8 us -> 63.3 us (0.977)
  starting transfers between devices: 30.3 us -> 29.1 us
    ppermute x8, starting transfers between devices: 20.4 us -> 18.1 us  [by_core(): return lax.ppermute(value, 'chaos', core_swap)]
    ppermute x6, starting transfers between devices: 6.39 us -> 7.46 us  [by_chip(): return lax.ppermute(value, 'chaos', chip_swap)]
  transfers between devices with their start and end apart: 19 -> 19, of which waited for: 4 -> 4; matrix products, arithmetic and copies ran while one was open for 0% -> 0% of each run, Pallas kernels for 38% -> 40%
where the time goes in v10:
time: 63.3 us; the launch traced here: 63.1 us
  Pallas kernels  29.3 us (46%)
  starting transfers between devices  29.1 us (46%)
  waiting for transfers between devices  3.26 us (5%)
  between operations  1.28 us (2%)
    ppermute x8, starting transfers between devices, by_core(): return lax.ppermute(value, 'chaos', core_swap)  18.1 us
    pallas_call x6, Pallas kernels, couple(): call(functools.partial(couple_kernel, first, outer_row, inner_rows), tupl...  8.45 us
    ppermute x6, starting transfers between devices, by_chip(): return lax.ppermute(value, 'chaos', chip_swap)  7.46 us
    ppermute x5, starting transfers between devices, by_tile(): return lax.ppermute(value, ('chaos', 'tile'), tile_swap)  3.55 us
    pallas_call x2, Pallas kernels, bend(): call(functools.partial(first_kernel, first), bents(count), (), 0.9 * coun...  3.37 us
    pallas_call x1, Pallas kernels, body(): call(second_inner_kernel, (shape((4, pair, width), F32),) + bents(2), (),...  3 us
    pallas_call x1, Pallas kernels, body(): call(functools.partial(table_kernel, terms, pair, hubs, slot_total), (sha...  2.29 us
    pallas_call x1, Pallas kernels, body(): call(edge_kernel, (row_block, row_block), [pltpu.VMEM((2, own, width), F3...  2.28 us
  transfers between devices with their start and end apart: 19, of which 4 were waited for; matrix products, arithmetic and copies ran while one was open for 0% of the time, Pallas kernels for 40%

profile of v10, /device:TPU:0, one launch (start us, length us, event | category | flops | bytes accessed | tf_op | source)
XLA Modules:
  0.0 63.1 jit_solution(4206199967974924927)
XLA Ops:
  0.7 2.3 %shard_map.86 = (f32[72,1024]{1,0:T(8,128)}, f32[72,1024]{1,0:T(8,128)}) custom-call(f32[72,8,1024]{2,1,0:T(8,128)} %field.3), custom_call_target="tpu_custom_call" | custom-call | flops 20000000000 | bytes 10 | tf_op jit(solution)/shard_map/pallas_call | solution.py:466
  5.5 3.6 %collective-permute-start.1 = (f32[5,72,1024]{2,1,0:T(8,128)S(1)}, f32[5,72,1024]{2,1,0:T(8,128)S(1)}, u32[]{:S(2)}, u32[]{:S(2)}) collective-permute-start(f32[5,72,1024]{2,1,0:T(8,128)S(1)} %get-tuple-element.44), channel_id=1, source_target_pairs={{0,8},{8,0},{16,24},{24,16},{1,9},{9,1},{17,25},{25,17},{2,10},{10... | collective-permute-start | bytes 4423688 | tf_op jit(solution)/shard_map/ppermute | solution.py:440
  9.7 2.3 %shard_map.88 = (bf16[12,144,208]{2,1,0:T(8,128)(2,1)S(1)}, bf16[11,64,144]{2,1,0:T(8,128)(2,1)S(1)}) custom-call(f32[8,1664]{1,0:T(8,128)S(1)} %stack.31.entries, f32[72,1024]{1,0:T(8,128)S(1)} %collective-permute-done.unused), custom_call_target="tpu_custom_call" | custom-call | flops 30000001024 | bytes 10 | tf_op jit(solution)/shard_map/pallas_call | solution.py:478
  12.0 1.3 %shard_map.89 = (bf16[1,144,1024]{2,1,0:T(8,128)(2,1)S(1)}, bf16[1,56,1024]{2,1,0:T(8,128)(2,1)S(1)}) custom-call(f32[5,72,1024]{2,1,0:T(8,128)S(1)} %get-tuple-element.43.keep, f32[5,72,1024]{2,1,0:T(8,128)S(1)} %collective-permute-done.1.got.unused, f32[11,8,1024]{2,1,0:T(8,128)S(1)} %copy-done, bf16[11,64,144]{2,1,0:T(8,128)(2,1)S(1)} %get-tuple-element.45.send_table, ...), custom_call_target="tpu_custom_call" | custom-call | flops 8999999488 | bytes 10 | tf_op jit(solution)/shard_map/pallas_call | solution.py:504
  13.4 1.6 %collective-permute-start.4 = (bf16[1,56,1024]{2,1,0:T(8,128)(2,1)S(1)}, bf16[1,56,1024]{2,1,0:T(8,128)(2,1)S(1)}, u32[]{:S(2)}, u32[]{:S(2)}) collective-permute-start(bf16[1,56,1024]{2,1,0:T(8,128)(2,1)S(1)} %get-tuple-element.46.unused), channel_id=1, source_target_pairs={{0,16},{8,24},{16,0},{24,8},{1,17},{9,25},{17,1},{25,9},{2,18},{10... | collective-permute-start | bytes 344072 | tf_op jit(solution)/shard_map/ppermute | solution.py:443
  14.9 2.0 %shard_map.90 = (bf16[2,144,1024]{2,1,0:T(8,128)(2,1)S(1)}, bf16[2,56,1024]{2,1,0:T(8,128)(2,1)S(1)}) custom-call(f32[5,72,1024]{2,1,0:T(8,128)S(1)} %get-tuple-element.43.keep, f32[5,72,1024]{2,1,0:T(8,128)S(1)} %collective-permute-done.1.got.unused, f32[11,8,1024]{2,1,0:T(8,128)S(1)} %copy-done, bf16[11,64,144]{2,1,0:T(8,128)(2,1)S(1)} %get-tuple-element.45.send_table, ...), custom_call_target="tpu_custom_call" | custom-call | flops 17999998976 | bytes 10 | tf_op jit(solution)/shard_map/pallas_call | solution.py:504
  18.3 1.1 %shard_map.92 = (f32[1,144,1024]{2,1,0:T(8,128)S(1)}, bf16[1,144,1024]{2,1,0:T(8,128)(2,1)S(1)}) custom-call(bf16[1,144,1024]{2,1,0:T(8,128)(2,1)S(1)} %get-tuple-element.49.bent, bf16[1,56,1024]{2,1,0:T(8,128)(2,1)S(1)} %collective-permute-done.4.got, f32[11,8,1024]{2,1,0:T(8,128)S(1)} %copy-done, bf16[12,144,208]{2,1,0:T(8,128)(2,1)S(1)} %get-tuple-element.50.table, ...), custom_call_target="tpu_custom_call" | custom-call | flops 10000000000 | bytes 10 | tf_op jit(solution)/shard_map/pallas_call | solution.py:516
  20.1 1.6 %collective-permute-start.5 = (bf16[1,56,1024]{2,1,0:T(8,128)(2,1)S(1)}, bf16[1,56,1024]{2,1,0:T(8,128)(2,1)S(1)}, u32[]{:S(2)}, u32[]{:S(2)}) collective-permute-start(bf16[1,56,1024]{2,1,0:T(8,128)(2,1)S(1)} %get-tuple-element.53.unused), channel_id=1, source_target_pairs={{0,16},{8,24},{16,0},{24,8},{1,17},{9,25},{17,1},{25,9},{2,18},{10... | collective-permute-start | bytes 344072 | tf_op jit(solution)/shard_map/ppermute | solution.py:443
  22.3 1.5 %collective-permute-done.6.got = bf16[2,56,1024]{2,1,0:T(8,128)(2,1)S(1)} collective-permute-done((bf16[2,56,1024]{2,1,0:T(8,128)(2,1)S(1)}, bf16[2,56,1024]{2,1,0:T(8,128)(2,1)S(1)}, u32[]{:S(2)}, u32[]{:S(2)}) %collective-permute-start.6) | collective-permute-done | bytes 229408 | tf_op jit(solution)/shard_map/ppermute | solution.py:443
  23.8 2.0 %shard_map.95 = (f32[2,144,1024]{2,1,0:T(8,128)S(1)}, bf16[2,144,1024]{2,1,0:T(8,128)(2,1)S(1)}) custom-call(bf16[2,144,1024]{2,1,0:T(8,128)(2,1)S(1)} %get-tuple-element.54.bent, bf16[2,56,1024]{2,1,0:T(8,128)(2,1)S(1)} %collective-permute-done.6.got, f32[11,8,1024]{2,1,0:T(8,128)S(1)} %copy-done, bf16[12,144,208]{2,1,0:T(8,128)(2,1)S(1)} %get-tuple-element.50.table, ...), custom_call_target="tpu_custom_call" | custom-call | flops 20000000000 | bytes 10 | tf_op jit(solution)/shard_map/pallas_call | solution.py:516
  25.8 4.3 %collective-permute-start.7 = (bf16[2,144,1024]{2,1,0:T(8,128)(2,1)S(1)}, bf16[2,144,1024]{2,1,0:T(8,128)(2,1)S(1)}, u32[]{:S(2)}, u32[]{:S(2)}) collective-permute-start(bf16[2,144,1024]{2,1,0:T(8,128)(2,1)S(1)} %get-tuple-element.55.unused), channel_id=1, source_target_pairs={{0,8},{8,0},{16,24},{24,16},{1,9},{9,1},{17,25},{25,17},{2,10},{10... | collective-permute-start | bytes 1769480 | tf_op jit(solution)/shard_map/ppermute | solution.py:440
  30.1 1.1 %shard_map.96 = (f32[1,144,1024]{2,1,0:T(8,128)S(1)}, bf16[1,144,1024]{2,1,0:T(8,128)(2,1)S(1)}) custom-call(bf16[1,144,1024]{2,1,0:T(8,128)(2,1)S(1)} %get-tuple-element.52.bent, bf16[1,56,1024]{2,1,0:T(8,128)(2,1)S(1)} %collective-permute-done.5.got, f32[11,8,1024]{2,1,0:T(8,128)S(1)} %copy-done, bf16[12,144,208]{2,1,0:T(8,128)(2,1)S(1)} %get-tuple-element.50.table, ...), custom_call_target="tpu_custom_call" | custom-call | flops 10000000000 | bytes 10 | tf_op jit(solution)/shard_map/pallas_call | solution.py:516
  32.1 3.0 %shard_map.97 = (f32[4,144,1024]{2,1,0:T(8,128)S(1)}, bf16[2,144,1024]{2,1,0:T(8,128)(2,1)S(1)}, bf16[2,56,1024]{2,1,0:T(8,128)(2,1)S(1)}) custom-call(f32[1,144,1024]{2,1,0:T(8,128)S(1)} %get-tuple-element.56.row_zero, f32[1,144,1024]{2,1,0:T(8,128)S(1)} %get-tuple-element.57.row_one, f32[2,144,1024]{2,1,0:T(8,128)S(1)} %get-tuple-element.58.others, ...), custom_call_target="tpu_custom_call" | custom-call | flops 27000000512 | bytes 10 | tf_op jit(solution)/shard_map/pallas_call | solution.py:542
  35.7 1.4 %shard_map.98 = (f32[1,144,1024]{2,1,0:T(8,128)S(1)}, f32[1,144,1024]{2,1,0:T(8,128)S(1)}, f32[3,72,1024]{2,1,0:T(8,128)S(1)}, f32[3,72,1024]{2,1,0:T(8,128)S(1)}) custom-call(f32[1,144,1024]{2,1,0:T(8,128)S(1)} %get-tuple-element.56.row_zero, f32[1,144,1024]{2,1,0:T(8,128)S(1)} %get-tuple-element.57.row_one, f32[4,144,1024]{2,1,0:T(8,128)S(1)} %get-tuple-element.59.held), custom_call_target="tpu_custom_call" | custom-call | flops 30000001024 | bytes 10 | tf_op jit(solution)/shard_map/pallas_call | solution.py:545
  37.9 1.6 %collective-permute-start.13 = (bf16[1,56,1024]{2,1,0:T(8,128)(2,1)S(1)}, bf16[1,56,1024]{2,1,0:T(8,128)(2,1)S(1)}, u32[]{:S(2)}, u32[]{:S(2)}) collective-permute-start(bf16[1,56,1024]{2,1,0:T(8,128)(2,1)S(1)} %get-tuple-element.70), channel_id=1, source_target_pairs={{0,16},{8,24},{16,0},{24,8},{1,17},{9,25},{17,1},{25,9},{2,18},{10... | collective-permute-start | bytes 344072 | tf_op jit(solution)/shard_map/ppermute | solution.py:443
  39.5 3.4 %collective-permute-start.12 = (f32[3,72,1024]{2,1,0:T(8,128)S(1)}, f32[3,72,1024]{2,1,0:T(8,128)S(1)}, u32[]{:S(2)}, u32[]{:S(2)}) collective-permute-start(f32[3,72,1024]{2,1,0:T(8,128)S(1)} %get-tuple-element.68), channel_id=1, source_target_pairs={{0,8},{8,0},{16,24},{24,16},{1,9},{9,1},{17,25},{25,17},{2,10},{10... | collective-permute-start | bytes 2654216 | tf_op jit(solution)/shard_map/ppermute | solution.py:440
  44.0 1.6 %collective-permute-start.14 = (bf16[1,56,1024]{2,1,0:T(8,128)(2,1)S(1)}, bf16[1,56,1024]{2,1,0:T(8,128)(2,1)S(1)}, u32[]{:S(2)}, u32[]{:S(2)}) collective-permute-start(bf16[1,56,1024]{2,1,0:T(8,128)(2,1)S(1)} %get-tuple-element.71.unused), channel_id=1, source_target_pairs={{0,16},{8,24},{16,0},{24,8},{1,17},{9,25},{17,1},{25,9},{2,18},{10... | collective-permute-start | bytes 344072 | tf_op jit(solution)/shard_map/ppermute | solution.py:443
  46.3 1.1 %shard_map.101 = (f32[1,144,1024]{2,1,0:T(8,128)S(1)}, bf16[1,144,1024]{2,1,0:T(8,128)(2,1)S(1)}) custom-call(bf16[1,144,1024]{2,1,0:T(8,128)(2,1)S(1)} %get-tuple-element.69.bent, bf16[1,56,1024]{2,1,0:T(8,128)(2,1)S(1)} %collective-permute-done.13.got, f32[11,8,1024]{2,1,0:T(8,128)S(1)} %copy-done, bf16[12,144,208]{2,1,0:T(8,128)(2,1)S(1)} %get-tuple-element.50.table, ...), custom_call_target="tpu_custom_call" | custom-call | flops 10000000000 | bytes 10 | tf_op jit(solution)/shard_map/pallas_call | solution.py:516
  48.1 2.0 %shard_map.103 = (f32[2,144,1024]{2,1,0:T(8,128)S(1)}, bf16[1,144,1024]{2,1,0:T(8,128)(2,1)S(1)}) custom-call(bf16[2,144,1024]{2,1,0:T(8,128)(2,1)S(1)} %get-tuple-element.75.bent, bf16[2,56,1024]{2,1,0:T(8,128)(2,1)S(1)} %collective-permute-done.10.unused.got, f32[11,8,1024]{2,1,0:T(8,128)S(1)} %copy-done, ...), custom_call_target="tpu_custom_call" | custom-call | flops 20000000000 | bytes 10 | tf_op jit(solution)/shard_map/pallas_call | solution.py:516
  50.1 4.9 %collective-permute-start.15 = (bf16[1,144,1024]{2,1,0:T(8,128)(2,1)S(1)}, bf16[1,144,1024]{2,1,0:T(8,128)(2,1)S(1)}, u32[]{:S(2)}, u32[]{:S(2)}) collective-permute-start(bf16[1,144,1024]{2,1,0:T(8,128)(2,1)S(1)} %get-tuple-element.77), channel_id=1, source_target_pairs={{0,8},{8,0},{16,24},{24,16},{1,9},{9,1},{17,25},{25,17},{2,10},{10... | collective-permute-start | bytes 884744 | tf_op jit(solution)/shard_map/ppermute | solution.py:440
  56.3 1.6 %shard_map.104 = (f32[4,72,1024]{2,1,0:T(8,128)S(1)}, f32[4,72,1024]{2,1,0:T(8,128)S(1)}) custom-call(f32[1,144,1024]{2,1,0:T(8,128)S(1)} %get-tuple-element.72.zero, f32[1,144,1024]{2,1,0:T(8,128)S(1)} %shard_map.102.one, f32[2,144,1024]{2,1,0:T(8,128)S(1)} %get-tuple-element.76.inners, bf16[1,144,1024]{2,1,0:T(8,128)(2,1)S(1)} %collective-permute-done.15.inner), custom_call_target="tpu_custom_call" | custom-call | flops 24999999488 | bytes 10 | tf_op jit(solution)/shard_map/pallas_call | solution.py:565
  58.3 1.5 %shard_map.105 = (f32[72,8,1024]{2,1,0:T(8,128)}, s32[8,128]{1,0:T(8,128)S(1)}) custom-call(f32[1,72,1024]{2,1,0:T(8,128)S(1)} %get-tuple-element.65.keep_zero, f32[3,72,1024]{2,1,0:T(8,128)S(1)} %get-tuple-element.66.keep, f32[1,72,1024]{2,1,0:T(8,128)S(1)} %collective-permute-done.11.got_zero, f32[3,72,1024]{2,1,0:T(8,128)S(1)} %collective-permute-done.12.got, ...), custom_call_target="tpu_custom_call" | custom-call | flops 19000000512 | bytes 10 | tf_op jit(solution)/shard_map/pallas_call | solution.py:571
  60.2 1.2 %collective-permute-done.18.far_halo = bf16[72,1024]{1,0:T(8,128)(2,1)S(1)} collective-permute-done((bf16[72,1024]{1,0:T(8,128)(2,1)S(1)}, bf16[72,1024]{1,0:T(8,128)(2,1)S(1)}, u32[]{:S(2)}, u32[]{:S(2)}) %collective-permute-start.18) | collective-permute-done | bytes 147488 | tf_op jit(solution)/shard_map/ppermute | solution.py:440
  61.4 1.5 %shard_map.107 = f32[72,8,1024]{2,1,0:T(8,128)} custom-call(f32[4,72,1024]{2,1,0:T(8,128)S(1)} %get-tuple-element.78.unused.keep, f32[4,72,1024]{2,1,0:T(8,128)S(1)} %collective-permute-done.16.got, bf16[1,144,1024]{2,1,0:T(8,128)(2,1)S(1)} %collective-permute-done.17.halo, bf16[72,1024]{1,0:T(8,128)(2,1)S(1)} %collective-permute-done.18.far_halo), custom_call_target="tpu_custom_call" | custom-call | flops 19000000512 | bytes 10 | tf_op jit(solution)/shard_map/pallas_call | solution.py:577
  (67 shorter events, 12.3 us)
Async XLA Ops:
  0.6 4.3 %copy-start.1 = (f32[72,8,1024]{2,1,0:T(8,128)S(1)}, f32[72,8,1024]{2,1,0:T(8,128)}, u32[]{:S(2)}) copy-start(f32[72,8,1024]{2,1,0:T(8,128)} %field.3) | copy-start | bytes 7077892
  0.7 3.6 %copy-start.3 = (s32[1606]{0:T(1024)S(1)}, s32[1606]{0:T(1024)}, u32[]{:S(2)}) copy-start(s32[1606]{0:T(1024)} %param.10) | copy-start | bytes 19276
  0.7 3.6 %copy-start.4 = (s32[1606]{0:T(1024)S(1)}, s32[1606]{0:T(1024)}, u32[]{:S(2)}) copy-start(s32[1606]{0:T(1024)} %param.11) | copy-start | bytes 19276
  0.7 3.7 %copy-start.5 = (bf16[1606]{0:T(1024)(128)(2,1)S(1)}, bf16[1606]{0:T(1024)(128)(2,1)}, u32[]{:S(2)}) copy-start(bf16[1606]{0:T(1024)(128)(2,1)} %param.12) | copy-start | bytes 9640
  3.0 1.9 %collective-permute-start = (f32[72,1024]{1,0:T(8,128)}, f32[72,1024]{1,0:T(8,128)S(1)}, u32[]{:S(2)}, u32[]{:S(2)}) collective-permute-start(f32[72,1024]{1,0:T(8,128)} %get-tuple-element.42), channel_id=1, source_target_pairs={{0,8},{8,0},{16,24},{24,16},{1,9},{9,1},{17,25},{25,17},{2,10},{10... | collective-permute-start | bytes 884744 | tf_op jit(solution)/shard_map/ppermute | solution.py:440
  3.5 15.9 %collective-permute-start.3 = (f32[72,1024]{1,0:T(8,128)}, f32[72,1024]{1,0:T(8,128)S(1)}, u32[]{:S(2)}, u32[]{:S(2)}) collective-permute-start(f32[72,1024]{1,0:T(8,128)} %get-tuple-element.48), channel_id=1, source_target_pairs={{8,1},{1,8},{9,2},{2,9},{10,3},{3,10},{11,4},{4,11},{12,5},{5,12},... | collective-permute-start | bytes 884744 | tf_op jit(solution)/shard_map/ppermute | solution.py:446
  5.4 6.6 %copy-start = (f32[11,8,1024]{2,1,0:T(8,128)S(1)}, f32[11,8,1024]{2,1,0:T(8,128)}, u32[]{:S(2)}) copy-start(f32[11,8,1024]{2,1,0:T(8,128)} %stiff.23) | copy-start | bytes 1081348
  5.5 6.5 %collective-permute-start.1 = (f32[5,72,1024]{2,1,0:T(8,128)S(1)}, f32[5,72,1024]{2,1,0:T(8,128)S(1)}, u32[]{:S(2)}, u32[]{:S(2)}) collective-permute-start(f32[5,72,1024]{2,1,0:T(8,128)S(1)} %get-tuple-element.44), channel_id=1, source_target_pairs={{0,8},{8,0},{16,24},{24,16},{1,9},{9,1},{17,25},{25,17},{2,10},{10... | collective-permute-start | bytes 4423688 | tf_op jit(solution)/shard_map/ppermute | solution.py:440
  9.0 10.4 %collective-permute-start.2 = (f32[72,1024]{1,0:T(8,128)S(1)}, f32[72,1024]{1,0:T(8,128)S(1)}, u32[]{:S(2)}, u32[]{:S(2)}) collective-permute-start(f32[72,1024]{1,0:T(8,128)S(1)} %collective-permute-done.unused), channel_id=1, source_target_pairs={{8,1},{1,8},{9,2},{2,9},{10,3},{3,10},{11,4},{4,11},{12,5},{5,12},... | collective-permute-start | bytes 884744 | tf_op jit(solution)/shard_map/ppermute | solution.py:446
  13.4 5.0 %collective-permute-start.4 = (bf16[1,56,1024]{2,1,0:T(8,128)(2,1)S(1)}, bf16[1,56,1024]{2,1,0:T(8,128)(2,1)S(1)}, u32[]{:S(2)}, u32[]{:S(2)}) collective-permute-start(bf16[1,56,1024]{2,1,0:T(8,128)(2,1)S(1)} %get-tuple-element.46.unused), channel_id=1, source_target_pairs={{0,16},{8,24},{16,0},{24,8},{1,17},{9,25},{17,1},{25,9},{2,18},{10... | collective-permute-start | bytes 344072 | tf_op jit(solution)/shard_map/ppermute | solution.py:443
  17.0 6.9 %collective-permute-start.6 = (bf16[2,56,1024]{2,1,0:T(8,128)(2,1)S(1)}, bf16[2,56,1024]{2,1,0:T(8,128)(2,1)S(1)}, u32[]{:S(2)}, u32[]{:S(2)}) collective-permute-start(bf16[2,56,1024]{2,1,0:T(8,128)(2,1)S(1)} %get-tuple-element.47.unused), channel_id=1, source_target_pairs={{0,16},{8,24},{16,0},{24,8},{1,17},{9,25},{17,1},{25,9},{2,18},{10... | collective-permute-start | bytes 688136 | tf_op jit(solution)/shard_map/ppermute | solution.py:443
  20.1 10.0 %collective-permute-start.5 = (bf16[1,56,1024]{2,1,0:T(8,128)(2,1)S(1)}, bf16[1,56,1024]{2,1,0:T(8,128)(2,1)S(1)}, u32[]{:S(2)}, u32[]{:S(2)}) collective-permute-start(bf16[1,56,1024]{2,1,0:T(8,128)(2,1)S(1)} %get-tuple-element.53.unused), channel_id=1, source_target_pairs={{0,16},{8,24},{16,0},{24,8},{1,17},{9,25},{17,1},{25,9},{2,18},{10... | collective-permute-start | bytes 344072 | tf_op jit(solution)/shard_map/ppermute | solution.py:443
  21.6 15.5 %collective-permute-start.9 = (bf16[1,144,1024]{2,1,0:T(8,128)(2,1)S(1)}, bf16[1,144,1024]{2,1,0:T(8,128)(2,1)S(1)}, u32[]{:S(2)}, u32[]{:S(2)}) collective-permute-start(bf16[1,144,1024]{2,1,0:T(8,128)(2,1)S(1)} %shard_map.94.unused), channel_id=1, source_target_pairs={{8,1},{1,8},{9,2},{2,9},{10,3},{3,10},{11,4},{4,11},{12,5},{5,12},... | collective-permute-start | bytes 884744 | tf_op jit(solution)/shard_map/ppermute | solution.py:446
  25.8 6.2 %collective-permute-start.7 = (bf16[2,144,1024]{2,1,0:T(8,128)(2,1)S(1)}, bf16[2,144,1024]{2,1,0:T(8,128)(2,1)S(1)}, u32[]{:S(2)}, u32[]{:S(2)}) collective-permute-start(bf16[2,144,1024]{2,1,0:T(8,128)(2,1)S(1)} %get-tuple-element.55.unused), channel_id=1, source_target_pairs={{0,8},{8,0},{16,24},{24,16},{1,9},{9,1},{17,25},{25,17},{2,10},{10... | collective-permute-start | bytes 1769480 | tf_op jit(solution)/shard_map/ppermute | solution.py:440
  31.2 5.9 %collective-permute-start.8 = (bf16[1,144,1024]{2,1,0:T(8,128)(2,1)S(1)}, bf16[1,144,1024]{2,1,0:T(8,128)(2,1)S(1)}, u32[]{:S(2)}, u32[]{:S(2)}) collective-permute-start(bf16[1,144,1024]{2,1,0:T(8,128)(2,1)S(1)} %get-tuple-element.62), channel_id=1, source_target_pairs={{8,1},{1,8},{9,2},{2,9},{10,3},{3,10},{11,4},{4,11},{12,5},{5,12},... | collective-permute-start | bytes 884744 | tf_op jit(solution)/shard_map/ppermute | solution.py:446
  35.1 7.8 %collective-permute-start.10 = (bf16[2,56,1024]{2,1,0:T(8,128)(2,1)S(1)}, bf16[2,56,1024]{2,1,0:T(8,128)(2,1)S(1)}, u32[]{:S(2)}, u32[]{:S(2)}) collective-permute-start(bf16[2,56,1024]{2,1,0:T(8,128)(2,1)S(1)} %get-tuple-element.64), channel_id=1, source_target_pairs={{0,16},{8,24},{16,0},{24,8},{1,17},{9,25},{17,1},{25,9},{2,18},{10... | collective-permute-start | bytes 688136 | tf_op jit(solution)/shard_map/ppermute | solution.py:443
  37.9 8.4 %collective-permute-start.13 = (bf16[1,56,1024]{2,1,0:T(8,128)(2,1)S(1)}, bf16[1,56,1024]{2,1,0:T(8,128)(2,1)S(1)}, u32[]{:S(2)}, u32[]{:S(2)}) collective-permute-start(bf16[1,56,1024]{2,1,0:T(8,128)(2,1)S(1)} %get-tuple-element.70), channel_id=1, source_target_pairs={{0,16},{8,24},{16,0},{24,8},{1,17},{9,25},{17,1},{25,9},{2,18},{10... | collective-permute-start | bytes 344072 | tf_op jit(solution)/shard_map/ppermute | solution.py:443
  39.5 18.9 %collective-permute-start.12 = (f32[3,72,1024]{2,1,0:T(8,128)S(1)}, f32[3,72,1024]{2,1,0:T(8,128)S(1)}, u32[]{:S(2)}, u32[]{:S(2)}) collective-permute-start(f32[3,72,1024]{2,1,0:T(8,128)S(1)} %get-tuple-element.68), channel_id=1, source_target_pairs={{0,8},{8,0},{16,24},{24,16},{1,9},{9,1},{17,25},{25,17},{2,10},{10... | collective-permute-start | bytes 2654216 | tf_op jit(solution)/shard_map/ppermute | solution.py:440
  44.0 11.1 %collective-permute-start.14 = (bf16[1,56,1024]{2,1,0:T(8,128)(2,1)S(1)}, bf16[1,56,1024]{2,1,0:T(8,128)(2,1)S(1)}, u32[]{:S(2)}, u32[]{:S(2)}) collective-permute-start(bf16[1,56,1024]{2,1,0:T(8,128)(2,1)S(1)} %get-tuple-element.71.unused), channel_id=1, source_target_pairs={{0,16},{8,24},{16,0},{24,8},{1,17},{9,25},{17,1},{25,9},{2,18},{10... | collective-permute-start | bytes 344072 | tf_op jit(solution)/shard_map/ppermute | solution.py:443
  45.6 12.8 %collective-permute-start.11 = (f32[1,72,1024]{2,1,0:T(8,128)S(1)}, f32[1,72,1024]{2,1,0:T(8,128)S(1)}, u32[]{:S(2)}, u32[]{:S(2)}) collective-permute-start(f32[1,72,1024]{2,1,0:T(8,128)S(1)} %get-tuple-element.67), channel_id=1, source_target_pairs={{0,8},{8,0},{16,24},{24,16},{1,9},{9,1},{17,25},{25,17},{2,10},{10... | collective-permute-start | bytes 884744 | tf_op jit(solution)/shard_map/ppermute | solution.py:440
  47.4 12.5 %collective-permute-start.17 = (bf16[1,144,1024]{2,1,0:T(8,128)(2,1)S(1)}, bf16[1,144,1024]{2,1,0:T(8,128)(2,1)S(1)}, u32[]{:S(2)}, u32[]{:S(2)}) collective-permute-start(bf16[1,144,1024]{2,1,0:T(8,128)(2,1)S(1)} %get-tuple-element.74.unused), channel_id=1, source_target_pairs={{8,1},{1,8},{9,2},{2,9},{10,3},{3,10},{11,4},{4,11},{12,5},{5,12},... | collective-permute-start | bytes 884744 | tf_op jit(solution)/shard_map/ppermute | solution.py:446
  50.1 6.1 %collective-permute-start.15 = (bf16[1,144,1024]{2,1,0:T(8,128)(2,1)S(1)}, bf16[1,144,1024]{2,1,0:T(8,128)(2,1)S(1)}, u32[]{:S(2)}, u32[]{:S(2)}) collective-permute-start(bf16[1,144,1024]{2,1,0:T(8,128)(2,1)S(1)} %get-tuple-element.77), channel_id=1, source_target_pairs={{0,8},{8,0},{16,24},{24,16},{1,9},{9,1},{17,25},{25,17},{2,10},{10... | collective-permute-start | bytes 884744 | tf_op jit(solution)/shard_map/ppermute | solution.py:440
  57.9 3.5 %collective-permute-start.16 = (f32[4,72,1024]{2,1,0:T(8,128)S(1)}, f32[4,72,1024]{2,1,0:T(8,128)S(1)}, u32[]{:S(2)}, u32[]{:S(2)}) collective-permute-start(f32[4,72,1024]{2,1,0:T(8,128)S(1)} %get-tuple-element.80), channel_id=1, source_target_pairs={{0,8},{8,0},{16,24},{24,16},{1,9},{9,1},{17,25},{25,17},{2,10},{10... | collective-permute-start | bytes 3538952 | tf_op jit(solution)/shard_map/ppermute | solution.py:440
  60.0 1.4 %collective-permute-start.18 = (bf16[72,1024]{1,0:T(8,128)(2,1)S(1)}, bf16[72,1024]{1,0:T(8,128)(2,1)S(1)}, u32[]{:S(2)}, u32[]{:S(2)}) collective-permute-start(bf16[72,1024]{1,0:T(8,128)(2,1)S(1)} %shard_map.106), channel_id=1, source_target_pairs={{0,8},{8,0},{16,24},{24,16},{1,9},{9,1},{17,25},{25,17},{2,10},{10... | collective-permute-start | bytes 442376 | tf_op jit(solution)/shard_map/ppermute | solution.py:440
  (2 other events, 7.1 us)

commit v11 on v10

--- a/solution.py
+++ b/solution.py
@@ -13,7 +13,7 @@
 NT = (((1,), (1,)), ((), ()))
 STEP = 16
 CHUNK = 8
-PIECES = 3
+PIECES = 1
 EARLY = 0.01
 
 
@@ -200,7 +200,7 @@
                 bent[row, far, :] = value.astype(BF16)
             return carry
 
-        lax.fori_loop(0, own // 8, chunk, 0, unroll=3)
+        lax.fori_loop(0, own // 8, chunk, 0, unroll=9)
     for row in range(count):
         fill_buffer(bent, stiff, send_table, buffer, row, row_place(first_row + row, stiff.shape[1]))
 
@@ -219,7 +219,7 @@
             base[pl.ds(group * own + at, 8), :] = across(here) + below
             return carry
 
-        lax.fori_loop(0, own // 8, chunk, 0, unroll=3)
+        lax.fori_loop(0, own // 8, chunk, 0, unroll=9)
 
 
 def first_outer_kernel(base, halo_near, halo_far, stiff, send_table, unused, bent, buffer):
@@ -288,7 +288,7 @@
             bent[row, cut, :] = value.astype(BF16)
         return carry
 
-    lax.fori_loop(0, pair // STEP, chunk, 0, unroll=3)
+    lax.fori_loop(0, pair // STEP, chunk, 0, unroll=9)
     for row in range(count):
         fill_buffer(bent, stiff, send_table, buffer, row, row_place(row + 2, stiff.shape[1]))
 
@@ -308,7 +308,7 @@
         ahead[0, cut, :] = five_point(outside, partial, held[0, cut, :])
         return carry
 
-    lax.fori_loop(0, pair // STEP, chunk, 0, unroll=3)
+    lax.fori_loop(0, pair // STEP, chunk, 0, unroll=9)
     share(held, keep, send, (0, 1, 2), pair // 2)
 
 
@@ -336,7 +336,7 @@
         bent[0, cut, :] = value.astype(BF16)
         return carry
 
-    lax.fori_loop(0, pair // STEP, chunk, 0, unroll=3)
+    lax.fori_loop(0, pair // STEP, chunk, 0, unroll=9)
     fill_buffer(bent, stiff, send_table, buffer, 0, row_place(1, stiff.shape[1]))
     share(zero, keep, send, (0,), pair // 2)
 
@@ -358,7 +358,7 @@
                 )
             return carry
 
-        lax.fori_loop(0, own // 8, chunk, 0, unroll=3)
+        lax.fori_loop(0, own // 8, chunk, 0, unroll=9)
 
 
 def write_tiles(near, far, out, lines, done):

time: 63.3 us -> 63.2 us (level)
  Pallas kernels: 29.3 us -> 26.2 us
  starting transfers between devices: 29.1 us -> 31.3 us
  waiting for transfers between devices: 3.26 us -> 4.09 us
    ppermute x8, starting transfers between devices: 18.1 us -> 20.1 us  [by_core(): return lax.ppermute(value, 'chaos', core_swap)]
    pallas_call x2, Pallas kernels: 3.37 us -> 2.16 us  [bend(): call(functools.partial(first_kernel, first), bents(count), (), 0.9 * coun...]
    ppermute x6, waiting for transfers between devices: 1.49 us -> 2.32 us  [by_chip(): return lax.ppermute(value, 'chaos', chip_swap)]
  transfers between devices with their start and end apart: 19 -> 19, of which waited for: 4 -> 5; matrix products, arithmetic and copies ran while one was open for 0% -> 0% of each run, Pallas kernels for 40% -> 36%
where the time goes in v11:
time: 63.2 us; the launch traced here: 63 us
  starting transfers between devices  31.3 us (50%)
  Pallas kernels  26.2 us (41%)
  waiting for transfers between devices  4.09 us (6%)
  between operations  1.27 us (2%)
    ppermute x8, starting transfers between devices, by_core(): return lax.ppermute(value, 'chaos', core_swap)  20.1 us
    pallas_call x6, Pallas kernels, couple(): call(functools.partial(couple_kernel, first, outer_row, inner_rows), tupl...  8.45 us
    ppermute x6, starting transfers between devices, by_chip(): return lax.ppermute(value, 'chaos', chip_swap)  7.6 us
    ppermute x5, starting transfers between devices, by_tile(): return lax.ppermute(value, ('chaos', 'tile'), tile_swap)  3.55 us
    pallas_call x1, Pallas kernels, body(): call(second_inner_kernel, (shape((4, pair, width), F32),) + bents(2), (),...  2.43 us
    ppermute x6, waiting for transfers between devices, by_chip(): return lax.ppermute(value, 'chaos', chip_swap)  2.32 us
    pallas_call x1, Pallas kernels, body(): call(functools.partial(table_kernel, terms, pair, hubs, slot_total), (sha...  2.29 us
    pallas_call x2, Pallas kernels, bend(): call(functools.partial(first_kernel, first), bents(count), (), 0.9 * coun...  2.16 us
  transfers between devices with their start and end apart: 19, of which 5 were waited for; matrix products, arithmetic and copies ran while one was open for 0% of the time, Pallas kernels for 36%

profile of v11, /device:TPU:0, one launch (start us, length us, event | category | flops | bytes accessed | tf_op | source)
XLA Modules:
  0.0 63.0 jit_solution(11755453800743207713)
XLA Ops:
  0.7 2.1 %shard_map.86 = (f32[72,1024]{1,0:T(8,128)}, f32[72,1024]{1,0:T(8,128)}) custom-call(f32[72,8,1024]{2,1,0:T(8,128)} %field.3), custom_call_target="tpu_custom_call" | custom-call | flops 20000000000 | bytes 10 | tf_op jit(solution)/shard_map/pallas_call | solution.py:466
  5.3 3.6 %collective-permute-start.1 = (f32[5,72,1024]{2,1,0:T(8,128)S(1)}, f32[5,72,1024]{2,1,0:T(8,128)S(1)}, u32[]{:S(2)}, u32[]{:S(2)}) collective-permute-start(f32[5,72,1024]{2,1,0:T(8,128)S(1)} %get-tuple-element.44), channel_id=1, source_target_pairs={{0,8},{8,0},{16,24},{24,16},{1,9},{9,1},{17,25},{25,17},{2,10},{10... | collective-permute-start | bytes 4423688 | tf_op jit(solution)/shard_map/ppermute | solution.py:440
  9.6 2.3 %shard_map.88 = (bf16[12,144,208]{2,1,0:T(8,128)(2,1)S(1)}, bf16[11,64,144]{2,1,0:T(8,128)(2,1)S(1)}) custom-call(f32[8,1664]{1,0:T(8,128)S(1)} %stack.31.entries, f32[72,1024]{1,0:T(8,128)S(1)} %collective-permute-done.unused), custom_call_target="tpu_custom_call" | custom-call | flops 30000001024 | bytes 10 | tf_op jit(solution)/shard_map/pallas_call | solution.py:478
  12.7 1.6 %collective-permute-start.4 = (bf16[1,56,1024]{2,1,0:T(8,128)(2,1)S(1)}, bf16[1,56,1024]{2,1,0:T(8,128)(2,1)S(1)}, u32[]{:S(2)}, u32[]{:S(2)}) collective-permute-start(bf16[1,56,1024]{2,1,0:T(8,128)(2,1)S(1)} %get-tuple-element.46.unused), channel_id=1, source_target_pairs={{0,16},{8,24},{16,0},{24,8},{1,17},{9,25},{17,1},{25,9},{2,18},{10... | collective-permute-start | bytes 344072 | tf_op jit(solution)/shard_map/ppermute | solution.py:443
  14.3 1.3 %shard_map.90 = (bf16[2,144,1024]{2,1,0:T(8,128)(2,1)S(1)}, bf16[2,56,1024]{2,1,0:T(8,128)(2,1)S(1)}) custom-call(f32[5,72,1024]{2,1,0:T(8,128)S(1)} %get-tuple-element.43.keep, f32[5,72,1024]{2,1,0:T(8,128)S(1)} %collective-permute-done.1.got.unused, f32[11,8,1024]{2,1,0:T(8,128)S(1)} %copy-done, bf16[11,64,144]{2,1,0:T(8,128)(2,1)S(1)} %get-tuple-element.45.send_table, ...), custom_call_target="tpu_custom_call" | custom-call | flops 17999998976 | bytes 10 | tf_op jit(solution)/shard_map/pallas_call | solution.py:504
  17.6 1.1 %shard_map.92 = (f32[1,144,1024]{2,1,0:T(8,128)S(1)}, bf16[1,144,1024]{2,1,0:T(8,128)(2,1)S(1)}) custom-call(bf16[1,144,1024]{2,1,0:T(8,128)(2,1)S(1)} %get-tuple-element.49.bent, bf16[1,56,1024]{2,1,0:T(8,128)(2,1)S(1)} %collective-permute-done.4.got, f32[11,8,1024]{2,1,0:T(8,128)S(1)} %copy-done, bf16[12,144,208]{2,1,0:T(8,128)(2,1)S(1)} %get-tuple-element.50.table, ...), custom_call_target="tpu_custom_call" | custom-call | flops 10000000000 | bytes 10 | tf_op jit(solution)/shard_map/pallas_call | solution.py:516
  19.3 1.6 %collective-permute-start.5 = (bf16[1,56,1024]{2,1,0:T(8,128)(2,1)S(1)}, bf16[1,56,1024]{2,1,0:T(8,128)(2,1)S(1)}, u32[]{:S(2)}, u32[]{:S(2)}) collective-permute-start(bf16[1,56,1024]{2,1,0:T(8,128)(2,1)S(1)} %get-tuple-element.53.unused), channel_id=1, source_target_pairs={{0,16},{8,24},{16,0},{24,8},{1,17},{9,25},{17,1},{25,9},{2,18},{10... | collective-permute-start | bytes 344072 | tf_op jit(solution)/shard_map/ppermute | solution.py:443
  21.6 1.3 %collective-permute-done.6.got = bf16[2,56,1024]{2,1,0:T(8,128)(2,1)S(1)} collective-permute-done((bf16[2,56,1024]{2,1,0:T(8,128)(2,1)S(1)}, bf16[2,56,1024]{2,1,0:T(8,128)(2,1)S(1)}, u32[]{:S(2)}, u32[]{:S(2)}) %collective-permute-start.6) | collective-permute-done | bytes 229408 | tf_op jit(solution)/shard_map/ppermute | solution.py:443
  22.9 2.0 %shard_map.95 = (f32[2,144,1024]{2,1,0:T(8,128)S(1)}, bf16[2,144,1024]{2,1,0:T(8,128)(2,1)S(1)}) custom-call(bf16[2,144,1024]{2,1,0:T(8,128)(2,1)S(1)} %get-tuple-element.54.bent, bf16[2,56,1024]{2,1,0:T(8,128)(2,1)S(1)} %collective-permute-done.6.got, f32[11,8,1024]{2,1,0:T(8,128)S(1)} %copy-done, bf16[12,144,208]{2,1,0:T(8,128)(2,1)S(1)} %get-tuple-element.50.table, ...), custom_call_target="tpu_custom_call" | custom-call | flops 20000000000 | bytes 10 | tf_op jit(solution)/shard_map/pallas_call | solution.py:516
  25.0 5.0 %collective-permute-start.7 = (bf16[2,144,1024]{2,1,0:T(8,128)(2,1)S(1)}, bf16[2,144,1024]{2,1,0:T(8,128)(2,1)S(1)}, u32[]{:S(2)}, u32[]{:S(2)}) collective-permute-start(bf16[2,144,1024]{2,1,0:T(8,128)(2,1)S(1)} %get-tuple-element.55.unused), channel_id=1, source_target_pairs={{0,8},{8,0},{16,24},{24,16},{1,9},{9,1},{17,25},{25,17},{2,10},{10... | collective-permute-start | bytes 1769480 | tf_op jit(solution)/shard_map/ppermute | solution.py:440
  30.0 1.1 %shard_map.96 = (f32[1,144,1024]{2,1,0:T(8,128)S(1)}, bf16[1,144,1024]{2,1,0:T(8,128)(2,1)S(1)}) custom-call(bf16[1,144,1024]{2,1,0:T(8,128)(2,1)S(1)} %get-tuple-element.52.bent, bf16[1,56,1024]{2,1,0:T(8,128)(2,1)S(1)} %collective-permute-done.5.got, f32[11,8,1024]{2,1,0:T(8,128)S(1)} %copy-done, bf16[12,144,208]{2,1,0:T(8,128)(2,1)S(1)} %get-tuple-element.50.table, ...), custom_call_target="tpu_custom_call" | custom-call | flops 10000000000 | bytes 10 | tf_op jit(solution)/shard_map/pallas_call | solution.py:516
  31.9 2.4 %shard_map.97 = (f32[4,144,1024]{2,1,0:T(8,128)S(1)}, bf16[2,144,1024]{2,1,0:T(8,128)(2,1)S(1)}, bf16[2,56,1024]{2,1,0:T(8,128)(2,1)S(1)}) custom-call(f32[1,144,1024]{2,1,0:T(8,128)S(1)} %get-tuple-element.56.row_zero, f32[1,144,1024]{2,1,0:T(8,128)S(1)} %get-tuple-element.57.row_one, f32[2,144,1024]{2,1,0:T(8,128)S(1)} %get-tuple-element.58.others, ...), custom_call_target="tpu_custom_call" | custom-call | flops 27000000512 | bytes 10 | tf_op jit(solution)/shard_map/pallas_call | solution.py:542
  35.0 1.2 %shard_map.98 = (f32[1,144,1024]{2,1,0:T(8,128)S(1)}, f32[1,144,1024]{2,1,0:T(8,128)S(1)}, f32[3,72,1024]{2,1,0:T(8,128)S(1)}, f32[3,72,1024]{2,1,0:T(8,128)S(1)}) custom-call(f32[1,144,1024]{2,1,0:T(8,128)S(1)} %get-tuple-element.56.row_zero, f32[1,144,1024]{2,1,0:T(8,128)S(1)} %get-tuple-element.57.row_one, f32[4,144,1024]{2,1,0:T(8,128)S(1)} %get-tuple-element.59.held), custom_call_target="tpu_custom_call" | custom-call | flops 30000001024 | bytes 10 | tf_op jit(solution)/shard_map/pallas_call | solution.py:545
  37.0 1.5 %collective-permute-start.13 = (bf16[1,56,1024]{2,1,0:T(8,128)(2,1)S(1)}, bf16[1,56,1024]{2,1,0:T(8,128)(2,1)S(1)}, u32[]{:S(2)}, u32[]{:S(2)}) collective-permute-start(bf16[1,56,1024]{2,1,0:T(8,128)(2,1)S(1)} %get-tuple-element.70), channel_id=1, source_target_pairs={{0,16},{8,24},{16,0},{24,8},{1,17},{9,25},{17,1},{25,9},{2,18},{10... | collective-permute-start | bytes 344072 | tf_op jit(solution)/shard_map/ppermute | solution.py:443
  38.5 3.9 %collective-permute-start.12 = (f32[3,72,1024]{2,1,0:T(8,128)S(1)}, f32[3,72,1024]{2,1,0:T(8,128)S(1)}, u32[]{:S(2)}, u32[]{:S(2)}) collective-permute-start(f32[3,72,1024]{2,1,0:T(8,128)S(1)} %get-tuple-element.68), channel_id=1, source_target_pairs={{0,8},{8,0},{16,24},{24,16},{1,9},{9,1},{17,25},{25,17},{2,10},{10... | collective-permute-start | bytes 2654216 | tf_op jit(solution)/shard_map/ppermute | solution.py:440
  43.3 1.7 %collective-permute-start.14 = (bf16[1,56,1024]{2,1,0:T(8,128)(2,1)S(1)}, bf16[1,56,1024]{2,1,0:T(8,128)(2,1)S(1)}, u32[]{:S(2)}, u32[]{:S(2)}) collective-permute-start(bf16[1,56,1024]{2,1,0:T(8,128)(2,1)S(1)} %get-tuple-element.71.unused), channel_id=1, source_target_pairs={{0,16},{8,24},{16,0},{24,8},{1,17},{9,25},{17,1},{25,9},{2,18},{10... | collective-permute-start | bytes 344072 | tf_op jit(solution)/shard_map/ppermute | solution.py:443
  45.3 1.1 %shard_map.101 = (f32[1,144,1024]{2,1,0:T(8,128)S(1)}, bf16[1,144,1024]{2,1,0:T(8,128)(2,1)S(1)}) custom-call(bf16[1,144,1024]{2,1,0:T(8,128)(2,1)S(1)} %get-tuple-element.69.bent, bf16[1,56,1024]{2,1,0:T(8,128)(2,1)S(1)} %collective-permute-done.13.got, f32[11,8,1024]{2,1,0:T(8,128)S(1)} %copy-done, bf16[12,144,208]{2,1,0:T(8,128)(2,1)S(1)} %get-tuple-element.50.table, ...), custom_call_target="tpu_custom_call" | custom-call | flops 10000000000 | bytes 10 | tf_op jit(solution)/shard_map/pallas_call | solution.py:516
  47.1 2.0 %shard_map.103 = (f32[2,144,1024]{2,1,0:T(8,128)S(1)}, bf16[1,144,1024]{2,1,0:T(8,128)(2,1)S(1)}) custom-call(bf16[2,144,1024]{2,1,0:T(8,128)(2,1)S(1)} %get-tuple-element.75.bent, bf16[2,56,1024]{2,1,0:T(8,128)(2,1)S(1)} %collective-permute-done.10.unused.got, f32[11,8,1024]{2,1,0:T(8,128)S(1)} %copy-done, ...), custom_call_target="tpu_custom_call" | custom-call | flops 20000000000 | bytes 10 | tf_op jit(solution)/shard_map/pallas_call | solution.py:516
  49.1 6.2 %collective-permute-start.15 = (bf16[1,144,1024]{2,1,0:T(8,128)(2,1)S(1)}, bf16[1,144,1024]{2,1,0:T(8,128)(2,1)S(1)}, u32[]{:S(2)}, u32[]{:S(2)}) collective-permute-start(bf16[1,144,1024]{2,1,0:T(8,128)(2,1)S(1)} %get-tuple-element.77), channel_id=1, source_target_pairs={{0,8},{8,0},{16,24},{24,16},{1,9},{9,1},{17,25},{25,17},{2,10},{10... | collective-permute-start | bytes 884744 | tf_op jit(solution)/shard_map/ppermute | solution.py:440
  55.3 1.1 %shard_map.102.one = f32[1,144,1024]{2,1,0:T(8,128)S(1)} custom-call(bf16[1,144,1024]{2,1,0:T(8,128)(2,1)S(1)} %get-tuple-element.73.bent, bf16[1,56,1024]{2,1,0:T(8,128)(2,1)S(1)} %collective-permute-done.14.got, f32[11,8,1024]{2,1,0:T(8,128)S(1)} %copy-done, bf16[12,144,208]{2,1,0:T(8,128)(2,1)S(1)} %get-tuple-element.50.table, ...), custom_call_target="tpu_custom_call" | custom-call | flops 10000000000 | bytes 10 | tf_op jit(solution)/shard_map/pallas_call | solution.py:516
  56.5 1.3 %shard_map.104 = (f32[4,72,1024]{2,1,0:T(8,128)S(1)}, f32[4,72,1024]{2,1,0:T(8,128)S(1)}) custom-call(f32[1,144,1024]{2,1,0:T(8,128)S(1)} %get-tuple-element.72.zero, f32[1,144,1024]{2,1,0:T(8,128)S(1)} %shard_map.102.one, f32[2,144,1024]{2,1,0:T(8,128)S(1)} %get-tuple-element.76.inners, bf16[1,144,1024]{2,1,0:T(8,128)(2,1)S(1)} %collective-permute-done.15.inner), custom_call_target="tpu_custom_call" | custom-call | flops 24999999488 | bytes 10 | tf_op jit(solution)/shard_map/pallas_call | solution.py:565
  58.2 1.5 %shard_map.105 = (f32[72,8,1024]{2,1,0:T(8,128)}, s32[8,128]{1,0:T(8,128)S(1)}) custom-call(f32[1,72,1024]{2,1,0:T(8,128)S(1)} %get-tuple-element.65.keep_zero, f32[3,72,1024]{2,1,0:T(8,128)S(1)} %get-tuple-element.66.keep, f32[1,72,1024]{2,1,0:T(8,128)S(1)} %collective-permute-done.11.got_zero, f32[3,72,1024]{2,1,0:T(8,128)S(1)} %collective-permute-done.12.got, ...), custom_call_target="tpu_custom_call" | custom-call | flops 19000000512 | bytes 10 | tf_op jit(solution)/shard_map/pallas_call | solution.py:571
  60.1 1.2 %collective-permute-done.18.far_halo = bf16[72,1024]{1,0:T(8,128)(2,1)S(1)} collective-permute-done((bf16[72,1024]{1,0:T(8,128)(2,1)S(1)}, bf16[72,1024]{1,0:T(8,128)(2,1)S(1)}, u32[]{:S(2)}, u32[]{:S(2)}) %collective-permute-start.18) | collective-permute-done | bytes 147488 | tf_op jit(solution)/shard_map/ppermute | solution.py:440
  61.3 1.5 %shard_map.107 = f32[72,8,1024]{2,1,0:T(8,128)} custom-call(f32[4,72,1024]{2,1,0:T(8,128)S(1)} %get-tuple-element.78.unused.keep, f32[4,72,1024]{2,1,0:T(8,128)S(1)} %collective-permute-done.16.got, bf16[1,144,1024]{2,1,0:T(8,128)(2,1)S(1)} %collective-permute-done.17.halo, bf16[72,1024]{1,0:T(8,128)(2,1)S(1)} %collective-permute-done.18.far_halo), custom_call_target="tpu_custom_call" | custom-call | flops 19000000512 | bytes 10 | tf_op jit(solution)/shard_map/pallas_call | solution.py:577
  (67 shorter events, 11.9 us)
Async XLA Ops:
  0.6 4.1 %copy-start.1 = (f32[72,8,1024]{2,1,0:T(8,128)S(1)}, f32[72,8,1024]{2,1,0:T(8,128)}, u32[]{:S(2)}) copy-start(f32[72,8,1024]{2,1,0:T(8,128)} %field.3) | copy-start | bytes 7077892
  0.7 3.5 %copy-start.3 = (s32[1606]{0:T(1024)S(1)}, s32[1606]{0:T(1024)}, u32[]{:S(2)}) copy-start(s32[1606]{0:T(1024)} %param.10) | copy-start | bytes 19276
  0.7 3.5 %copy-start.4 = (s32[1606]{0:T(1024)S(1)}, s32[1606]{0:T(1024)}, u32[]{:S(2)}) copy-start(s32[1606]{0:T(1024)} %param.11) | copy-start | bytes 19276
  0.7 3.5 %copy-start.5 = (bf16[1606]{0:T(1024)(128)(2,1)S(1)}, bf16[1606]{0:T(1024)(128)(2,1)}, u32[]{:S(2)}) copy-start(bf16[1606]{0:T(1024)(128)(2,1)} %param.12) | copy-start | bytes 9640
  2.8 1.9 %collective-permute-start = (f32[72,1024]{1,0:T(8,128)}, f32[72,1024]{1,0:T(8,128)S(1)}, u32[]{:S(2)}, u32[]{:S(2)}) collective-permute-start(f32[72,1024]{1,0:T(8,128)} %get-tuple-element.42), channel_id=1, source_target_pairs={{0,8},{8,0},{16,24},{24,16},{1,9},{9,1},{17,25},{25,17},{2,10},{10... | collective-permute-start | bytes 884744 | tf_op jit(solution)/shard_map/ppermute | solution.py:440
  3.3 15.3 %collective-permute-start.3 = (f32[72,1024]{1,0:T(8,128)}, f32[72,1024]{1,0:T(8,128)S(1)}, u32[]{:S(2)}, u32[]{:S(2)}) collective-permute-start(f32[72,1024]{1,0:T(8,128)} %get-tuple-element.48), channel_id=1, source_target_pairs={{8,1},{1,8},{9,2},{2,9},{10,3},{3,10},{11,4},{4,11},{12,5},{5,12},... | collective-permute-start | bytes 884744 | tf_op jit(solution)/shard_map/ppermute | solution.py:446
  5.3 6.6 %copy-start = (f32[11,8,1024]{2,1,0:T(8,128)S(1)}, f32[11,8,1024]{2,1,0:T(8,128)}, u32[]{:S(2)}) copy-start(f32[11,8,1024]{2,1,0:T(8,128)} %stiff.23) | copy-start | bytes 1081348
  5.3 6.5 %collective-permute-start.1 = (f32[5,72,1024]{2,1,0:T(8,128)S(1)}, f32[5,72,1024]{2,1,0:T(8,128)S(1)}, u32[]{:S(2)}, u32[]{:S(2)}) collective-permute-start(f32[5,72,1024]{2,1,0:T(8,128)S(1)} %get-tuple-element.44), channel_id=1, source_target_pairs={{0,8},{8,0},{16,24},{24,16},{1,9},{9,1},{17,25},{25,17},{2,10},{10... | collective-permute-start | bytes 4423688 | tf_op jit(solution)/shard_map/ppermute | solution.py:440
  8.9 9.8 %collective-permute-start.2 = (f32[72,1024]{1,0:T(8,128)S(1)}, f32[72,1024]{1,0:T(8,128)S(1)}, u32[]{:S(2)}, u32[]{:S(2)}) collective-permute-start(f32[72,1024]{1,0:T(8,128)S(1)} %collective-permute-done.unused), channel_id=1, source_target_pairs={{8,1},{1,8},{9,2},{2,9},{10,3},{3,10},{11,4},{4,11},{12,5},{5,12},... | collective-permute-start | bytes 884744 | tf_op jit(solution)/shard_map/ppermute | solution.py:446
  12.7 4.9 %collective-permute-start.4 = (bf16[1,56,1024]{2,1,0:T(8,128)(2,1)S(1)}, bf16[1,56,1024]{2,1,0:T(8,128)(2,1)S(1)}, u32[]{:S(2)}, u32[]{:S(2)}) collective-permute-start(bf16[1,56,1024]{2,1,0:T(8,128)(2,1)S(1)} %get-tuple-element.46.unused), channel_id=1, source_target_pairs={{0,16},{8,24},{16,0},{24,8},{1,17},{9,25},{17,1},{25,9},{2,18},{10... | collective-permute-start | bytes 344072 | tf_op jit(solution)/shard_map/ppermute | solution.py:443
  15.6 7.3 %collective-permute-start.6 = (bf16[2,56,1024]{2,1,0:T(8,128)(2,1)S(1)}, bf16[2,56,1024]{2,1,0:T(8,128)(2,1)S(1)}, u32[]{:S(2)}, u32[]{:S(2)}) collective-permute-start(bf16[2,56,1024]{2,1,0:T(8,128)(2,1)S(1)} %get-tuple-element.47.unused), channel_id=1, source_target_pairs={{0,16},{8,24},{16,0},{24,8},{1,17},{9,25},{17,1},{25,9},{2,18},{10... | collective-permute-start | bytes 688136 | tf_op jit(solution)/shard_map/ppermute | solution.py:443
  19.3 10.7 %collective-permute-start.5 = (bf16[1,56,1024]{2,1,0:T(8,128)(2,1)S(1)}, bf16[1,56,1024]{2,1,0:T(8,128)(2,1)S(1)}, u32[]{:S(2)}, u32[]{:S(2)}) collective-permute-start(bf16[1,56,1024]{2,1,0:T(8,128)(2,1)S(1)} %get-tuple-element.53.unused), channel_id=1, source_target_pairs={{0,16},{8,24},{16,0},{24,8},{1,17},{9,25},{17,1},{25,9},{2,18},{10... | collective-permute-start | bytes 344072 | tf_op jit(solution)/shard_map/ppermute | solution.py:443
  20.9 15.3 %collective-permute-start.9 = (bf16[1,144,1024]{2,1,0:T(8,128)(2,1)S(1)}, bf16[1,144,1024]{2,1,0:T(8,128)(2,1)S(1)}, u32[]{:S(2)}, u32[]{:S(2)}) collective-permute-start(bf16[1,144,1024]{2,1,0:T(8,128)(2,1)S(1)} %shard_map.94.unused), channel_id=1, source_target_pairs={{8,1},{1,8},{9,2},{2,9},{10,3},{3,10},{11,4},{4,11},{12,5},{5,12},... | collective-permute-start | bytes 884744 | tf_op jit(solution)/shard_map/ppermute | solution.py:446
  25.0 7.0 %collective-permute-start.7 = (bf16[2,144,1024]{2,1,0:T(8,128)(2,1)S(1)}, bf16[2,144,1024]{2,1,0:T(8,128)(2,1)S(1)}, u32[]{:S(2)}, u32[]{:S(2)}) collective-permute-start(bf16[2,144,1024]{2,1,0:T(8,128)(2,1)S(1)} %get-tuple-element.55.unused), channel_id=1, source_target_pairs={{0,8},{8,0},{16,24},{24,16},{1,9},{9,1},{17,25},{25,17},{2,10},{10... | collective-permute-start | bytes 1769480 | tf_op jit(solution)/shard_map/ppermute | solution.py:440
  31.1 5.2 %collective-permute-start.8 = (bf16[1,144,1024]{2,1,0:T(8,128)(2,1)S(1)}, bf16[1,144,1024]{2,1,0:T(8,128)(2,1)S(1)}, u32[]{:S(2)}, u32[]{:S(2)}) collective-permute-start(bf16[1,144,1024]{2,1,0:T(8,128)(2,1)S(1)} %get-tuple-element.62), channel_id=1, source_target_pairs={{8,1},{1,8},{9,2},{2,9},{10,3},{3,10},{11,4},{4,11},{12,5},{5,12},... | collective-permute-start | bytes 884744 | tf_op jit(solution)/shard_map/ppermute | solution.py:446
  34.4 8.1 %collective-permute-start.10 = (bf16[2,56,1024]{2,1,0:T(8,128)(2,1)S(1)}, bf16[2,56,1024]{2,1,0:T(8,128)(2,1)S(1)}, u32[]{:S(2)}, u32[]{:S(2)}) collective-permute-start(bf16[2,56,1024]{2,1,0:T(8,128)(2,1)S(1)} %get-tuple-element.64), channel_id=1, source_target_pairs={{0,16},{8,24},{16,0},{24,8},{1,17},{9,25},{17,1},{25,9},{2,18},{10... | collective-permute-start | bytes 688136 | tf_op jit(solution)/shard_map/ppermute | solution.py:443
  37.0 8.3 %collective-permute-start.13 = (bf16[1,56,1024]{2,1,0:T(8,128)(2,1)S(1)}, bf16[1,56,1024]{2,1,0:T(8,128)(2,1)S(1)}, u32[]{:S(2)}, u32[]{:S(2)}) collective-permute-start(bf16[1,56,1024]{2,1,0:T(8,128)(2,1)S(1)} %get-tuple-element.70), channel_id=1, source_target_pairs={{0,16},{8,24},{16,0},{24,8},{1,17},{9,25},{17,1},{25,9},{2,18},{10... | collective-permute-start | bytes 344072 | tf_op jit(solution)/shard_map/ppermute | solution.py:443
  38.5 19.7 %collective-permute-start.12 = (f32[3,72,1024]{2,1,0:T(8,128)S(1)}, f32[3,72,1024]{2,1,0:T(8,128)S(1)}, u32[]{:S(2)}, u32[]{:S(2)}) collective-permute-start(f32[3,72,1024]{2,1,0:T(8,128)S(1)} %get-tuple-element.68), channel_id=1, source_target_pairs={{0,8},{8,0},{16,24},{24,16},{1,9},{9,1},{17,25},{25,17},{2,10},{10... | collective-permute-start | bytes 2654216 | tf_op jit(solution)/shard_map/ppermute | solution.py:440
  43.3 12.0 %collective-permute-start.14 = (bf16[1,56,1024]{2,1,0:T(8,128)(2,1)S(1)}, bf16[1,56,1024]{2,1,0:T(8,128)(2,1)S(1)}, u32[]{:S(2)}, u32[]{:S(2)}) collective-permute-start(bf16[1,56,1024]{2,1,0:T(8,128)(2,1)S(1)} %get-tuple-element.71.unused), channel_id=1, source_target_pairs={{0,16},{8,24},{16,0},{24,8},{1,17},{9,25},{17,1},{25,9},{2,18},{10... | collective-permute-start | bytes 344072 | tf_op jit(solution)/shard_map/ppermute | solution.py:443
  45.0 13.2 %collective-permute-start.11 = (f32[1,72,1024]{2,1,0:T(8,128)S(1)}, f32[1,72,1024]{2,1,0:T(8,128)S(1)}, u32[]{:S(2)}, u32[]{:S(2)}) collective-permute-start(f32[1,72,1024]{2,1,0:T(8,128)S(1)} %get-tuple-element.67), channel_id=1, source_target_pairs={{0,8},{8,0},{16,24},{24,16},{1,9},{9,1},{17,25},{25,17},{2,10},{10... | collective-permute-start | bytes 884744 | tf_op jit(solution)/shard_map/ppermute | solution.py:440
  46.4 13.4 %collective-permute-start.17 = (bf16[1,144,1024]{2,1,0:T(8,128)(2,1)S(1)}, bf16[1,144,1024]{2,1,0:T(8,128)(2,1)S(1)}, u32[]{:S(2)}, u32[]{:S(2)}) collective-permute-start(bf16[1,144,1024]{2,1,0:T(8,128)(2,1)S(1)} %get-tuple-element.74.unused), channel_id=1, source_target_pairs={{8,1},{1,8},{9,2},{2,9},{10,3},{3,10},{11,4},{4,11},{12,5},{5,12},... | collective-permute-start | bytes 884744 | tf_op jit(solution)/shard_map/ppermute | solution.py:446
  49.1 7.4 %collective-permute-start.15 = (bf16[1,144,1024]{2,1,0:T(8,128)(2,1)S(1)}, bf16[1,144,1024]{2,1,0:T(8,128)(2,1)S(1)}, u32[]{:S(2)}, u32[]{:S(2)}) collective-permute-start(bf16[1,144,1024]{2,1,0:T(8,128)(2,1)S(1)} %get-tuple-element.77), channel_id=1, source_target_pairs={{0,8},{8,0},{16,24},{24,16},{1,9},{9,1},{17,25},{25,17},{2,10},{10... | collective-permute-start | bytes 884744 | tf_op jit(solution)/shard_map/ppermute | solution.py:440
  57.8 3.5 %collective-permute-start.16 = (f32[4,72,1024]{2,1,0:T(8,128)S(1)}, f32[4,72,1024]{2,1,0:T(8,128)S(1)}, u32[]{:S(2)}, u32[]{:S(2)}) collective-permute-start(f32[4,72,1024]{2,1,0:T(8,128)S(1)} %get-tuple-element.80), channel_id=1, source_target_pairs={{0,8},{8,0},{16,24},{24,16},{1,9},{9,1},{17,25},{25,17},{2,10},{10... | collective-permute-start | bytes 3538952 | tf_op jit(solution)/shard_map/ppermute | solution.py:440
  59.9 1.4 %collective-permute-start.18 = (bf16[72,1024]{1,0:T(8,128)(2,1)S(1)}, bf16[72,1024]{1,0:T(8,128)(2,1)S(1)}, u32[]{:S(2)}, u32[]{:S(2)}) collective-permute-start(bf16[72,1024]{1,0:T(8,128)(2,1)S(1)} %shard_map.106), channel_id=1, source_target_pairs={{0,8},{8,0},{16,24},{24,16},{1,9},{9,1},{17,25},{25,17},{2,10},{10... | collective-permute-start | bytes 442376 | tf_op jit(solution)/shard_map/ppermute | solution.py:440
  (2 other events, 6.8 us)

commit v12 on v11

--- a/solution.py
+++ b/solution.py
@@ -170,13 +170,15 @@
 def fill_buffer(value_ref, stiff, send_table, buffer, row, place):
     hubs = buffer.shape[1]
     width = buffer.shape[2]
-    terms = send_table.shape[0]
+    terms, deep, pair = send_table.shape
+    lines = send_table[...].reshape(terms * deep, pair)
     for start in range(0, width, 256):
         cut = slice(start, start + 256)
         value = value_ref[row, :, cut]
-        total = jnp.dot(send_table[0], value, preferred_element_type=F32)
+        parts = jnp.dot(lines, value, preferred_element_type=F32)
+        total = parts[:deep]
         for mode in range(1, terms):
-            part = jnp.dot(send_table[mode], value, preferred_element_type=F32)
+            part = parts[mode * deep : (mode + 1) * deep]
             total = total + stiff[mode, pl.ds(place, 1), cut] * part
         buffer[row, :, cut] = total[:hubs].astype(BF16)
 

time: 63.2 us -> 63.1 us (level)
  transfers between devices with their start and end apart: 19 -> 19, of which waited for: 5 -> 5; matrix products, arithmetic and copies ran while one was open for 0% -> 0% of each run, Pallas kernels for 36% -> 35%
where the time goes in v12:
time: 63.1 us; the launch traced here: 62.9 us
  starting transfers between devices  31.1 us (49%)
  Pallas kernels  26 us (41%)
  waiting for transfers between devices  4.32 us (7%)
  between operations  1.27 us (2%)
    ppermute x8, starting transfers between devices, by_core(): return lax.ppermute(value, 'chaos', core_swap)  20 us
    pallas_call x6, Pallas kernels, couple(): call(functools.partial(couple_kernel, first, outer_row, inner_rows), tupl...  8.45 us
    ppermute x6, starting transfers between devices, by_chip(): return lax.ppermute(value, 'chaos', chip_swap)  7.59 us
    ppermute x5, starting transfers between devices, by_tile(): return lax.ppermute(value, ('chaos', 'tile'), tile_swap)  3.55 us
    ppermute x6, waiting for transfers between devices, by_chip(): return lax.ppermute(value, 'chaos', chip_swap)  2.56 us
    pallas_call x1, Pallas kernels, body(): call(second_inner_kernel, (shape((4, pair, width), F32),) + bents(2), (),...  2.41 us
    pallas_call x1, Pallas kernels, body(): call(functools.partial(table_kernel, terms, pair, hubs, slot_total), (sha...  2.29 us
    pallas_call x1, Pallas kernels, body(): call(edge_kernel, (row_block, row_block), [pltpu.VMEM((2, own, width), F3...  2.13 us
  transfers between devices with their start and end apart: 19, of which 5 were waited for; matrix products, arithmetic and copies ran while one was open for 0% of the time, Pallas kernels for 35%

profile of v12, /device:TPU:0, one launch (start us, length us, event | category | flops | bytes accessed | tf_op | source)
XLA Modules:
  0.0 62.9 jit_solution(18071265281647454834)
XLA Ops:
  0.7 2.1 %shard_map.86 = (f32[72,1024]{1,0:T(8,128)}, f32[72,1024]{1,0:T(8,128)}) custom-call(f32[72,8,1024]{2,1,0:T(8,128)} %field.3), custom_call_target="tpu_custom_call" | custom-call | flops 20000000000 | bytes 10 | tf_op jit(solution)/shard_map/pallas_call | solution.py:468
  5.3 3.6 %collective-permute-start.1 = (f32[5,72,1024]{2,1,0:T(8,128)S(1)}, f32[5,72,1024]{2,1,0:T(8,128)S(1)}, u32[]{:S(2)}, u32[]{:S(2)}) collective-permute-start(f32[5,72,1024]{2,1,0:T(8,128)S(1)} %get-tuple-element.44), channel_id=1, source_target_pairs={{0,8},{8,0},{16,24},{24,16},{1,9},{9,1},{17,25},{25,17},{2,10},{10... | collective-permute-start | bytes 4423688 | tf_op jit(solution)/shard_map/ppermute | solution.py:442
  9.6 2.3 %shard_map.88 = (bf16[12,144,208]{2,1,0:T(8,128)(2,1)S(1)}, bf16[11,64,144]{2,1,0:T(8,128)(2,1)S(1)}) custom-call(f32[8,1664]{1,0:T(8,128)S(1)} %stack.31.entries, f32[72,1024]{1,0:T(8,128)S(1)} %collective-permute-done.unused), custom_call_target="tpu_custom_call" | custom-call | flops 30000001024 | bytes 10 | tf_op jit(solution)/shard_map/pallas_call | solution.py:480
  12.7 1.5 %collective-permute-start.4 = (bf16[1,56,1024]{2,1,0:T(8,128)(2,1)S(1)}, bf16[1,56,1024]{2,1,0:T(8,128)(2,1)S(1)}, u32[]{:S(2)}, u32[]{:S(2)}) collective-permute-start(bf16[1,56,1024]{2,1,0:T(8,128)(2,1)S(1)} %get-tuple-element.46.unused), channel_id=1, source_target_pairs={{0,16},{8,24},{16,0},{24,8},{1,17},{9,25},{17,1},{25,9},{2,18},{10... | collective-permute-start | bytes 344072 | tf_op jit(solution)/shard_map/ppermute | solution.py:445
  14.2 1.2 %shard_map.90 = (bf16[2,144,1024]{2,1,0:T(8,128)(2,1)S(1)}, bf16[2,56,1024]{2,1,0:T(8,128)(2,1)S(1)}) custom-call(f32[5,72,1024]{2,1,0:T(8,128)S(1)} %get-tuple-element.43.keep, f32[5,72,1024]{2,1,0:T(8,128)S(1)} %collective-permute-done.1.got.unused, f32[11,8,1024]{2,1,0:T(8,128)S(1)} %copy-done, bf16[11,64,144]{2,1,0:T(8,128)(2,1)S(1)} %get-tuple-element.45.send_table, ...), custom_call_target="tpu_custom_call" | custom-call | flops 17999998976 | bytes 10 | tf_op jit(solution)/shard_map/pallas_call | solution.py:506
  17.5 1.1 %shard_map.92 = (f32[1,144,1024]{2,1,0:T(8,128)S(1)}, bf16[1,144,1024]{2,1,0:T(8,128)(2,1)S(1)}) custom-call(bf16[1,144,1024]{2,1,0:T(8,128)(2,1)S(1)} %get-tuple-element.49.bent, bf16[1,56,1024]{2,1,0:T(8,128)(2,1)S(1)} %collective-permute-done.4.got, f32[11,8,1024]{2,1,0:T(8,128)S(1)} %copy-done, bf16[12,144,208]{2,1,0:T(8,128)(2,1)S(1)} %get-tuple-element.50.table, ...), custom_call_target="tpu_custom_call" | custom-call | flops 10000000000 | bytes 10 | tf_op jit(solution)/shard_map/pallas_call | solution.py:518
  19.2 1.5 %collective-permute-start.5 = (bf16[1,56,1024]{2,1,0:T(8,128)(2,1)S(1)}, bf16[1,56,1024]{2,1,0:T(8,128)(2,1)S(1)}, u32[]{:S(2)}, u32[]{:S(2)}) collective-permute-start(bf16[1,56,1024]{2,1,0:T(8,128)(2,1)S(1)} %get-tuple-element.53.unused), channel_id=1, source_target_pairs={{0,16},{8,24},{16,0},{24,8},{1,17},{9,25},{17,1},{25,9},{2,18},{10... | collective-permute-start | bytes 344072 | tf_op jit(solution)/shard_map/ppermute | solution.py:445
  21.5 1.5 %collective-permute-done.6.got = bf16[2,56,1024]{2,1,0:T(8,128)(2,1)S(1)} collective-permute-done((bf16[2,56,1024]{2,1,0:T(8,128)(2,1)S(1)}, bf16[2,56,1024]{2,1,0:T(8,128)(2,1)S(1)}, u32[]{:S(2)}, u32[]{:S(2)}) %collective-permute-start.6) | collective-permute-done | bytes 229408 | tf_op jit(solution)/shard_map/ppermute | solution.py:445
  23.0 2.0 %shard_map.95 = (f32[2,144,1024]{2,1,0:T(8,128)S(1)}, bf16[2,144,1024]{2,1,0:T(8,128)(2,1)S(1)}) custom-call(bf16[2,144,1024]{2,1,0:T(8,128)(2,1)S(1)} %get-tuple-element.54.bent, bf16[2,56,1024]{2,1,0:T(8,128)(2,1)S(1)} %collective-permute-done.6.got, f32[11,8,1024]{2,1,0:T(8,128)S(1)} %copy-done, bf16[12,144,208]{2,1,0:T(8,128)(2,1)S(1)} %get-tuple-element.50.table, ...), custom_call_target="tpu_custom_call" | custom-call | flops 20000000000 | bytes 10 | tf_op jit(solution)/shard_map/pallas_call | solution.py:518
  25.0 4.9 %collective-permute-start.7 = (bf16[2,144,1024]{2,1,0:T(8,128)(2,1)S(1)}, bf16[2,144,1024]{2,1,0:T(8,128)(2,1)S(1)}, u32[]{:S(2)}, u32[]{:S(2)}) collective-permute-start(bf16[2,144,1024]{2,1,0:T(8,128)(2,1)S(1)} %get-tuple-element.55.unused), channel_id=1, source_target_pairs={{0,8},{8,0},{16,24},{24,16},{1,9},{9,1},{17,25},{25,17},{2,10},{10... | collective-permute-start | bytes 1769480 | tf_op jit(solution)/shard_map/ppermute | solution.py:442
  29.9 1.1 %shard_map.96 = (f32[1,144,1024]{2,1,0:T(8,128)S(1)}, bf16[1,144,1024]{2,1,0:T(8,128)(2,1)S(1)}) custom-call(bf16[1,144,1024]{2,1,0:T(8,128)(2,1)S(1)} %get-tuple-element.52.bent, bf16[1,56,1024]{2,1,0:T(8,128)(2,1)S(1)} %collective-permute-done.5.got, f32[11,8,1024]{2,1,0:T(8,128)S(1)} %copy-done, bf16[12,144,208]{2,1,0:T(8,128)(2,1)S(1)} %get-tuple-element.50.table, ...), custom_call_target="tpu_custom_call" | custom-call | flops 10000000000 | bytes 10 | tf_op jit(solution)/shard_map/pallas_call | solution.py:518
  31.9 2.4 %shard_map.97 = (f32[4,144,1024]{2,1,0:T(8,128)S(1)}, bf16[2,144,1024]{2,1,0:T(8,128)(2,1)S(1)}, bf16[2,56,1024]{2,1,0:T(8,128)(2,1)S(1)}) custom-call(f32[1,144,1024]{2,1,0:T(8,128)S(1)} %get-tuple-element.56.row_zero, f32[1,144,1024]{2,1,0:T(8,128)S(1)} %get-tuple-element.57.row_one, f32[2,144,1024]{2,1,0:T(8,128)S(1)} %get-tuple-element.58.others, ...), custom_call_target="tpu_custom_call" | custom-call | flops 27000000512 | bytes 10 | tf_op jit(solution)/shard_map/pallas_call | solution.py:544
  34.9 1.2 %shard_map.98 = (f32[1,144,1024]{2,1,0:T(8,128)S(1)}, f32[1,144,1024]{2,1,0:T(8,128)S(1)}, f32[3,72,1024]{2,1,0:T(8,128)S(1)}, f32[3,72,1024]{2,1,0:T(8,128)S(1)}) custom-call(f32[1,144,1024]{2,1,0:T(8,128)S(1)} %get-tuple-element.56.row_zero, f32[1,144,1024]{2,1,0:T(8,128)S(1)} %get-tuple-element.57.row_one, f32[4,144,1024]{2,1,0:T(8,128)S(1)} %get-tuple-element.59.held), custom_call_target="tpu_custom_call" | custom-call | flops 30000001024 | bytes 10 | tf_op jit(solution)/shard_map/pallas_call | solution.py:547
  36.9 1.6 %collective-permute-start.13 = (bf16[1,56,1024]{2,1,0:T(8,128)(2,1)S(1)}, bf16[1,56,1024]{2,1,0:T(8,128)(2,1)S(1)}, u32[]{:S(2)}, u32[]{:S(2)}) collective-permute-start(bf16[1,56,1024]{2,1,0:T(8,128)(2,1)S(1)} %get-tuple-element.70), channel_id=1, source_target_pairs={{0,16},{8,24},{16,0},{24,8},{1,17},{9,25},{17,1},{25,9},{2,18},{10... | collective-permute-start | bytes 344072 | tf_op jit(solution)/shard_map/ppermute | solution.py:445
  38.5 3.9 %collective-permute-start.12 = (f32[3,72,1024]{2,1,0:T(8,128)S(1)}, f32[3,72,1024]{2,1,0:T(8,128)S(1)}, u32[]{:S(2)}, u32[]{:S(2)}) collective-permute-start(f32[3,72,1024]{2,1,0:T(8,128)S(1)} %get-tuple-element.68), channel_id=1, source_target_pairs={{0,8},{8,0},{16,24},{24,16},{1,9},{9,1},{17,25},{25,17},{2,10},{10... | collective-permute-start | bytes 2654216 | tf_op jit(solution)/shard_map/ppermute | solution.py:442
  43.2 1.7 %collective-permute-start.14 = (bf16[1,56,1024]{2,1,0:T(8,128)(2,1)S(1)}, bf16[1,56,1024]{2,1,0:T(8,128)(2,1)S(1)}, u32[]{:S(2)}, u32[]{:S(2)}) collective-permute-start(bf16[1,56,1024]{2,1,0:T(8,128)(2,1)S(1)} %get-tuple-element.71.unused), channel_id=1, source_target_pairs={{0,16},{8,24},{16,0},{24,8},{1,17},{9,25},{17,1},{25,9},{2,18},{10... | collective-permute-start | bytes 344072 | tf_op jit(solution)/shard_map/ppermute | solution.py:445
  45.2 1.1 %shard_map.101 = (f32[1,144,1024]{2,1,0:T(8,128)S(1)}, bf16[1,144,1024]{2,1,0:T(8,128)(2,1)S(1)}) custom-call(bf16[1,144,1024]{2,1,0:T(8,128)(2,1)S(1)} %get-tuple-element.69.bent, bf16[1,56,1024]{2,1,0:T(8,128)(2,1)S(1)} %collective-permute-done.13.got, f32[11,8,1024]{2,1,0:T(8,128)S(1)} %copy-done, bf16[12,144,208]{2,1,0:T(8,128)(2,1)S(1)} %get-tuple-element.50.table, ...), custom_call_target="tpu_custom_call" | custom-call | flops 10000000000 | bytes 10 | tf_op jit(solution)/shard_map/pallas_call | solution.py:518
  47.0 2.0 %shard_map.103 = (f32[2,144,1024]{2,1,0:T(8,128)S(1)}, bf16[1,144,1024]{2,1,0:T(8,128)(2,1)S(1)}) custom-call(bf16[2,144,1024]{2,1,0:T(8,128)(2,1)S(1)} %get-tuple-element.75.bent, bf16[2,56,1024]{2,1,0:T(8,128)(2,1)S(1)} %collective-permute-done.10.unused.got, f32[11,8,1024]{2,1,0:T(8,128)S(1)} %copy-done, ...), custom_call_target="tpu_custom_call" | custom-call | flops 20000000000 | bytes 10 | tf_op jit(solution)/shard_map/pallas_call | solution.py:518
  49.1 6.1 %collective-permute-start.15 = (bf16[1,144,1024]{2,1,0:T(8,128)(2,1)S(1)}, bf16[1,144,1024]{2,1,0:T(8,128)(2,1)S(1)}, u32[]{:S(2)}, u32[]{:S(2)}) collective-permute-start(bf16[1,144,1024]{2,1,0:T(8,128)(2,1)S(1)} %get-tuple-element.77), channel_id=1, source_target_pairs={{0,8},{8,0},{16,24},{24,16},{1,9},{9,1},{17,25},{25,17},{2,10},{10... | collective-permute-start | bytes 884744 | tf_op jit(solution)/shard_map/ppermute | solution.py:442
  55.2 1.1 %shard_map.102.one = f32[1,144,1024]{2,1,0:T(8,128)S(1)} custom-call(bf16[1,144,1024]{2,1,0:T(8,128)(2,1)S(1)} %get-tuple-element.73.bent, bf16[1,56,1024]{2,1,0:T(8,128)(2,1)S(1)} %collective-permute-done.14.got, f32[11,8,1024]{2,1,0:T(8,128)S(1)} %copy-done, bf16[12,144,208]{2,1,0:T(8,128)(2,1)S(1)} %get-tuple-element.50.table, ...), custom_call_target="tpu_custom_call" | custom-call | flops 10000000000 | bytes 10 | tf_op jit(solution)/shard_map/pallas_call | solution.py:518
  56.4 1.3 %shard_map.104 = (f32[4,72,1024]{2,1,0:T(8,128)S(1)}, f32[4,72,1024]{2,1,0:T(8,128)S(1)}) custom-call(f32[1,144,1024]{2,1,0:T(8,128)S(1)} %get-tuple-element.72.zero, f32[1,144,1024]{2,1,0:T(8,128)S(1)} %shard_map.102.one, f32[2,144,1024]{2,1,0:T(8,128)S(1)} %get-tuple-element.76.inners, bf16[1,144,1024]{2,1,0:T(8,128)(2,1)S(1)} %collective-permute-done.15.inner), custom_call_target="tpu_custom_call" | custom-call | flops 24999999488 | bytes 10 | tf_op jit(solution)/shard_map/pallas_call | solution.py:567
  58.1 1.5 %shard_map.105 = (f32[72,8,1024]{2,1,0:T(8,128)}, s32[8,128]{1,0:T(8,128)S(1)}) custom-call(f32[1,72,1024]{2,1,0:T(8,128)S(1)} %get-tuple-element.65.keep_zero, f32[3,72,1024]{2,1,0:T(8,128)S(1)} %get-tuple-element.66.keep, f32[1,72,1024]{2,1,0:T(8,128)S(1)} %collective-permute-done.11.got_zero, f32[3,72,1024]{2,1,0:T(8,128)S(1)} %collective-permute-done.12.got, ...), custom_call_target="tpu_custom_call" | custom-call | flops 19000000512 | bytes 10 | tf_op jit(solution)/shard_map/pallas_call | solution.py:573
  59.9 1.2 %collective-permute-done.18.far_halo = bf16[72,1024]{1,0:T(8,128)(2,1)S(1)} collective-permute-done((bf16[72,1024]{1,0:T(8,128)(2,1)S(1)}, bf16[72,1024]{1,0:T(8,128)(2,1)S(1)}, u32[]{:S(2)}, u32[]{:S(2)}) %collective-permute-start.18) | collective-permute-done | bytes 147488 | tf_op jit(solution)/shard_map/ppermute | solution.py:442
  61.2 1.5 %shard_map.107 = f32[72,8,1024]{2,1,0:T(8,128)} custom-call(f32[4,72,1024]{2,1,0:T(8,128)S(1)} %get-tuple-element.78.unused.keep, f32[4,72,1024]{2,1,0:T(8,128)S(1)} %collective-permute-done.16.got, bf16[1,144,1024]{2,1,0:T(8,128)(2,1)S(1)} %collective-permute-done.17.halo, bf16[72,1024]{1,0:T(8,128)(2,1)S(1)} %collective-permute-done.18.far_halo), custom_call_target="tpu_custom_call" | custom-call | flops 19000000512 | bytes 10 | tf_op jit(solution)/shard_map/pallas_call | solution.py:579
  (67 shorter events, 11.9 us)
Async XLA Ops:
  0.6 4.1 %copy-start.1 = (f32[72,8,1024]{2,1,0:T(8,128)S(1)}, f32[72,8,1024]{2,1,0:T(8,128)}, u32[]{:S(2)}) copy-start(f32[72,8,1024]{2,1,0:T(8,128)} %field.3) | copy-start | bytes 7077892
  0.7 3.5 %copy-start.3 = (s32[1606]{0:T(1024)S(1)}, s32[1606]{0:T(1024)}, u32[]{:S(2)}) copy-start(s32[1606]{0:T(1024)} %param.10) | copy-start | bytes 19276
  0.7 3.5 %copy-start.4 = (s32[1606]{0:T(1024)S(1)}, s32[1606]{0:T(1024)}, u32[]{:S(2)}) copy-start(s32[1606]{0:T(1024)} %param.11) | copy-start | bytes 19276
  0.7 3.5 %copy-start.5 = (bf16[1606]{0:T(1024)(128)(2,1)S(1)}, bf16[1606]{0:T(1024)(128)(2,1)}, u32[]{:S(2)}) copy-start(bf16[1606]{0:T(1024)(128)(2,1)} %param.12) | copy-start | bytes 9640
  2.8 1.9 %collective-permute-start = (f32[72,1024]{1,0:T(8,128)}, f32[72,1024]{1,0:T(8,128)S(1)}, u32[]{:S(2)}, u32[]{:S(2)}) collective-permute-start(f32[72,1024]{1,0:T(8,128)} %get-tuple-element.42), channel_id=1, source_target_pairs={{0,8},{8,0},{16,24},{24,16},{1,9},{9,1},{17,25},{25,17},{2,10},{10... | collective-permute-start | bytes 884744 | tf_op jit(solution)/shard_map/ppermute | solution.py:442
  3.3 15.3 %collective-permute-start.3 = (f32[72,1024]{1,0:T(8,128)}, f32[72,1024]{1,0:T(8,128)S(1)}, u32[]{:S(2)}, u32[]{:S(2)}) collective-permute-start(f32[72,1024]{1,0:T(8,128)} %get-tuple-element.48), channel_id=1, source_target_pairs={{8,1},{1,8},{9,2},{2,9},{10,3},{3,10},{11,4},{4,11},{12,5},{5,12},... | collective-permute-start | bytes 884744 | tf_op jit(solution)/shard_map/ppermute | solution.py:448
  5.3 6.6 %copy-start = (f32[11,8,1024]{2,1,0:T(8,128)S(1)}, f32[11,8,1024]{2,1,0:T(8,128)}, u32[]{:S(2)}) copy-start(f32[11,8,1024]{2,1,0:T(8,128)} %stiff.23) | copy-start | bytes 1081348
  5.3 6.5 %collective-permute-start.1 = (f32[5,72,1024]{2,1,0:T(8,128)S(1)}, f32[5,72,1024]{2,1,0:T(8,128)S(1)}, u32[]{:S(2)}, u32[]{:S(2)}) collective-permute-start(f32[5,72,1024]{2,1,0:T(8,128)S(1)} %get-tuple-element.44), channel_id=1, source_target_pairs={{0,8},{8,0},{16,24},{24,16},{1,9},{9,1},{17,25},{25,17},{2,10},{10... | collective-permute-start | bytes 4423688 | tf_op jit(solution)/shard_map/ppermute | solution.py:442
  8.9 9.8 %collective-permute-start.2 = (f32[72,1024]{1,0:T(8,128)S(1)}, f32[72,1024]{1,0:T(8,128)S(1)}, u32[]{:S(2)}, u32[]{:S(2)}) collective-permute-start(f32[72,1024]{1,0:T(8,128)S(1)} %collective-permute-done.unused), channel_id=1, source_target_pairs={{8,1},{1,8},{9,2},{2,9},{10,3},{3,10},{11,4},{4,11},{12,5},{5,12},... | collective-permute-start | bytes 884744 | tf_op jit(solution)/shard_map/ppermute | solution.py:448
  12.7 4.9 %collective-permute-start.4 = (bf16[1,56,1024]{2,1,0:T(8,128)(2,1)S(1)}, bf16[1,56,1024]{2,1,0:T(8,128)(2,1)S(1)}, u32[]{:S(2)}, u32[]{:S(2)}) collective-permute-start(bf16[1,56,1024]{2,1,0:T(8,128)(2,1)S(1)} %get-tuple-element.46.unused), channel_id=1, source_target_pairs={{0,16},{8,24},{16,0},{24,8},{1,17},{9,25},{17,1},{25,9},{2,18},{10... | collective-permute-start | bytes 344072 | tf_op jit(solution)/shard_map/ppermute | solution.py:445
  15.5 7.5 %collective-permute-start.6 = (bf16[2,56,1024]{2,1,0:T(8,128)(2,1)S(1)}, bf16[2,56,1024]{2,1,0:T(8,128)(2,1)S(1)}, u32[]{:S(2)}, u32[]{:S(2)}) collective-permute-start(bf16[2,56,1024]{2,1,0:T(8,128)(2,1)S(1)} %get-tuple-element.47.unused), channel_id=1, source_target_pairs={{0,16},{8,24},{16,0},{24,8},{1,17},{9,25},{17,1},{25,9},{2,18},{10... | collective-permute-start | bytes 688136 | tf_op jit(solution)/shard_map/ppermute | solution.py:445
  19.2 10.7 %collective-permute-start.5 = (bf16[1,56,1024]{2,1,0:T(8,128)(2,1)S(1)}, bf16[1,56,1024]{2,1,0:T(8,128)(2,1)S(1)}, u32[]{:S(2)}, u32[]{:S(2)}) collective-permute-start(bf16[1,56,1024]{2,1,0:T(8,128)(2,1)S(1)} %get-tuple-element.53.unused), channel_id=1, source_target_pairs={{0,16},{8,24},{16,0},{24,8},{1,17},{9,25},{17,1},{25,9},{2,18},{10... | collective-permute-start | bytes 344072 | tf_op jit(solution)/shard_map/ppermute | solution.py:445
  20.8 15.3 %collective-permute-start.9 = (bf16[1,144,1024]{2,1,0:T(8,128)(2,1)S(1)}, bf16[1,144,1024]{2,1,0:T(8,128)(2,1)S(1)}, u32[]{:S(2)}, u32[]{:S(2)}) collective-permute-start(bf16[1,144,1024]{2,1,0:T(8,128)(2,1)S(1)} %shard_map.94.unused), channel_id=1, source_target_pairs={{8,1},{1,8},{9,2},{2,9},{10,3},{3,10},{11,4},{4,11},{12,5},{5,12},... | collective-permute-start | bytes 884744 | tf_op jit(solution)/shard_map/ppermute | solution.py:448
  25.0 6.9 %collective-permute-start.7 = (bf16[2,144,1024]{2,1,0:T(8,128)(2,1)S(1)}, bf16[2,144,1024]{2,1,0:T(8,128)(2,1)S(1)}, u32[]{:S(2)}, u32[]{:S(2)}) collective-permute-start(bf16[2,144,1024]{2,1,0:T(8,128)(2,1)S(1)} %get-tuple-element.55.unused), channel_id=1, source_target_pairs={{0,8},{8,0},{16,24},{24,16},{1,9},{9,1},{17,25},{25,17},{2,10},{10... | collective-permute-start | bytes 1769480 | tf_op jit(solution)/shard_map/ppermute | solution.py:442
  31.0 5.1 %collective-permute-start.8 = (bf16[1,144,1024]{2,1,0:T(8,128)(2,1)S(1)}, bf16[1,144,1024]{2,1,0:T(8,128)(2,1)S(1)}, u32[]{:S(2)}, u32[]{:S(2)}) collective-permute-start(bf16[1,144,1024]{2,1,0:T(8,128)(2,1)S(1)} %get-tuple-element.62), channel_id=1, source_target_pairs={{8,1},{1,8},{9,2},{2,9},{10,3},{3,10},{11,4},{4,11},{12,5},{5,12},... | collective-permute-start | bytes 884744 | tf_op jit(solution)/shard_map/ppermute | solution.py:448
  34.3 8.1 %collective-permute-start.10 = (bf16[2,56,1024]{2,1,0:T(8,128)(2,1)S(1)}, bf16[2,56,1024]{2,1,0:T(8,128)(2,1)S(1)}, u32[]{:S(2)}, u32[]{:S(2)}) collective-permute-start(bf16[2,56,1024]{2,1,0:T(8,128)(2,1)S(1)} %get-tuple-element.64), channel_id=1, source_target_pairs={{0,16},{8,24},{16,0},{24,8},{1,17},{9,25},{17,1},{25,9},{2,18},{10... | collective-permute-start | bytes 688136 | tf_op jit(solution)/shard_map/ppermute | solution.py:445
  36.9 8.3 %collective-permute-start.13 = (bf16[1,56,1024]{2,1,0:T(8,128)(2,1)S(1)}, bf16[1,56,1024]{2,1,0:T(8,128)(2,1)S(1)}, u32[]{:S(2)}, u32[]{:S(2)}) collective-permute-start(bf16[1,56,1024]{2,1,0:T(8,128)(2,1)S(1)} %get-tuple-element.70), channel_id=1, source_target_pairs={{0,16},{8,24},{16,0},{24,8},{1,17},{9,25},{17,1},{25,9},{2,18},{10... | collective-permute-start | bytes 344072 | tf_op jit(solution)/shard_map/ppermute | solution.py:445
  38.5 19.6 %collective-permute-start.12 = (f32[3,72,1024]{2,1,0:T(8,128)S(1)}, f32[3,72,1024]{2,1,0:T(8,128)S(1)}, u32[]{:S(2)}, u32[]{:S(2)}) collective-permute-start(f32[3,72,1024]{2,1,0:T(8,128)S(1)} %get-tuple-element.68), channel_id=1, source_target_pairs={{0,8},{8,0},{16,24},{24,16},{1,9},{9,1},{17,25},{25,17},{2,10},{10... | collective-permute-start | bytes 2654216 | tf_op jit(solution)/shard_map/ppermute | solution.py:442
  43.2 12.0 %collective-permute-start.14 = (bf16[1,56,1024]{2,1,0:T(8,128)(2,1)S(1)}, bf16[1,56,1024]{2,1,0:T(8,128)(2,1)S(1)}, u32[]{:S(2)}, u32[]{:S(2)}) collective-permute-start(bf16[1,56,1024]{2,1,0:T(8,128)(2,1)S(1)} %get-tuple-element.71.unused), channel_id=1, source_target_pairs={{0,16},{8,24},{16,0},{24,8},{1,17},{9,25},{17,1},{25,9},{2,18},{10... | collective-permute-start | bytes 344072 | tf_op jit(solution)/shard_map/ppermute | solution.py:445
  44.9 13.2 %collective-permute-start.11 = (f32[1,72,1024]{2,1,0:T(8,128)S(1)}, f32[1,72,1024]{2,1,0:T(8,128)S(1)}, u32[]{:S(2)}, u32[]{:S(2)}) collective-permute-start(f32[1,72,1024]{2,1,0:T(8,128)S(1)} %get-tuple-element.67), channel_id=1, source_target_pairs={{0,8},{8,0},{16,24},{24,16},{1,9},{9,1},{17,25},{25,17},{2,10},{10... | collective-permute-start | bytes 884744 | tf_op jit(solution)/shard_map/ppermute | solution.py:442
  46.4 13.3 %collective-permute-start.17 = (bf16[1,144,1024]{2,1,0:T(8,128)(2,1)S(1)}, bf16[1,144,1024]{2,1,0:T(8,128)(2,1)S(1)}, u32[]{:S(2)}, u32[]{:S(2)}) collective-permute-start(bf16[1,144,1024]{2,1,0:T(8,128)(2,1)S(1)} %get-tuple-element.74.unused), channel_id=1, source_target_pairs={{8,1},{1,8},{9,2},{2,9},{10,3},{3,10},{11,4},{4,11},{12,5},{5,12},... | collective-permute-start | bytes 884744 | tf_op jit(solution)/shard_map/ppermute | solution.py:448
  49.1 7.3 %collective-permute-start.15 = (bf16[1,144,1024]{2,1,0:T(8,128)(2,1)S(1)}, bf16[1,144,1024]{2,1,0:T(8,128)(2,1)S(1)}, u32[]{:S(2)}, u32[]{:S(2)}) collective-permute-start(bf16[1,144,1024]{2,1,0:T(8,128)(2,1)S(1)} %get-tuple-element.77), channel_id=1, source_target_pairs={{0,8},{8,0},{16,24},{24,16},{1,9},{9,1},{17,25},{25,17},{2,10},{10... | collective-permute-start | bytes 884744 | tf_op jit(solution)/shard_map/ppermute | solution.py:442
  57.7 3.5 %collective-permute-start.16 = (f32[4,72,1024]{2,1,0:T(8,128)S(1)}, f32[4,72,1024]{2,1,0:T(8,128)S(1)}, u32[]{:S(2)}, u32[]{:S(2)}) collective-permute-start(f32[4,72,1024]{2,1,0:T(8,128)S(1)} %get-tuple-element.80), channel_id=1, source_target_pairs={{0,8},{8,0},{16,24},{24,16},{1,9},{9,1},{17,25},{25,17},{2,10},{10... | collective-permute-start | bytes 3538952 | tf_op jit(solution)/shard_map/ppermute | solution.py:442
  59.7 1.4 %collective-permute-start.18 = (bf16[72,1024]{1,0:T(8,128)(2,1)S(1)}, bf16[72,1024]{1,0:T(8,128)(2,1)S(1)}, u32[]{:S(2)}, u32[]{:S(2)}) collective-permute-start(bf16[72,1024]{1,0:T(8,128)(2,1)S(1)} %shard_map.106), channel_id=1, source_target_pairs={{0,8},{8,0},{16,24},{24,16},{1,9},{9,1},{17,25},{25,17},{2,10},{10... | collective-permute-start | bytes 442376 | tf_op jit(solution)/shard_map/ppermute | solution.py:442
  (2 other events, 6.8 us)

commit v13 on v12

--- a/solution.py
+++ b/solution.py
@@ -400,16 +400,17 @@
     return jnp.where(first, lower, upper), jnp.where(first, upper, lower)
 
 
-def cut_kernel(halo, unused, part):
-    part[...] = halves(halo, part.shape[0])[1].astype(BF16)
-
-
-def last_merge_kernel(keep, got, halo, far_halo, out, lines, done):
-    near_line = halves(halo, keep.shape[1])[0]
+def cut_kernel(halo, keep, unused, part, line):
+    near, far = halves(halo, part.shape[0])
+    part[...] = far.astype(BF16)
+    line[...] = keep[0] + near
+
+
+def last_merge_kernel(keep, got, line, far_halo, out, lines, done):
     far_line = far_halo[...].astype(F32)
 
     def near(i, cut):
-        return keep[0, cut, :] + near_line[cut] if i == 0 else keep[i, cut, :]
+        return line[cut, :] if i == 0 else keep[i, cut, :]
 
     def far(i, cut):
         return got[0, cut, :] + far_line[cut] if i == 0 else got[i, cut, :]
@@ -573,11 +574,12 @@
     first_apply, token = call(
         merge_kernel, (whole, TOKEN), writers, 1.9, [VMEM] * 4 + [ANY], 6, (ANY, VMEM)
     )(keep_out, keep_in, got_out, got_in, keep)
-    far_halo = by_core(
-        call(cut_kernel, shape((own, width), BF16), (), 0.3, [VMEM, ANY])(near, token)
-    )
+    part, line = call(
+        cut_kernel, (shape((own, width), BF16), row_block), (), 0.3, [VMEM, VMEM, ANY]
+    )(near, keep, token)
+    far_halo = by_core(part)
     second_apply = call(last_merge_kernel, whole, writers, 1.9, [VMEM] * 4, 6, ANY)(
-        keep, got, near, far_halo
+        keep, got, line, far_halo
     )
     return first_apply, second_apply
 

time: 63.1 us -> 63.2 us (level)
  transfers between devices with their start and end apart: 19 -> 19, of which waited for: 5 -> 5; matrix products, arithmetic and copies ran while one was open for 0% -> 0% of each run, Pallas kernels for 35% -> 36%
where the time goes in v13:
time: 63.2 us; the launch traced here: 62.9 us
  starting transfers between devices  31.1 us (49%)
  Pallas kernels  26 us (41%)
  waiting for transfers between devices  4.32 us (7%)
  between operations  1.27 us (2%)
    ppermute x8, starting transfers between devices, by_core(): return lax.ppermute(value, 'chaos', core_swap)  20 us
    pallas_call x6, Pallas kernels, couple(): call(functools.partial(couple_kernel, first, outer_row, inner_rows), tupl...  8.45 us
    ppermute x6, starting transfers between devices, by_chip(): return lax.ppermute(value, 'chaos', chip_swap)  7.59 us
    ppermute x5, starting transfers between devices, by_tile(): return lax.ppermute(value, ('chaos', 'tile'), tile_swap)  3.55 us
    ppermute x6, waiting for transfers between devices, by_chip(): return lax.ppermute(value, 'chaos', chip_swap)  2.56 us
    pallas_call x1, Pallas kernels, body(): call(second_inner_kernel, (shape((4, pair, width), F32),) + bents(2), (),...  2.41 us
    pallas_call x1, Pallas kernels, body(): call(functools.partial(table_kernel, terms, pair, hubs, slot_total), (sha...  2.29 us
    pallas_call x1, Pallas kernels, body(): call(edge_kernel, (row_block, row_block), [pltpu.VMEM((2, own, width), F3...  2.13 us
  transfers between devices with their start and end apart: 19, of which 5 were waited for; matrix products, arithmetic and copies ran while one was open for 0% of the time, Pallas kernels for 36%

profile of v13, /device:TPU:0, one launch (start us, length us, event | category | flops | bytes accessed | tf_op | source)
XLA Modules:
  0.0 62.9 jit_solution(2897812189616617723)
XLA Ops:
  0.7 2.1 %shard_map.86 = (f32[72,1024]{1,0:T(8,128)}, f32[72,1024]{1,0:T(8,128)}) custom-call(f32[72,8,1024]{2,1,0:T(8,128)} %field.3), custom_call_target="tpu_custom_call" | custom-call | flops 20000000000 | bytes 10 | tf_op jit(solution)/shard_map/pallas_call | solution.py:469
  5.3 3.6 %collective-permute-start.1 = (f32[5,72,1024]{2,1,0:T(8,128)S(1)}, f32[5,72,1024]{2,1,0:T(8,128)S(1)}, u32[]{:S(2)}, u32[]{:S(2)}) collective-permute-start(f32[5,72,1024]{2,1,0:T(8,128)S(1)} %get-tuple-element.46), channel_id=1, source_target_pairs={{0,8},{8,0},{16,24},{24,16},{1,9},{9,1},{17,25},{25,17},{2,10},{10... | collective-permute-start | bytes 4423688 | tf_op jit(solution)/shard_map/ppermute | solution.py:443
  9.6 2.3 %shard_map.88 = (bf16[12,144,208]{2,1,0:T(8,128)(2,1)S(1)}, bf16[11,64,144]{2,1,0:T(8,128)(2,1)S(1)}) custom-call(f32[8,1664]{1,0:T(8,128)S(1)} %stack.31.entries, f32[72,1024]{1,0:T(8,128)S(1)} %collective-permute-done.unused), custom_call_target="tpu_custom_call" | custom-call | flops 30000001024 | bytes 10 | tf_op jit(solution)/shard_map/pallas_call | solution.py:481
  12.7 1.5 %collective-permute-start.4 = (bf16[1,56,1024]{2,1,0:T(8,128)(2,1)S(1)}, bf16[1,56,1024]{2,1,0:T(8,128)(2,1)S(1)}, u32[]{:S(2)}, u32[]{:S(2)}) collective-permute-start(bf16[1,56,1024]{2,1,0:T(8,128)(2,1)S(1)} %get-tuple-element.48.unused), channel_id=1, source_target_pairs={{0,16},{8,24},{16,0},{24,8},{1,17},{9,25},{17,1},{25,9},{2,18},{10... | collective-permute-start | bytes 344072 | tf_op jit(solution)/shard_map/ppermute | solution.py:446
  14.2 1.2 %shard_map.90 = (bf16[2,144,1024]{2,1,0:T(8,128)(2,1)S(1)}, bf16[2,56,1024]{2,1,0:T(8,128)(2,1)S(1)}) custom-call(f32[5,72,1024]{2,1,0:T(8,128)S(1)} %get-tuple-element.45.keep, f32[5,72,1024]{2,1,0:T(8,128)S(1)} %collective-permute-done.1.got.unused, f32[11,8,1024]{2,1,0:T(8,128)S(1)} %copy-done, bf16[11,64,144]{2,1,0:T(8,128)(2,1)S(1)} %get-tuple-element.47.send_table, ...), custom_call_target="tpu_custom_call" | custom-call | flops 17999998976 | bytes 10 | tf_op jit(solution)/shard_map/pallas_call | solution.py:507
  17.5 1.1 %shard_map.92 = (f32[1,144,1024]{2,1,0:T(8,128)S(1)}, bf16[1,144,1024]{2,1,0:T(8,128)(2,1)S(1)}) custom-call(bf16[1,144,1024]{2,1,0:T(8,128)(2,1)S(1)} %get-tuple-element.51.bent, bf16[1,56,1024]{2,1,0:T(8,128)(2,1)S(1)} %collective-permute-done.4.got, f32[11,8,1024]{2,1,0:T(8,128)S(1)} %copy-done, bf16[12,144,208]{2,1,0:T(8,128)(2,1)S(1)} %get-tuple-element.52.table, ...), custom_call_target="tpu_custom_call" | custom-call | flops 10000000000 | bytes 10 | tf_op jit(solution)/shard_map/pallas_call | solution.py:519
  19.2 1.5 %collective-permute-start.5 = (bf16[1,56,1024]{2,1,0:T(8,128)(2,1)S(1)}, bf16[1,56,1024]{2,1,0:T(8,128)(2,1)S(1)}, u32[]{:S(2)}, u32[]{:S(2)}) collective-permute-start(bf16[1,56,1024]{2,1,0:T(8,128)(2,1)S(1)} %get-tuple-element.55.unused), channel_id=1, source_target_pairs={{0,16},{8,24},{16,0},{24,8},{1,17},{9,25},{17,1},{25,9},{2,18},{10... | collective-permute-start | bytes 344072 | tf_op jit(solution)/shard_map/ppermute | solution.py:446
  21.5 1.5 %collective-permute-done.6.got = bf16[2,56,1024]{2,1,0:T(8,128)(2,1)S(1)} collective-permute-done((bf16[2,56,1024]{2,1,0:T(8,128)(2,1)S(1)}, bf16[2,56,1024]{2,1,0:T(8,128)(2,1)S(1)}, u32[]{:S(2)}, u32[]{:S(2)}) %collective-permute-start.6) | collective-permute-done | bytes 229408 | tf_op jit(solution)/shard_map/ppermute | solution.py:446
  23.0 2.0 %shard_map.95 = (f32[2,144,1024]{2,1,0:T(8,128)S(1)}, bf16[2,144,1024]{2,1,0:T(8,128)(2,1)S(1)}) custom-call(bf16[2,144,1024]{2,1,0:T(8,128)(2,1)S(1)} %get-tuple-element.56.bent, bf16[2,56,1024]{2,1,0:T(8,128)(2,1)S(1)} %collective-permute-done.6.got, f32[11,8,1024]{2,1,0:T(8,128)S(1)} %copy-done, bf16[12,144,208]{2,1,0:T(8,128)(2,1)S(1)} %get-tuple-element.52.table, ...), custom_call_target="tpu_custom_call" | custom-call | flops 20000000000 | bytes 10 | tf_op jit(solution)/shard_map/pallas_call | solution.py:519
  25.0 4.9 %collective-permute-start.7 = (bf16[2,144,1024]{2,1,0:T(8,128)(2,1)S(1)}, bf16[2,144,1024]{2,1,0:T(8,128)(2,1)S(1)}, u32[]{:S(2)}, u32[]{:S(2)}) collective-permute-start(bf16[2,144,1024]{2,1,0:T(8,128)(2,1)S(1)} %get-tuple-element.57.unused), channel_id=1, source_target_pairs={{0,8},{8,0},{16,24},{24,16},{1,9},{9,1},{17,25},{25,17},{2,10},{10... | collective-permute-start | bytes 1769480 | tf_op jit(solution)/shard_map/ppermute | solution.py:443
  29.9 1.1 %shard_map.96 = (f32[1,144,1024]{2,1,0:T(8,128)S(1)}, bf16[1,144,1024]{2,1,0:T(8,128)(2,1)S(1)}) custom-call(bf16[1,144,1024]{2,1,0:T(8,128)(2,1)S(1)} %get-tuple-element.54.bent, bf16[1,56,1024]{2,1,0:T(8,128)(2,1)S(1)} %collective-permute-done.5.got, f32[11,8,1024]{2,1,0:T(8,128)S(1)} %copy-done, bf16[12,144,208]{2,1,0:T(8,128)(2,1)S(1)} %get-tuple-element.52.table, ...), custom_call_target="tpu_custom_call" | custom-call | flops 10000000000 | bytes 10 | tf_op jit(solution)/shard_map/pallas_call | solution.py:519
  31.9 2.4 %shard_map.97 = (f32[4,144,1024]{2,1,0:T(8,128)S(1)}, bf16[2,144,1024]{2,1,0:T(8,128)(2,1)S(1)}, bf16[2,56,1024]{2,1,0:T(8,128)(2,1)S(1)}) custom-call(f32[1,144,1024]{2,1,0:T(8,128)S(1)} %get-tuple-element.58.row_zero, f32[1,144,1024]{2,1,0:T(8,128)S(1)} %get-tuple-element.59.row_one, f32[2,144,1024]{2,1,0:T(8,128)S(1)} %get-tuple-element.60.others, ...), custom_call_target="tpu_custom_call" | custom-call | flops 27000000512 | bytes 10 | tf_op jit(solution)/shard_map/pallas_call | solution.py:545
  34.9 1.2 %shard_map.98 = (f32[1,144,1024]{2,1,0:T(8,128)S(1)}, f32[1,144,1024]{2,1,0:T(8,128)S(1)}, f32[3,72,1024]{2,1,0:T(8,128)S(1)}, f32[3,72,1024]{2,1,0:T(8,128)S(1)}) custom-call(f32[1,144,1024]{2,1,0:T(8,128)S(1)} %get-tuple-element.58.row_zero, f32[1,144,1024]{2,1,0:T(8,128)S(1)} %get-tuple-element.59.row_one, f32[4,144,1024]{2,1,0:T(8,128)S(1)} %get-tuple-element.61.held), custom_call_target="tpu_custom_call" | custom-call | flops 30000001024 | bytes 10 | tf_op jit(solution)/shard_map/pallas_call | solution.py:548
  36.9 1.6 %collective-permute-start.13 = (bf16[1,56,1024]{2,1,0:T(8,128)(2,1)S(1)}, bf16[1,56,1024]{2,1,0:T(8,128)(2,1)S(1)}, u32[]{:S(2)}, u32[]{:S(2)}) collective-permute-start(bf16[1,56,1024]{2,1,0:T(8,128)(2,1)S(1)} %get-tuple-element.72), channel_id=1, source_target_pairs={{0,16},{8,24},{16,0},{24,8},{1,17},{9,25},{17,1},{25,9},{2,18},{10... | collective-permute-start | bytes 344072 | tf_op jit(solution)/shard_map/ppermute | solution.py:446
  38.5 3.9 %collective-permute-start.12 = (f32[3,72,1024]{2,1,0:T(8,128)S(1)}, f32[3,72,1024]{2,1,0:T(8,128)S(1)}, u32[]{:S(2)}, u32[]{:S(2)}) collective-permute-start(f32[3,72,1024]{2,1,0:T(8,128)S(1)} %get-tuple-element.70), channel_id=1, source_target_pairs={{0,8},{8,0},{16,24},{24,16},{1,9},{9,1},{17,25},{25,17},{2,10},{10... | collective-permute-start | bytes 2654216 | tf_op jit(solution)/shard_map/ppermute | solution.py:443
  43.2 1.7 %collective-permute-start.14 = (bf16[1,56,1024]{2,1,0:T(8,128)(2,1)S(1)}, bf16[1,56,1024]{2,1,0:T(8,128)(2,1)S(1)}, u32[]{:S(2)}, u32[]{:S(2)}) collective-permute-start(bf16[1,56,1024]{2,1,0:T(8,128)(2,1)S(1)} %get-tuple-element.73.unused), channel_id=1, source_target_pairs={{0,16},{8,24},{16,0},{24,8},{1,17},{9,25},{17,1},{25,9},{2,18},{10... | collective-permute-start | bytes 344072 | tf_op jit(solution)/shard_map/ppermute | solution.py:446
  45.2 1.1 %shard_map.101 = (f32[1,144,1024]{2,1,0:T(8,128)S(1)}, bf16[1,144,1024]{2,1,0:T(8,128)(2,1)S(1)}) custom-call(bf16[1,144,1024]{2,1,0:T(8,128)(2,1)S(1)} %get-tuple-element.71.bent, bf16[1,56,1024]{2,1,0:T(8,128)(2,1)S(1)} %collective-permute-done.13.got, f32[11,8,1024]{2,1,0:T(8,128)S(1)} %copy-done, bf16[12,144,208]{2,1,0:T(8,128)(2,1)S(1)} %get-tuple-element.52.table, ...), custom_call_target="tpu_custom_call" | custom-call | flops 10000000000 | bytes 10 | tf_op jit(solution)/shard_map/pallas_call | solution.py:519
  47.0 2.0 %shard_map.103 = (f32[2,144,1024]{2,1,0:T(8,128)S(1)}, bf16[1,144,1024]{2,1,0:T(8,128)(2,1)S(1)}) custom-call(bf16[2,144,1024]{2,1,0:T(8,128)(2,1)S(1)} %get-tuple-element.77.bent, bf16[2,56,1024]{2,1,0:T(8,128)(2,1)S(1)} %collective-permute-done.10.unused.got, f32[11,8,1024]{2,1,0:T(8,128)S(1)} %copy-done, ...), custom_call_target="tpu_custom_call" | custom-call | flops 20000000000 | bytes 10 | tf_op jit(solution)/shard_map/pallas_call | solution.py:519
  49.1 6.1 %collective-permute-start.15 = (bf16[1,144,1024]{2,1,0:T(8,128)(2,1)S(1)}, bf16[1,144,1024]{2,1,0:T(8,128)(2,1)S(1)}, u32[]{:S(2)}, u32[]{:S(2)}) collective-permute-start(bf16[1,144,1024]{2,1,0:T(8,128)(2,1)S(1)} %get-tuple-element.79), channel_id=1, source_target_pairs={{0,8},{8,0},{16,24},{24,16},{1,9},{9,1},{17,25},{25,17},{2,10},{10... | collective-permute-start | bytes 884744 | tf_op jit(solution)/shard_map/ppermute | solution.py:443
  55.2 1.1 %shard_map.102.one = f32[1,144,1024]{2,1,0:T(8,128)S(1)} custom-call(bf16[1,144,1024]{2,1,0:T(8,128)(2,1)S(1)} %get-tuple-element.75.bent, bf16[1,56,1024]{2,1,0:T(8,128)(2,1)S(1)} %collective-permute-done.14.got, f32[11,8,1024]{2,1,0:T(8,128)S(1)} %copy-done, bf16[12,144,208]{2,1,0:T(8,128)(2,1)S(1)} %get-tuple-element.52.table, ...), custom_call_target="tpu_custom_call" | custom-call | flops 10000000000 | bytes 10 | tf_op jit(solution)/shard_map/pallas_call | solution.py:519
  56.4 1.3 %shard_map.104 = (f32[4,72,1024]{2,1,0:T(8,128)S(1)}, f32[4,72,1024]{2,1,0:T(8,128)S(1)}) custom-call(f32[1,144,1024]{2,1,0:T(8,128)S(1)} %get-tuple-element.74.zero, f32[1,144,1024]{2,1,0:T(8,128)S(1)} %shard_map.102.one, f32[2,144,1024]{2,1,0:T(8,128)S(1)} %get-tuple-element.78.inners, bf16[1,144,1024]{2,1,0:T(8,128)(2,1)S(1)} %collective-permute-done.15.inner), custom_call_target="tpu_custom_call" | custom-call | flops 24999999488 | bytes 10 | tf_op jit(solution)/shard_map/pallas_call | solution.py:568
  58.1 1.5 %shard_map.105 = (f32[72,8,1024]{2,1,0:T(8,128)}, s32[8,128]{1,0:T(8,128)S(1)}) custom-call(f32[1,72,1024]{2,1,0:T(8,128)S(1)} %get-tuple-element.67.keep_zero, f32[3,72,1024]{2,1,0:T(8,128)S(1)} %get-tuple-element.68.keep, f32[1,72,1024]{2,1,0:T(8,128)S(1)} %collective-permute-done.11.got_zero, f32[3,72,1024]{2,1,0:T(8,128)S(1)} %collective-permute-done.12.got, ...), custom_call_target="tpu_custom_call" | custom-call | flops 19000000512 | bytes 10 | tf_op jit(solution)/shard_map/pallas_call | solution.py:574
  60.0 1.2 %collective-permute-done.18.far_halo = bf16[72,1024]{1,0:T(8,128)(2,1)S(1)} collective-permute-done((bf16[72,1024]{1,0:T(8,128)(2,1)S(1)}, bf16[72,1024]{1,0:T(8,128)(2,1)S(1)}, u32[]{:S(2)}, u32[]{:S(2)}) %collective-permute-start.18) | collective-permute-done | bytes 147488 | tf_op jit(solution)/shard_map/ppermute | solution.py:443
  61.2 1.5 %shard_map.107 = f32[72,8,1024]{2,1,0:T(8,128)} custom-call(f32[4,72,1024]{2,1,0:T(8,128)S(1)} %get-tuple-element.80.unused.keep, f32[4,72,1024]{2,1,0:T(8,128)S(1)} %collective-permute-done.16.got, f32[72,1024]{1,0:T(8,128)S(1)} %get-tuple-element.84.line, bf16[72,1024]{1,0:T(8,128)(2,1)S(1)} %collective-permute-done.18.far_halo), custom_call_target="tpu_custom_call" | custom-call | flops 19000000512 | bytes 10 | tf_op jit(solution)/shard_map/pallas_call | solution.py:581
  (67 shorter events, 12.0 us)
Async XLA Ops:
  0.6 4.1 %copy-start.1 = (f32[72,8,1024]{2,1,0:T(8,128)S(1)}, f32[72,8,1024]{2,1,0:T(8,128)}, u32[]{:S(2)}) copy-start(f32[72,8,1024]{2,1,0:T(8,128)} %field.3) | copy-start | bytes 7077892
  0.7 3.5 %copy-start.3 = (s32[1606]{0:T(1024)S(1)}, s32[1606]{0:T(1024)}, u32[]{:S(2)}) copy-start(s32[1606]{0:T(1024)} %param.10) | copy-start | bytes 19276
  0.7 3.5 %copy-start.4 = (s32[1606]{0:T(1024)S(1)}, s32[1606]{0:T(1024)}, u32[]{:S(2)}) copy-start(s32[1606]{0:T(1024)} %param.11) | copy-start | bytes 19276
  0.7 3.5 %copy-start.5 = (bf16[1606]{0:T(1024)(128)(2,1)S(1)}, bf16[1606]{0:T(1024)(128)(2,1)}, u32[]{:S(2)}) copy-start(bf16[1606]{0:T(1024)(128)(2,1)} %param.12) | copy-start | bytes 9640
  2.8 1.9 %collective-permute-start = (f32[72,1024]{1,0:T(8,128)}, f32[72,1024]{1,0:T(8,128)S(1)}, u32[]{:S(2)}, u32[]{:S(2)}) collective-permute-start(f32[72,1024]{1,0:T(8,128)} %get-tuple-element.44), channel_id=1, source_target_pairs={{0,8},{8,0},{16,24},{24,16},{1,9},{9,1},{17,25},{25,17},{2,10},{10... | collective-permute-start | bytes 884744 | tf_op jit(solution)/shard_map/ppermute | solution.py:443
  3.3 15.3 %collective-permute-start.3 = (f32[72,1024]{1,0:T(8,128)}, f32[72,1024]{1,0:T(8,128)S(1)}, u32[]{:S(2)}, u32[]{:S(2)}) collective-permute-start(f32[72,1024]{1,0:T(8,128)} %get-tuple-element.50), channel_id=1, source_target_pairs={{8,1},{1,8},{9,2},{2,9},{10,3},{3,10},{11,4},{4,11},{12,5},{5,12},... | collective-permute-start | bytes 884744 | tf_op jit(solution)/shard_map/ppermute | solution.py:449
  5.3 6.6 %copy-start = (f32[11,8,1024]{2,1,0:T(8,128)S(1)}, f32[11,8,1024]{2,1,0:T(8,128)}, u32[]{:S(2)}) copy-start(f32[11,8,1024]{2,1,0:T(8,128)} %stiff.23) | copy-start | bytes 1081348
  5.3 6.5 %collective-permute-start.1 = (f32[5,72,1024]{2,1,0:T(8,128)S(1)}, f32[5,72,1024]{2,1,0:T(8,128)S(1)}, u32[]{:S(2)}, u32[]{:S(2)}) collective-permute-start(f32[5,72,1024]{2,1,0:T(8,128)S(1)} %get-tuple-element.46), channel_id=1, source_target_pairs={{0,8},{8,0},{16,24},{24,16},{1,9},{9,1},{17,25},{25,17},{2,10},{10... | collective-permute-start | bytes 4423688 | tf_op jit(solution)/shard_map/ppermute | solution.py:443
  8.9 9.8 %collective-permute-start.2 = (f32[72,1024]{1,0:T(8,128)S(1)}, f32[72,1024]{1,0:T(8,128)S(1)}, u32[]{:S(2)}, u32[]{:S(2)}) collective-permute-start(f32[72,1024]{1,0:T(8,128)S(1)} %collective-permute-done.unused), channel_id=1, source_target_pairs={{8,1},{1,8},{9,2},{2,9},{10,3},{3,10},{11,4},{4,11},{12,5},{5,12},... | collective-permute-start | bytes 884744 | tf_op jit(solution)/shard_map/ppermute | solution.py:449
  12.7 4.9 %collective-permute-start.4 = (bf16[1,56,1024]{2,1,0:T(8,128)(2,1)S(1)}, bf16[1,56,1024]{2,1,0:T(8,128)(2,1)S(1)}, u32[]{:S(2)}, u32[]{:S(2)}) collective-permute-start(bf16[1,56,1024]{2,1,0:T(8,128)(2,1)S(1)} %get-tuple-element.48.unused), channel_id=1, source_target_pairs={{0,16},{8,24},{16,0},{24,8},{1,17},{9,25},{17,1},{25,9},{2,18},{10... | collective-permute-start | bytes 344072 | tf_op jit(solution)/shard_map/ppermute | solution.py:446
  15.5 7.5 %collective-permute-start.6 = (bf16[2,56,1024]{2,1,0:T(8,128)(2,1)S(1)}, bf16[2,56,1024]{2,1,0:T(8,128)(2,1)S(1)}, u32[]{:S(2)}, u32[]{:S(2)}) collective-permute-start(bf16[2,56,1024]{2,1,0:T(8,128)(2,1)S(1)} %get-tuple-element.49.unused), channel_id=1, source_target_pairs={{0,16},{8,24},{16,0},{24,8},{1,17},{9,25},{17,1},{25,9},{2,18},{10... | collective-permute-start | bytes 688136 | tf_op jit(solution)/shard_map/ppermute | solution.py:446
  19.2 10.7 %collective-permute-start.5 = (bf16[1,56,1024]{2,1,0:T(8,128)(2,1)S(1)}, bf16[1,56,1024]{2,1,0:T(8,128)(2,1)S(1)}, u32[]{:S(2)}, u32[]{:S(2)}) collective-permute-start(bf16[1,56,1024]{2,1,0:T(8,128)(2,1)S(1)} %get-tuple-element.55.unused), channel_id=1, source_target_pairs={{0,16},{8,24},{16,0},{24,8},{1,17},{9,25},{17,1},{25,9},{2,18},{10... | collective-permute-start | bytes 344072 | tf_op jit(solution)/shard_map/ppermute | solution.py:446
  20.8 15.3 %collective-permute-start.9 = (bf16[1,144,1024]{2,1,0:T(8,128)(2,1)S(1)}, bf16[1,144,1024]{2,1,0:T(8,128)(2,1)S(1)}, u32[]{:S(2)}, u32[]{:S(2)}) collective-permute-start(bf16[1,144,1024]{2,1,0:T(8,128)(2,1)S(1)} %shard_map.94.unused), channel_id=1, source_target_pairs={{8,1},{1,8},{9,2},{2,9},{10,3},{3,10},{11,4},{4,11},{12,5},{5,12},... | collective-permute-start | bytes 884744 | tf_op jit(solution)/shard_map/ppermute | solution.py:449
  25.0 6.9 %collective-permute-start.7 = (bf16[2,144,1024]{2,1,0:T(8,128)(2,1)S(1)}, bf16[2,144,1024]{2,1,0:T(8,128)(2,1)S(1)}, u32[]{:S(2)}, u32[]{:S(2)}) collective-permute-start(bf16[2,144,1024]{2,1,0:T(8,128)(2,1)S(1)} %get-tuple-element.57.unused), channel_id=1, source_target_pairs={{0,8},{8,0},{16,24},{24,16},{1,9},{9,1},{17,25},{25,17},{2,10},{10... | collective-permute-start | bytes 1769480 | tf_op jit(solution)/shard_map/ppermute | solution.py:443
  31.0 5.1 %collective-permute-start.8 = (bf16[1,144,1024]{2,1,0:T(8,128)(2,1)S(1)}, bf16[1,144,1024]{2,1,0:T(8,128)(2,1)S(1)}, u32[]{:S(2)}, u32[]{:S(2)}) collective-permute-start(bf16[1,144,1024]{2,1,0:T(8,128)(2,1)S(1)} %get-tuple-element.64), channel_id=1, source_target_pairs={{8,1},{1,8},{9,2},{2,9},{10,3},{3,10},{11,4},{4,11},{12,5},{5,12},... | collective-permute-start | bytes 884744 | tf_op jit(solution)/shard_map/ppermute | solution.py:449
  34.3 8.1 %collective-permute-start.10 = (bf16[2,56,1024]{2,1,0:T(8,128)(2,1)S(1)}, bf16[2,56,1024]{2,1,0:T(8,128)(2,1)S(1)}, u32[]{:S(2)}, u32[]{:S(2)}) collective-permute-start(bf16[2,56,1024]{2,1,0:T(8,128)(2,1)S(1)} %get-tuple-element.66), channel_id=1, source_target_pairs={{0,16},{8,24},{16,0},{24,8},{1,17},{9,25},{17,1},{25,9},{2,18},{10... | collective-permute-start | bytes 688136 | tf_op jit(solution)/shard_map/ppermute | solution.py:446
  36.9 8.3 %collective-permute-start.13 = (bf16[1,56,1024]{2,1,0:T(8,128)(2,1)S(1)}, bf16[1,56,1024]{2,1,0:T(8,128)(2,1)S(1)}, u32[]{:S(2)}, u32[]{:S(2)}) collective-permute-start(bf16[1,56,1024]{2,1,0:T(8,128)(2,1)S(1)} %get-tuple-element.72), channel_id=1, source_target_pairs={{0,16},{8,24},{16,0},{24,8},{1,17},{9,25},{17,1},{25,9},{2,18},{10... | collective-permute-start | bytes 344072 | tf_op jit(solution)/shard_map/ppermute | solution.py:446
  38.5 19.6 %collective-permute-start.12 = (f32[3,72,1024]{2,1,0:T(8,128)S(1)}, f32[3,72,1024]{2,1,0:T(8,128)S(1)}, u32[]{:S(2)}, u32[]{:S(2)}) collective-permute-start(f32[3,72,1024]{2,1,0:T(8,128)S(1)} %get-tuple-element.70), channel_id=1, source_target_pairs={{0,8},{8,0},{16,24},{24,16},{1,9},{9,1},{17,25},{25,17},{2,10},{10... | collective-permute-start | bytes 2654216 | tf_op jit(solution)/shard_map/ppermute | solution.py:443
  43.2 12.0 %collective-permute-start.14 = (bf16[1,56,1024]{2,1,0:T(8,128)(2,1)S(1)}, bf16[1,56,1024]{2,1,0:T(8,128)(2,1)S(1)}, u32[]{:S(2)}, u32[]{:S(2)}) collective-permute-start(bf16[1,56,1024]{2,1,0:T(8,128)(2,1)S(1)} %get-tuple-element.73.unused), channel_id=1, source_target_pairs={{0,16},{8,24},{16,0},{24,8},{1,17},{9,25},{17,1},{25,9},{2,18},{10... | collective-permute-start | bytes 344072 | tf_op jit(solution)/shard_map/ppermute | solution.py:446
  44.9 13.2 %collective-permute-start.11 = (f32[1,72,1024]{2,1,0:T(8,128)S(1)}, f32[1,72,1024]{2,1,0:T(8,128)S(1)}, u32[]{:S(2)}, u32[]{:S(2)}) collective-permute-start(f32[1,72,1024]{2,1,0:T(8,128)S(1)} %get-tuple-element.69), channel_id=1, source_target_pairs={{0,8},{8,0},{16,24},{24,16},{1,9},{9,1},{17,25},{25,17},{2,10},{10... | collective-permute-start | bytes 884744 | tf_op jit(solution)/shard_map/ppermute | solution.py:443
  46.4 13.3 %collective-permute-start.17 = (bf16[1,144,1024]{2,1,0:T(8,128)(2,1)S(1)}, bf16[1,144,1024]{2,1,0:T(8,128)(2,1)S(1)}, u32[]{:S(2)}, u32[]{:S(2)}) collective-permute-start(bf16[1,144,1024]{2,1,0:T(8,128)(2,1)S(1)} %get-tuple-element.76.unused), channel_id=1, source_target_pairs={{8,1},{1,8},{9,2},{2,9},{10,3},{3,10},{11,4},{4,11},{12,5},{5,12},... | collective-permute-start | bytes 884744 | tf_op jit(solution)/shard_map/ppermute | solution.py:449
  49.1 7.3 %collective-permute-start.15 = (bf16[1,144,1024]{2,1,0:T(8,128)(2,1)S(1)}, bf16[1,144,1024]{2,1,0:T(8,128)(2,1)S(1)}, u32[]{:S(2)}, u32[]{:S(2)}) collective-permute-start(bf16[1,144,1024]{2,1,0:T(8,128)(2,1)S(1)} %get-tuple-element.79), channel_id=1, source_target_pairs={{0,8},{8,0},{16,24},{24,16},{1,9},{9,1},{17,25},{25,17},{2,10},{10... | collective-permute-start | bytes 884744 | tf_op jit(solution)/shard_map/ppermute | solution.py:443
  57.7 3.5 %collective-permute-start.16 = (f32[4,72,1024]{2,1,0:T(8,128)S(1)}, f32[4,72,1024]{2,1,0:T(8,128)S(1)}, u32[]{:S(2)}, u32[]{:S(2)}) collective-permute-start(f32[4,72,1024]{2,1,0:T(8,128)S(1)} %get-tuple-element.82), channel_id=1, source_target_pairs={{0,8},{8,0},{16,24},{24,16},{1,9},{9,1},{17,25},{25,17},{2,10},{10... | collective-permute-start | bytes 3538952 | tf_op jit(solution)/shard_map/ppermute | solution.py:443
  59.8 1.4 %collective-permute-start.18 = (bf16[72,1024]{1,0:T(8,128)(2,1)S(1)}, bf16[72,1024]{1,0:T(8,128)(2,1)S(1)}, u32[]{:S(2)}, u32[]{:S(2)}) collective-permute-start(bf16[72,1024]{1,0:T(8,128)(2,1)S(1)} %get-tuple-element.85), channel_id=1, source_target_pairs={{0,8},{8,0},{16,24},{24,16},{1,9},{9,1},{17,25},{25,17},{2,10},{10... | collective-permute-start | bytes 442376 | tf_op jit(solution)/shard_map/ppermute | solution.py:443
  (2 other events, 6.8 us)
